TPU v7x, 32 devices: a whole 2x2x4 slice. The times are simulated.
32 devices in a mesh: ep: 8 (over y, x, core), tp: 4 (over z).
Axes of the slice: x: 2, y: 2, z: 4, core: 2. Of those that a mesh axis runs over, the one named last changes fastest.
Arguments:
- inputs: bfloat16 [8192, 1536], P('ep'), may hold values from -6 to 6
- routes: int32 [8192, 4], P('ep'), may hold values from 0 to 7, all different within a row; in each aligned block of 1024 rows (0 to 1023, 1024 to 2047, ...) at most 640 rows name the same one
- norm_gain: float32 [1536], replicated, may hold values from 0.1 to 1.9
- query_weight: bfloat16 [1536, 1536], P(None, 'tp'), may hold values from -0.15625 to 0.15625
- key_weight: bfloat16 [1536, 512], P(None, 'tp'), may hold values from -0.15625 to 0.15625
- value_weight: bfloat16 [1536, 512], P(None, 'tp'), may hold values from -0.15625 to 0.15625
- output_weight: bfloat16 [1536, 1536], P('tp'), may hold values from -0.875 to 0.875
- mixer_gain: float32 [1536], replicated, may hold values from 0.1 to 1.9
- router_weight: bfloat16 [1536, 8], replicated, may hold values from -0.078125 to 0.078125
- gate_weight: bfloat16 [8, 1536, 512], P('ep', None, 'tp'), may hold values from -0.15625 to 0.15625
- up_weight: bfloat16 [8, 1536, 512], P('ep', None, 'tp'), may hold values from -0.15625 to 0.15625
- down_weight: bfloat16 [8, 512, 1536], P('ep', 'tp'), may hold values from -1 to 1
- cotangent: bfloat16 [8192, 1536], P('ep'), may hold values from -6 to 6
Outputs:
- result: bfloat16 [8192, 1536], P('ep')
- grad_inputs: bfloat16 [8192, 1536], P('ep')
- grad_norm_gain: float32 [1536], replicated
- grad_query_weight: float32 [1536, 1536], P(None, 'tp')
- grad_key_weight: float32 [1536, 512], P(None, 'tp')
- grad_value_weight: float32 [1536, 512], P(None, 'tp')
- grad_output_weight: float32 [1536, 1536], P('tp')
- grad_mixer_gain: float32 [1536], replicated
- grad_router_weight: float32 [1536, 8], replicated
- grad_gate_weight: float32 [8, 1536, 512], P('ep', None, 'tp')
- grad_up_weight: float32 [8, 1536, 512], P('ep', None, 'tp')
- grad_down_weight: float32 [8, 512, 1536], P('ep', 'tp')
Inputs may be any that keep to these rules, and one draw needn't show every extreme that they name: `routes`: each row names 4 different experts. Among the 1024 rows of one index of ep no expert is named more than 640 times, and in every draw some expert is named exactly 640 times by the rows of some index; every expert is named by some row.
All inputs are finite; a program needn't handle non-finite values.
Results may differ from a plain program's by a relative error of at most 0.025.
Values may be sent and summed in bfloat16 or wider, within the bound.
No kernel may reach another device: no remote copies, remote signals or barrier semaphores. Data moves between devices by JAX's collectives and lax.ppermute only.
A program may use at most 384 MiB of HBM per device.

v0:
```python
import jax
import jax.numpy as jnp
from jax import lax
from jax.sharding import PartitionSpec as P

HD = 64
LEN = 1024


EPS = 1e-06
MASKED = -1e30


def rotary_tables(positions, depth):
    half = depth // 2
    freqs = 10000.0 ** (-jnp.arange(half, dtype=jnp.float32) * 2.0 / depth)
    angles = positions[:, None] * freqs[None, :]
    return (jnp.cos(angles), jnp.sin(angles))


def rotate(values, cosine, sine):
    half = values.shape[-1] // 2
    first = values[..., :half]
    second = values[..., half:]
    cos_b = cosine[:, None, :]
    sin_b = sine[:, None, :]
    return jnp.concatenate(
        [first * cos_b - second * sin_b, second * cos_b + first * sin_b], axis=-1
    )


def unrotate(grads, cosine, sine):
    half = grads.shape[-1] // 2
    first = grads[..., :half]
    second = grads[..., half:]
    cos_b = cosine[:, None, :]
    sin_b = sine[:, None, :]
    return jnp.concatenate(
        [first * cos_b + second * sin_b, second * cos_b - first * sin_b], axis=-1
    )


def block_scores(query_block, keys, start, scale):
    scores = (
        jnp.einsum("qgrd,kgd->grqk", query_block, keys, preferred_element_type=jnp.float32) * scale
    )
    rows_at = start + jnp.arange(query_block.shape[0])[:, None]
    cols_at = jnp.arange(keys.shape[0])[None, :]
    return jnp.where(rows_at >= cols_at, scores, MASKED)


def attention_forward(query, key, value, scale):
    tokens, heads, depth = query.shape
    groups = key.shape[1]
    repeat = heads // groups
    seqs = tokens // LEN
    block = min(512, LEN)
    count = LEN // block
    query_seq = query.reshape(seqs, count, block, groups, repeat, depth)
    key_seq = key.reshape(seqs, LEN, groups, depth)
    value_seq = value.reshape(seqs, LEN, groups, depth)

    def one_sequence(pieces):
        query_blocks, keys, values = pieces

        def one_block(item):
            query_block, index = item
            scores = block_scores(query_block, keys, index * block, scale)
            peak = jnp.max(scores, axis=-1, keepdims=True)
            weights = jnp.exp(scores - peak)
            totals = jnp.sum(weights, axis=-1, keepdims=True)
            probs = weights / totals
            mixed = jnp.einsum(
                "grqk,kgd->qgrd",
                probs.astype(jnp.bfloat16),
                values,
                preferred_element_type=jnp.float32,
            )
            return (mixed.astype(jnp.bfloat16), peak + jnp.log(totals))

        return lax.map(one_block, (query_blocks, jnp.arange(count)))

    mixed, log_totals = lax.map(one_sequence, (query_seq, key_seq, value_seq))
    return (mixed.reshape(tokens, heads * depth), log_totals)


def attention_backward(query, key, value, log_totals, grad_mixed, scale):
    tokens, heads, depth = query.shape
    groups = key.shape[1]
    repeat = heads // groups
    seqs = tokens // LEN
    block = min(512, LEN)
    count = LEN // block
    query_seq = query.reshape(seqs, count, block, groups, repeat, depth)
    key_seq = key.reshape(seqs, LEN, groups, depth)
    value_seq = value.reshape(seqs, LEN, groups, depth)
    grad_seq = grad_mixed.reshape(seqs, count, block, groups, repeat, depth)

    def one_sequence(pieces):
        query_blocks, keys, values, total_blocks, grad_blocks = pieces

        def one_block(carry, item):
            query_block, total_block, grad_block, index = item
            scores = block_scores(query_block, keys, index * block, scale)
            probs = jnp.exp(scores - total_block)
            grad_probs = jnp.einsum(
                "qgrd,kgd->grqk", grad_block, values, preferred_element_type=jnp.float32
            )
            inner = jnp.sum(probs * grad_probs, axis=-1, keepdims=True)
            grad_scores = (probs * (grad_probs - inner)).astype(jnp.bfloat16)
            grad_query = (
                jnp.einsum("grqk,kgd->qgrd", grad_scores, keys, preferred_element_type=jnp.float32)
                * scale
            )
            grad_keys = (
                carry[0]
                + jnp.einsum(
                    "grqk,qgrd->kgd", grad_scores, query_block, preferred_element_type=jnp.float32
                )
                * scale
            )
            grad_values = carry[1] + jnp.einsum(
                "grqk,qgrd->kgd",
                probs.astype(jnp.bfloat16),
                grad_block,
                preferred_element_type=jnp.float32,
            )
            return ((grad_keys, grad_values), grad_query)

        zeros = jnp.zeros(keys.shape, jnp.float32)
        (grad_keys, grad_values), grad_queries = lax.scan(
            one_block, (zeros, zeros), (query_blocks, total_blocks, grad_blocks, jnp.arange(count))
        )
        return (grad_queries, grad_keys, grad_values)

    grad_query, grad_key, grad_value = lax.map(
        one_sequence, (query_seq, key_seq, value_seq, log_totals, grad_seq)
    )
    return (
        grad_query.reshape(tokens, heads, depth),
        grad_key.reshape(tokens, groups, depth),
        grad_value.reshape(tokens, groups, depth),
    )


def slot_places(routes, experts, capacity, offset):
    tokens, top = routes.shape
    flat_routes = routes.reshape(-1)
    onehot = (flat_routes[:, None] == jnp.arange(experts, dtype=jnp.int32)[None, :]).astype(
        jnp.int32
    )
    before = jnp.cumsum(onehot, axis=0) - onehot
    slots = jnp.sum(before * onehot, axis=1).reshape(tokens, top)
    local = slots - offset
    valid = (local >= 0) & (local < capacity)
    places = jnp.where(valid, routes * capacity + local, experts * capacity)
    return (places, valid)


def slot_owners(places, gates, total):
    tokens, top = places.shape
    owner_ids = jnp.broadcast_to(jnp.arange(tokens, dtype=jnp.int32)[:, None], (tokens, top))
    owners = (
        jnp.full((total,), tokens, jnp.int32)
        .at[places.reshape(-1)]
        .set(owner_ids.reshape(-1), mode="drop")
    )
    slot_gates = (
        jnp.zeros((total,), jnp.float32).at[places.reshape(-1)].set(gates.reshape(-1), mode="drop")
    )
    return (owners, slot_gates)


def gather_owned(rows, owners):
    padded = jnp.concatenate([rows, jnp.zeros((1, rows.shape[1]), rows.dtype)], axis=0)
    return jnp.take(padded, owners, axis=0)


def take_rows(flat, places, valid, index):
    picked = jnp.take(flat, jnp.minimum(places[:, index], flat.shape[0] - 1), axis=0)
    return picked.astype(jnp.float32) * valid[:, index, None].astype(jnp.float32)


def body(
    inputs,
    routes,
    norm_gain,
    query_weight,
    key_weight,
    value_weight,
    output_weight,
    mixer_gain,
    router_weight,
    gate_weight,
    up_weight,
    down_weight,
    cotangent,
):
    tokens, width = inputs.shape
    experts = router_weight.shape[1]
    top = routes.shape[1]
    tp_size = lax.axis_size("tp")
    capacity = tp_size * ((tokens * top * 5 + 16 * experts - 1) // (16 * experts))
    scale = HD ** (-0.5)
    heads_local = query_weight.shape[1] // HD
    groups_local = key_weight.shape[1] // HD
    inputs32 = inputs.astype(jnp.float32)
    inverse_one = lax.rsqrt(jnp.mean(inputs32 * inputs32, axis=-1, keepdims=True) + EPS)
    unit_one = inputs32 * inverse_one
    normed = (unit_one * norm_gain).astype(jnp.bfloat16)
    query_raw = jnp.dot(normed, query_weight, preferred_element_type=jnp.float32)
    key_raw = jnp.dot(normed, key_weight, preferred_element_type=jnp.float32)
    value_raw = jnp.dot(normed, value_weight, preferred_element_type=jnp.float32)
    positions = (jnp.arange(tokens) % LEN).astype(jnp.float32)
    cosine, sine = rotary_tables(positions, HD)
    query = rotate(query_raw.reshape(tokens, heads_local, HD), cosine, sine).astype(jnp.bfloat16)
    key = rotate(key_raw.reshape(tokens, groups_local, HD), cosine, sine).astype(jnp.bfloat16)
    value = value_raw.reshape(tokens, groups_local, HD).astype(jnp.bfloat16)
    mixed, log_totals = attention_forward(query, key, value, scale)
    branch = jnp.dot(mixed, output_weight, preferred_element_type=jnp.float32)
    attended = inputs32 + lax.psum(branch.astype(jnp.bfloat16), "tp").astype(jnp.float32)
    inverse_two = lax.rsqrt(jnp.mean(attended * attended, axis=-1, keepdims=True) + EPS)
    unit_two = attended * inverse_two
    routed_in = (unit_two * mixer_gain).astype(jnp.bfloat16)
    logits = jnp.dot(routed_in, router_weight, preferred_element_type=jnp.float32)
    picked = jnp.take_along_axis(logits, routes, axis=1)
    gates = jax.nn.softmax(picked, axis=-1)
    places_all, valid_all = slot_places(routes, experts, capacity, 0)
    owners, slot_gates = slot_owners(places_all, gates, experts * capacity)
    send_buffer = gather_owned(routed_in, owners).reshape(experts, capacity, width)
    arrived = lax.all_to_all(send_buffer, "ep", split_axis=0, concat_axis=0, tiled=True)
    sources = arrived.shape[0]
    pieces = 4
    per_piece = sources * capacity // pieces
    arrived_rows = arrived.reshape(pieces, per_piece, width)
    gate_matrix = gate_weight[0]
    up_matrix = up_weight[0]
    down_matrix = down_weight[0]

    def expert_forward(rows):
        gate_vals = jnp.dot(rows, gate_matrix, preferred_element_type=jnp.float32)
        up_vals = jnp.dot(rows, up_matrix, preferred_element_type=jnp.float32)
        hidden = (jax.nn.silu(gate_vals) * up_vals).astype(jnp.bfloat16)
        share = jnp.dot(hidden, down_matrix, preferred_element_type=jnp.float32).astype(
            jnp.bfloat16
        )
        return (gate_vals, up_vals, hidden, share)

    gate_vals, up_vals, hidden, shares = lax.map(expert_forward, arrived_rows)
    shares = shares.reshape(sources, capacity, width)
    returned = lax.all_to_all(shares, "ep", split_axis=0, concat_axis=0, tiled=True)
    places, valid = (places_all, valid_all)
    flat_returned = returned.reshape(-1, width)
    grad_top = cotangent.astype(jnp.float32)
    combined = jnp.zeros((tokens, width), jnp.float32)
    gate_terms = []
    for index in range(top):
        fetched = take_rows(flat_returned, places, valid, index)
        combined = combined + gates[:, index, None] * fetched
        gate_terms.append(jnp.sum(grad_top * fetched, axis=-1))
    grad_gate_part = jnp.stack(gate_terms, axis=1)
    combined = lax.psum(combined.astype(jnp.bfloat16), "tp").astype(jnp.float32)
    result = (attended + combined).astype(jnp.bfloat16)
    grad_buffer = (
        (gather_owned(grad_top, owners) * slot_gates[:, None])
        .astype(jnp.bfloat16)
        .reshape(experts, capacity, width)
    )
    grad_arrived = lax.all_to_all(grad_buffer, "ep", split_axis=0, concat_axis=0, tiled=True)

    def expert_backward(carry, item):
        rows, gate_block, up_block, hidden_block, grad_rows = item
        sigma = jax.nn.sigmoid(gate_block)
        active = gate_block * sigma
        grad_hidden = jnp.dot(grad_rows, down_matrix.T, preferred_element_type=jnp.float32)
        grad_gate_vals = (
            grad_hidden * up_block * sigma * (1.0 + gate_block * (1.0 - sigma))
        ).astype(jnp.bfloat16)
        grad_up_vals = (grad_hidden * active).astype(jnp.bfloat16)
        grad_gate_w = carry[0] + jnp.dot(rows.T, grad_gate_vals, preferred_element_type=jnp.float32)
        grad_up_w = carry[1] + jnp.dot(rows.T, grad_up_vals, preferred_element_type=jnp.float32)
        grad_down_w = carry[2] + jnp.dot(
            hidden_block.T, grad_rows, preferred_element_type=jnp.float32
        )
        grad_in = jnp.dot(
            grad_gate_vals, gate_matrix.T, preferred_element_type=jnp.float32
        ) + jnp.dot(grad_up_vals, up_matrix.T, preferred_element_type=jnp.float32)
        return ((grad_gate_w, grad_up_w, grad_down_w), grad_in.astype(jnp.bfloat16))

    start_carry = (
        jnp.zeros(gate_matrix.shape, jnp.float32),
        jnp.zeros(up_matrix.shape, jnp.float32),
        jnp.zeros(down_matrix.shape, jnp.float32),
    )
    (grad_gate_w, grad_up_w, grad_down_w), grad_shares = lax.scan(
        expert_backward,
        start_carry,
        (arrived_rows, gate_vals, up_vals, hidden, grad_arrived.reshape(pieces, per_piece, width)),
    )
    grad_shares = grad_shares.reshape(sources, capacity, width)
    grad_returned = lax.all_to_all(grad_shares, "ep", split_axis=0, concat_axis=0, tiled=True)
    flat_grad = grad_returned.reshape(-1, width)
    grad_routed_part = jnp.zeros((tokens, width), jnp.float32)
    for index in range(top):
        grad_routed_part = grad_routed_part + take_rows(flat_grad, places, valid, index)
    grad_routed_part, grad_gates = (
        lax.psum(grad_routed_part.astype(jnp.bfloat16), "tp").astype(jnp.float32),
        lax.psum(grad_gate_part.astype(jnp.bfloat16), "tp").astype(jnp.float32),
    )
    inner_gate = jnp.sum(gates * grad_gates, axis=-1, keepdims=True)
    grad_picked = gates * (grad_gates - inner_gate)
    chosen = (routes[:, :, None] == jnp.arange(experts, dtype=jnp.int32)[None, None, :]).astype(
        jnp.float32
    )
    grad_logits = jnp.sum(grad_picked[:, :, None] * chosen, axis=1).astype(jnp.bfloat16)
    grad_router = jnp.dot(routed_in.T, grad_logits, preferred_element_type=jnp.float32)
    grad_routed = grad_routed_part + jnp.dot(
        grad_logits, router_weight.T, preferred_element_type=jnp.float32
    )
    grad_mixer = jnp.sum(grad_routed * unit_two, axis=0)
    scaled_two = grad_routed * mixer_gain
    grad_attended = grad_top + inverse_two * (
        scaled_two - unit_two * jnp.mean(scaled_two * unit_two, axis=-1, keepdims=True)
    )
    grad_branch = grad_attended.astype(jnp.bfloat16)
    grad_output = jnp.dot(mixed.T, grad_branch, preferred_element_type=jnp.float32)
    grad_mixed = jnp.dot(grad_branch, output_weight.T, preferred_element_type=jnp.float32).astype(
        jnp.bfloat16
    )
    grad_query_rot, grad_key_rot, grad_value_f = attention_backward(
        query, key, value, log_totals, grad_mixed, scale
    )
    grad_query = (
        unrotate(grad_query_rot, cosine, sine)
        .astype(jnp.bfloat16)
        .reshape(tokens, heads_local * HD)
    )
    grad_key = (
        unrotate(grad_key_rot, cosine, sine).astype(jnp.bfloat16).reshape(tokens, groups_local * HD)
    )
    grad_value = grad_value_f.astype(jnp.bfloat16).reshape(tokens, groups_local * HD)
    grad_query_w = jnp.dot(normed.T, grad_query, preferred_element_type=jnp.float32)
    grad_key_w = jnp.dot(normed.T, grad_key, preferred_element_type=jnp.float32)
    grad_value_w = jnp.dot(normed.T, grad_value, preferred_element_type=jnp.float32)
    grad_normed = jnp.dot(grad_query, query_weight.T, preferred_element_type=jnp.float32)
    grad_normed = grad_normed + jnp.dot(grad_key, key_weight.T, preferred_element_type=jnp.float32)
    grad_normed = grad_normed + jnp.dot(
        grad_value, value_weight.T, preferred_element_type=jnp.float32
    )
    grad_normed = lax.psum(grad_normed.astype(jnp.bfloat16), "tp").astype(jnp.float32)
    grad_norm = jnp.sum(grad_normed * unit_one, axis=0)
    scaled_one = grad_normed * norm_gain
    grad_inputs = grad_attended + inverse_one * (
        scaled_one - unit_one * jnp.mean(scaled_one * unit_one, axis=-1, keepdims=True)
    )
    summed = (
        lax.psum(grad_query_w.astype(jnp.bfloat16), "ep").astype(jnp.float32),
        lax.psum(grad_key_w.astype(jnp.bfloat16), "ep").astype(jnp.float32),
        lax.psum(grad_value_w.astype(jnp.bfloat16), "ep").astype(jnp.float32),
        lax.psum(grad_output.astype(jnp.bfloat16), "ep").astype(jnp.float32),
        lax.psum(grad_norm.astype(jnp.bfloat16), "ep").astype(jnp.float32),
        lax.psum(grad_mixer.astype(jnp.bfloat16), "ep").astype(jnp.float32),
        lax.psum(grad_router.astype(jnp.bfloat16), "ep").astype(jnp.float32),
    )
    return (
        result,
        grad_inputs.astype(jnp.bfloat16),
        summed[4],
        summed[0],
        summed[1],
        summed[2],
        summed[3],
        summed[5],
        summed[6],
        grad_gate_w[None],
        grad_up_w[None],
        grad_down_w[None],
    )


def solution(mesh):
    placed = (
        P("ep", None),
        P("ep", None),
        P(),
        P(None, "tp"),
        P(None, "tp"),
        P(None, "tp"),
        P("tp", None),
        P(),
        P(),
        P("ep", None, "tp"),
        P("ep", None, "tp"),
        P("ep", "tp", None),
        P("ep", None),
    )
    return jax.shard_map(
        body,
        mesh=mesh,
        in_specs=placed,
        out_specs=(
            P("ep", None),
            P("ep", None),
            P(),
            P(None, "tp"),
            P(None, "tp"),
            P(None, "tp"),
            P("tp", None),
            P(),
            P(),
            P("ep", None, "tp"),
            P("ep", None, "tp"),
            P("ep", "tp", None),
        ),
        check_vma=False,
    )
```

profile of v0, /device:TPU:0, one launch (start us, length us, event | category | flops | bytes accessed | tf_op | source)
XLA Modules:
  0.0 1848.4 jit_solution(17803264337639803303)
XLA Ops:
  20.5 25.3 %while.80 = (s32[]{:T(128)}, bf16[2,512,2,3,64]{1,4,3,2,0:T(8,128)(2,1)S(1)}, f32[2,2,3,512,1]{3,2,1,4,0:T(4,128)S(1)}, s32[2]{0:T(128)S(1)}, bf16[2,512,2,3,64]...) while((s32[]{:T(128)}, ...), condition=%wide.region_4.5_spmd, body=%wide.region_1.4_spmd.sunk | while | flops 843773440 | bytes 41279628 | solution.py:81
  28.5 4.9 fusion.237
  41.0 4.9 fusion.237
  56.8 15.7 scatter_custom_fusion
  72.6 102.6 %all-reduce.10.cloned.1.call-done = bf16[1024,1536]{1,0:T(8,128)(2,1)} async-done(((bf16[1024,1536]{1,0:T(8,128)(2,1)}), bf16[1024,1536]{1,0:T(8,128)(2,1)}) %all-reduce.10.cloned.1.call-update) | async-done | bytes 3145744 | tf_op jit(solution)/shard_map/psum | solution.py:221
  175.2 4.1 multiply_reduce_fusion.2
  184.5 33.6 %gather_fusion = bf16[5120,1536]{1,0:T(8,128)(2,1)} fusion(bf16[1025,1536]{1,0:T(8,128)(2,1)} %concatenate.31, s32[5120]{0:T(1024)S(1)} %fusion.127), kind=kCustom, calls=%fused_computation.8 | custom fusion | bytes 31477760 | tf_op jit(solution)/shard_map/jit(_take)/gather | solution.py:176
  218.2 13.6 broadcast_select_fusion
  231.8 5.6 all-to-all-start
  237.4 172.7 %all-to-all-done = bf16[8,640,1536]{2,1,0:T(8,128)(2,1)} async-done(((bf16[8,640,1536]{2,1,0:T(8,128)(2,1)}), bf16[8,640,1536]{2,1,0:T(8,128)(2,1)}, u32[]{:S(2)}, u32[]{:S(2)}) %all-to-all-start) | async-done | bytes 15728672 | tf_op jit(solution)/shard_map/all_to_all | solution.py:231
  410.1 6.6 broadcast.256.clone
  416.8 49.0 %while.81 = (s32[]{:T(128)}, f32[4,1280,128]{2,1,0:T(8,128)}, f32[4,1280,128]{2,1,0:T(8,128)}, bf16[4,1280,128]{2,1,0:T(8,128)(2,1)}, bf16[4,1280,1536]{2,1,0:T(...) while((s32[]{:T(128)}, f32[4,1280,128]{2,1,0:T(8,128)}, ...), condition=%wide.region_14.15_spmd, body=%wide.region_13.14_spmd.sunk | while | flops 1512898560 | bytes 17893492 | solution.py:249
  416.8 4.1 bitcast_dynamic-update-slice_fusion.10
  420.9 4.1 bitcast_dynamic-update-slice_fusion.9
  429.0 4.1 bitcast_dynamic-update-slice_fusion.10
  433.2 4.1 bitcast_dynamic-update-slice_fusion.9
  441.3 4.1 bitcast_dynamic-update-slice_fusion.10
  445.4 4.2 bitcast_dynamic-update-slice_fusion.9
  453.5 4.1 bitcast_dynamic-update-slice_fusion.10
  457.7 4.1 bitcast_dynamic-update-slice_fusion.9
  465.8 5.9 all-to-all-start.1
  472.2 5.5 concatenate.32
  477.7 36.6 %gather_fusion.1 = f32[5120,1536]{1,0:T(8,128)} fusion(f32[1025,1536]{1,0:T(8,128)} %concatenate.32, s32[5120]{0:T(1024)S(1)} %fusion.127), kind=kCustom, calls=%fused_computation.9 | custom fusion | bytes 62935040 | tf_op jit(solution)/shard_map/jit(_take)/gather | solution.py:176
  521.3 24.5 %gather_fusion.2 = f32[4096]{0:T(1024)S(1)} fusion(f32[1024,8]{0,1:T(8,128)S(1)} %fusion.152, s32[4096]{0:T(1024)S(1)} %reshape.433), kind=kCustom, calls=%fused_computation.10 | custom fusion | bytes 65536 | tf_op jit(solution)/shard_map/jit(take_along_axis)/gather | solution.py:226
  546.6 97.8 %all-to-all-done.1 = bf16[8,640,1536]{2,1,0:T(8,128)(2,1)} async-done(((bf16[8,640,1536]{2,1,0:T(8,128)(2,1)}), bf16[8,640,1536]{2,1,0:T(8,128)(2,1)}, u32[]{:S(2)}, u32[]{:S(2)}) %all-to-all-start.1) | async-done | bytes 15728672 | tf_op jit(solution)/shard_map/all_to_all | solution.py:251
  644.4 14.8 gather_fusion.6
  659.1 14.8 gather_fusion.5
  673.9 15.2 gather_fusion.4
  689.2 14.8 gather_fusion.3
  704.1 8.5 fusion.108
  712.7 9.6 psum.87
  723.4 15.7 scatter_custom_fusion.1
  739.1 17.2 multiply_convert_fusion.1
  756.3 5.6 all-to-all-start.2
  762.0 172.6 %all-to-all-done.2 = bf16[8,640,1536]{2,1,0:T(8,128)(2,1)} async-done(((bf16[8,640,1536]{2,1,0:T(8,128)(2,1)}), bf16[8,640,1536]{2,1,0:T(8,128)(2,1)}, u32[]{:S(2)}, u32[]{:S(2)}) %all-to-all-start.2) | async-done | bytes 15728672 | tf_op jit(solution)/shard_map/all_to_all | solution.py:269
  934.7 6.7 broadcast.256
  941.4 75.9 %while.82 = (s32[]{:T(128)}, f32[1536,128]{1,0:T(8,128)}, f32[1536,128]{1,0:T(8,128)}, f32[128,1536]{1,0:T(8,128)S(1)}, bf16[4,1280,1536]{2,1,0:T(8,128)(2,1)}, ...) while((s32[]{:T(128)}, f32[1536,128]{1,0:T(8,128)}, ...), condition=%wide.region_18.20_spmd.clone, body=%wide.region_17.19_spmd.clone.sunk | while | flops 3027140608 | bytes 57477916 | solution.py:295
  948.9 3.9 fusion.256
  967.8 3.9 fusion.256
  986.8 3.9 fusion.256
  1005.8 3.9 fusion.256
  1017.4 180.2 %all_to_all.20 = bf16[8,640,1536]{2,1,0:T(8,128)(2,1)} all-to-all(bf16[8,640,1536]{2,1,0:T(8,128)(2,1)} %bitcast.416), channel_id=1, replica_groups=mesh['ep'=8,'tp'=4] {'ep'}, dimensions={0} | all-to-all | bytes 31457280 | tf_op jit(solution)/shard_map/all_to_all | solution.py:301
  1197.6 14.8 gather_fusion.10
  1212.3 14.8 gather_fusion.9
  1227.1 14.8 gather_fusion.8
  1242.0 14.8 gather_fusion.7
  1256.9 8.7 add_convert_fusion.1
  1266.5 117.2 %all-reduce.12.cloned.1.call-done = bf16[1024,1536]{1,0:T(8,128)(2,1)} async-done(((bf16[1024,1536]{1,0:T(8,128)(2,1)}), bf16[1024,1536]{1,0:T(8,128)(2,1)}) %all-reduce.12.cloned.1.call-update) | async-done | bytes 3145744 | tf_op jit(solution)/shard_map/psum | solution.py:307
  1383.7 6.0 multiply_reduce_fusion
  1403.3 86.7 %while.83 = (s32[]{:T(128)}, f32[1024,2,64]{0,2,1:T(8,128)S(1)}, f32[1024,2,64]{0,2,1:T(8,128)}, f32[2,512,2,3,64]{1,0,4,3,2:T(2,128)}, bf16[2,512,2,3,64]{1,4,3...) while((s32[]{:T(128)}, f32[1024,2,64]{0,2,1:T(8,128)S(1)}, ...), condition=%wide.region_30.32_spmd.clone, body=%wide.region_28.31_spmd.clone.sunk | while | flops 2061825536 | bytes 104947920 | solution.py:131
  1407.9 5.1 fusion.272
  1412.9 7.8 fusion.269
  1420.8 6.8 fusion.270
  1431.7 15.0 dynamic_update_slice.68
  1450.9 5.2 fusion.272
  1456.1 7.8 fusion.269
  1464.0 6.8 fusion.270
  1474.9 15.0 dynamic_update_slice.68
  1506.2 9.7 add_convert_fusion.3
  1525.0 50.3 %all-reduce.14.cloned.1.call-done = (bf16[1536,384]{1,0:T(8,128)(2,1)}, bf16[1536,128]{1,0:T(8,128)(2,1)}, bf16[1536,128]{1,0:T(8,128)(2,1)}, bf16[384,1536]{1,0:T(8,128)(2,1)}) async-done(((bf16[1536,384]{1,0:T(8,128)(2,1)}, bf16[1536,128]{1,0:T(8,128)(2,1)}, bf16[1536,128]{1,0:T(8,128)(2,1)}, bf16[384,1536]{1,0:T(8,128)(2,1)}), (bf16[1536,384]{1,0:T(8,128)(2,1)}, bf16[1536,128]{1,0:T(8,128)(2,1)}, ...) | async-done | bytes 3145744 | tf_op jit(solution)/shard_map/psum | solution.py:357
  1583.7 217.8 %all-reduce.16.cloned.1.call-done = (bf16[1024,1536]{1,0:T(8,128)(2,1)}, bf16[1024,1536]{1,0:T(8,128)(2,1)}) async-done(((bf16[1024,1536]{1,0:T(8,128)(2,1)}, bf16[1024,1536]{1,0:T(8,128)(2,1)}), (bf16[1024,1536]{1,0:T(8,128)(2,1)}, bf16[1024,1536]{1,0:T(8,128)(2,1)})) %all-reduce.16.cloned.1.call-update) | async-done | bytes 6291472 | tf_op jit(solution)/shard_map/psum | solution.py:262
  1801.5 4.1 fusion.114
  1805.7 24.0 %all-reduce.2 = (bf16[1536]{0:T(1024)(128)(2,1)S(1)}, bf16[1536]{0:T(1024)(128)(2,1)S(1)}, bf16[1536,8]{0,1:T(8,128)(2,1)S(1)}) all-reduce(bf16[1536]{0:T(1024)(128)(2,1)S(1)} %get-tuple-element.455, bf16[1536]{0:T(1024)(128)(2,1)S(1)} %copy-done.91, ...), channel_id=1, replica_groups=mesh['ep'=8,'tp'=4] {'ep'}, use_global_device_ids=true, to_apply=%region_34.36 | all-reduce | flops 15360 | bytes 61440 | tf_op jit(solution)/shard_map/psum | solution.py:361
  1831.5 10.2 fusion.107
  (392 shorter events, 193.3 us)
Async XLA Ops:
  7.2 40.6 %copy-start = (bf16[384,1536]{1,0:T(8,128)(2,1)S(1)}, bf16[384,1536]{1,0:T(8,128)(2,1)}, u32[]{:S(2)}) copy-start(bf16[384,1536]{1,0:T(8,128)(2,1)} %param.29) | copy-start | bytes 3538948
  7.2 168.0 %all-reduce.10.cloned.1.call-start = ((), (), s32[]{:S(2)}) async-start(), calls=%async_computation.4 | async-start | bytes 6291456 | tf_op jit(solution)/shard_map/psum | solution.py:221
  7.3 7.4 copy-start.23
  51.3 128.0 %copy-start.69 = (f32[1536]{0:T(1024)S(1)}, f32[1536]{0:T(1024)}, u32[]{:S(2)}) copy-start(f32[1536]{0:T(1024)} %param.30) | copy-start | bytes 18436
  55.9 125.2 %copy-start.38 = (s32[1024,4]{0,1:T(4,128)}, s32[1024,4]{0,1:T(4,128)S(1)}, u32[]{:S(2)}) copy-start(s32[1024,4]{0,1:T(4,128)S(1)} %copy.104) | copy-start | bytes 49156
  55.9 125.2 %copy-start.40 = (s32[1024,4]{0,1:T(4,128)}, s32[1024,4]{0,1:T(4,128)S(1)}, u32[]{:S(2)}) copy-start(s32[1024,4]{0,1:T(4,128)S(1)} %add_select_fusion) | copy-start | bytes 49156
  56.8 124.3 %copy-start.89 = (s32[4096,1]{0,1:T(1,128)}, s32[4096,1]{0,1:T(1,128)S(1)}, u32[]{:S(2)}) copy-start(s32[4096,1]{0,1:T(1,128)S(1)} %compare_select_fusion) | copy-start | bytes 49156
  72.6 145.6 %copy-start.61 = (pred[8,640]{1,0:T(8,128)(4,1)}, pred[8,640]{1,0:T(8,128)(4,1)S(1)}, u32[]{:S(2)}) copy-start(pred[8,640]{1,0:T(8,128)(4,1)S(1)} %broadcast_in_dim.167) | copy-start | bytes 15364
  231.8 178.4 %all-to-all-start = ((bf16[8,640,1536]{2,1,0:T(8,128)(2,1)}), bf16[8,640,1536]{2,1,0:T(8,128)(2,1)}, u32[]{:S(2)}, u32[]{:S(2)}) async-start(bf16[8,640,1536]{2,1,0:T(8,128)(2,1)} %broadcast_select_fusion), calls=%async_computation | async-start | bytes 31457280 | tf_op jit(solution)/shard_map/all_to_all | solution.py:231
  465.8 178.6 %all-to-all-start.1 = ((bf16[8,640,1536]{2,1,0:T(8,128)(2,1)}), bf16[8,640,1536]{2,1,0:T(8,128)(2,1)}, u32[]{:S(2)}, u32[]{:S(2)}) async-start(bf16[8,640,1536]{2,1,0:T(8,128)(2,1)} %bitcast.417), calls=%async_computation.1 | async-start | bytes 31457280 | tf_op jit(solution)/shard_map/all_to_all | solution.py:251
  477.7 36.6 %copy-start.41 = (s32[1024,4]{0,1:T(4,128)S(1)}, s32[1024,4]{0,1:T(4,128)}, u32[]{:S(2)}) copy-start(s32[1024,4]{0,1:T(4,128)} %copy-done.40) | copy-start | bytes 49156
  477.7 40.2 %copy-start.39 = (s32[1024,4]{0,1:T(4,128)S(1)}, s32[1024,4]{0,1:T(4,128)}, u32[]{:S(2)}) copy-start(s32[1024,4]{0,1:T(4,128)} %copy-done.38) | copy-start | bytes 49156
  477.7 40.8 %copy-start.71 = (bf16[1536,8]{0,1:T(8,128)(2,1)S(1)}, bf16[1536,8]{0,1:T(8,128)(2,1)}, u32[]{:S(2)}) copy-start(bf16[1536,8]{0,1:T(8,128)(2,1)} %param.31) | copy-start | bytes 73732
  521.3 25.3 %copy-start.33 = (s32[1024,4]{0,1:T(4,128)S(1)}, s32[1024,4]{0,1:T(4,128)}, u32[]{:S(2)}) copy-start(s32[1024,4]{0,1:T(4,128)} %param.24) | copy-start | bytes 49156
  521.3 123.1 %copy-start.68 = (s32[1024]{0:T(1024)S(1)}, s32[1024]{0:T(1024)}, u32[]{:S(2)}) copy-start(s32[1024]{0:T(1024)} %fusion.145) | copy-start | bytes 12292
  644.4 14.8 copy-start.66
  659.1 14.8 copy-start.67
  673.9 15.2 copy-start.65
  689.2 14.8 copy-start.45
  689.2 14.8 copy-start.48
  689.2 14.8 copy-start.51
  689.2 14.8 copy-start.54
  689.2 14.8 copy-start.73
  689.2 14.8 copy-start.76
  689.2 14.8 copy-start.79
  689.2 14.8 copy-start.82
  704.0 35.0 %copy-start.62 = (pred[8,640]{1,0:T(8,128)(4,1)S(1)}, pred[8,640]{1,0:T(8,128)(4,1)}, u32[]{:S(2)}) copy-start(pred[8,640]{1,0:T(8,128)(4,1)} %copy-done.61) | copy-start | bytes 15364
  722.9 33.4 %copy-start.35 = (f32[1024,4]{0,1:T(4,128)}, f32[1024,4]{0,1:T(4,128)S(1)}, u32[]{:S(2)}) copy-start(f32[1024,4]{0,1:T(4,128)S(1)} %get-tuple-element.551) | copy-start | bytes 49156
  756.3 178.4 %all-to-all-start.2 = ((bf16[8,640,1536]{2,1,0:T(8,128)(2,1)}), bf16[8,640,1536]{2,1,0:T(8,128)(2,1)}, u32[]{:S(2)}, u32[]{:S(2)}) async-start(bf16[8,640,1536]{2,1,0:T(8,128)(2,1)} %multiply_convert_fusion.1), calls=%async_computation.2 | async-start | bytes 31457280 | tf_op jit(solution)/shard_map/all_to_all | solution.py:269
  762.0 621.7 %all-reduce.12.cloned.1.call-start = ((), (), s32[]{:S(2)}) async-start(), calls=%async_computation.5 | async-start | bytes 6291456 | tf_op jit(solution)/shard_map/psum | solution.py:307
  934.7 6.7 copy-start.16
  934.7 6.7 copy-start.18
  934.7 6.7 copy-start.20
  948.9 7.2 copy-start.95
  967.8 7.2 copy-start.95
  986.8 7.2 copy-start.95
  1005.8 7.2 copy-start.95
  1017.4 180.2 %copy-start.14 = (f32[128,1536]{1,0:T(8,128)}, f32[128,1536]{1,0:T(8,128)S(1)}, u32[]{:S(2)}) copy-start(f32[128,1536]{1,0:T(8,128)S(1)} %get-tuple-element.282) | copy-start | bytes 2359300
  1241.9 14.8 copy-start.46
  1241.9 14.8 copy-start.49
  1241.9 14.8 copy-start.52
  1241.9 14.8 copy-start.55
  1241.9 14.8 copy-start.74
  1241.9 14.8 copy-start.77
  1242.0 14.8 copy-start.80
  1242.0 14.8 copy-start.83
  1256.8 8.9 copy-start.36
  1256.8 8.9 copy-start.44
  1256.8 8.9 copy-start.90
  1256.8 8.9 copy-start.34
  1256.9 126.8 %copy-start.64 = (f32[1024]{0:T(1024)S(1)}, f32[1024]{0:T(1024)}, u32[]{:S(2)}) copy-start(f32[1024]{0:T(1024)} %copy-done.63) | copy-start | bytes 12292
  1256.9 126.8 %copy-start.70 = (f32[1536]{0:T(1024)S(1)}, f32[1536]{0:T(1024)}, u32[]{:S(2)}) copy-start(f32[1536]{0:T(1024)} %param.30) | copy-start | bytes 18436
  1256.9 126.8 %copy-start.72 = (bf16[1536,8]{0,1:T(8,128)(2,1)S(1)}, bf16[1536,8]{0,1:T(8,128)(2,1)}, u32[]{:S(2)}) copy-start(bf16[1536,8]{0,1:T(8,128)(2,1)} %param.31) | copy-start | bytes 73732
  1265.7 309.6 %all-reduce.14.cloned.1.call-start = ((), (), s32[]{:S(2)}) async-start(), calls=%async_computation.6 | async-start | bytes 6291456 | tf_op jit(solution)/shard_map/psum | solution.py:357
  1265.8 123.9 %copy-start.57 = (bf16[1024,8]{0,1:T(8,128)(2,1)}, bf16[1024,8]{0,1:T(8,128)(2,1)S(1)}, u32[]{:S(2)}) copy-start(bf16[1024,8]{0,1:T(8,128)(2,1)S(1)} %select_reduce_fusion) | copy-start | bytes 49156
  1395.6 7.7 copy-start.7
  1395.6 7.7 copy-start.9
  1493.5 7.6 copy-start.4
  1506.0 295.5 %all-reduce.16.cloned.1.call-start = ((), (), s32[]{:S(2)}) async-start(), calls=%async_computation.7 | async-start | bytes 12582912 | tf_op jit(solution)/shard_map/psum | solution.py:262
  1506.1 9.7 copy-start.24
  1522.5 279.0 %copy-start.42 = (f32[1536]{0:T(1024)S(1)}, f32[1536]{0:T(1024)}, u32[]{:S(2)}) copy-start(f32[1536]{0:T(1024)} %param.25) | copy-start | bytes 18436
  1522.5 279.0 %copy-start.60 = (f32[1024]{0:T(1024)S(1)}, f32[1024]{0:T(1024)}, u32[]{:S(2)}) copy-start(f32[1024]{0:T(1024)} %copy-done.59) | copy-start | bytes 12292
  1575.2 6.8 copy-start.29
  1579.2 226.5 %copy-start.91 = (bf16[1536]{0:T(1024)(128)(2,1)S(1)}, bf16[1536]{0:T(1024)(128)(2,1)}, u32[]{:S(2)}) copy-start(bf16[1536]{0:T(1024)(128)(2,1)} %get-tuple-element.453) | copy-start | bytes 9220
  (51 other events, 193.0 us)
Sparse Core Ops, SparseCore 0:
  51.4 123.7 all-reduce.9
  1265.8 117.8 all-reduce.11
  1506.1 69.0 all-reduce.13
  1578.2 223.2 all-reduce.15
where the time goes:
time: 1860 us; the launch traced here: 1850 us
  waiting for transfers between devices  931 us (50%)
  local copies, waits for them, and re-layouts  322 us (17%)
  blocking collectives  214 us (12%)
  matrix products  210 us (11%)
  other arithmetic  135 us (7%)
    psum x1, waiting for transfers between devices, body(): combined = lax.psum(combined.astype(jnp.bfloat16), 'tp').astype(jnp.float32)  218 us
    all_to_all x1, blocking collectives, body(): lax.all_to_all(grad_shares, 'ep', split_axis=0, concat_axis=0, tiled=True)  180 us
    all_to_all x1, waiting for transfers between devices, body(): lax.all_to_all(send_buffer, 'ep', split_axis=0, concat_axis=0, tiled=True)  173 us
    all_to_all x1, waiting for transfers between devices, body(): lax.all_to_all(grad_buffer, 'ep', split_axis=0, concat_axis=0, tiled=True)  173 us
    gather x8, local copies, waits for them, and re-layouts, take_rows(): jnp.take(flat, jnp.minimum(places[:, index], flat.shape[0] - 1), axis=0)  119 us
    psum x1, waiting for transfers between devices, body(): lax.psum(grad_routed_part.astype(jnp.bfloat16), 'tp').astype(jnp.float32)  117 us
    psum x1, waiting for transfers between devices, body(): lax.psum(branch.astype(jnp.bfloat16), 'tp').astype(jnp.float32)  103 us
    all_to_all x1, waiting for transfers between devices, body(): lax.all_to_all(shares, 'ep', split_axis=0, concat_axis=0, tiled=True)  97.8 us
  transfers between devices with their start and end apart: 7, of which 7 were waited for; matrix products, arithmetic and copies ran while one was open for 7% of the time, Pallas kernels for 0%

commit v1 on v0

v1 whole, which is shorter than its diff:
```python
import jax
import jax.numpy as jnp
from jax import lax
from jax.sharding import PartitionSpec as P

HD = 64
LEN = 1024
EPS = 1e-06
MASKED = -1e30
BF = jnp.bfloat16
F32 = jnp.float32


def rotary_tables(positions, depth):
    half = depth // 2
    freqs = 10000.0 ** (-jnp.arange(half, dtype=jnp.float32) * 2.0 / depth)
    angles = positions[:, None] * freqs[None, :]
    return (jnp.cos(angles), jnp.sin(angles))


def rotate(values, cosine, sine):
    half = values.shape[-1] // 2
    first = values[..., :half]
    second = values[..., half:]
    cos_b = cosine[:, None, :]
    sin_b = sine[:, None, :]
    return jnp.concatenate(
        [first * cos_b - second * sin_b, second * cos_b + first * sin_b], axis=-1
    )


def unrotate(grads, cosine, sine):
    return rotate(grads, cosine, -sine)


def block_scores(query_block, keys, start, scale):
    scores = jnp.einsum("qgrd,kgd->grqk", query_block, keys, preferred_element_type=F32) * scale
    rows_at = start + jnp.arange(query_block.shape[0])[:, None]
    cols_at = jnp.arange(keys.shape[0])[None, :]
    return jnp.where(rows_at >= cols_at, scores, MASKED)


BLOCK = 256


def attention_forward(query, key, value, scale):
    tokens, heads, depth = query.shape
    groups = key.shape[1]
    repeat = heads // groups
    outs, logs = [], []
    for start in range(0, tokens, BLOCK):
        stop = start + BLOCK
        queries = query[start:stop].reshape(BLOCK, groups, repeat, depth)
        scores = block_scores(queries, key[:stop], start, scale)
        peak = jnp.max(scores, axis=-1, keepdims=True)
        weights = jnp.exp(scores - peak)
        totals = jnp.sum(weights, axis=-1, keepdims=True)
        probs = (weights / totals).astype(BF)
        mixed = jnp.einsum("grqk,kgd->qgrd", probs, value[:stop], preferred_element_type=F32)
        outs.append(mixed.astype(BF).reshape(BLOCK, heads * depth))
        logs.append(peak + jnp.log(totals))
    return (jnp.concatenate(outs, axis=0), logs)


def attention_backward(query, key, value, logs, grad_mixed, scale):
    tokens, heads, depth = query.shape
    groups = key.shape[1]
    repeat = heads // groups
    grad_key = jnp.zeros(key.shape, F32)
    grad_value = jnp.zeros(key.shape, F32)
    grad_queries = []
    for number, start in enumerate(range(0, tokens, BLOCK)):
        stop = start + BLOCK
        queries = query[start:stop].reshape(BLOCK, groups, repeat, depth)
        grads = grad_mixed[start:stop].reshape(BLOCK, groups, repeat, depth)
        keys = key[:stop]
        scores = block_scores(queries, keys, start, scale)
        probs = jnp.exp(scores - logs[number])
        grad_probs = jnp.einsum("qgrd,kgd->grqk", grads, value[:stop], preferred_element_type=F32)
        inner = jnp.sum(probs * grad_probs, axis=-1, keepdims=True)
        grad_scores = (probs * (grad_probs - inner)).astype(BF)
        grad_queries.append(
            jnp.einsum("grqk,kgd->qgrd", grad_scores, keys, preferred_element_type=F32).reshape(
                BLOCK, heads, depth
            )
            * scale
        )
        more_key = (
            jnp.einsum("grqk,qgrd->kgd", grad_scores, queries, preferred_element_type=F32) * scale
        )
        more_value = jnp.einsum(
            "grqk,qgrd->kgd", probs.astype(BF), grads, preferred_element_type=F32
        )
        grad_key = grad_key.at[:stop].add(more_key)
        grad_value = grad_value.at[:stop].add(more_value)
    return (jnp.concatenate(grad_queries, axis=0), grad_key, grad_value)


def swap(x, bit):
    return lax.ppermute(x, "ep", [(i, i ^ bit) for i in range(lax.axis_size("ep"))])


def gather_ep(x):
    n = lax.axis_size("ep")
    if n != 8:
        return lax.all_gather(x, "ep")
    first = [x] + [swap(x, k) for k in (2, 4, 6)]
    second = [swap(v, 1) for v in first]
    return jnp.stack([v for pair in zip(first, second) for v in pair])


def scatter_ep(x):
    n = lax.axis_size("ep")
    if n != 8:
        return lax.psum_scatter(x, "ep", scatter_dimension=0, tiled=False).astype(F32)
    other = swap(x[1::2], 1)
    mine = (x[0::2].astype(F32) + other.astype(F32)).astype(BF)
    got = [mine[0]] + [swap(mine[j], 2 * j) for j in (1, 2, 3)]
    return sum(v.astype(F32) for v in got)


def step_right(x, upto=None):
    n = lax.axis_size("tp")
    return lax.ppermute(x, "tp", [(i, i + 1) for i in range(n - 1 if upto is None else upto)])


def step_left(x, upto=None):
    n = lax.axis_size("tp")
    return lax.ppermute(x, "tp", [(n - 1 - i, n - 2 - i) for i in range(n - 1 if upto is None else upto)])


def gather_tp(x):
    n = lax.axis_size("tp")
    at = lax.axis_index("tp")
    right, left = [x], [x]
    for _ in range(1, n):
        right.append(step_right(right[-1]))
        left.append(step_left(left[-1]))
    return [x] + [jnp.where(at >= s, right[s], left[n - s]) for s in range(1, n)]


def scatter_tp(parts):
    n = lax.axis_size("tp")
    right = left = None
    for t in range(1, n):
        give_right = parts[t]
        give_left = parts[n - t]
        if right is not None:
            give_right = (give_right.astype(F32) + right.astype(F32)).astype(BF)
            give_left = (give_left.astype(F32) + left.astype(F32)).astype(BF)
        right = step_right(give_right, t)
        left = step_left(give_left, t)
    return parts[0].astype(F32) + right.astype(F32) + left.astype(F32)


def exchange_tp(pieces):
    n = lax.axis_size("tp")
    at = lax.axis_index("tp")
    out = jnp.zeros_like(pieces)
    own = lax.dynamic_index_in_dim(pieces, at, 0, False)
    out = lax.dynamic_update_index_in_dim(out, own, at, 0)
    for s in range(1, n):
        piece = lax.dynamic_index_in_dim(pieces, lax.rem(at + s, n), 0, False)
        got = lax.ppermute(piece, "tp", [(i, (i + s) % n) for i in range(n)])
        out = lax.dynamic_update_index_in_dim(out, got, lax.rem(at - s + n, n), 0)
    return out


def gather_tp_in_order(x):
    n = lax.axis_size("tp")
    at = lax.axis_index("tp")
    out = jnp.zeros((n,) + x.shape, x.dtype)
    for s, block in enumerate(gather_tp(x)):
        out = lax.dynamic_update_index_in_dim(out, block, lax.rem(at - s + n, n), 0)
    return out


def sum_all(x):
    for axis in ("ep", "tp"):
        n = lax.axis_size(axis)
        bit = 1
        while bit < n:
            x = x + lax.ppermute(x, axis, [(i, i ^ bit) for i in range(n)])
            bit *= 2
    return x


def body(
    inputs,
    routes,
    norm_gain,
    query_weight,
    key_weight,
    value_weight,
    output_weight,
    mixer_gain,
    router_weight,
    gate_weight,
    up_weight,
    down_weight,
    cotangent,
):
    tokens, width = inputs.shape
    experts = router_weight.shape[1]
    n_ep = lax.axis_size("ep")
    n_tp = lax.axis_size("tp")
    ep_at = lax.axis_index("ep")
    tp_at = lax.axis_index("tp")
    quarter = tokens // n_tp
    scale = HD ** (-0.5)
    heads_width = query_weight.shape[1]
    groups_width = key_weight.shape[1]
    heads_local = heads_width // HD
    groups_local = groups_width // HD

    def mine(x):
        return lax.dynamic_slice_in_dim(x, tp_at * quarter, quarter, 0)

    output_rows = output_weight.shape[0]
    part = output_rows // n_ep
    output_part = lax.dynamic_slice_in_dim(output_weight, ep_at * part, part, 0)
    output_whole = lax.all_gather(output_part, ("tp", "ep"), tiled=True)
    qkv_weight = jnp.concatenate([query_weight, key_weight, value_weight], axis=1)
    part_in = width // n_ep
    qkv_part = lax.dynamic_slice_in_dim(qkv_weight, ep_at * part_in, part_in, 0)
    qkv_whole = lax.all_gather(qkv_part, ("tp", "ep"), tiled=True).reshape(
        n_tp, width, heads_width + 2 * groups_width
    )
    gate_matrix = jnp.concatenate(gather_tp(gate_weight[0]), axis=1)
    up_matrix = jnp.concatenate(gather_tp(up_weight[0]), axis=1)
    down_matrix = jnp.concatenate(gather_tp(down_weight[0]), axis=0)
    routes_mine = mine(routes)
    grad_top_mine = mine(cotangent)
    routes_all = lax.all_gather(routes_mine, "ep")
    if n_ep == 8:
        slots = jnp.bitwise_xor(jnp.arange(n_ep), ep_at)
        routes_all = jnp.take(routes_all, slots, axis=0)
    grad_top_all = gather_ep(grad_top_mine)

    inputs32 = inputs.astype(F32)
    inverse_one = lax.rsqrt(jnp.mean(inputs32 * inputs32, axis=-1, keepdims=True) + EPS)
    unit_one = inputs32 * inverse_one
    normed = (unit_one * norm_gain).astype(BF)
    query_raw = jnp.dot(normed, query_weight, preferred_element_type=F32)
    key_raw = jnp.dot(normed, key_weight, preferred_element_type=F32)
    value_raw = jnp.dot(normed, value_weight, preferred_element_type=F32)
    positions = (jnp.arange(tokens) % LEN).astype(F32)
    cosine, sine = rotary_tables(positions, HD)
    query = rotate(query_raw.reshape(tokens, heads_local, HD), cosine, sine).astype(BF)
    key = rotate(key_raw.reshape(tokens, groups_local, HD), cosine, sine).astype(BF)
    value = value_raw.reshape(tokens, groups_local, HD).astype(BF)
    mixed, logs = attention_forward(query, key, value, scale)

    mixed_mine = exchange_tp(mixed.reshape(n_tp, quarter, heads_width))
    mixed_mine = mixed_mine.transpose(1, 0, 2).reshape(quarter, n_tp * heads_width)
    branch = jnp.dot(mixed_mine, output_whole, preferred_element_type=F32)
    inputs_mine = mine(inputs).astype(F32)
    attended = inputs_mine + branch
    inverse_two = lax.rsqrt(jnp.mean(attended * attended, axis=-1, keepdims=True) + EPS)
    unit_two = attended * inverse_two
    routed_in = (unit_two * mixer_gain).astype(BF)

    def gate_table(rows, chosen_routes):
        logits = jnp.dot(rows, router_weight, preferred_element_type=F32)
        ids = jnp.arange(experts, dtype=jnp.int32)
        chosen = jnp.any(chosen_routes[:, :, None] == ids[None, None, :], axis=1)
        logits = jnp.where(chosen, logits, MASKED)
        weights = jnp.exp(logits - jnp.max(logits, axis=-1, keepdims=True))
        weights = jnp.where(chosen, weights, 0.0)
        return weights / jnp.sum(weights, axis=-1, keepdims=True)

    routed_all = gather_ep(routed_in).reshape(-1, width)
    gates = gate_table(routed_in, routes_mine)
    gates_all = gate_table(routed_all, routes_all.reshape(-1, routes.shape[1]))
    own_gate = lax.dynamic_slice_in_dim(gates_all, ep_at, 1, 1)
    grad_rows = grad_top_all.reshape(-1, width)
    gate_vals = jnp.dot(routed_all, gate_matrix, preferred_element_type=F32)
    up_vals = jnp.dot(routed_all, up_matrix, preferred_element_type=F32)
    sigma = jax.nn.sigmoid(gate_vals)
    active = gate_vals * sigma
    hidden = (active * up_vals).astype(BF)
    expert_out = jnp.dot(hidden, down_matrix, preferred_element_type=F32)
    combined = (own_gate * expert_out).astype(BF)
    grad_gate_own = jnp.sum(grad_rows.astype(F32) * expert_out, axis=-1)
    grad_out = (own_gate * grad_rows.astype(F32)).astype(BF)
    grad_hidden = jnp.dot(grad_out, down_matrix.T, preferred_element_type=F32)
    grad_gate_vals = (grad_hidden * up_vals * sigma * (1.0 + gate_vals * (1.0 - sigma))).astype(BF)
    grad_up_vals = (grad_hidden * active).astype(BF)
    grad_gate_w = jnp.dot(routed_all.T, grad_gate_vals, preferred_element_type=F32).astype(BF)
    grad_up_w = jnp.dot(routed_all.T, grad_up_vals, preferred_element_type=F32).astype(BF)
    grad_down_w = jnp.dot(hidden.T, grad_out, preferred_element_type=F32).astype(BF)
    grad_in = (
        jnp.dot(grad_gate_vals, gate_matrix.T, preferred_element_type=F32)
        + jnp.dot(grad_up_vals, up_matrix.T, preferred_element_type=F32)
    ).astype(BF)

    combined_mine = scatter_ep(combined.reshape(n_ep, quarter, width))
    result_mine = (attended + combined_mine).astype(BF)
    result = gather_tp_in_order(result_mine).reshape(tokens, width)
    grad_gates = lax.all_to_all(
        grad_gate_own.reshape(n_ep, quarter), "ep", split_axis=0, concat_axis=0, tiled=True
    ) if n_ep != 8 else None
    if grad_gates is None:
        ordered = jnp.take(grad_gate_own.reshape(n_ep, quarter), slots, axis=0)
        grad_gates = lax.all_to_all(ordered, "ep", split_axis=0, concat_axis=0, tiled=True)
    grad_gates = grad_gates.T
    grad_routed_part = scatter_ep(grad_in.reshape(n_ep, quarter, width))
    inner_gate = jnp.sum(gates * grad_gates, axis=-1, keepdims=True)
    grad_logits = (gates * (grad_gates - inner_gate)).astype(BF)
    grad_router = jnp.dot(routed_in.T, grad_logits, preferred_element_type=F32)
    grad_routed = grad_routed_part + jnp.dot(
        grad_logits, router_weight.T, preferred_element_type=F32
    )
    grad_top = grad_top_mine.astype(F32)
    grad_mixer = jnp.sum(grad_routed * unit_two, axis=0)
    scaled_two = grad_routed * mixer_gain
    grad_attended = grad_top + inverse_two * (
        scaled_two - unit_two * jnp.mean(scaled_two * unit_two, axis=-1, keepdims=True)
    )
    grad_branch = grad_attended.astype(BF)
    grad_mixed_mine = jnp.dot(grad_branch, output_whole.T, preferred_element_type=F32).astype(BF)
    grad_mixed = exchange_tp(
        grad_mixed_mine.reshape(quarter, n_tp, heads_width).transpose(1, 0, 2)
    ).reshape(tokens, heads_local, HD)

    hidden_part = gate_weight.shape[2]

    def cut(x, axis):
        return [
            lax.slice_in_dim(x, s * hidden_part, (s + 1) * hidden_part, axis=axis)
            for s in range(n_tp)
        ]

    grad_gate_w = scatter_tp(cut(grad_gate_w, 1))
    grad_up_w = scatter_tp(cut(grad_up_w, 1))
    grad_down_w = scatter_tp(cut(grad_down_w, 0))

    grad_output = jnp.dot(mixed_mine.T, grad_branch, preferred_element_type=F32).astype(BF)
    grad_output = grad_output.reshape(n_tp, n_ep, part, width).transpose(1, 0, 2, 3)
    grad_output = lax.psum_scatter(
        grad_output.reshape(n_ep, n_tp * part, width), "ep", scatter_dimension=0, tiled=False
    )
    grad_output = lax.psum_scatter(
        grad_output.reshape(n_tp, part, width), "tp", scatter_dimension=0, tiled=False
    )
    grad_output = lax.all_gather(grad_output, "ep", tiled=True).astype(F32)

    grad_query_rot, grad_key_rot, grad_value_f = attention_backward(
        query, key, value, logs, grad_mixed, scale
    )
    grad_query = unrotate(grad_query_rot, cosine, sine).astype(BF).reshape(tokens, heads_width)
    grad_key = unrotate(grad_key_rot, cosine, sine).astype(BF).reshape(tokens, groups_width)
    grad_value = grad_value_f.astype(BF).reshape(tokens, groups_width)
    grad_qkv = jnp.concatenate([grad_query, grad_key, grad_value], axis=1)
    grad_qkv_w = jnp.dot(normed.T, grad_qkv, preferred_element_type=F32).astype(BF)
    grad_qkv_w = lax.psum(grad_qkv_w, "ep").astype(F32)

    grad_qkv_mine = exchange_tp(grad_qkv.reshape(n_tp, quarter, -1))
    grad_normed = jnp.einsum("jtc,jdc->td", grad_qkv_mine, qkv_whole, preferred_element_type=F32)
    inverse_mine = mine(inverse_one)
    unit_mine = inputs_mine * inverse_mine
    grad_norm = jnp.sum(grad_normed * unit_mine, axis=0)
    scaled_one = grad_normed * norm_gain
    grad_inputs_mine = grad_attended + inverse_mine * (
        scaled_one - unit_mine * jnp.mean(scaled_one * unit_mine, axis=-1, keepdims=True)
    )
    grad_inputs = gather_tp_in_order(grad_inputs_mine.astype(BF)).reshape(tokens, width)
    small = sum_all(jnp.concatenate([grad_mixer[None], grad_router.T], axis=0))
    grad_norm = sum_all(grad_norm[None])[0]
    return (
        result,
        grad_inputs,
        grad_norm,
        grad_qkv_w[:, :heads_width],
        grad_qkv_w[:, heads_width : heads_width + groups_width],
        grad_qkv_w[:, heads_width + groups_width :],
        grad_output,
        small[0],
        small[1:].T,
        grad_gate_w[None],
        grad_up_w[None],
        grad_down_w[None],
    )


def solution(mesh):
    placed = (
        P("ep", None),
        P("ep", None),
        P(),
        P(None, "tp"),
        P(None, "tp"),
        P(None, "tp"),
        P("tp", None),
        P(),
        P(),
        P("ep", None, "tp"),
        P("ep", None, "tp"),
        P("ep", "tp", None),
        P("ep", None),
    )
    return jax.shard_map(
        body,
        mesh=mesh,
        in_specs=placed,
        out_specs=(
            P("ep", None),
            P("ep", None),
            P(),
            P(None, "tp"),
            P(None, "tp"),
            P(None, "tp"),
            P("tp", None),
            P(),
            P(),
            P("ep", None, "tp"),
            P("ep", None, "tp"),
            P("ep", "tp", None),
        ),
        check_vma=False,
    )
```

time: 1860 us -> 757 us (0.41)
  waiting for transfers between devices: 931 us -> 218 us
  local copies, waits for them, and re-layouts: 322 us -> 117 us
  blocking collectives: 214 us -> 9.06 us
  starting transfers between devices: 17.3 us -> 200 us
  matrix products: 210 us -> 113 us
  other arithmetic: 135 us -> 69.8 us
    psum x4 -> x1, waiting for transfers between devices: 488 us -> 0.02 us  [body(): grad_qkv_w = lax.psum(grad_qkv_w, 'ep').astype(F32)]
    all_to_all x3 -> x1, waiting for transfers between devices: 443 us -> 0.01 us  [body(): lax.all_to_all(ordered, 'ep', split_axis=0, concat_axis=0, tiled=True)]
    gather x15 -> x2, local copies, waits for them, and re-layouts: 215 us -> 1.26 us  [the longest x1 0.68 us: body(): ordered = jnp.take(grad_gate_own.reshape(n_ep, quarter), slots, axis=0)]
    ppermute x0 -> x89, waiting for transfers between devices: none -> 204 us  [the longest x22 62.6 us: swap(): lax.ppermute(x, 'ep', [(i, i ^ bit) for i in range(lax.axis_size('ep'))])]
    ppermute x0 -> x89, starting transfers between devices: none -> 196 us  [the longest x24 118 us: step_right(): lax.ppermute(x, 'tp', [(i, i + 1) for i in range(n - 1 if upto is None el...]
    all_to_all x1 -> x0, blocking collectives: 180 us -> none  [body(): lax.all_to_all(grad_shares, 'ep', split_axis=0, concat_axis=0, tiled=True)]
    dot_general x65 -> x45, matrix products: 210 us -> 113 us  [the longest x1 10.2 us: body(): jnp.dot(grad_up_vals, up_matrix.T, preferred_element_type=F32)]
    convert_element_type x18 -> x17, other arithmetic: 74.8 us -> 18.9 us  [the longest x6 5.52 us: scatter_tp(): give_right = (give_right.astype(F32) + right.astype(F32)).astype(BF)]
  transfers between devices with their start and end apart: 7 -> 96, of which waited for: 7 -> 35; matrix products, arithmetic and copies ran while one was open for 7% -> 38% of each run, Pallas kernels for 0% -> 0%
where the time goes in v1:
time: 757 us; the launch traced here: 745 us
  waiting for transfers between devices  218 us (29%)
  starting transfers between devices  200 us (26%)
  local copies, waits for them, and re-layouts  117 us (15%)
  matrix products  113 us (15%)
  other arithmetic  69.8 us (9%)
  between operations  17.1 us (2%)
  blocking collectives  9.06 us (1%)
    ppermute x24, starting transfers between devices, step_right(): lax.ppermute(x, 'tp', [(i, i + 1) for i in range(n - 1 if upto is None el...  118 us
    ppermute x22, waiting for transfers between devices, swap(): lax.ppermute(x, 'ep', [(i, i ^ bit) for i in range(lax.axis_size('ep'))])  62.6 us
    ppermute x24, waiting for transfers between devices, step_left(): lax.ppermute(x, 'tp', [(n - 1 - i, n - 2 - i) for i in range(n - 1 if upt...  51.8 us
    ppermute x24, waiting for transfers between devices, step_right(): lax.ppermute(x, 'tp', [(i, i + 1) for i in range(n - 1 if upto is None el...  45.6 us
    ppermute x10, waiting for transfers between devices, sum_all(): x = x + lax.ppermute(x, axis, [(i, i ^ bit) for i in range(n)])  30.1 us
    ppermute x24, starting transfers between devices, step_left(): lax.ppermute(x, 'tp', [(n - 1 - i, n - 2 - i) for i in range(n - 1 if upt...  29.3 us
    unnamed x239, local copies, waits for them, and re-layouts  27.7 us
    ppermute x9, starting transfers between devices, exchange_tp(): got = lax.ppermute(piece, 'tp', [(i, (i + s) % n) for i in range(n)])  21.5 us
  transfers between devices with their start and end apart: 96, of which 35 were waited for; matrix products, arithmetic and copies ran while one was open for 38% of the time, Pallas kernels for 0%

profile of v1, /device:TPU:0, one launch (start us, length us, event | category | flops | bytes accessed | tf_op | source)
XLA Modules:
  0.0 744.7 jit_solution(4442357662216046830)
XLA Ops:
  21.1 2.9 fusion.168
  52.1 9.1 %all-gather = s32[2048,4]{0,1:T(4,128)S(1)} all-gather(s32[256,4]{0,1:T(4,128)S(1)} %constant_dynamic-slice_fusion.10), channel_id=2, replica_groups=mesh['ep'=8,'tp'=4] {'ep'}, dimensions={0}, use_global_device_ids=true | all-gather | bytes 36864 | tf_op jit(solution)/shard_map/all_gather | solution.py:234
  71.6 5.3 collective-permute-start.22
  85.2 4.6 collective-permute-start.16
  91.1 4.6 collective-permute-start.26
  101.5 4.6 collective-permute-start.10
  110.0 4.6 collective-permute-start.20
  115.3 5.1 collective-permute-done.11
  123.0 7.8 %collective-permute-done.18 = bf16[1536,128]{1,0:T(8,128)(2,1)S(1)} collective-permute-done((bf16[1536,128]{1,0:T(8,128)(2,1)S(1)}, bf16[1536,128]{1,0:T(8,128)(2,1)S(1)}, u32[]{:S(2)}, u32[]{:S(2)}) %collective-permute-start.18) | collective-permute-done | bytes 393248 | tf_op jit(solution)/shard_map/ppermute | solution.py:129
  134.0 10.3 %collective-permute-done.12 = bf16[1536,128]{1,0:T(8,128)(2,1)S(1)} collective-permute-done((bf16[1536,128]{1,0:T(8,128)(2,1)S(1)}, bf16[1536,128]{1,0:T(8,128)(2,1)S(1)}, u32[]{:S(2)}, u32[]{:S(2)}) %collective-permute-start.12) | collective-permute-done | bytes 393248 | tf_op jit(solution)/shard_map/ppermute | solution.py:129
  150.4 7.1 collective-permute-done.27
  157.5 4.4 collective-permute-start.21
  163.7 15.6 %collective-permute-done.21 = bf16[1536,128]{1,0:T(8,128)(2,1)S(1)} collective-permute-done((bf16[1536,128]{1,0:T(8,128)(2,1)S(1)}, bf16[1536,128]{1,0:T(8,128)(2,1)S(1)}, u32[]{:S(2)}, u32[]{:S(2)}) %collective-permute-start.21) | collective-permute-done | bytes 393248 | tf_op jit(solution)/shard_map/ppermute | solution.py:124
  181.3 11.9 %collective-permute-start.15 = (bf16[1536,128]{1,0:T(8,128)(2,1)S(1)}, bf16[1536,128]{1,0:T(8,128)(2,1)S(1)}, u32[]{:S(2)}, u32[]{:S(2)}) collective-permute-start(bf16[1536,128]{1,0:T(8,128)(2,1)S(1)} %collective-permute-done.14), channel_id=1, source_target_pairs={{0,1},{1,2},{2,3},{4,5},{5,6},{6,7},{8,9},{9,10},{10,11},{12,13},{... | collective-permute-start | bytes 1179656 | tf_op jit(solution)/shard_map/ppermute | solution.py:124
  200.8 7.2 collective-permute-done.13
  214.9 4.3 multiply_reduce_fusion.2
  226.1 13.8 %collective-permute-done.4 = bf16[256,1536]{1,0:T(8,128)(2,1)S(1)} collective-permute-done((bf16[256,1536]{1,0:T(8,128)(2,1)S(1)}, bf16[256,1536]{1,0:T(8,128)(2,1)S(1)}, u32[]{:S(2)}, u32[]{:S(2)}) %collective-permute-start.4) | collective-permute-done | bytes 786464 | tf_op jit(solution)/shard_map/ppermute | solution.py:100
  239.9 17.9 %collective-permute-done.6 = bf16[256,1536]{1,0:T(8,128)(2,1)S(1)} collective-permute-done((bf16[256,1536]{1,0:T(8,128)(2,1)S(1)}, bf16[256,1536]{1,0:T(8,128)(2,1)S(1)}, u32[]{:S(2)}, u32[]{:S(2)}) %collective-permute-start.6) | collective-permute-done | bytes 786464 | tf_op jit(solution)/shard_map/ppermute | solution.py:100
  263.2 4.0 fusion
  267.2 5.9 fusion.115
  273.2 5.9 fusion.112
  279.2 7.7 %multiply_convert_fusion.2 = (bf16[2048,512]{1,0:T(8,128)(2,1)S(1)}, bf16[2048,512]{1,0:T(8,128)(2,1)S(1)}, bf16[2048,512]{1,0:T(8,128)(2,1)S(1)}) fusion(f32[2048,512]{1,0:T(8,128)} %fusion.112, f32[2048,512]{1,0:T(8,128)} %fusion.115, bf16[2048,1536]{1,0:T(8,128)(2,1)S(1)} %bitcast.460, bf16[1536,128]{1,0:T(8,128)(2,1)S(1)} %copy-done.62, ...), kind=kOutput, calls=%fused_computation.37 | convolution fusion | flops 3243245568 | bytes 22544384 | tf_op jit(solution)/shard_map/dot_general | solution.py:277
  287.0 3.6 convolution_convert_fusion.2
  291.5 5.0 collective-permute-start.83
  298.1 3.6 convolution_convert_fusion.3
  306.2 3.6 convolution_convert_fusion.4
  313.1 7.8 %fusion.1 = (f32[2048]{0:T(1024)S(1)}, bf16[2048,1536]{1,0:T(8,128)(2,1)}) fusion(bf16[8,256,1536]{2,1,0:T(8,128)(2,1)} %bitcast_dynamic-update-slice_fusion.4, f32[2048]{0:T(1024)S(1)} %bitcast.516, bf16[2048,512]{1,0:T(8,128)(2,1)S(1)} %copy-done.95, bf16[128,1536]{1,0:T(8,128)(2,1)S(1)} %copy-done.59, bf16[128,1536]{1,0:T(8,128)(2,1)S(1)} %copy-done.54, ...), kind=kOutput, calls=%fused_computation.5 | convolution fusion | flops 3243243520 | bytes 16269312 | tf_op jit(solution)/shard_map/dot_general | solution.py:282
  322.3 3.3 all-to-all-start
  326.0 10.2 %fusion.114 = f32[2048,1536]{1,0:T(8,128)} fusion(bf16[2048,512]{1,0:T(8,128)(2,1)} %copy-done.92, bf16[1536,128]{1,0:T(8,128)(2,1)} %broadcast_select_fusion.3, bf16[1536,128]{1,0:T(8,128)(2,1)} %broadcast_select_fusion.5, bf16[1536,128]{1,0:T(8,128)(2,1)} %broadcast_select_fusion.7, bf16[1536,128]{1,0:T(8,128)(2,1)} %bitcast.524), kind=kOutput, calls=%fused_computation.249 | convolution fusion | flops 3227516928 | bytes 16252928 | tf_op jit(solution)/shard_map/dot_general | solution.py:294
  336.2 7.3 add_convert_fusion
  361.3 3.3 collective-permute-done.84
  365.3 7.0 collective-permute-start.72
  373.8 10.7 %collective-permute-start.85 = (bf16[128,1536]{1,0:T(8,128)(2,1)S(1)}, bf16[128,1536]{1,0:T(8,128)(2,1)S(1)}, u32[]{:S(2)}, u32[]{:S(2)}) collective-permute-start(bf16[128,1536]{1,0:T(8,128)(2,1)S(1)} %get-tuple-element.156), channel_id=1, source_target_pairs={{0,1},{1,2},{2,3},{4,5},{5,6},{6,7},{8,9},{9,10},{10,11},{12,13},{... | collective-permute-start | bytes 1179656 | tf_op jit(solution)/shard_map/ppermute | solution.py:124
  386.0 6.6 collective-permute-start.79
  395.2 7.0 collective-permute-start.73
  412.2 14.6 %collective-permute-done.46 = bf16[256,1536]{1,0:T(8,128)(2,1)S(1)} collective-permute-done((bf16[256,1536]{1,0:T(8,128)(2,1)S(1)}, bf16[256,1536]{1,0:T(8,128)(2,1)S(1)}, u32[]{:S(2)}, u32[]{:S(2)}) %collective-permute-start.46) | collective-permute-done | bytes 786464 | tf_op jit(solution)/shard_map/ppermute | solution.py:100
  426.8 13.8 %collective-permute-done.47 = bf16[256,1536]{1,0:T(8,128)(2,1)S(1)} collective-permute-done((bf16[256,1536]{1,0:T(8,128)(2,1)S(1)}, bf16[256,1536]{1,0:T(8,128)(2,1)S(1)}, u32[]{:S(2)}, u32[]{:S(2)}) %collective-permute-start.47) | collective-permute-done | bytes 786464 | tf_op jit(solution)/shard_map/ppermute | solution.py:100
  445.0 3.7 convolution_convert_fusion.5
  451.1 5.3 convolution_convert_fusion
  463.0 3.2 collective-permute-start.49
  470.6 2.9 collective-permute-start.51
  478.9 4.9 copy.186
  506.0 3.2 fusion.10
  534.4 3.8 constant_dynamic-slice_fusion
  540.1 2.9 collective-permute-start.52
  544.9 3.5 bitcast_dynamic-update-slice_fusion.15
  560.0 4.4 collective-permute-start.54
  568.6 7.2 collective-permute-start.32
  577.5 11.1 %collective-permute-done.54 = bf16[256,640]{1,0:T(8,128)(2,1)S(1)} collective-permute-done((bf16[256,640]{1,0:T(8,128)(2,1)}, bf16[256,640]{1,0:T(8,128)(2,1)S(1)}, u32[]{:S(2)}, u32[]{:S(2)}) %collective-permute-start.54) | collective-permute-done | bytes 327712 | tf_op jit(solution)/shard_map/ppermute | solution.py:164
  589.4 6.0 fusion.37
  600.0 3.1 bitcast_dynamic-update-slice_fusion.3
  606.6 5.5 collective-permute-start.55
  613.7 4.2 convolution_convert_fusion.1
  629.5 4.4 collective-permute-start.59
  633.9 10.9 %collective-permute-done.34 = bf16[256,1536]{1,0:T(8,128)(2,1)} collective-permute-done((bf16[256,1536]{1,0:T(8,128)(2,1)}, bf16[256,1536]{1,0:T(8,128)(2,1)}, u32[]{:S(2)}, u32[]{:S(2)}) %collective-permute-start.34) | collective-permute-done | bytes 786464 | tf_op jit(solution)/shard_map/ppermute | solution.py:129
  646.8 3.3 collective-permute-start.65
  650.7 28.1 %collective-permute-done.65 = f32[1,1536]{1,0:T(1,128)S(1)} collective-permute-done((f32[1,1536]{1,0:T(1,128)S(1)}, f32[1,1536]{1,0:T(1,128)S(1)}, u32[]{:S(2)}, u32[]{:S(2)}) %collective-permute-start.65) | collective-permute-done | bytes 6176 | tf_op jit(solution)/shard_map/ppermute | solution.py:183
  683.6 4.0 collective-permute-start.37
  688.9 5.4 collective-permute-start.60
  697.7 10.7 %reduce-scatter.5.cloned.1.call-done = bf16[1,48,1536]{2,1,0:T(8,128)(2,1)} async-done(((bf16[4,48,1536]{2,1,0:T(8,128)(2,1)}), bf16[1,48,1536]{2,1,0:T(8,128)(2,1)}) %reduce-scatter.5.cloned.1.call-update) | async-done | bytes 147472 | tf_op jit(solution)/shard_map/reduce_scatter | solution.py:343
  708.3 4.8 collective-permute-done.37
  718.8 10.1 %collective-permute-done.60 = bf16[256,1536]{1,0:T(8,128)(2,1)} collective-permute-done((bf16[256,1536]{1,0:T(8,128)(2,1)S(1)}, bf16[256,1536]{1,0:T(8,128)(2,1)}, u32[]{:S(2)}, u32[]{:S(2)}) %collective-permute-start.60) | collective-permute-done | bytes 786464 | tf_op jit(solution)/shard_map/ppermute | solution.py:124
  731.1 3.4 all-gather.10.cloned.1.call-done
  734.5 3.0 bitcast_convert_fusion
  (587 shorter events, 292.8 us)
Async XLA Ops:
  7.2 207.7 %all-gather.6.cloned.1.call-start = ((), (), s32[]{:S(2)}) async-start(), calls=%async_computation.3 | async-start | bytes 4866048 | tf_op jit(solution)/shard_map/all_gather | solution.py:222
  9.7 72.1 %collective-permute-start.38 = (bf16[256,1536]{1,0:T(8,128)(2,1)}, bf16[256,1536]{1,0:T(8,128)(2,1)}, u32[]{:S(2)}, u32[]{:S(2)}) collective-permute-start(bf16[256,1536]{1,0:T(8,128)(2,1)} %get-tuple-element.132), channel_id=1, source_target_pairs={{0,4},{4,0},{8,12},{12,8},{16,20},{20,16},{24,28},{28,24},{1,5},{5... | collective-permute-start | bytes 2359304 | tf_op jit(solution)/shard_map/ppermute | solution.py:100
  10.2 80.9 %collective-permute-start.39 = (bf16[256,1536]{1,0:T(8,128)(2,1)}, bf16[256,1536]{1,0:T(8,128)(2,1)}, u32[]{:S(2)}, u32[]{:S(2)}) collective-permute-start(bf16[256,1536]{1,0:T(8,128)(2,1)} %get-tuple-element.132), channel_id=1, source_target_pairs={{0,8},{4,12},{8,0},{12,4},{16,24},{20,28},{24,16},{28,20},{1,9},{5... | collective-permute-start | bytes 2359304 | tf_op jit(solution)/shard_map/ppermute | solution.py:100
  13.4 576.0 %all-gather.8.cloned.1.call-start = ((), (), s32[]{:S(2)}) async-start(), calls=%async_computation.4 | async-start | bytes 8110080 | tf_op jit(solution)/shard_map/all_gather | solution.py:226
  41.6 22.9 %collective-permute-start = (bf16[256,384]{1,0:T(8,128)(2,1)}, bf16[256,384]{1,0:T(8,128)(2,1)}, u32[]{:S(2)}, u32[]{:S(2)}) collective-permute-start(bf16[256,384]{1,0:T(8,128)(2,1)} %get-tuple-element.190), channel_id=1, source_target_pairs={{0,1},{1,2},{2,3},{3,0},{4,5},{5,6},{6,7},{7,4},{8,9},{9,10},{10,1... | collective-permute-start | bytes 589832 | tf_op jit(solution)/shard_map/ppermute | solution.py:164
  43.2 25.3 %collective-permute-start.1 = (bf16[256,384]{1,0:T(8,128)(2,1)}, bf16[256,384]{1,0:T(8,128)(2,1)}, u32[]{:S(2)}, u32[]{:S(2)}) collective-permute-start(bf16[256,384]{1,0:T(8,128)(2,1)} %get-tuple-element.189), channel_id=1, source_target_pairs={{0,2},{1,3},{2,0},{3,1},{4,6},{5,7},{6,4},{7,5},{8,10},{9,11},{10,... | collective-permute-start | bytes 589832 | tf_op jit(solution)/shard_map/ppermute | solution.py:164
  45.8 25.8 %collective-permute-start.2 = (bf16[256,384]{1,0:T(8,128)(2,1)}, bf16[256,384]{1,0:T(8,128)(2,1)}, u32[]{:S(2)}, u32[]{:S(2)}) collective-permute-start(bf16[256,384]{1,0:T(8,128)(2,1)} %get-tuple-element.188), channel_id=1, source_target_pairs={{0,3},{1,0},{2,1},{3,2},{4,7},{5,4},{6,5},{7,6},{8,11},{9,8},{10,9... | collective-permute-start | bytes 589832 | tf_op jit(solution)/shard_map/ppermute | solution.py:164
  64.5 129.6 %collective-permute-start.41 = (bf16[256,1536]{1,0:T(8,128)(2,1)}, bf16[256,1536]{1,0:T(8,128)(2,1)}, u32[]{:S(2)}, u32[]{:S(2)}) collective-permute-start(bf16[256,1536]{1,0:T(8,128)(2,1)} %get-tuple-element.132), channel_id=1, source_target_pairs={{0,16},{4,20},{8,24},{12,28},{16,0},{20,4},{24,8},{28,12},{1,17},{... | collective-permute-start | bytes 2359304 | tf_op jit(solution)/shard_map/ppermute | solution.py:100
  100.2 20.2 %collective-permute-start.11 = (bf16[1536,128]{1,0:T(8,128)(2,1)S(1)}, bf16[1536,128]{1,0:T(8,128)(2,1)S(1)}, u32[]{:S(2)}, u32[]{:S(2)}) collective-permute-start(bf16[1536,128]{1,0:T(8,128)(2,1)S(1)} %bitcast.526), channel_id=1, source_target_pairs={{3,2},{2,1},{1,0},{7,6},{6,5},{5,4},{11,10},{10,9},{9,8},{15,14},{... | collective-permute-start | bytes 1179656 | tf_op jit(solution)/shard_map/ppermute | solution.py:129
  101.5 20.2 %collective-permute-start.10 = (bf16[1536,128]{1,0:T(8,128)(2,1)S(1)}, bf16[1536,128]{1,0:T(8,128)(2,1)S(1)}, u32[]{:S(2)}, u32[]{:S(2)}) collective-permute-start(bf16[1536,128]{1,0:T(8,128)(2,1)S(1)} %bitcast.527), channel_id=1, source_target_pairs={{0,1},{1,2},{2,3},{4,5},{5,6},{6,7},{8,9},{9,10},{10,11},{12,13},{... | collective-permute-start | bytes 1179656 | tf_op jit(solution)/shard_map/ppermute | solution.py:124
  108.7 22.1 %collective-permute-start.18 = (bf16[1536,128]{1,0:T(8,128)(2,1)S(1)}, bf16[1536,128]{1,0:T(8,128)(2,1)S(1)}, u32[]{:S(2)}, u32[]{:S(2)}) collective-permute-start(bf16[1536,128]{1,0:T(8,128)(2,1)S(1)} %collective-permute-done.17), channel_id=1, source_target_pairs={{3,2},{2,1},{1,0},{7,6},{6,5},{5,4},{11,10},{10,9},{9,8},{15,14},{... | collective-permute-start | bytes 1179656 | tf_op jit(solution)/shard_map/ppermute | solution.py:129
  110.0 23.1 %collective-permute-start.20 = (bf16[1536,128]{1,0:T(8,128)(2,1)S(1)}, bf16[1536,128]{1,0:T(8,128)(2,1)S(1)}, u32[]{:S(2)}, u32[]{:S(2)}) collective-permute-start(bf16[1536,128]{1,0:T(8,128)(2,1)S(1)} %collective-permute-done.16), channel_id=1, source_target_pairs={{0,1},{1,2},{2,3},{4,5},{5,6},{6,7},{8,9},{9,10},{10,11},{12,13},{... | collective-permute-start | bytes 1179656 | tf_op jit(solution)/shard_map/ppermute | solution.py:124
  120.4 74.9 %collective-permute-start.43 = (bf16[256,1536]{1,0:T(8,128)(2,1)}, bf16[256,1536]{1,0:T(8,128)(2,1)}, u32[]{:S(2)}, u32[]{:S(2)}) collective-permute-start(bf16[256,1536]{1,0:T(8,128)(2,1)} %get-tuple-element.132), channel_id=1, source_target_pairs={{0,24},{4,28},{8,16},{12,20},{16,8},{20,12},{24,0},{28,4},{1,25},{... | collective-permute-start | bytes 2359304 | tf_op jit(solution)/shard_map/ppermute | solution.py:100
  121.7 22.6 %collective-permute-start.12 = (bf16[1536,128]{1,0:T(8,128)(2,1)S(1)}, bf16[1536,128]{1,0:T(8,128)(2,1)S(1)}, u32[]{:S(2)}, u32[]{:S(2)}) collective-permute-start(bf16[1536,128]{1,0:T(8,128)(2,1)S(1)} %collective-permute-done.11), channel_id=1, source_target_pairs={{3,2},{2,1},{1,0},{7,6},{6,5},{5,4},{11,10},{10,9},{9,8},{15,14},{... | collective-permute-start | bytes 1179656 | tf_op jit(solution)/shard_map/ppermute | solution.py:129
  133.1 75.7 %collective-permute-start.40 = (bf16[256,1536]{1,0:T(8,128)(2,1)}, bf16[256,1536]{1,0:T(8,128)(2,1)S(1)}, u32[]{:S(2)}, u32[]{:S(2)}) collective-permute-start(bf16[256,1536]{1,0:T(8,128)(2,1)} %collective-permute-done.39), channel_id=1, source_target_pairs={{0,4},{4,0},{8,12},{12,8},{16,20},{20,16},{24,28},{28,24},{1,5},{5... | collective-permute-start | bytes 2359304 | tf_op jit(solution)/shard_map/ppermute | solution.py:100
  148.3 33.0 %collective-permute-start.25 = (bf16[128,1536]{1,0:T(8,128)(2,1)S(1)}, bf16[128,1536]{1,0:T(8,128)(2,1)S(1)}, u32[]{:S(2)}, u32[]{:S(2)}) collective-permute-start(bf16[128,1536]{1,0:T(8,128)(2,1)S(1)} %collective-permute-done.24), channel_id=1, source_target_pairs={{3,2},{2,1},{1,0},{7,6},{6,5},{5,4},{11,10},{10,9},{9,8},{15,14},{... | collective-permute-start | bytes 1179656 | tf_op jit(solution)/shard_map/ppermute | solution.py:129
  157.5 21.8 %collective-permute-start.21 = (bf16[1536,128]{1,0:T(8,128)(2,1)S(1)}, bf16[1536,128]{1,0:T(8,128)(2,1)S(1)}, u32[]{:S(2)}, u32[]{:S(2)}) collective-permute-start(bf16[1536,128]{1,0:T(8,128)(2,1)S(1)} %collective-permute-done.20), channel_id=1, source_target_pairs={{0,1},{1,2},{2,3},{4,5},{5,6},{6,7},{8,9},{9,10},{10,11},{12,13},{... | collective-permute-start | bytes 1179656 | tf_op jit(solution)/shard_map/ppermute | solution.py:124
  198.0 25.1 %collective-permute-start.44 = (bf16[256,1536]{1,0:T(8,128)(2,1)}, bf16[256,1536]{1,0:T(8,128)(2,1)}, u32[]{:S(2)}, u32[]{:S(2)}) collective-permute-start(bf16[256,1536]{1,0:T(8,128)(2,1)} %collective-permute-done.43), channel_id=1, source_target_pairs={{0,4},{4,0},{8,12},{12,8},{16,20},{20,16},{24,28},{28,24},{1,5},{5... | collective-permute-start | bytes 2359304 | tf_op jit(solution)/shard_map/ppermute | solution.py:100
  219.4 38.9 %collective-permute-start.3 = (bf16[256,1536]{1,0:T(8,128)(2,1)S(1)}, bf16[256,1536]{1,0:T(8,128)(2,1)S(1)}, u32[]{:S(2)}, u32[]{:S(2)}) collective-permute-start(bf16[256,1536]{1,0:T(8,128)(2,1)S(1)} %get-tuple-element.138), channel_id=1, source_target_pairs={{0,4},{4,0},{8,12},{12,8},{16,20},{20,16},{24,28},{28,24},{1,5},{5... | collective-permute-start | bytes 2359304 | tf_op jit(solution)/shard_map/ppermute | solution.py:100
  219.5 20.4 %collective-permute-start.4 = (bf16[256,1536]{1,0:T(8,128)(2,1)S(1)}, bf16[256,1536]{1,0:T(8,128)(2,1)S(1)}, u32[]{:S(2)}, u32[]{:S(2)}) collective-permute-start(bf16[256,1536]{1,0:T(8,128)(2,1)S(1)} %get-tuple-element.138), channel_id=1, source_target_pairs={{0,8},{4,12},{8,0},{12,4},{16,24},{20,28},{24,16},{28,20},{1,9},{5... | collective-permute-start | bytes 2359304 | tf_op jit(solution)/shard_map/ppermute | solution.py:100
  221.4 36.5 %collective-permute-start.6 = (bf16[256,1536]{1,0:T(8,128)(2,1)S(1)}, bf16[256,1536]{1,0:T(8,128)(2,1)S(1)}, u32[]{:S(2)}, u32[]{:S(2)}) collective-permute-start(bf16[256,1536]{1,0:T(8,128)(2,1)S(1)} %get-tuple-element.138), channel_id=1, source_target_pairs={{0,16},{4,20},{8,24},{12,28},{16,0},{20,4},{24,8},{28,12},{1,17},{... | collective-permute-start | bytes 2359304 | tf_op jit(solution)/shard_map/ppermute | solution.py:100
  222.8 35.0 %collective-permute-start.8 = (bf16[256,1536]{1,0:T(8,128)(2,1)S(1)}, bf16[256,1536]{1,0:T(8,128)(2,1)S(1)}, u32[]{:S(2)}, u32[]{:S(2)}) collective-permute-start(bf16[256,1536]{1,0:T(8,128)(2,1)S(1)} %get-tuple-element.138), channel_id=1, source_target_pairs={{0,24},{4,28},{8,16},{12,20},{16,8},{20,12},{24,0},{28,4},{1,25},{... | collective-permute-start | bytes 2359304 | tf_op jit(solution)/shard_map/ppermute | solution.py:100
  291.5 59.4 %collective-permute-start.83 = (bf16[128,1536]{1,0:T(8,128)(2,1)}, bf16[128,1536]{1,0:T(8,128)(2,1)}, u32[]{:S(2)}, u32[]{:S(2)}) collective-permute-start(bf16[128,1536]{1,0:T(8,128)(2,1)} %get-tuple-element.160), channel_id=1, source_target_pairs={{0,1},{4,5},{8,9},{12,13},{16,17},{20,21},{24,25},{28,29}} | collective-permute-start | bytes 1179656 | tf_op jit(solution)/shard_map/ppermute | solution.py:124
  296.5 55.3 %collective-permute-start.86 = (bf16[128,1536]{1,0:T(8,128)(2,1)}, bf16[128,1536]{1,0:T(8,128)(2,1)}, u32[]{:S(2)}, u32[]{:S(2)}) collective-permute-start(bf16[128,1536]{1,0:T(8,128)(2,1)} %get-tuple-element.161), channel_id=1, source_target_pairs={{3,2},{7,6},{11,10},{15,14},{19,18},{23,22},{27,26},{31,30}} | collective-permute-start | bytes 1179656 | tf_op jit(solution)/shard_map/ppermute | solution.py:129
  302.8 50.9 %collective-permute-start.77 = (bf16[1536,128]{1,0:T(8,128)(2,1)}, bf16[1536,128]{1,0:T(8,128)(2,1)}, u32[]{:S(2)}, u32[]{:S(2)}) collective-permute-start(bf16[1536,128]{1,0:T(8,128)(2,1)} %get-tuple-element.166), channel_id=1, source_target_pairs={{0,1},{4,5},{8,9},{12,13},{16,17},{20,21},{24,25},{28,29}} | collective-permute-start | bytes 1179656 | tf_op jit(solution)/shard_map/ppermute | solution.py:124
  304.8 49.0 %collective-permute-start.80 = (bf16[1536,128]{1,0:T(8,128)(2,1)}, bf16[1536,128]{1,0:T(8,128)(2,1)}, u32[]{:S(2)}, u32[]{:S(2)}) collective-permute-start(bf16[1536,128]{1,0:T(8,128)(2,1)} %get-tuple-element.167), channel_id=1, source_target_pairs={{3,2},{7,6},{11,10},{15,14},{19,18},{23,22},{27,26},{31,30}} | collective-permute-start | bytes 1179656 | tf_op jit(solution)/shard_map/ppermute | solution.py:129
  310.9 45.6 %collective-permute-start.71 = (bf16[1536,128]{1,0:T(8,128)(2,1)}, bf16[1536,128]{1,0:T(8,128)(2,1)}, u32[]{:S(2)}, u32[]{:S(2)}) collective-permute-start(bf16[1536,128]{1,0:T(8,128)(2,1)} %get-tuple-element.172), channel_id=1, source_target_pairs={{0,1},{4,5},{8,9},{12,13},{16,17},{20,21},{24,25},{28,29}} | collective-permute-start | bytes 1179656 | tf_op jit(solution)/shard_map/ppermute | solution.py:124
  322.3 26.7 %all-to-all-start = ((f32[8,1,256]{2,1,0:T(1,128)}), f32[8,1,256]{2,1,0:T(1,128)S(1)}, u32[]{:S(2)}, u32[]{:S(2)}) async-start(f32[8,1,256]{2,1,0:T(1,128)} %copy.161), calls=%async_computation | async-start | bytes 16384 | tf_op jit(solution)/shard_map/all_to_all | solution.py:305
  325.7 353.7 %reduce-scatter.3.cloned.1.call-start = ((), (), s32[]{:S(2)}) async-start(), calls=%async_computation.6 | async-start | bytes 5308416 | tf_op jit(solution)/shard_map/reduce_scatter | solution.py:340
  351.8 53.4 %collective-permute-start.45 = (bf16[4,256,1536]{2,1,0:T(8,128)(2,1)}, bf16[4,256,1536]{2,1,0:T(8,128)(2,1)S(1)}, u32[]{:S(2)}, u32[]{:S(2)}) collective-permute-start(bf16[4,256,1536]{2,1,0:T(8,128)(2,1)} %slice.376), channel_id=1, source_target_pairs={{0,4},{4,0},{8,12},{12,8},{16,20},{20,16},{24,28},{28,24},{1,5},{5... | collective-permute-start | bytes 9437192 | tf_op jit(solution)/shard_map/ppermute | solution.py:100
  353.7 56.2 %collective-permute-start.28 = (bf16[4,256,1536]{2,1,0:T(8,128)(2,1)}, bf16[4,256,1536]{2,1,0:T(8,128)(2,1)S(1)}, u32[]{:S(2)}, u32[]{:S(2)}) collective-permute-start(bf16[4,256,1536]{2,1,0:T(8,128)(2,1)} %slice.370), channel_id=1, source_target_pairs={{0,4},{4,0},{8,12},{12,8},{16,20},{20,16},{24,28},{28,24},{1,5},{5... | collective-permute-start | bytes 9437192 | tf_op jit(solution)/shard_map/ppermute | solution.py:100
  365.3 19.3 %collective-permute-start.72 = (bf16[1536,128]{1,0:T(8,128)(2,1)S(1)}, bf16[1536,128]{1,0:T(8,128)(2,1)S(1)}, u32[]{:S(2)}, u32[]{:S(2)}) collective-permute-start(bf16[1536,128]{1,0:T(8,128)(2,1)S(1)} %get-tuple-element.170), channel_id=1, source_target_pairs={{0,1},{1,2},{4,5},{5,6},{8,9},{9,10},{12,13},{13,14},{16,17},{17,1... | collective-permute-start | bytes 1179656 | tf_op jit(solution)/shard_map/ppermute | solution.py:124
  373.8 19.9 %collective-permute-start.85 = (bf16[128,1536]{1,0:T(8,128)(2,1)S(1)}, bf16[128,1536]{1,0:T(8,128)(2,1)S(1)}, u32[]{:S(2)}, u32[]{:S(2)}) collective-permute-start(bf16[128,1536]{1,0:T(8,128)(2,1)S(1)} %get-tuple-element.156), channel_id=1, source_target_pairs={{0,1},{1,2},{2,3},{4,5},{5,6},{6,7},{8,9},{9,10},{10,11},{12,13},{... | collective-permute-start | bytes 1179656 | tf_op jit(solution)/shard_map/ppermute | solution.py:124
  395.2 207.9 %collective-permute-start.73 = (bf16[1536,128]{1,0:T(8,128)(2,1)}, bf16[1536,128]{1,0:T(8,128)(2,1)}, u32[]{:S(2)}, u32[]{:S(2)}) collective-permute-start(bf16[1536,128]{1,0:T(8,128)(2,1)} %get-tuple-element.168), channel_id=1, source_target_pairs={{0,1},{1,2},{2,3},{4,5},{5,6},{6,7},{8,9},{9,10},{10,11},{12,13},{... | collective-permute-start | bytes 1179656 | tf_op jit(solution)/shard_map/ppermute | solution.py:124
  406.3 20.5 %collective-permute-start.46 = (bf16[256,1536]{1,0:T(8,128)(2,1)S(1)}, bf16[256,1536]{1,0:T(8,128)(2,1)S(1)}, u32[]{:S(2)}, u32[]{:S(2)}) collective-permute-start(bf16[256,1536]{1,0:T(8,128)(2,1)S(1)} %get-tuple-element.144), channel_id=1, source_target_pairs={{0,8},{4,12},{8,0},{12,4},{16,24},{20,28},{24,16},{28,20},{1,9},{5... | collective-permute-start | bytes 2359304 | tf_op jit(solution)/shard_map/ppermute | solution.py:100
  407.8 32.7 %collective-permute-start.47 = (bf16[256,1536]{1,0:T(8,128)(2,1)S(1)}, bf16[256,1536]{1,0:T(8,128)(2,1)S(1)}, u32[]{:S(2)}, u32[]{:S(2)}) collective-permute-start(bf16[256,1536]{1,0:T(8,128)(2,1)S(1)} %get-tuple-element.146), channel_id=1, source_target_pairs={{0,16},{4,20},{8,24},{12,28},{16,0},{20,4},{24,8},{28,12},{1,17},{... | collective-permute-start | bytes 2359304 | tf_op jit(solution)/shard_map/ppermute | solution.py:100
  409.3 31.2 %collective-permute-start.48 = (bf16[256,1536]{1,0:T(8,128)(2,1)S(1)}, bf16[256,1536]{1,0:T(8,128)(2,1)S(1)}, u32[]{:S(2)}, u32[]{:S(2)}) collective-permute-start(bf16[256,1536]{1,0:T(8,128)(2,1)S(1)} %get-tuple-element.145), channel_id=1, source_target_pairs={{0,24},{4,28},{8,16},{12,20},{16,8},{20,12},{24,0},{28,4},{1,25},{... | collective-permute-start | bytes 2359304 | tf_op jit(solution)/shard_map/ppermute | solution.py:100
  442.3 31.3 %collective-permute-start.66 = (f32[9,1536]{1,0:T(8,128)}, f32[9,1536]{1,0:T(8,128)}, u32[]{:S(2)}, u32[]{:S(2)}) collective-permute-start(f32[9,1536]{1,0:T(8,128)} %pad_maximum_fusion.13), channel_id=1, source_target_pairs={{0,4},{4,0},{8,12},{12,8},{16,20},{20,16},{24,28},{28,24},{1,5},{5... | collective-permute-start | bytes 165896 | tf_op jit(solution)/shard_map/ppermute | solution.py:183
  463.0 23.8 %collective-permute-start.49 = (bf16[256,384]{1,0:T(8,128)(2,1)}, bf16[256,384]{1,0:T(8,128)(2,1)}, u32[]{:S(2)}, u32[]{:S(2)}) collective-permute-start(bf16[256,384]{1,0:T(8,128)(2,1)} %bitcast.444), channel_id=1, source_target_pairs={{0,1},{1,2},{2,3},{3,0},{4,5},{5,6},{6,7},{7,4},{8,9},{9,10},{10,1... | collective-permute-start | bytes 589832 | tf_op jit(solution)/shard_map/ppermute | solution.py:164
  468.0 21.5 %collective-permute-start.50 = (bf16[256,384]{1,0:T(8,128)(2,1)}, bf16[256,384]{1,0:T(8,128)(2,1)}, u32[]{:S(2)}, u32[]{:S(2)}) collective-permute-start(bf16[256,384]{1,0:T(8,128)(2,1)} %bitcast.443), channel_id=1, source_target_pairs={{0,2},{1,3},{2,0},{3,1},{4,6},{5,7},{6,4},{7,5},{8,10},{9,11},{10,... | collective-permute-start | bytes 589832 | tf_op jit(solution)/shard_map/ppermute | solution.py:164
  470.6 22.1 %collective-permute-start.51 = (bf16[256,384]{1,0:T(8,128)(2,1)}, bf16[256,384]{1,0:T(8,128)(2,1)}, u32[]{:S(2)}, u32[]{:S(2)}) collective-permute-start(bf16[256,384]{1,0:T(8,128)(2,1)} %bitcast.442), channel_id=1, source_target_pairs={{0,3},{1,0},{2,1},{3,2},{4,7},{5,4},{6,5},{7,6},{8,11},{9,8},{10,9... | collective-permute-start | bytes 589832 | tf_op jit(solution)/shard_map/ppermute | solution.py:164
  483.8 195.7 %all-reduce.4.cloned.1.call-start = ((), (), s32[]{:S(2)}) async-start(), calls=%async_computation.5 | async-start | bytes 3932160 | tf_op jit(solution)/shard_map/psum | solution.py:356
  483.8 121.5 %collective-permute-start.76 = (bf16[1536,128]{1,0:T(8,128)(2,1)}, bf16[1536,128]{1,0:T(8,128)(2,1)}, u32[]{:S(2)}, u32[]{:S(2)}) collective-permute-start(bf16[1536,128]{1,0:T(8,128)(2,1)} %get-tuple-element.169), channel_id=1, source_target_pairs={{3,2},{2,1},{1,0},{7,6},{6,5},{5,4},{11,10},{10,9},{9,8},{15,14},{... | collective-permute-start | bytes 1179656 | tf_op jit(solution)/shard_map/ppermute | solution.py:129
  486.9 52.8 %collective-permute-start.29 = (bf16[256,1536]{1,0:T(8,128)(2,1)}, bf16[256,1536]{1,0:T(8,128)(2,1)}, u32[]{:S(2)}, u32[]{:S(2)}) collective-permute-start(bf16[256,1536]{1,0:T(8,128)(2,1)} %get-tuple-element.147), channel_id=1, source_target_pairs={{0,8},{4,12},{8,0},{12,4},{16,24},{20,28},{24,16},{28,20},{1,9},{5... | collective-permute-start | bytes 2359304 | tf_op jit(solution)/shard_map/ppermute | solution.py:100
  489.5 50.6 %collective-permute-start.30 = (bf16[256,1536]{1,0:T(8,128)(2,1)}, bf16[256,1536]{1,0:T(8,128)(2,1)}, u32[]{:S(2)}, u32[]{:S(2)}) collective-permute-start(bf16[256,1536]{1,0:T(8,128)(2,1)} %get-tuple-element.149), channel_id=1, source_target_pairs={{0,16},{4,20},{8,24},{12,28},{16,0},{20,4},{24,8},{28,12},{1,17},{... | collective-permute-start | bytes 2359304 | tf_op jit(solution)/shard_map/ppermute | solution.py:100
  492.7 50.3 %collective-permute-start.31 = (bf16[256,1536]{1,0:T(8,128)(2,1)}, bf16[256,1536]{1,0:T(8,128)(2,1)}, u32[]{:S(2)}, u32[]{:S(2)}) collective-permute-start(bf16[256,1536]{1,0:T(8,128)(2,1)} %get-tuple-element.148), channel_id=1, source_target_pairs={{0,24},{4,28},{8,16},{12,20},{16,8},{20,12},{24,0},{28,4},{1,25},{... | collective-permute-start | bytes 2359304 | tf_op jit(solution)/shard_map/ppermute | solution.py:100
  540.1 20.0 %collective-permute-start.52 = (bf16[256,640]{1,0:T(8,128)(2,1)}, bf16[256,640]{1,0:T(8,128)(2,1)}, u32[]{:S(2)}, u32[]{:S(2)}) collective-permute-start(bf16[256,640]{1,0:T(8,128)(2,1)} %bitcast.149), channel_id=1, source_target_pairs={{0,1},{1,2},{2,3},{3,0},{4,5},{5,6},{6,7},{7,4},{8,9},{9,10},{10,1... | collective-permute-start | bytes 983048 | tf_op jit(solution)/shard_map/ppermute | solution.py:164
  557.8 54.4 %collective-permute-start.33 = (bf16[256,1536]{1,0:T(8,128)(2,1)}, bf16[256,1536]{1,0:T(8,128)(2,1)}, u32[]{:S(2)}, u32[]{:S(2)}) collective-permute-start(bf16[256,1536]{1,0:T(8,128)(2,1)} %get-tuple-element.134), channel_id=1, source_target_pairs={{3,2},{2,1},{1,0},{7,6},{6,5},{5,4},{11,10},{10,9},{9,8},{15,14},{... | collective-permute-start | bytes 2359304 | tf_op jit(solution)/shard_map/ppermute | solution.py:129
  560.0 28.6 %collective-permute-start.54 = (bf16[256,640]{1,0:T(8,128)(2,1)}, bf16[256,640]{1,0:T(8,128)(2,1)S(1)}, u32[]{:S(2)}, u32[]{:S(2)}) collective-permute-start(bf16[256,640]{1,0:T(8,128)(2,1)} %bitcast.508), channel_id=1, source_target_pairs={{0,3},{1,0},{2,1},{3,2},{4,7},{5,4},{6,5},{7,6},{8,11},{9,8},{10,9... | collective-permute-start | bytes 983048 | tf_op jit(solution)/shard_map/ppermute | solution.py:164
  568.6 55.8 %collective-permute-start.32 = (bf16[256,1536]{1,0:T(8,128)(2,1)}, bf16[256,1536]{1,0:T(8,128)(2,1)}, u32[]{:S(2)}, u32[]{:S(2)}) collective-permute-start(bf16[256,1536]{1,0:T(8,128)(2,1)} %get-tuple-element.134), channel_id=1, source_target_pairs={{0,1},{1,2},{2,3},{4,5},{5,6},{6,7},{8,9},{9,10},{10,11},{12,13},{... | collective-permute-start | bytes 2359304 | tf_op jit(solution)/shard_map/ppermute | solution.py:124
  605.3 22.7 %collective-permute-start.56 = (bf16[256,1536]{1,0:T(8,128)(2,1)}, bf16[256,1536]{1,0:T(8,128)(2,1)}, u32[]{:S(2)}, u32[]{:S(2)}) collective-permute-start(bf16[256,1536]{1,0:T(8,128)(2,1)} %get-tuple-element.129), channel_id=1, source_target_pairs={{3,2},{2,1},{1,0},{7,6},{6,5},{5,4},{11,10},{10,9},{9,8},{15,14},{... | collective-permute-start | bytes 2359304 | tf_op jit(solution)/shard_map/ppermute | solution.py:129
  606.6 22.9 %collective-permute-start.55 = (bf16[256,1536]{1,0:T(8,128)(2,1)}, bf16[256,1536]{1,0:T(8,128)(2,1)}, u32[]{:S(2)}, u32[]{:S(2)}) collective-permute-start(bf16[256,1536]{1,0:T(8,128)(2,1)} %get-tuple-element.129), channel_id=1, source_target_pairs={{0,1},{1,2},{2,3},{4,5},{5,6},{6,7},{8,9},{9,10},{10,11},{12,13},{... | collective-permute-start | bytes 2359304 | tf_op jit(solution)/shard_map/ppermute | solution.py:124
  612.1 32.7 %collective-permute-start.34 = (bf16[256,1536]{1,0:T(8,128)(2,1)}, bf16[256,1536]{1,0:T(8,128)(2,1)}, u32[]{:S(2)}, u32[]{:S(2)}) collective-permute-start(bf16[256,1536]{1,0:T(8,128)(2,1)} %collective-permute-done.33), channel_id=1, source_target_pairs={{3,2},{2,1},{1,0},{7,6},{6,5},{5,4},{11,10},{10,9},{9,8},{15,14},{... | collective-permute-start | bytes 2359304 | tf_op jit(solution)/shard_map/ppermute | solution.py:129
  617.9 90.4 %reduce-scatter.5.cloned.1.call-start = ((), (), s32[]{:S(2)}) async-start(), calls=%async_computation.7 | async-start | bytes 737280 | tf_op jit(solution)/shard_map/reduce_scatter | solution.py:343
  621.7 25.0 %collective-permute-start.64 = (f32[1,1536]{1,0:T(1,128)S(1)}, f32[1,1536]{1,0:T(1,128)S(1)}, u32[]{:S(2)}, u32[]{:S(2)}) collective-permute-start(f32[1,1536]{1,0:T(1,128)S(1)} %add.513), channel_id=1, source_target_pairs={{0,1},{1,0},{2,3},{3,2},{4,5},{5,4},{6,7},{7,6},{8,9},{9,8},{10,11... | collective-permute-start | bytes 18440 | tf_op jit(solution)/shard_map/ppermute | solution.py:183
  624.4 59.2 %collective-permute-start.36 = (bf16[256,1536]{1,0:T(8,128)(2,1)}, bf16[256,1536]{1,0:T(8,128)(2,1)S(1)}, u32[]{:S(2)}, u32[]{:S(2)}) collective-permute-start(bf16[256,1536]{1,0:T(8,128)(2,1)} %collective-permute-done.32), channel_id=1, source_target_pairs={{0,1},{1,2},{2,3},{4,5},{5,6},{6,7},{8,9},{9,10},{10,11},{12,13},{... | collective-permute-start | bytes 2359304 | tf_op jit(solution)/shard_map/ppermute | solution.py:124
  628.0 59.7 %collective-permute-start.57 = (bf16[256,1536]{1,0:T(8,128)(2,1)}, bf16[256,1536]{1,0:T(8,128)(2,1)S(1)}, u32[]{:S(2)}, u32[]{:S(2)}) collective-permute-start(bf16[256,1536]{1,0:T(8,128)(2,1)} %collective-permute-done.56), channel_id=1, source_target_pairs={{3,2},{2,1},{1,0},{7,6},{6,5},{5,4},{11,10},{10,9},{9,8},{15,14},{... | collective-permute-start | bytes 2359304 | tf_op jit(solution)/shard_map/ppermute | solution.py:129
  629.5 59.5 %collective-permute-start.59 = (bf16[256,1536]{1,0:T(8,128)(2,1)}, bf16[256,1536]{1,0:T(8,128)(2,1)S(1)}, u32[]{:S(2)}, u32[]{:S(2)}) collective-permute-start(bf16[256,1536]{1,0:T(8,128)(2,1)} %collective-permute-done.55), channel_id=1, source_target_pairs={{0,1},{1,2},{2,3},{4,5},{5,6},{6,7},{8,9},{9,10},{10,11},{12,13},{... | collective-permute-start | bytes 2359304 | tf_op jit(solution)/shard_map/ppermute | solution.py:124
  644.8 49.6 %collective-permute-start.35 = (bf16[256,1536]{1,0:T(8,128)(2,1)}, bf16[256,1536]{1,0:T(8,128)(2,1)S(1)}, u32[]{:S(2)}, u32[]{:S(2)}) collective-permute-start(bf16[256,1536]{1,0:T(8,128)(2,1)} %collective-permute-done.34), channel_id=1, source_target_pairs={{3,2},{2,1},{1,0},{7,6},{6,5},{5,4},{11,10},{10,9},{9,8},{15,14},{... | collective-permute-start | bytes 2359304 | tf_op jit(solution)/shard_map/ppermute | solution.py:129
  646.8 32.0 %collective-permute-start.65 = (f32[1,1536]{1,0:T(1,128)S(1)}, f32[1,1536]{1,0:T(1,128)S(1)}, u32[]{:S(2)}, u32[]{:S(2)}) collective-permute-start(f32[1,1536]{1,0:T(1,128)S(1)} %add.514), channel_id=1, source_target_pairs={{0,2},{1,3},{2,0},{3,1},{4,6},{5,7},{6,4},{7,5},{8,10},{9,11},{10,... | collective-permute-start | bytes 18440 | tf_op jit(solution)/shard_map/ppermute | solution.py:183
  679.4 55.0 %all-gather.10.cloned.1.call-start = ((), (), s32[]{:S(2)}) async-start(), calls=%async_computation.8 | async-start | bytes 1327104 | tf_op jit(solution)/shard_map/all_gather | solution.py:346
  683.6 29.6 %collective-permute-start.37 = (bf16[256,1536]{1,0:T(8,128)(2,1)S(1)}, bf16[256,1536]{1,0:T(8,128)(2,1)}, u32[]{:S(2)}, u32[]{:S(2)}) collective-permute-start(bf16[256,1536]{1,0:T(8,128)(2,1)S(1)} %collective-permute-done.36), channel_id=1, source_target_pairs={{0,1},{1,2},{2,3},{4,5},{5,6},{6,7},{8,9},{9,10},{10,11},{12,13},{... | collective-permute-start | bytes 2359304 | tf_op jit(solution)/shard_map/ppermute | solution.py:124
  687.6 27.9 %collective-permute-start.58 = (bf16[256,1536]{1,0:T(8,128)(2,1)S(1)}, bf16[256,1536]{1,0:T(8,128)(2,1)}, u32[]{:S(2)}, u32[]{:S(2)}) collective-permute-start(bf16[256,1536]{1,0:T(8,128)(2,1)S(1)} %collective-permute-done.57), channel_id=1, source_target_pairs={{3,2},{2,1},{1,0},{7,6},{6,5},{5,4},{11,10},{10,9},{9,8},{15,14},{... | collective-permute-start | bytes 2359304 | tf_op jit(solution)/shard_map/ppermute | solution.py:129
  688.9 39.9 %collective-permute-start.60 = (bf16[256,1536]{1,0:T(8,128)(2,1)S(1)}, bf16[256,1536]{1,0:T(8,128)(2,1)}, u32[]{:S(2)}, u32[]{:S(2)}) collective-permute-start(bf16[256,1536]{1,0:T(8,128)(2,1)S(1)} %collective-permute-done.59), channel_id=1, source_target_pairs={{0,1},{1,2},{2,3},{4,5},{5,6},{6,7},{8,9},{9,10},{10,11},{12,13},{... | collective-permute-start | bytes 2359304 | tf_op jit(solution)/shard_map/ppermute | solution.py:124
  (142 other events, 1684.7 us)
Sparse Core Ops, SparseCore 0:
  13.5 83.8 all-gather.5
  100.3 87.0 all-gather.7
  483.9 69.2 reduce-scatter.2
  618.0 61.1 all-reduce.3
  681.5 26.7 reduce-scatter.4
  710.2 24.2 all-gather.9

commit v2 on v1

v2 whole, which is shorter than its diff:
```python
import functools

import jax
import jax.numpy as jnp
from jax import lax
from jax.experimental import pallas as pl
from jax.experimental.pallas import tpu as pltpu
from jax.sharding import PartitionSpec as P

HD = 64
LEN = 1024
EPS = 1e-06
MASKED = -1e30
BF = jnp.bfloat16
F32 = jnp.float32
BLOCK = 256
LANES = 128
NT = (((1,), (1,)), ((), ()))
TN = (((0,), (0,)), ((), ()))


def mul(a, b, dims=(((1,), (0,)), ((), ()))):
    return lax.dot_general(a, b, dims, preferred_element_type=F32)


def rotate_lanes(y, cos, sin_a, sin_b):
    return y * cos + pltpu.roll(y, 128 - HD // 2, 1) * sin_a + pltpu.roll(y, HD // 2, 1) * sin_b


def rotary_lanes(tokens):
    positions = (jnp.arange(tokens) % LEN).astype(F32)
    lane = jnp.arange(128)
    freqs = 10000.0 ** (-(lane % (HD // 2)).astype(F32) * 2.0 / HD)
    angles = positions[:, None] * freqs[None, :]
    cos, sin = jnp.cos(angles), jnp.sin(angles)
    first = (lane % HD < HD // 2)[None, :]
    return cos, jnp.where(first, -sin, 0.0), jnp.where(first, 0.0, sin)


def causal(block):
    key_at = lax.broadcasted_iota(jnp.int32, (block, block), 0)
    query_at = lax.broadcasted_iota(jnp.int32, (block, block), 1)
    return key_at <= query_at


def attend_kernel(at_ref, x_ref, gain_ref, w_ref, cos_ref, sin_a_ref, sin_b_ref, *refs):
    pieces, (normed_ref, q_ref, k_ref, v_ref, log_ref, vt_ref, out_ref) = refs[:-7], refs[-7:]
    tokens = x_ref.shape[0]
    heads, groups = q_ref.shape[0], k_ref.shape[0]
    repeat = heads // groups
    per = 128 // HD
    scale = HD ** (-0.5)

    @pl.loop(0, tokens // BLOCK)
    def _(i):
        at = pl.multiple_of(i * BLOCK, BLOCK)
        rows = pl.ds(at, BLOCK)
        x = x_ref[rows, :].astype(F32)
        inverse = lax.rsqrt(jnp.mean(x * x, axis=-1, keepdims=True) + EPS)
        normed = (x * inverse * gain_ref[...]).astype(BF)
        normed_ref[rows, :] = normed
        raw = mul(normed, w_ref[...])
        tables = (cos_ref[rows, :], sin_a_ref[rows, :], sin_b_ref[rows, :])
        for h in range(0, heads, per):
            turned = rotate_lanes(raw[:, h * HD : h * HD + 128], *tables) * scale
            for u in range(per):
                q_ref[h + u, rows, :] = turned[:, u * HD : (u + 1) * HD].astype(BF)
        for g in range(0, groups, per):
            lane = (heads + g) * HD
            turned = rotate_lanes(raw[:, lane : lane + 128], *tables)
            lane = (heads + groups + g) * HD
            value = raw[:, lane : lane + 128]
            turned_value = value.T
            for u in range(per):
                k_ref[g + u, rows, :] = turned[:, u * HD : (u + 1) * HD].astype(BF)
                v_ref[g + u, rows, :] = value[:, u * HD : (u + 1) * HD].astype(BF)
                vt_ref[g + u, :, rows] = turned_value[u * HD : (u + 1) * HD].astype(BF)

    keep = causal(BLOCK)

    @pl.loop(0, heads)
    def _(h):
        g = h // repeat
        for i in range(tokens // BLOCK):
            start, stop = i * BLOCK, (i + 1) * BLOCK
            query = q_ref[h, start:stop, :]
            parts = [jnp.where(keep, mul(k_ref[g, start:stop, :], query, NT), MASKED)]
            if i:
                parts.append(mul(k_ref[g, :start, :], query, NT))
            peak = jnp.max(parts[0], axis=0, keepdims=True)
            for part in parts[1:]:
                peak = jnp.maximum(peak, jnp.max(part, axis=0, keepdims=True))
            weights = [jnp.exp(part - peak) for part in parts]
            total = sum(jnp.sum(w, axis=0, keepdims=True) for w in weights)
            shrink = 1.0 / total
            mixed = mul(vt_ref[g, :, start:stop], (weights[0] * shrink).astype(BF))
            if i:
                mixed += mul(vt_ref[g, :, :start], (weights[1] * shrink).astype(BF))
            out_ref[h, :, start:stop] = mixed
            log_ref[h, :, start:stop] = peak + jnp.log(total)

    for s, piece_ref in enumerate(pieces):
        span = pl.ds(pl.multiple_of(lax.rem(at_ref[0] + s, len(pieces)) * BLOCK, BLOCK), BLOCK)
        for h in range(0, heads, per):
            pair = jnp.concatenate([out_ref[h + u, :, span] for u in range(per)], axis=0)
            piece_ref[:, h * HD : h * HD + 128] = pair.T.astype(BF)


VMEM = pl.BlockSpec(memory_space=pltpu.VMEM)
SMEM = pl.BlockSpec(memory_space=pltpu.SMEM)


def attend(x, gain, weight, tables, heads, groups, at):
    tokens, width = x.shape
    count = tokens // BLOCK
    return pl.pallas_call(
        attend_kernel,
        in_specs=[SMEM] + [VMEM] * 6,
        out_shape=[jax.ShapeDtypeStruct((BLOCK, heads * HD), BF)] * count
        + [
            jax.ShapeDtypeStruct((tokens, width), BF),
            jax.ShapeDtypeStruct((heads, tokens, HD), BF),
            jax.ShapeDtypeStruct((groups, tokens, HD), BF),
            jax.ShapeDtypeStruct((groups, tokens, HD), BF),
            jax.ShapeDtypeStruct((heads, 1, tokens), F32),
        ],
        scratch_shapes=[pltpu.VMEM((groups, HD, tokens), BF), pltpu.VMEM((heads, HD, tokens), F32)],
        compiler_params=pltpu.CompilerParams(vmem_limit_bytes=48 << 20),
        cost_estimate=pl.CostEstimate(
            flops=2 * tokens * width * weight.shape[1] + 3 * heads * tokens * tokens * HD,
            bytes_accessed=6 * tokens * width,
            transcendentals=heads * tokens * tokens // 2,
        ),
    )(at[None], x, gain[None], weight, *tables)


def attend_back_kernel(at_ref, q_ref, k_ref, v_ref, log_ref, cos_ref, sin_a_ref, sin_b_ref, *refs):
    do_ref, kt_ref, dq_ref, dk_ref, dv_ref = refs[-5:]
    out_ref = refs[-6]
    count = (len(refs) - 6) // 2
    grad_refs, pieces = refs[:count], refs[count : 2 * count]
    tokens = q_ref.shape[1]
    heads, groups = q_ref.shape[0], k_ref.shape[0]
    repeat = heads // groups
    per = 128 // HD
    scale = HD ** (-0.5)
    dk_ref[...] = jnp.zeros_like(dk_ref)
    dv_ref[...] = jnp.zeros_like(dv_ref)

    def span_of(s):
        return pl.ds(pl.multiple_of(lax.rem(at_ref[0] + s, count) * BLOCK, BLOCK), BLOCK)

    for s, grad_ref in enumerate(grad_refs):
        for h in range(heads):
            do_ref[h, span_of(s), :] = grad_ref[:, h * HD : (h + 1) * HD]

    @pl.loop(0, tokens // BLOCK)
    def _(i):
        rows = pl.ds(pl.multiple_of(i * BLOCK, BLOCK), BLOCK)
        for g in range(groups):
            kt_ref[g, :, rows] = k_ref[g, rows, :].astype(F32).T.astype(BF)

    keep = causal(BLOCK)

    @pl.loop(0, heads)
    def _(h):
        g = h // repeat
        for i in range(tokens // BLOCK):
            start, stop = i * BLOCK, (i + 1) * BLOCK
            query = q_ref[h, start:stop, :]
            grads = do_ref[h, start:stop, :]
            log_total = log_ref[h, :, start:stop]
            spans = [(start, stop)] + ([(0, start)] if i else [])
            probs, grad_probs = [], []
            for lo, hi in spans:
                scores = mul(k_ref[g, lo:hi, :], query, NT)
                if hi == stop:
                    scores = jnp.where(keep, scores, MASKED)
                probs.append(jnp.exp(scores - log_total))
                grad_probs.append(mul(v_ref[g, lo:hi, :], grads, NT))
            inner = sum(jnp.sum(p * d, axis=0, keepdims=True) for p, d in zip(probs, grad_probs))
            dq = None
            for (lo, hi), p, d in zip(spans, probs, grad_probs):
                ds = (p * (d - inner)).astype(BF)
                dk_ref[g, lo:hi, :] += mul(ds, query)
                dv_ref[g, lo:hi, :] += mul(p.astype(BF), grads)
                term = mul(kt_ref[g, :, lo:hi], ds)
                dq = term if dq is None else dq + term
            dq_ref[h, :, start:stop] = dq * scale

    @pl.loop(0, tokens // BLOCK)
    def _(i):
        rows = pl.ds(pl.multiple_of(i * BLOCK, BLOCK), BLOCK)
        tables = (cos_ref[rows, :], -sin_a_ref[rows, :], -sin_b_ref[rows, :])
        for h in range(0, heads, per):
            pair = jnp.concatenate([dq_ref[h + u, :, rows] for u in range(per)], axis=0).T
            out_ref[rows, h * HD : h * HD + 128] = rotate_lanes(pair, *tables).astype(BF)
        for g in range(0, groups, per):
            pair = jnp.concatenate([dk_ref[g + u, rows, :] for u in range(per)], axis=1)
            lane = (heads + g) * HD
            out_ref[rows, lane : lane + 128] = rotate_lanes(pair, *tables).astype(BF)
            pair = jnp.concatenate([dv_ref[g + u, rows, :] for u in range(per)], axis=1)
            lane = (heads + groups + g) * HD
            out_ref[rows, lane : lane + 128] = pair.astype(BF)

    for s, piece_ref in enumerate(pieces):
        piece_ref[...] = out_ref[span_of(s), :]


def attend_back(grad_pieces, q, k, v, logs, tables, at):
    heads, tokens, _ = q.shape
    groups = k.shape[0]
    count = len(grad_pieces)
    lanes = (heads + 2 * groups) * HD
    return pl.pallas_call(
        attend_back_kernel,
        in_specs=[SMEM] + [VMEM] * (7 + count),
        out_shape=[jax.ShapeDtypeStruct((BLOCK, lanes), BF)] * count + [jax.ShapeDtypeStruct((tokens, lanes), BF)],
        scratch_shapes=[
            pltpu.VMEM((heads, tokens, HD), BF),
            pltpu.VMEM((groups, HD, tokens), BF),
            pltpu.VMEM((heads, HD, tokens), F32),
            pltpu.VMEM((groups, tokens, HD), F32),
            pltpu.VMEM((groups, tokens, HD), F32),
        ],
        compiler_params=pltpu.CompilerParams(vmem_limit_bytes=48 << 20),
        cost_estimate=pl.CostEstimate(
            flops=6 * heads * tokens * tokens * HD,
            bytes_accessed=6 * tokens * heads * HD,
            transcendentals=heads * tokens * tokens // 2,
        ),
    )(at[None], q, k, v, logs, *tables, *grad_pieces)


def expert_kernel(order_ref, rows_ref, extra_ref, router_ref, gu_ref, down_ref, out_ref, gin_ref, wgu_ref, wdown_ref, agu, adown, *, top):
    step = pl.program_id(0)
    steps = pl.num_programs(0)
    hidden_width, width = down_ref.shape
    own = order_ref[steps]
    experts = order_ref[steps + 1]

    @pl.when(step == 0)
    def _():
        agu[...] = jnp.zeros_like(agu)
        adown[...] = jnp.zeros_like(adown)

    rows = rows_ref[...]
    grads32 = extra_ref[:, :width].astype(F32)
    named = extra_ref[:, width:].astype(F32)

    lane = lax.broadcasted_iota(jnp.int32, (rows.shape[0], LANES), 1)
    lane32 = lane.astype(F32)
    chosen = lane32 == named[:, 0:1]
    for k in range(1, top):
        chosen = chosen | (lane32 == named[:, k : k + 1])
    logits = jnp.where(chosen, mul(rows, router_ref[...]), MASKED)
    weights = jnp.where(chosen, jnp.exp(logits - jnp.max(logits, axis=-1, keepdims=True)), 0.0)
    mine = jnp.sum(jnp.where(lane == own, weights, 0.0), axis=-1, keepdims=True)
    gate = mine / jnp.sum(weights, axis=-1, keepdims=True)

    both = mul(rows, gu_ref[...], NT)
    gate_vals = both[:, :hidden_width]
    up_vals = both[:, hidden_width:]
    sigma = jax.nn.sigmoid(gate_vals)
    active = gate_vals * sigma
    hidden = (active * up_vals).astype(BF)
    grad_out = (gate * grads32).astype(BF)
    grad_hidden = mul(grad_out, down_ref[...], NT)
    expert_out = mul(hidden, down_ref[...])
    out_ref[...] = (gate * expert_out).astype(BF)
    score = jnp.sum(grads32 * expert_out, axis=-1, keepdims=True)
    high = score.astype(BF).astype(F32)
    scores = jnp.where(lane == own, high, jnp.where(lane == own + experts, score - high, 0.0))
    gin_ref[:, width:] = scores.astype(BF)
    grad_gate_vals = (grad_hidden * up_vals * sigma * (1.0 + gate_vals * (1.0 - sigma))).astype(BF)
    grad_up_vals = (grad_hidden * active).astype(BF)
    grad_both = jnp.concatenate([grad_gate_vals, grad_up_vals], axis=1)
    gin_ref[:, :width] = mul(grad_both, gu_ref[...]).astype(BF)
    agu[...] += mul(grad_both, rows, TN)
    adown[...] += mul(hidden, grad_out, TN)

    @pl.when(step == steps - 1)
    def _():
        wgu_ref[...] = agu[...].astype(BF)
        wdown_ref[...] = adown[...].astype(BF)


def run_experts(order, rows, extra, router, gate_up, down, top):
    count, width = rows.shape
    wide = extra.shape[1]
    hidden = down.shape[0]
    whole_gu = pl.BlockSpec((2 * hidden, width), lambda i, o: (0, 0))
    whole_down = pl.BlockSpec((hidden, width), lambda i, o: (0, 0))
    by_slot = pl.BlockSpec((BLOCK, width), lambda i, o: (i, 0))
    return pl.pallas_call(
        functools.partial(expert_kernel, top=top),
        grid_spec=pltpu.PrefetchScalarGridSpec(
            num_scalar_prefetch=1,
            grid=(count // BLOCK,),
            in_specs=[
                by_slot,
                pl.BlockSpec((BLOCK, wide), lambda i, o: (o[i], 0)),
                pl.BlockSpec((width, LANES), lambda i, o: (0, 0)),
                whole_gu,
                whole_down,
            ],
            out_specs=[by_slot, pl.BlockSpec((BLOCK, wide), lambda i, o: (i, 0)), whole_gu, whole_down],
            scratch_shapes=[pltpu.VMEM((2 * hidden, width), F32), pltpu.VMEM((hidden, width), F32)],
        ),
        out_shape=[
            jax.ShapeDtypeStruct((count, width), BF),
            jax.ShapeDtypeStruct((count, wide), BF),
            jax.ShapeDtypeStruct((2 * hidden, width), BF),
            jax.ShapeDtypeStruct((hidden, width), BF),
        ],
        compiler_params=pltpu.CompilerParams(vmem_limit_bytes=58 << 20),
        cost_estimate=pl.CostEstimate(
            flops=18 * count * width * hidden,
            bytes_accessed=8 * count * width + 18 * hidden * width,
            transcendentals=count * hidden,
        ),
    )(order, rows, extra, router, gate_up, down)


def after(x, *others):
    return lax.optimization_barrier((x, others))[0]


def swap(x, bit):
    return lax.ppermute(x, "ep", [(i, i ^ bit) for i in range(lax.axis_size("ep"))])


def turn(x, by):
    n = lax.axis_size("tp")
    return lax.ppermute(x, "tp", [(i, (i + by) % n) for i in range(n)])


def gather_ep(x):
    n = lax.axis_size("ep")
    if n != 8:
        whole = lax.all_gather(x, "ep")
        return [whole[k] for k in range(n)]
    first = [x] + [swap(x, k) for k in (2, 4, 6)]
    second = [swap(v, 1) for v in first]
    return [v for pair in zip(first, second) for v in pair]


def scatter_slots(x):
    if lax.axis_size("ep") != 8:
        return lax.psum_scatter(x, "ep", scatter_dimension=0, tiled=False).astype(F32)
    other = swap(x[1::2], 1)
    mine = (x[0::2].astype(F32) + other.astype(F32)).astype(BF)
    got = [mine[0]] + [swap(mine[j], 2 * j) for j in (1, 2, 3)]
    return sum(v.astype(F32) for v in got)


def scatter_devices(x):
    n = lax.axis_size("ep")
    if n != 8:
        return lax.psum_scatter(x, "ep", scatter_dimension=0, tiled=False).astype(F32)
    at = lax.axis_index("ep")
    core, chip = lax.rem(at, 2), lax.div(at, 2)
    x = x.reshape((n // 2, 2) + x.shape[1:])
    other = swap(lax.dynamic_index_in_dim(x, 1 - core, 1, False), 1)
    mine = lax.dynamic_index_in_dim(x, core, 1, False)
    mine = (mine.astype(F32) + other.astype(F32)).astype(BF)

    def of(j):
        return lax.dynamic_index_in_dim(mine, jnp.bitwise_xor(chip, j), 0, False)

    got = [of(0)] + [swap(of(j), 2 * j) for j in (1, 2, 3)]
    return sum(v.astype(F32) for v in got)


def slot_devices():
    n = lax.axis_size("ep")
    order = jnp.arange(n, dtype=jnp.int32)
    return jnp.bitwise_xor(order, lax.axis_index("ep")) if n == 8 else order


def in_device_order(blocks, shape, put):
    order = slot_devices()
    out = jnp.zeros(shape, blocks[0].dtype)
    for k, block in enumerate(blocks):
        out = put(out, block, order[k])
    return out


def step_right(x, upto=None):
    n = lax.axis_size("tp")
    return lax.ppermute(x, "tp", [(i, i + 1) for i in range(n - 1 if upto is None else upto)])


def step_left(x, upto=None):
    n = lax.axis_size("tp")
    return lax.ppermute(x, "tp", [(n - 1 - i, n - 2 - i) for i in range(n - 1 if upto is None else upto)])


def meet(at, right, left):
    n = lax.axis_size("tp")
    return [right[0]] + [jnp.where(at >= s, right[s], left[n - s]) for s in range(1, n)]


def body(
    inputs,
    routes,
    norm_gain,
    query_weight,
    key_weight,
    value_weight,
    output_weight,
    mixer_gain,
    router_weight,
    gate_weight,
    up_weight,
    down_weight,
    cotangent,
):
    tokens, width = inputs.shape
    experts = router_weight.shape[1]
    top = routes.shape[1]
    n_ep = lax.axis_size("ep")
    n_tp = lax.axis_size("tp")
    ep_at = lax.axis_index("ep").astype(jnp.int32)
    tp_at = lax.axis_index("tp").astype(jnp.int32)
    quarter = tokens // n_tp
    heads_width = query_weight.shape[1]
    groups_width = key_weight.shape[1]

    def mine(x):
        return lax.dynamic_slice_in_dim(x, tp_at * quarter, quarter, 0)

    hidden_part = gate_weight.shape[2]
    expert_part = jnp.concatenate([gate_weight[0].T, up_weight[0].T, down_weight[0]], axis=0)
    right, left = [expert_part], [expert_part]
    right.append(step_right(expert_part))
    left.append(step_left(expert_part))

    part = output_weight.shape[0] // n_ep
    output_part = lax.dynamic_slice_in_dim(output_weight, ep_at * part, part, 0)
    output_part = jnp.stack([output_part] + [turn(output_part, s) for s in range(1, n_tp)])

    routes_mine = mine(routes)
    grad_top_mine = mine(cotangent)
    named = jnp.pad(routes_mine.astype(BF), ((0, 0), (0, LANES - top)), constant_values=-1.0)
    extra = jnp.concatenate([grad_top_mine, named], axis=1)
    extra_all = lax.all_gather(extra, "ep", tiled=True)

    qkv_weight = jnp.concatenate([query_weight, key_weight, value_weight], axis=1)
    tables = rotary_lanes(tokens)
    *mixed, normed, query, key, value, logs = attend(
        inputs, norm_gain, qkv_weight, tables, heads_width // HD, groups_width // HD, tp_at
    )
    mixed = [mixed[0]] + [turn(mixed[s], s) for s in range(1, n_tp)]

    output_blocks = gather_ep(output_part)
    output_whole = in_device_order(
        output_blocks,
        (n_tp, n_ep, part, width),
        lambda out, block, at: lax.dynamic_update_slice(out, block[:, None], (0, at, 0, 0)),
    ).reshape(n_tp * heads_width, width)

    mixed_mine = jnp.concatenate(mixed, axis=1)
    branch = mul(mixed_mine, output_whole)
    inputs_mine = mine(inputs).astype(F32)
    attended = inputs_mine + branch
    inverse_two = lax.rsqrt(jnp.mean(attended * attended, axis=-1, keepdims=True) + EPS)
    unit_two = attended * inverse_two
    routed_in = (unit_two * mixer_gain).astype(BF)

    right[1], left[1] = after((right[1], left[1]), mixed)
    for _ in range(2, n_tp):
        right.append(step_right(right[-1]))
        left.append(step_left(left[-1]))
    expert_parts = meet(tp_at, right, left)
    gate_up = jnp.concatenate(
        [w[:hidden_part] for w in expert_parts] + [w[hidden_part : 2 * hidden_part] for w in expert_parts], axis=0
    )
    down = jnp.concatenate([w[2 * hidden_part :] for w in expert_parts], axis=0)

    routed_all = jnp.concatenate(gather_ep(routed_in), axis=0)
    router = jnp.pad(router_weight, ((0, 0), (0, LANES - experts)))
    order = jnp.concatenate([slot_devices(), ep_at[None], jnp.full((1,), experts, jnp.int32)])
    combined, grad_in, grad_gate_up, grad_down = run_experts(
        order, routed_all, extra_all, router, gate_up, down, top
    )
    logits = mul(routed_in, router_weight)
    ids = jnp.arange(experts, dtype=jnp.int32)
    chosen = jnp.any(routes_mine[:, :, None] == ids[None, None, :], axis=1)
    logits = jnp.where(chosen, logits, MASKED)
    weights = jnp.where(chosen, jnp.exp(logits - jnp.max(logits, axis=-1, keepdims=True)), 0.0)
    gates = weights / jnp.sum(weights, axis=-1, keepdims=True)

    grad_in = scatter_slots(grad_in.reshape(n_ep, quarter, -1))
    grad_gates = grad_in[:, width : width + experts] + grad_in[:, width + experts : width + 2 * experts]
    inner_gate = jnp.sum(gates * grad_gates, axis=-1, keepdims=True)
    grad_logits = (gates * (grad_gates - inner_gate)).astype(BF)
    grad_routed = grad_in[:, :width] + mul(grad_logits, router_weight, NT)
    grad_top = grad_top_mine.astype(F32)
    scaled_two = grad_routed * mixer_gain
    grad_attended = grad_top + inverse_two * (
        scaled_two - unit_two * jnp.mean(scaled_two * unit_two, axis=-1, keepdims=True)
    )
    grad_branch = grad_attended.astype(BF)
    grad_mixed = mul(grad_branch, output_whole, NT).astype(BF)
    grad_mixed = [grad_mixed[:, s * heads_width : (s + 1) * heads_width] for s in range(n_tp)]
    grad_mixed = [grad_mixed[0]] + [turn(grad_mixed[s], -s) for s in range(1, n_tp)]

    hidden_all = n_tp * hidden_part

    def term(s):
        at = s * hidden_part
        return jnp.concatenate(
            [
                grad_gate_up[at : at + hidden_part],
                grad_gate_up[hidden_all + at : hidden_all + at + hidden_part],
                grad_down[at : at + hidden_part],
            ],
            axis=0,
        )

    terms = [term(s) for s in range(n_tp)]
    go_right = go_left = None
    for t in range(1, n_tp):
        give_right, give_left = terms[t], terms[n_tp - t]
        if go_right is not None:
            give_right = (give_right.astype(F32) + go_right.astype(F32)).astype(BF)
            give_left = (give_left.astype(F32) + go_left.astype(F32)).astype(BF)
        if t == n_tp - 1:
            give_right, give_left = after((give_right, give_left), grad_mixed)
        go_right = step_right(give_right, t)
        go_left = step_left(give_left, t)
    grad_expert = terms[0].astype(F32) + go_right.astype(F32) + go_left.astype(F32)
    grad_gate_w = grad_expert[:hidden_part].T
    grad_up_w = grad_expert[hidden_part : 2 * hidden_part].T
    grad_down_w = grad_expert[2 * hidden_part :]

    combined = after(combined, grad_branch)
    combined_mine = scatter_slots(combined.reshape(n_ep, quarter, width))
    result_mine = (attended + combined_mine).astype(BF)
    result = lax.all_gather(result_mine, "tp", tiled=True)

    *grad_qkv, grad_qkv_all = attend_back(grad_mixed, query, key, value, logs, tables, tp_at)
    grad_qkv = [grad_qkv[0]] + [turn(grad_qkv[s], s) for s in range(1, n_tp)]
    grad_qkv_w = mul(normed, grad_qkv_all, TN).astype(BF)
    grad_qkv_w = lax.psum(grad_qkv_w, "ep").astype(F32)

    grad_router = mul(routed_in, grad_logits, TN)
    grad_mixer = jnp.sum(grad_routed * unit_two, axis=0)
    few = -(-(1 + experts) // n_ep)
    few_pad = -(-few // 16) * 16
    small = jnp.concatenate([grad_mixer[None], grad_router.T], axis=0).astype(BF)
    small = jnp.pad(small, ((0, few * n_ep - 1 - experts), (0, 0))).reshape(n_ep, few, width)
    small = jnp.pad(small, ((0, 0), (0, few_pad - few), (0, 0)))
    grad_output = mul(mixed_mine, grad_branch, TN).astype(BF)
    grad_output = grad_output.reshape(n_tp, n_ep, part, width).transpose(1, 0, 2, 3)
    grad_output = jnp.concatenate([grad_output.reshape(n_ep, n_tp * part, width), small], axis=1)
    grad_output = scatter_devices(grad_output).astype(BF)
    pieces = [
        jnp.concatenate([grad_output[s * part : (s + 1) * part], grad_output[n_tp * part :]], axis=0)
        for s in range(n_tp)
    ]
    pieces = [pieces[0]] + [turn(pieces[s], -s) for s in range(1, n_tp)]
    grad_output = sum(v.astype(F32) for v in pieces).astype(BF)
    grad_output = in_device_order(
        gather_ep(grad_output),
        (n_ep, part + few_pad, width),
        lambda out, block, at: lax.dynamic_update_index_in_dim(out, block, at, 0),
    )
    small = grad_output[:, part : part + few].reshape(n_ep * few, width)[: 1 + experts].astype(F32)
    grad_output = grad_output[:, :part].reshape(heads_width, width).astype(F32)

    part_in = width // n_ep
    qkv_part = lax.dynamic_slice_in_dim(qkv_weight, ep_at * part_in, part_in, 0)
    qkv_part = after(qkv_part, routed_in)
    qkv_whole = lax.all_gather(qkv_part, ("tp", "ep"), tiled=True).reshape(n_tp, width, -1)
    grad_normed = sum(
        mul(grad_qkv[s], lax.dynamic_index_in_dim(qkv_whole, lax.rem(tp_at - s + n_tp, n_tp), 0, False), NT)
        for s in range(n_tp)
    )
    inverse_one = lax.rsqrt(jnp.mean(inputs_mine * inputs_mine, axis=-1, keepdims=True) + EPS)
    unit_one = inputs_mine * inverse_one
    grad_norm = jnp.sum(grad_normed * unit_one, axis=0)
    scaled_one = grad_normed * norm_gain
    grad_inputs = grad_attended + inverse_one * (
        scaled_one - unit_one * jnp.mean(scaled_one * unit_one, axis=-1, keepdims=True)
    )
    grad_inputs = grad_inputs.astype(BF)
    right, left = [grad_inputs], [grad_inputs]
    for _ in range(1, n_tp):
        right.append(step_right(right[-1]))
        left.append(step_left(left[-1]))
    grad_inputs = jnp.zeros((tokens, width), BF)
    for s, block in enumerate(meet(tp_at, right, left)):
        grad_inputs = lax.dynamic_update_slice(
            grad_inputs, block, (lax.rem(tp_at - s + n_tp, n_tp) * quarter, 0)
        )
    grad_norm = grad_norm[None]
    for axis in ("ep", "tp"):
        n = lax.axis_size(axis)
        bit = 1
        while bit < n:
            grad_norm = grad_norm + lax.ppermute(grad_norm, axis, [(i, i ^ bit) for i in range(n)])
            bit *= 2
    return (
        result,
        grad_inputs,
        grad_norm[0],
        grad_qkv_w[:, :heads_width],
        grad_qkv_w[:, heads_width : heads_width + groups_width],
        grad_qkv_w[:, heads_width + groups_width :],
        grad_output,
        small[0],
        small[1:].T,
        grad_gate_w[None],
        grad_up_w[None],
        grad_down_w[None],
    )


def solution(mesh):
    placed = (
        P("ep", None),
        P("ep", None),
        P(),
        P(None, "tp"),
        P(None, "tp"),
        P(None, "tp"),
        P("tp", None),
        P(),
        P(),
        P("ep", None, "tp"),
        P("ep", None, "tp"),
        P("ep", "tp", None),
        P("ep", None),
    )
    return jax.shard_map(
        body,
        mesh=mesh,
        in_specs=placed,
        out_specs=(
            P("ep", None),
            P("ep", None),
            P(),
            P(None, "tp"),
            P(None, "tp"),
            P(None, "tp"),
            P("tp", None),
            P(),
            P(),
            P("ep", None, "tp"),
            P("ep", None, "tp"),
            P("ep", "tp", None),
        ),
        check_vma=False,
    )
```

time: 757 us -> 694 us (0.917)
  matrix products: 113 us -> 22.8 us
  Pallas kernels: 0 us -> 83.5 us
  waiting for transfers between devices: 218 us -> 298 us
  starting transfers between devices: 200 us -> 132 us
  local copies, waits for them, and re-layouts: 117 us -> 63.4 us
  other arithmetic: 69.8 us -> 54 us
  between operations: 17.1 us -> 30.7 us
  blocking collectives: 9.06 us -> 0 us
    dot_general x45 -> x11, matrix products: 113 us -> 22.8 us  [mul(): return lax.dot_general(a, b, dims, preferred_element_type=F32)]
    pallas_call x0 -> x3, Pallas kernels: none -> 83.5 us  [the longest x1 41.6 us: run_experts(): pl.pallas_call(functools.partial(expert_kernel, top=top), grid_spec=pltpu...]
    ppermute x24 -> x9, starting transfers between devices: 118 us -> 56.6 us  [step_right(): lax.ppermute(x, 'tp', [(i, i + 1) for i in range(n - 1 if upto is None el...]
    all_gather x3, waiting for transfers between devices: 3.42 us -> 55.3 us  [the longest x1 55.3 us: body(): result = lax.all_gather(result_mine, 'tp', tiled=True)]
    ppermute x22 -> x33, waiting for transfers between devices: 62.6 us -> 95.8 us  [swap(): lax.ppermute(x, 'ep', [(i, i ^ bit) for i in range(lax.axis_size('ep'))])]
    ppermute x19 -> x20, waiting for transfers between devices: 43.7 us -> 70.2 us  [the longest x5 35.2 us: body(): lax.ppermute(grad_norm, axis, [(i, i ^ bit) for i in range(n)])]
    ppermute x24 -> x9, starting transfers between devices: 29.3 us -> 11.5 us  [step_left(): lax.ppermute(x, 'tp', [(n - 1 - i, n - 2 - i) for i in range(n - 1 if upt...]
    dynamic_update_slice x12 -> x14, local copies, waits for them, and re-layouts: 18.1 us -> 0.45 us  [the longest x7 0.31 us: body(): lax.dynamic_update_slice(out, block[:, None], (0, at, 0, 0))]
  transfers between devices with their start and end apart: 96 -> 75, of which waited for: 35 -> 32; matrix products, arithmetic and copies ran while one was open for 38% -> 18% of each run, Pallas kernels for 0% -> 12%
where the time goes in v2:
time: 694 us; the launch traced here: 684 us
  waiting for transfers between devices  298 us (43%)
  starting transfers between devices  132 us (19%)
  Pallas kernels  83.5 us (12%)
  local copies, waits for them, and re-layouts  63.4 us (9%)
  other arithmetic  54 us (8%)
  between operations  30.7 us (4%)
  matrix products  22.8 us (3%)
    ppermute x33, waiting for transfers between devices, swap(): lax.ppermute(x, 'ep', [(i, i ^ bit) for i in range(lax.axis_size('ep'))])  95.8 us
    ppermute x9, starting transfers between devices, step_right(): lax.ppermute(x, 'tp', [(i, i + 1) for i in range(n - 1 if upto is None el...  56.6 us
    all_gather x1, waiting for transfers between devices, body(): result = lax.all_gather(result_mine, 'tp', tiled=True)  55.3 us
    ppermute x9, waiting for transfers between devices, step_left(): lax.ppermute(x, 'tp', [(n - 1 - i, n - 2 - i) for i in range(n - 1 if upt...  47.4 us
    pallas_call x1, Pallas kernels, run_experts(): pl.pallas_call(functools.partial(expert_kernel, top=top), grid_spec=pltpu...  41.6 us
    ppermute x5, waiting for transfers between devices, body(): lax.ppermute(grad_norm, axis, [(i, i ^ bit) for i in range(n)])  35.2 us
    ppermute x15, waiting for transfers between devices, turn(): return lax.ppermute(x, 'tp', [(i, (i + by) % n) for i in range(n)])  34.9 us
    ppermute x15, starting transfers between devices, turn(): return lax.ppermute(x, 'tp', [(i, (i + by) % n) for i in range(n)])  33.7 us
  transfers between devices with their start and end apart: 75, of which 32 were waited for; matrix products, arithmetic and copies ran while one was open for 18% of the time, Pallas kernels for 12%

profile of v2, /device:TPU:0, one launch (start us, length us, event | category | flops | bytes accessed | tf_op | source)
XLA Modules:
  0.0 684.3 jit_solution(15218260353282458775)
XLA Ops:
  11.7 3.0 collective-permute-start.3
  14.7 2.6 collective-permute-start.4
  21.0 21.0 %shard_map.220 = (bf16[256,384]{1,0:T(8,128)(2,1)S(1)}, bf16[256,384]{1,0:T(8,128)(2,1)S(1)}, bf16[256,384]{1,0:T(8,128)(2,1)S(1)}, bf16[256,384]{1,0:T(8,128)(2...) custom-call(s32[1]{0:T(128)} %bitcast.at_ref, ...), custom_call_target="tpu_custom_call" | custom-call | flops 3221225472 | bytes 9437184 | tf_op jit(solution)/shard_map/pallas_call | solution.py:116
  50.7 2.4 pad_maximum_fusion.1
  75.2 3.1 collective-permute-start.2
  80.3 3.3 collective-permute-done.2
  83.6 4.7 collective-permute-start.20
  89.7 9.9 %collective-permute-done.9 = bf16[4,48,1536]{2,1,0:T(8,128)(2,1)S(1)} collective-permute-done((bf16[4,48,1536]{2,1,0:T(8,128)(2,1)S(1)}, bf16[4,48,1536]{2,1,0:T(8,128)(2,1)S(1)}, u32[]{:S(2)}, u32[]{:S(2)}) %collective-permute-start.9) | collective-permute-done | bytes 589856 | tf_op jit(solution)/shard_map/ppermute | solution.py:330
  102.5 3.2 multiply_reduce_fusion.2
  111.6 2.5 collective-permute-start.18
  118.1 5.6 collective-permute-start.24
  128.7 7.5 %collective-permute-done.16 = bf16[256,1536]{1,0:T(8,128)(2,1)} collective-permute-done((bf16[256,1536]{1,0:T(8,128)(2,1)S(1)}, bf16[256,1536]{1,0:T(8,128)(2,1)}, u32[]{:S(2)}, u32[]{:S(2)}) %collective-permute-start.16) | collective-permute-done | bytes 786464 | tf_op jit(solution)/shard_map/ppermute | solution.py:330
  136.2 11.5 %collective-permute-done.18 = bf16[256,1536]{1,0:T(8,128)(2,1)} collective-permute-done((bf16[256,1536]{1,0:T(8,128)(2,1)S(1)}, bf16[256,1536]{1,0:T(8,128)(2,1)}, u32[]{:S(2)}, u32[]{:S(2)}) %collective-permute-start.18) | collective-permute-done | bytes 786464 | tf_op jit(solution)/shard_map/ppermute | solution.py:330
  153.1 6.5 collective-permute-start.25
  168.1 31.2 %collective-permute-done.23 = bf16[384,1536]{1,0:T(8,128)(2,1)S(1)} collective-permute-done((bf16[384,1536]{1,0:T(8,128)(2,1)}, bf16[384,1536]{1,0:T(8,128)(2,1)S(1)}, u32[]{:S(2)}, u32[]{:S(2)}) %collective-permute-start.23) | collective-permute-done | bytes 1179680 | tf_op jit(solution)/shard_map/ppermute | solution.py:396
  199.5 2.8 collective-permute-done.25
  206.9 41.6 %shard_map.221 = (bf16[2048,1536]{1,0:T(8,128)(2,1)}, bf16[2048,1664]{1,0:T(8,128)(2,1)}, bf16[1024,1536]{1,0:T(8,128)(2,1)}, bf16[512,1536]{1,0:T(8,128)(2,1)}) custom-call(s32[10]{0:T(128)} %pad_add_fusion.order_ref, bf16[2048,1536]{1,0:T(8,128)(2,1)} %constant_dynamic-update-slice_fusion.7.rows_ref, ...), custom_call_target="tpu_custom_call" | custom-call | flops 28991029248 | bytes 39321600 | tf_op jit(solution)/shard_map/pallas_call | solution.py:295
  248.5 4.2 slice.220
  255.3 10.8 %collective-permute-start.65 = (bf16[384,1536]{1,0:T(8,128)(2,1)}, bf16[384,1536]{1,0:T(8,128)(2,1)}, u32[]{:S(2)}, u32[]{:S(2)}) collective-permute-start(bf16[384,1536]{1,0:T(8,128)(2,1)} %pad_maximum_fusion.4), channel_id=1, source_target_pairs={{0,1},{4,5},{8,9},{12,13},{16,17},{20,21},{24,25},{28,29}} | collective-permute-start | bytes 3538952 | tf_op jit(solution)/shard_map/ppermute | solution.py:391
  273.6 17.7 %collective-permute-done.65 = bf16[384,1536]{1,0:T(8,128)(2,1)} collective-permute-done((bf16[384,1536]{1,0:T(8,128)(2,1)}, bf16[384,1536]{1,0:T(8,128)(2,1)}, u32[]{:S(2)}, u32[]{:S(2)}) %collective-permute-start.65) | collective-permute-done | bytes 1179680 | tf_op jit(solution)/shard_map/ppermute | solution.py:391
  291.3 3.5 fusion.8
  295.5 3.8 add_convert_fusion
  299.7 2.3 collective-permute-start.28
  303.7 6.2 collective-permute-start.66
  311.3 10.2 %collective-permute-done.27 = bf16[256,1664]{1,0:T(8,128)(2,1)S(1)} collective-permute-done((bf16[256,1664]{1,0:T(8,128)(2,1)S(1)}, bf16[256,1664]{1,0:T(8,128)(2,1)S(1)}, u32[]{:S(2)}, u32[]{:S(2)}) %collective-permute-start.27) | collective-permute-done | bytes 852000 | tf_op jit(solution)/shard_map/ppermute | solution.py:330
  321.5 17.3 %collective-permute-done.28 = bf16[256,1664]{1,0:T(8,128)(2,1)S(1)} collective-permute-done((bf16[256,1664]{1,0:T(8,128)(2,1)S(1)}, bf16[256,1664]{1,0:T(8,128)(2,1)S(1)}, u32[]{:S(2)}, u32[]{:S(2)}) %collective-permute-start.28) | collective-permute-done | bytes 852000 | tf_op jit(solution)/shard_map/ppermute | solution.py:330
  340.4 3.1 fusion.64
  345.6 10.9 %collective-permute-start.34 = (bf16[256,384]{1,0:T(8,128)(2,1)}, bf16[256,384]{1,0:T(8,128)(2,1)S(1)}, u32[]{:S(2)}, u32[]{:S(2)}) collective-permute-start(bf16[256,384]{1,0:T(8,128)(2,1)} %get-tuple-element.144), channel_id=1, source_target_pairs={{0,3},{1,0},{2,1},{3,2},{4,7},{5,4},{6,5},{7,6},{8,11},{9,8},{10,9... | collective-permute-start | bytes 589832 | tf_op jit(solution)/shard_map/ppermute | solution.py:335
  357.7 2.9 convolution_convert_fusion
  362.7 9.3 %collective-permute-done.35.refs_2_ = bf16[256,384]{1,0:T(8,128)(2,1)S(1)} collective-permute-done((bf16[256,384]{1,0:T(8,128)(2,1)S(1)}, bf16[256,384]{1,0:T(8,128)(2,1)S(1)}, u32[]{:S(2)}, u32[]{:S(2)}) %collective-permute-start.35) | collective-permute-done | bytes 196640 | tf_op jit(solution)/shard_map/ppermute | solution.py:335
  373.7 20.9 %shard_map.222 = (bf16[256,640]{1,0:T(8,128)(2,1)S(1)}, bf16[256,640]{1,0:T(8,128)(2,1)S(1)}, bf16[256,640]{1,0:T(8,128)(2,1)S(1)}, bf16[256,640]{1,0:T(8,128)(2,1)S(1)}, bf16[1024,640]{1,0:T(8,128)(2,1)S(1)}) custom-call(s32[1]{0:T(128)} %bitcast.at_ref, bf16[6,1024,64]{2,1,0:T(8,128)(2,1)} %copy-done.4, bf16[2,1024,64]{2,1,0:T(8,128)(2,1)S(1)} %copy-done.6, ...), custom_call_target="tpu_custom_call" | custom-call | flops 2415919104 | bytes 2359296 | tf_op jit(solution)/shard_map/pallas_call | solution.py:215
  397.5 2.8 collective-permute-start.39
  400.4 3.9 convolution_convert_fusion.1
  404.6 2.6 collective-permute-done.37
  407.2 2.4 fusion.16
  409.6 9.8 %collective-permute-done.38 = bf16[256,640]{1,0:T(8,128)(2,1)S(1)} collective-permute-done((bf16[256,640]{1,0:T(8,128)(2,1)S(1)}, bf16[256,640]{1,0:T(8,128)(2,1)S(1)}, u32[]{:S(2)}, u32[]{:S(2)}) %collective-permute-start.38) | collective-permute-done | bytes 327712 | tf_op jit(solution)/shard_map/ppermute | solution.py:335
  419.4 2.4 fusion.14
  421.8 2.5 fusion.12
  424.3 2.8 fusion.31
  433.8 8.5 %collective-permute-start.69 = (bf16[384,1536]{1,0:T(8,128)(2,1)S(1)}, bf16[384,1536]{1,0:T(8,128)(2,1)S(1)}, u32[]{:S(2)}, u32[]{:S(2)}) collective-permute-start(bf16[384,1536]{1,0:T(8,128)(2,1)S(1)} %add_convert_fusion.3), channel_id=1, source_target_pairs={{0,1},{1,2},{2,3},{4,5},{5,6},{6,7},{8,9},{9,10},{10,11},{12,13},{... | collective-permute-start | bytes 3538952 | tf_op jit(solution)/shard_map/ppermute | solution.py:391
  445.1 2.2 collective-permute-done.47
  448.5 2.5 collective-permute-done.48
  451.1 2.7 collective-permute-start.49
  453.8 28.8 %collective-permute-done.49 = f32[1,1536]{1,0:T(1,128)S(1)} collective-permute-done((f32[1,1536]{1,0:T(1,128)S(1)}, f32[1,1536]{1,0:T(1,128)S(1)}, u32[]{:S(2)}, u32[]{:S(2)}) %collective-permute-start.49) | collective-permute-done | bytes 6176 | tf_op jit(solution)/shard_map/ppermute | solution.py:603
  482.5 2.9 collective-permute-start.50
  487.1 2.3 collective-permute-start.40
  489.5 3.8 slice.229
  493.8 2.5 fusion.66
  497.9 7.0 %collective-permute-done.40 = bf16[256,1536]{1,0:T(8,128)(2,1)} collective-permute-done((bf16[256,1536]{1,0:T(8,128)(2,1)}, bf16[256,1536]{1,0:T(8,128)(2,1)}, u32[]{:S(2)}, u32[]{:S(2)}) %collective-permute-start.40) | collective-permute-done | bytes 786464 | tf_op jit(solution)/shard_map/ppermute | solution.py:391
  506.2 7.0 %collective-permute-start.44 = (bf16[256,1536]{1,0:T(8,128)(2,1)}, bf16[256,1536]{1,0:T(8,128)(2,1)}, u32[]{:S(2)}, u32[]{:S(2)}) collective-permute-start(bf16[256,1536]{1,0:T(8,128)(2,1)} %collective-permute-done.40), channel_id=1, source_target_pairs={{0,1},{1,2},{2,3},{4,5},{5,6},{6,7},{8,9},{9,10},{10,11},{12,13},{... | collective-permute-start | bytes 2359304 | tf_op jit(solution)/shard_map/ppermute | solution.py:391
  516.2 2.4 copy.64
  519.8 6.5 collective-permute-done.42
  527.6 5.1 collective-permute-start.45
  532.7 3.1 fusion
  537.7 8.1 %collective-permute-done.43 = bf16[256,1536]{1,0:T(8,128)(2,1)S(1)} collective-permute-done((bf16[256,1536]{1,0:T(8,128)(2,1)}, bf16[256,1536]{1,0:T(8,128)(2,1)S(1)}, u32[]{:S(2)}, u32[]{:S(2)}) %collective-permute-start.43) | collective-permute-done | bytes 786464 | tf_op jit(solution)/shard_map/ppermute | solution.py:396
  550.3 2.7 add_convert_fusion.1
  553.1 11.0 %collective-permute-done.53 = bf16[208,1536]{1,0:T(8,128)(2,1)S(1)} collective-permute-done((bf16[208,1536]{1,0:T(8,128)(2,1)S(1)}, bf16[208,1536]{1,0:T(8,128)(2,1)S(1)}, u32[]{:S(2)}, u32[]{:S(2)}) %collective-permute-start.53) | collective-permute-done | bytes 639008 | tf_op jit(solution)/shard_map/ppermute | solution.py:330
  564.5 2.3 collective-permute-start.55
  570.9 2.5 collective-permute-done.55
  573.4 7.4 %collective-permute-done.56 = bf16[64,1536]{1,0:T(8,128)(2,1)S(1)} collective-permute-done((bf16[64,1536]{1,0:T(8,128)(2,1)S(1)}, bf16[64,1536]{1,0:T(8,128)(2,1)S(1)}, u32[]{:S(2)}, u32[]{:S(2)}) %collective-permute-start.56) | collective-permute-done | bytes 196640 | tf_op jit(solution)/shard_map/ppermute | solution.py:335
  586.0 19.1 %collective-permute-done.59 = bf16[64,1536]{1,0:T(8,128)(2,1)S(1)} collective-permute-done((bf16[64,1536]{1,0:T(8,128)(2,1)S(1)}, bf16[64,1536]{1,0:T(8,128)(2,1)S(1)}, u32[]{:S(2)}, u32[]{:S(2)}) %collective-permute-start.59) | collective-permute-done | bytes 196640 | tf_op jit(solution)/shard_map/ppermute | solution.py:330
  609.0 4.2 collective-permute-done.61
  618.2 55.3 %all-gather.6.cloned.1.call-done = bf16[1024,1536]{1,0:T(8,128)(2,1)} async-done(((bf16[256,1536]{1,0:T(8,128)(2,1)}), bf16[1024,1536]{1,0:T(8,128)(2,1)}) %all-gather.6.cloned.1.call-update) | async-done | bytes 3145744 | tf_op jit(solution)/shard_map/all_gather | solution.py:541
  673.5 3.9 copy.109
  (363 shorter events, 135.2 us)
Async XLA Ops:
  7.2 199.7 %all-gather.4.cloned.1.call-start = ((), (), s32[]{:S(2)}) async-start(), calls=%async_computation | async-start | bytes 7667712 | tf_op jit(solution)/shard_map/all_gather | solution.py:447
  10.9 393.7 %all-gather.8.cloned.1.call-start = ((), (), s32[]{:S(2)}) async-start(), calls=%async_computation.2 | async-start | bytes 8110080 | tf_op jit(solution)/shard_map/all_gather | solution.py:576
  11.7 57.0 %collective-permute-start.3 = (bf16[48,1536]{1,0:T(8,128)(2,1)}, bf16[48,1536]{1,0:T(8,128)(2,1)}, u32[]{:S(2)}, u32[]{:S(2)}) collective-permute-start(bf16[48,1536]{1,0:T(8,128)(2,1)} %constant_dynamic-slice_fusion.3), channel_id=1, source_target_pairs={{0,1},{1,2},{2,3},{3,0},{4,5},{5,6},{6,7},{7,4},{8,9},{9,10},{10,1... | collective-permute-start | bytes 442376 | tf_op jit(solution)/shard_map/ppermute | solution.py:335
  14.7 54.0 %collective-permute-start.4 = (bf16[48,1536]{1,0:T(8,128)(2,1)}, bf16[48,1536]{1,0:T(8,128)(2,1)}, u32[]{:S(2)}, u32[]{:S(2)}) collective-permute-start(bf16[48,1536]{1,0:T(8,128)(2,1)} %constant_dynamic-slice_fusion.3), channel_id=1, source_target_pairs={{0,2},{1,3},{2,0},{3,1},{4,6},{5,7},{6,4},{7,5},{8,10},{9,11},{10,... | collective-permute-start | bytes 442376 | tf_op jit(solution)/shard_map/ppermute | solution.py:335
  17.3 51.5 %collective-permute-start.5 = (bf16[48,1536]{1,0:T(8,128)(2,1)}, bf16[48,1536]{1,0:T(8,128)(2,1)}, u32[]{:S(2)}, u32[]{:S(2)}) collective-permute-start(bf16[48,1536]{1,0:T(8,128)(2,1)} %constant_dynamic-slice_fusion.3), channel_id=1, source_target_pairs={{0,3},{1,0},{2,1},{3,2},{4,7},{5,4},{6,5},{7,6},{8,11},{9,8},{10,9... | collective-permute-start | bytes 442376 | tf_op jit(solution)/shard_map/ppermute | solution.py:335
  45.4 27.6 %collective-permute-start = (bf16[256,384]{1,0:T(8,128)(2,1)S(1)}, bf16[256,384]{1,0:T(8,128)(2,1)}, u32[]{:S(2)}, u32[]{:S(2)}) collective-permute-start(bf16[256,384]{1,0:T(8,128)(2,1)S(1)} %get-tuple-element.37), channel_id=1, source_target_pairs={{0,1},{1,2},{2,3},{3,0},{4,5},{5,6},{6,7},{7,4},{8,9},{9,10},{10,1... | collective-permute-start | bytes 589832 | tf_op jit(solution)/shard_map/ppermute | solution.py:335
  46.2 29.0 %collective-permute-start.1 = (bf16[256,384]{1,0:T(8,128)(2,1)S(1)}, bf16[256,384]{1,0:T(8,128)(2,1)}, u32[]{:S(2)}, u32[]{:S(2)}) collective-permute-start(bf16[256,384]{1,0:T(8,128)(2,1)S(1)} %get-tuple-element.38), channel_id=1, source_target_pairs={{0,2},{1,3},{2,0},{3,1},{4,6},{5,7},{6,4},{7,5},{8,10},{9,11},{10,... | collective-permute-start | bytes 589832 | tf_op jit(solution)/shard_map/ppermute | solution.py:335
  69.9 18.4 %collective-permute-start.6 = (bf16[4,48,1536]{2,1,0:T(8,128)(2,1)S(1)}, bf16[4,48,1536]{2,1,0:T(8,128)(2,1)S(1)}, u32[]{:S(2)}, u32[]{:S(2)}) collective-permute-start(bf16[4,48,1536]{2,1,0:T(8,128)(2,1)S(1)} %pad_maximum_fusion.5), channel_id=1, source_target_pairs={{0,4},{4,0},{8,12},{12,8},{16,20},{20,16},{24,28},{28,24},{1,5},{5... | collective-permute-start | bytes 1769480 | tf_op jit(solution)/shard_map/ppermute | solution.py:330
  70.0 19.6 %collective-permute-start.7 = (bf16[4,48,1536]{2,1,0:T(8,128)(2,1)S(1)}, bf16[4,48,1536]{2,1,0:T(8,128)(2,1)S(1)}, u32[]{:S(2)}, u32[]{:S(2)}) collective-permute-start(bf16[4,48,1536]{2,1,0:T(8,128)(2,1)S(1)} %pad_maximum_fusion.5), channel_id=1, source_target_pairs={{0,8},{4,12},{8,0},{12,4},{16,24},{20,28},{24,16},{28,20},{1,9},{5... | collective-permute-start | bytes 1769480 | tf_op jit(solution)/shard_map/ppermute | solution.py:330
  71.5 28.0 %collective-permute-start.9 = (bf16[4,48,1536]{2,1,0:T(8,128)(2,1)S(1)}, bf16[4,48,1536]{2,1,0:T(8,128)(2,1)S(1)}, u32[]{:S(2)}, u32[]{:S(2)}) collective-permute-start(bf16[4,48,1536]{2,1,0:T(8,128)(2,1)S(1)} %pad_maximum_fusion.5), channel_id=1, source_target_pairs={{0,16},{4,20},{8,24},{12,28},{16,0},{20,4},{24,8},{28,12},{1,17},{... | collective-permute-start | bytes 1769480 | tf_op jit(solution)/shard_map/ppermute | solution.py:330
  73.1 26.5 %collective-permute-start.11 = (bf16[4,48,1536]{2,1,0:T(8,128)(2,1)S(1)}, bf16[4,48,1536]{2,1,0:T(8,128)(2,1)S(1)}, u32[]{:S(2)}, u32[]{:S(2)}) collective-permute-start(bf16[4,48,1536]{2,1,0:T(8,128)(2,1)S(1)} %pad_maximum_fusion.5), channel_id=1, source_target_pairs={{0,24},{4,28},{8,16},{12,20},{16,8},{20,12},{24,0},{28,4},{1,25},{... | collective-permute-start | bytes 1769480 | tf_op jit(solution)/shard_map/ppermute | solution.py:330
  83.6 28.0 %collective-permute-start.20 = (bf16[384,1536]{1,0:T(8,128)(2,1)}, bf16[384,1536]{1,0:T(8,128)(2,1)}, u32[]{:S(2)}, u32[]{:S(2)}) collective-permute-start(bf16[384,1536]{1,0:T(8,128)(2,1)} %pad_maximum_fusion.1), channel_id=1, source_target_pairs={{0,1},{1,2},{2,3},{4,5},{5,6},{6,7},{8,9},{9,10},{10,11},{12,13},{... | collective-permute-start | bytes 3538952 | tf_op jit(solution)/shard_map/ppermute | solution.py:391
  88.3 28.5 %collective-permute-start.21 = (bf16[384,1536]{1,0:T(8,128)(2,1)}, bf16[384,1536]{1,0:T(8,128)(2,1)}, u32[]{:S(2)}, u32[]{:S(2)}) collective-permute-start(bf16[384,1536]{1,0:T(8,128)(2,1)} %pad_maximum_fusion.1), channel_id=1, source_target_pairs={{3,2},{2,1},{1,0},{7,6},{6,5},{5,4},{11,10},{10,9},{9,8},{15,14},{... | collective-permute-start | bytes 3538952 | tf_op jit(solution)/shard_map/ppermute | solution.py:396
  89.6 10.6 %collective-permute-start.8 = (bf16[4,48,1536]{2,1,0:T(8,128)(2,1)S(1)}, bf16[4,48,1536]{2,1,0:T(8,128)(2,1)S(1)}, u32[]{:S(2)}, u32[]{:S(2)}) collective-permute-start(bf16[4,48,1536]{2,1,0:T(8,128)(2,1)S(1)} %collective-permute-done.7), channel_id=1, source_target_pairs={{0,4},{4,0},{8,12},{12,8},{16,20},{20,16},{24,28},{28,24},{1,5},{5... | collective-permute-start | bytes 1769480 | tf_op jit(solution)/shard_map/ppermute | solution.py:330
  108.0 10.1 %collective-permute-start.13 = (bf16[256,1536]{1,0:T(8,128)(2,1)S(1)}, bf16[256,1536]{1,0:T(8,128)(2,1)}, u32[]{:S(2)}, u32[]{:S(2)}) collective-permute-start(bf16[256,1536]{1,0:T(8,128)(2,1)S(1)} %get-tuple-element.107), channel_id=1, source_target_pairs={{0,4},{4,0},{8,12},{12,8},{16,20},{20,16},{24,28},{28,24},{1,5},{5... | collective-permute-start | bytes 2359304 | tf_op jit(solution)/shard_map/ppermute | solution.py:330
  108.2 20.5 %collective-permute-start.14 = (bf16[256,1536]{1,0:T(8,128)(2,1)S(1)}, bf16[256,1536]{1,0:T(8,128)(2,1)}, u32[]{:S(2)}, u32[]{:S(2)}) collective-permute-start(bf16[256,1536]{1,0:T(8,128)(2,1)S(1)} %get-tuple-element.107), channel_id=1, source_target_pairs={{0,8},{4,12},{8,0},{12,4},{16,24},{20,28},{24,16},{28,20},{1,9},{5... | collective-permute-start | bytes 2359304 | tf_op jit(solution)/shard_map/ppermute | solution.py:330
  108.6 27.6 %collective-permute-start.16 = (bf16[256,1536]{1,0:T(8,128)(2,1)S(1)}, bf16[256,1536]{1,0:T(8,128)(2,1)}, u32[]{:S(2)}, u32[]{:S(2)}) collective-permute-start(bf16[256,1536]{1,0:T(8,128)(2,1)S(1)} %get-tuple-element.107), channel_id=1, source_target_pairs={{0,16},{4,20},{8,24},{12,28},{16,0},{20,4},{24,8},{28,12},{1,17},{... | collective-permute-start | bytes 2359304 | tf_op jit(solution)/shard_map/ppermute | solution.py:330
  111.6 36.1 %collective-permute-start.18 = (bf16[256,1536]{1,0:T(8,128)(2,1)S(1)}, bf16[256,1536]{1,0:T(8,128)(2,1)}, u32[]{:S(2)}, u32[]{:S(2)}) collective-permute-start(bf16[256,1536]{1,0:T(8,128)(2,1)S(1)} %get-tuple-element.107), channel_id=1, source_target_pairs={{0,24},{4,28},{8,16},{12,20},{16,8},{20,12},{24,0},{28,4},{1,25},{... | collective-permute-start | bytes 2359304 | tf_op jit(solution)/shard_map/ppermute | solution.py:330
  116.8 35.0 %collective-permute-start.22 = (bf16[384,1536]{1,0:T(8,128)(2,1)}, bf16[384,1536]{1,0:T(8,128)(2,1)}, u32[]{:S(2)}, u32[]{:S(2)}) collective-permute-start(bf16[384,1536]{1,0:T(8,128)(2,1)} %collective-permute-done.21), channel_id=1, source_target_pairs={{3,2},{2,1},{1,0},{7,6},{6,5},{5,4},{11,10},{10,9},{9,8},{15,14},{... | collective-permute-start | bytes 3538952 | tf_op jit(solution)/shard_map/ppermute | solution.py:396
  118.1 35.0 %collective-permute-start.24 = (bf16[384,1536]{1,0:T(8,128)(2,1)}, bf16[384,1536]{1,0:T(8,128)(2,1)}, u32[]{:S(2)}, u32[]{:S(2)}) collective-permute-start(bf16[384,1536]{1,0:T(8,128)(2,1)} %collective-permute-done.20), channel_id=1, source_target_pairs={{0,1},{1,2},{2,3},{4,5},{5,6},{6,7},{8,9},{9,10},{10,11},{12,13},{... | collective-permute-start | bytes 3538952 | tf_op jit(solution)/shard_map/ppermute | solution.py:391
  126.7 367.1 %all-reduce.6.cloned.1.call-start = ((), (), s32[]{:S(2)}) async-start(), calls=%async_computation.3 | async-start | bytes 3932160 | tf_op jit(solution)/shard_map/psum | solution.py:546
  128.6 32.4 %collective-permute-start.15 = (bf16[256,1536]{1,0:T(8,128)(2,1)}, bf16[256,1536]{1,0:T(8,128)(2,1)S(1)}, u32[]{:S(2)}, u32[]{:S(2)}) collective-permute-start(bf16[256,1536]{1,0:T(8,128)(2,1)} %collective-permute-done.14), channel_id=1, source_target_pairs={{0,4},{4,0},{8,12},{12,8},{16,20},{20,16},{24,28},{28,24},{1,5},{5... | collective-permute-start | bytes 2359304 | tf_op jit(solution)/shard_map/ppermute | solution.py:330
  136.2 27.9 %collective-permute-start.17 = (bf16[256,1536]{1,0:T(8,128)(2,1)}, bf16[256,1536]{1,0:T(8,128)(2,1)S(1)}, u32[]{:S(2)}, u32[]{:S(2)}) collective-permute-start(bf16[256,1536]{1,0:T(8,128)(2,1)} %collective-permute-done.16), channel_id=1, source_target_pairs={{0,4},{4,0},{8,12},{12,8},{16,20},{20,16},{24,28},{28,24},{1,5},{5... | collective-permute-start | bytes 2359304 | tf_op jit(solution)/shard_map/ppermute | solution.py:330
  147.6 19.5 %collective-permute-start.19 = (bf16[256,1536]{1,0:T(8,128)(2,1)}, bf16[256,1536]{1,0:T(8,128)(2,1)S(1)}, u32[]{:S(2)}, u32[]{:S(2)}) collective-permute-start(bf16[256,1536]{1,0:T(8,128)(2,1)} %collective-permute-done.18), channel_id=1, source_target_pairs={{0,4},{4,0},{8,12},{12,8},{16,20},{20,16},{24,28},{28,24},{1,5},{5... | collective-permute-start | bytes 2359304 | tf_op jit(solution)/shard_map/ppermute | solution.py:330
  151.8 47.5 %collective-permute-start.23 = (bf16[384,1536]{1,0:T(8,128)(2,1)}, bf16[384,1536]{1,0:T(8,128)(2,1)S(1)}, u32[]{:S(2)}, u32[]{:S(2)}) collective-permute-start(bf16[384,1536]{1,0:T(8,128)(2,1)} %collective-permute-done.22), channel_id=1, source_target_pairs={{3,2},{2,1},{1,0},{7,6},{6,5},{5,4},{11,10},{10,9},{9,8},{15,14},{... | collective-permute-start | bytes 3538952 | tf_op jit(solution)/shard_map/ppermute | solution.py:396
  153.1 49.2 %collective-permute-start.25 = (bf16[384,1536]{1,0:T(8,128)(2,1)}, bf16[384,1536]{1,0:T(8,128)(2,1)S(1)}, u32[]{:S(2)}, u32[]{:S(2)}) collective-permute-start(bf16[384,1536]{1,0:T(8,128)(2,1)} %collective-permute-done.24), channel_id=1, source_target_pairs={{0,1},{1,2},{2,3},{4,5},{5,6},{6,7},{8,9},{9,10},{10,11},{12,13},{... | collective-permute-start | bytes 3538952 | tf_op jit(solution)/shard_map/ppermute | solution.py:391
  252.7 42.8 %collective-permute-start.26 = (bf16[4,256,1664]{2,1,0:T(8,128)(2,1)}, bf16[4,256,1664]{2,1,0:T(8,128)(2,1)}, u32[]{:S(2)}, u32[]{:S(2)}) collective-permute-start(bf16[4,256,1664]{2,1,0:T(8,128)(2,1)} %slice.220), channel_id=1, source_target_pairs={{0,4},{4,0},{8,12},{12,8},{16,20},{20,16},{24,28},{28,24},{1,5},{5... | collective-permute-start | bytes 10223624 | tf_op jit(solution)/shard_map/ppermute | solution.py:330
  255.3 35.9 %collective-permute-start.65 = (bf16[384,1536]{1,0:T(8,128)(2,1)}, bf16[384,1536]{1,0:T(8,128)(2,1)}, u32[]{:S(2)}, u32[]{:S(2)}) collective-permute-start(bf16[384,1536]{1,0:T(8,128)(2,1)} %pad_maximum_fusion.4), channel_id=1, source_target_pairs={{0,1},{4,5},{8,9},{12,13},{16,17},{20,21},{24,25},{28,29}} | collective-permute-start | bytes 3538952 | tf_op jit(solution)/shard_map/ppermute | solution.py:391
  267.2 24.0 %collective-permute-start.67 = (bf16[384,1536]{1,0:T(8,128)(2,1)}, bf16[384,1536]{1,0:T(8,128)(2,1)}, u32[]{:S(2)}, u32[]{:S(2)}) collective-permute-start(bf16[384,1536]{1,0:T(8,128)(2,1)} %pad_maximum_fusion.2), channel_id=1, source_target_pairs={{3,2},{7,6},{11,10},{15,14},{19,18},{23,22},{27,26},{31,30}} | collective-permute-start | bytes 3538952 | tf_op jit(solution)/shard_map/ppermute | solution.py:396
  294.8 15.2 %collective-permute-start.68 = (bf16[384,1536]{1,0:T(8,128)(2,1)S(1)}, bf16[384,1536]{1,0:T(8,128)(2,1)S(1)}, u32[]{:S(2)}, u32[]{:S(2)}) collective-permute-start(bf16[384,1536]{1,0:T(8,128)(2,1)S(1)} %get-tuple-element.134), channel_id=1, source_target_pairs={{3,2},{2,1},{7,6},{6,5},{11,10},{10,9},{15,14},{14,13},{19,18},{18... | collective-permute-start | bytes 3538952 | tf_op jit(solution)/shard_map/ppermute | solution.py:396
  299.5 21.9 %collective-permute-start.27 = (bf16[256,1664]{1,0:T(8,128)(2,1)S(1)}, bf16[256,1664]{1,0:T(8,128)(2,1)S(1)}, u32[]{:S(2)}, u32[]{:S(2)}) collective-permute-start(bf16[256,1664]{1,0:T(8,128)(2,1)S(1)} %get-tuple-element.108), channel_id=1, source_target_pairs={{0,8},{4,12},{8,0},{12,4},{16,24},{20,28},{24,16},{28,20},{1,9},{5... | collective-permute-start | bytes 2555912 | tf_op jit(solution)/shard_map/ppermute | solution.py:330
  299.7 39.1 %collective-permute-start.28 = (bf16[256,1664]{1,0:T(8,128)(2,1)S(1)}, bf16[256,1664]{1,0:T(8,128)(2,1)S(1)}, u32[]{:S(2)}, u32[]{:S(2)}) collective-permute-start(bf16[256,1664]{1,0:T(8,128)(2,1)S(1)} %get-tuple-element.110), channel_id=1, source_target_pairs={{0,16},{4,20},{8,24},{12,28},{16,0},{20,4},{24,8},{28,12},{1,17},{... | collective-permute-start | bytes 2555912 | tf_op jit(solution)/shard_map/ppermute | solution.py:330
  302.0 36.8 %collective-permute-start.29 = (bf16[256,1664]{1,0:T(8,128)(2,1)S(1)}, bf16[256,1664]{1,0:T(8,128)(2,1)S(1)}, u32[]{:S(2)}, u32[]{:S(2)}) collective-permute-start(bf16[256,1664]{1,0:T(8,128)(2,1)S(1)} %get-tuple-element.109), channel_id=1, source_target_pairs={{0,24},{4,28},{8,16},{12,20},{16,8},{20,12},{24,0},{28,4},{1,25},{... | collective-permute-start | bytes 2555912 | tf_op jit(solution)/shard_map/ppermute | solution.py:330
  303.7 128.5 %collective-permute-start.66 = (bf16[384,1536]{1,0:T(8,128)(2,1)}, bf16[384,1536]{1,0:T(8,128)(2,1)}, u32[]{:S(2)}, u32[]{:S(2)}) collective-permute-start(bf16[384,1536]{1,0:T(8,128)(2,1)} %get-tuple-element.135), channel_id=1, source_target_pairs={{0,1},{1,2},{4,5},{5,6},{8,9},{9,10},{12,13},{13,14},{16,17},{17,1... | collective-permute-start | bytes 3538952 | tf_op jit(solution)/shard_map/ppermute | solution.py:391
  345.6 17.1 %collective-permute-start.34 = (bf16[256,384]{1,0:T(8,128)(2,1)}, bf16[256,384]{1,0:T(8,128)(2,1)S(1)}, u32[]{:S(2)}, u32[]{:S(2)}) collective-permute-start(bf16[256,384]{1,0:T(8,128)(2,1)} %get-tuple-element.144), channel_id=1, source_target_pairs={{0,3},{1,0},{2,1},{3,2},{4,7},{5,4},{6,5},{7,6},{8,11},{9,8},{10,9... | collective-permute-start | bytes 589832 | tf_op jit(solution)/shard_map/ppermute | solution.py:335
  356.5 15.6 %collective-permute-start.35 = (bf16[256,384]{1,0:T(8,128)(2,1)S(1)}, bf16[256,384]{1,0:T(8,128)(2,1)S(1)}, u32[]{:S(2)}, u32[]{:S(2)}) collective-permute-start(bf16[256,384]{1,0:T(8,128)(2,1)S(1)} %get-tuple-element.143), channel_id=1, source_target_pairs={{0,2},{1,3},{2,0},{3,1},{4,6},{5,7},{6,4},{7,5},{8,10},{9,11},{10,... | collective-permute-start | bytes 589832 | tf_op jit(solution)/shard_map/ppermute | solution.py:335
  356.5 15.6 %collective-permute-start.36 = (bf16[256,384]{1,0:T(8,128)(2,1)S(1)}, bf16[256,384]{1,0:T(8,128)(2,1)S(1)}, u32[]{:S(2)}, u32[]{:S(2)}) collective-permute-start(bf16[256,384]{1,0:T(8,128)(2,1)S(1)} %get-tuple-element.142), channel_id=1, source_target_pairs={{0,1},{1,2},{2,3},{3,0},{4,5},{5,6},{6,7},{7,4},{8,9},{9,10},{10,1... | collective-permute-start | bytes 589832 | tf_op jit(solution)/shard_map/ppermute | solution.py:335
  362.7 169.9 %collective-permute-start.51 = (bf16[4,208,1536]{2,1,0:T(8,128)(2,1)}, bf16[4,208,1536]{2,1,0:T(8,128)(2,1)}, u32[]{:S(2)}, u32[]{:S(2)}) collective-permute-start(bf16[4,208,1536]{2,1,0:T(8,128)(2,1)} %fusion.4), channel_id=1, source_target_pairs={{0,4},{4,0},{8,12},{12,8},{16,20},{20,16},{24,28},{28,24},{1,5},{5... | collective-permute-start | bytes 7667720 | tf_op jit(solution)/shard_map/ppermute | solution.py:330
  394.6 12.6 %collective-permute-start.37 = (bf16[256,640]{1,0:T(8,128)(2,1)S(1)}, bf16[256,640]{1,0:T(8,128)(2,1)S(1)}, u32[]{:S(2)}, u32[]{:S(2)}) collective-permute-start(bf16[256,640]{1,0:T(8,128)(2,1)S(1)} %get-tuple-element.51), channel_id=1, source_target_pairs={{0,1},{1,2},{2,3},{3,0},{4,5},{5,6},{6,7},{7,4},{8,9},{9,10},{10,1... | collective-permute-start | bytes 983048 | tf_op jit(solution)/shard_map/ppermute | solution.py:335
  395.5 23.8 %collective-permute-start.38 = (bf16[256,640]{1,0:T(8,128)(2,1)S(1)}, bf16[256,640]{1,0:T(8,128)(2,1)S(1)}, u32[]{:S(2)}, u32[]{:S(2)}) collective-permute-start(bf16[256,640]{1,0:T(8,128)(2,1)S(1)} %get-tuple-element.52), channel_id=1, source_target_pairs={{0,2},{1,3},{2,0},{3,1},{4,6},{5,7},{6,4},{7,5},{8,10},{9,11},{10,... | collective-permute-start | bytes 983048 | tf_op jit(solution)/shard_map/ppermute | solution.py:335
  397.5 24.2 %collective-permute-start.39 = (bf16[256,640]{1,0:T(8,128)(2,1)S(1)}, bf16[256,640]{1,0:T(8,128)(2,1)S(1)}, u32[]{:S(2)}, u32[]{:S(2)}) collective-permute-start(bf16[256,640]{1,0:T(8,128)(2,1)S(1)} %get-tuple-element.53), channel_id=1, source_target_pairs={{0,3},{1,0},{2,1},{3,2},{4,7},{5,4},{6,5},{7,6},{8,11},{9,8},{10,9... | collective-permute-start | bytes 983048 | tf_op jit(solution)/shard_map/ppermute | solution.py:335
  404.3 269.2 %all-gather.6.cloned.1.call-start = ((), (), s32[]{:S(2)}) async-start(), calls=%async_computation.1 | async-start | bytes 3932160 | tf_op jit(solution)/shard_map/all_gather | solution.py:541
  427.2 16.4 %collective-permute-start.46 = (f32[1,1536]{1,0:T(1,128)S(1)}, f32[1,1536]{1,0:T(1,128)S(1)}, u32[]{:S(2)}, u32[]{:S(2)}) collective-permute-start(f32[1,1536]{1,0:T(1,128)S(1)} %broadcast_in_dim.149), channel_id=1, source_target_pairs={{0,4},{4,0},{8,12},{12,8},{16,20},{20,16},{24,28},{28,24},{1,5},{5... | collective-permute-start | bytes 18440 | tf_op jit(solution)/shard_map/ppermute | solution.py:603
  430.8 63.1 %collective-permute-start.41 = (bf16[256,1536]{1,0:T(8,128)(2,1)}, bf16[256,1536]{1,0:T(8,128)(2,1)}, u32[]{:S(2)}, u32[]{:S(2)}) collective-permute-start(bf16[256,1536]{1,0:T(8,128)(2,1)} %get-tuple-element.103), channel_id=1, source_target_pairs={{3,2},{2,1},{1,0},{7,6},{6,5},{5,4},{11,10},{10,9},{9,8},{15,14},{... | collective-permute-start | bytes 2359304 | tf_op jit(solution)/shard_map/ppermute | solution.py:396
  433.8 72.5 %collective-permute-start.69 = (bf16[384,1536]{1,0:T(8,128)(2,1)S(1)}, bf16[384,1536]{1,0:T(8,128)(2,1)S(1)}, u32[]{:S(2)}, u32[]{:S(2)}) collective-permute-start(bf16[384,1536]{1,0:T(8,128)(2,1)S(1)} %add_convert_fusion.3), channel_id=1, source_target_pairs={{0,1},{1,2},{2,3},{4,5},{5,6},{6,7},{8,9},{9,10},{10,11},{12,13},{... | collective-permute-start | bytes 3538952 | tf_op jit(solution)/shard_map/ppermute | solution.py:391
  442.3 70.9 %collective-permute-start.70 = (bf16[384,1536]{1,0:T(8,128)(2,1)S(1)}, bf16[384,1536]{1,0:T(8,128)(2,1)}, u32[]{:S(2)}, u32[]{:S(2)}) collective-permute-start(bf16[384,1536]{1,0:T(8,128)(2,1)S(1)} %copy-done.40), channel_id=1, source_target_pairs={{3,2},{2,1},{1,0},{7,6},{6,5},{5,4},{11,10},{10,9},{9,8},{15,14},{... | collective-permute-start | bytes 3538952 | tf_op jit(solution)/shard_map/ppermute | solution.py:396
  451.1 31.5 %collective-permute-start.49 = (f32[1,1536]{1,0:T(1,128)S(1)}, f32[1,1536]{1,0:T(1,128)S(1)}, u32[]{:S(2)}, u32[]{:S(2)}) collective-permute-start(f32[1,1536]{1,0:T(1,128)S(1)} %add.347), channel_id=1, source_target_pairs={{0,1},{1,0},{2,3},{3,2},{4,5},{5,4},{6,7},{7,6},{8,9},{9,8},{10,11... | collective-permute-start | bytes 18440 | tf_op jit(solution)/shard_map/ppermute | solution.py:603
  487.1 17.8 %collective-permute-start.40 = (bf16[256,1536]{1,0:T(8,128)(2,1)}, bf16[256,1536]{1,0:T(8,128)(2,1)}, u32[]{:S(2)}, u32[]{:S(2)}) collective-permute-start(bf16[256,1536]{1,0:T(8,128)(2,1)} %get-tuple-element.103), channel_id=1, source_target_pairs={{0,1},{1,2},{2,3},{4,5},{5,6},{6,7},{8,9},{9,10},{10,11},{12,13},{... | collective-permute-start | bytes 2359304 | tf_op jit(solution)/shard_map/ppermute | solution.py:391
  493.8 56.5 %collective-permute-start.30 = (bf16[4,256,1536]{2,1,0:T(8,128)(2,1)}, bf16[4,256,1536]{2,1,0:T(8,128)(2,1)}, u32[]{:S(2)}, u32[]{:S(2)}) collective-permute-start(bf16[4,256,1536]{2,1,0:T(8,128)(2,1)} %slice.229), channel_id=1, source_target_pairs={{0,4},{4,0},{8,12},{12,8},{16,20},{20,16},{24,28},{28,24},{1,5},{5... | collective-permute-start | bytes 9437192 | tf_op jit(solution)/shard_map/ppermute | solution.py:330
  504.9 21.4 %collective-permute-start.42 = (bf16[256,1536]{1,0:T(8,128)(2,1)}, bf16[256,1536]{1,0:T(8,128)(2,1)}, u32[]{:S(2)}, u32[]{:S(2)}) collective-permute-start(bf16[256,1536]{1,0:T(8,128)(2,1)} %collective-permute-done.41), channel_id=1, source_target_pairs={{3,2},{2,1},{1,0},{7,6},{6,5},{5,4},{11,10},{10,9},{9,8},{15,14},{... | collective-permute-start | bytes 2359304 | tf_op jit(solution)/shard_map/ppermute | solution.py:396
  506.2 21.3 %collective-permute-start.44 = (bf16[256,1536]{1,0:T(8,128)(2,1)}, bf16[256,1536]{1,0:T(8,128)(2,1)}, u32[]{:S(2)}, u32[]{:S(2)}) collective-permute-start(bf16[256,1536]{1,0:T(8,128)(2,1)} %collective-permute-done.40), channel_id=1, source_target_pairs={{0,1},{1,2},{2,3},{4,5},{5,6},{6,7},{8,9},{9,10},{10,11},{12,13},{... | collective-permute-start | bytes 2359304 | tf_op jit(solution)/shard_map/ppermute | solution.py:391
  526.3 19.5 %collective-permute-start.43 = (bf16[256,1536]{1,0:T(8,128)(2,1)}, bf16[256,1536]{1,0:T(8,128)(2,1)S(1)}, u32[]{:S(2)}, u32[]{:S(2)}) collective-permute-start(bf16[256,1536]{1,0:T(8,128)(2,1)} %collective-permute-done.42), channel_id=1, source_target_pairs={{3,2},{2,1},{1,0},{7,6},{6,5},{5,4},{11,10},{10,9},{9,8},{15,14},{... | collective-permute-start | bytes 2359304 | tf_op jit(solution)/shard_map/ppermute | solution.py:396
  527.6 56.1 %collective-permute-start.45 = (bf16[256,1536]{1,0:T(8,128)(2,1)}, bf16[256,1536]{1,0:T(8,128)(2,1)S(1)}, u32[]{:S(2)}, u32[]{:S(2)}) collective-permute-start(bf16[256,1536]{1,0:T(8,128)(2,1)} %collective-permute-done.44), channel_id=1, source_target_pairs={{0,1},{1,2},{2,3},{4,5},{5,6},{6,7},{8,9},{9,10},{10,11},{12,13},{... | collective-permute-start | bytes 2359304 | tf_op jit(solution)/shard_map/ppermute | solution.py:391
  535.9 17.1 %collective-permute-start.52 = (bf16[208,1536]{1,0:T(8,128)(2,1)S(1)}, bf16[208,1536]{1,0:T(8,128)(2,1)S(1)}, u32[]{:S(2)}, u32[]{:S(2)}) collective-permute-start(bf16[208,1536]{1,0:T(8,128)(2,1)S(1)} %get-tuple-element.122), channel_id=1, source_target_pairs={{0,8},{4,12},{8,0},{12,4},{16,24},{20,28},{24,16},{28,20},{1,9},{5... | collective-permute-start | bytes 1916936 | tf_op jit(solution)/shard_map/ppermute | solution.py:330
  537.4 26.7 %collective-permute-start.53 = (bf16[208,1536]{1,0:T(8,128)(2,1)S(1)}, bf16[208,1536]{1,0:T(8,128)(2,1)S(1)}, u32[]{:S(2)}, u32[]{:S(2)}) collective-permute-start(bf16[208,1536]{1,0:T(8,128)(2,1)S(1)} %get-tuple-element.124), channel_id=1, source_target_pairs={{0,16},{4,20},{8,24},{12,28},{16,0},{20,4},{24,8},{28,12},{1,17},{... | collective-permute-start | bytes 1916936 | tf_op jit(solution)/shard_map/ppermute | solution.py:330
  545.8 18.3 %collective-permute-start.54 = (bf16[208,1536]{1,0:T(8,128)(2,1)S(1)}, bf16[208,1536]{1,0:T(8,128)(2,1)S(1)}, u32[]{:S(2)}, u32[]{:S(2)}) collective-permute-start(bf16[208,1536]{1,0:T(8,128)(2,1)S(1)} %get-tuple-element.123), channel_id=1, source_target_pairs={{0,24},{4,28},{8,16},{12,20},{16,8},{20,12},{24,0},{28,4},{1,25},{... | collective-permute-start | bytes 1916936 | tf_op jit(solution)/shard_map/ppermute | solution.py:330
  564.5 8.8 %collective-permute-start.55 = (bf16[64,1536]{1,0:T(8,128)(2,1)S(1)}, bf16[64,1536]{1,0:T(8,128)(2,1)S(1)}, u32[]{:S(2)}, u32[]{:S(2)}) collective-permute-start(bf16[64,1536]{1,0:T(8,128)(2,1)S(1)} %get-tuple-element.149), channel_id=1, source_target_pairs={{0,3},{1,0},{2,1},{3,2},{4,7},{5,4},{6,5},{7,6},{8,11},{9,8},{10,9... | collective-permute-start | bytes 589832 | tf_op jit(solution)/shard_map/ppermute | solution.py:335
  566.8 13.9 %collective-permute-start.56 = (bf16[64,1536]{1,0:T(8,128)(2,1)S(1)}, bf16[64,1536]{1,0:T(8,128)(2,1)S(1)}, u32[]{:S(2)}, u32[]{:S(2)}) collective-permute-start(bf16[64,1536]{1,0:T(8,128)(2,1)S(1)} %get-tuple-element.150), channel_id=1, source_target_pairs={{0,2},{1,3},{2,0},{3,1},{4,6},{5,7},{6,4},{7,5},{8,10},{9,11},{10,... | collective-permute-start | bytes 589832 | tf_op jit(solution)/shard_map/ppermute | solution.py:335
  567.8 14.4 %collective-permute-start.57 = (bf16[64,1536]{1,0:T(8,128)(2,1)S(1)}, bf16[64,1536]{1,0:T(8,128)(2,1)S(1)}, u32[]{:S(2)}, u32[]{:S(2)}) collective-permute-start(bf16[64,1536]{1,0:T(8,128)(2,1)S(1)} %concatenate.80), channel_id=1, source_target_pairs={{0,1},{1,2},{2,3},{3,0},{4,5},{5,6},{6,7},{7,4},{8,9},{9,10},{10,1... | collective-permute-start | bytes 589832 | tf_op jit(solution)/shard_map/ppermute | solution.py:335
  570.2 35.6 %collective-permute-start.31 = (bf16[256,1536]{1,0:T(8,128)(2,1)S(1)}, bf16[256,1536]{1,0:T(8,128)(2,1)S(1)}, u32[]{:S(2)}, u32[]{:S(2)}) collective-permute-start(bf16[256,1536]{1,0:T(8,128)(2,1)S(1)} %get-tuple-element.119), channel_id=1, source_target_pairs={{0,8},{4,12},{8,0},{12,4},{16,24},{20,28},{24,16},{28,20},{1,9},{5... | collective-permute-start | bytes 2359304 | tf_op jit(solution)/shard_map/ppermute | solution.py:330
  573.4 34.2 %collective-permute-start.32 = (bf16[256,1536]{1,0:T(8,128)(2,1)S(1)}, bf16[256,1536]{1,0:T(8,128)(2,1)S(1)}, u32[]{:S(2)}, u32[]{:S(2)}) collective-permute-start(bf16[256,1536]{1,0:T(8,128)(2,1)S(1)} %get-tuple-element.121), channel_id=1, source_target_pairs={{0,16},{4,20},{8,24},{12,28},{16,0},{20,4},{24,8},{28,12},{1,17},{... | collective-permute-start | bytes 2359304 | tf_op jit(solution)/shard_map/ppermute | solution.py:330
  580.8 26.8 %collective-permute-start.33 = (bf16[256,1536]{1,0:T(8,128)(2,1)S(1)}, bf16[256,1536]{1,0:T(8,128)(2,1)S(1)}, u32[]{:S(2)}, u32[]{:S(2)}) collective-permute-start(bf16[256,1536]{1,0:T(8,128)(2,1)S(1)} %get-tuple-element.120), channel_id=1, source_target_pairs={{0,24},{4,28},{8,16},{12,20},{16,8},{20,12},{24,0},{28,4},{1,25},{... | collective-permute-start | bytes 2359304 | tf_op jit(solution)/shard_map/ppermute | solution.py:330
  582.5 22.6 %collective-permute-start.59 = (bf16[64,1536]{1,0:T(8,128)(2,1)S(1)}, bf16[64,1536]{1,0:T(8,128)(2,1)S(1)}, u32[]{:S(2)}, u32[]{:S(2)}) collective-permute-start(bf16[64,1536]{1,0:T(8,128)(2,1)S(1)} %get-tuple-element.101), channel_id=1, source_target_pairs={{0,8},{4,12},{8,0},{12,4},{16,24},{20,28},{24,16},{28,20},{1,9},{5... | collective-permute-start | bytes 589832 | tf_op jit(solution)/shard_map/ppermute | solution.py:330
  586.0 23.0 %collective-permute-start.58 = (bf16[64,1536]{1,0:T(8,128)(2,1)S(1)}, bf16[64,1536]{1,0:T(8,128)(2,1)S(1)}, u32[]{:S(2)}, u32[]{:S(2)}) collective-permute-start(bf16[64,1536]{1,0:T(8,128)(2,1)S(1)} %get-tuple-element.101), channel_id=1, source_target_pairs={{0,4},{4,0},{8,12},{12,8},{16,20},{20,16},{24,28},{28,24},{1,5},{5... | collective-permute-start | bytes 589832 | tf_op jit(solution)/shard_map/ppermute | solution.py:330
  (74 other events, 870.2 us)
Sparse Core Ops, SparseCore 0:
  11.1 50.4 all-gather.3
  126.8 92.2 all-gather.7
  404.4 57.9 all-reduce.5
  609.1 64.3 all-gather.5

commit v3 on v2

v3 whole, which is shorter than its diff:
```python
import functools

import jax
import jax.numpy as jnp
from jax import lax
from jax.experimental import pallas as pl
from jax.experimental.pallas import tpu as pltpu
from jax.sharding import PartitionSpec as P

HD = 64
LEN = 1024
EPS = 1e-06
MASKED = -1e30
BF = jnp.bfloat16
F32 = jnp.float32
BLOCK = 256
LANES = 128
NT = (((1,), (1,)), ((), ()))
TN = (((0,), (0,)), ((), ()))


def takes(us):
    return pl.CostEstimate(flops=int(us * 1.15e9), bytes_accessed=0, transcendentals=0)


def mul(a, b, dims=(((1,), (0,)), ((), ()))):
    return lax.dot_general(a, b, dims, preferred_element_type=F32)


def rotate_lanes(y, cos, sin_a, sin_b):
    return y * cos + pltpu.roll(y, 128 - HD // 2, 1) * sin_a + pltpu.roll(y, HD // 2, 1) * sin_b


def rotary_lanes(tokens):
    positions = (jnp.arange(tokens) % LEN).astype(F32)
    lane = jnp.arange(128)
    freqs = 10000.0 ** (-(lane % (HD // 2)).astype(F32) * 2.0 / HD)
    angles = positions[:, None] * freqs[None, :]
    cos, sin = jnp.cos(angles), jnp.sin(angles)
    first = (lane % HD < HD // 2)[None, :]
    return cos, jnp.where(first, -sin, 0.0), jnp.where(first, 0.0, sin)


def causal(block):
    key_at = lax.broadcasted_iota(jnp.int32, (block, block), 0)
    query_at = lax.broadcasted_iota(jnp.int32, (block, block), 1)
    return key_at <= query_at


def attend_kernel(x_ref, gain_ref, w_ref, cos_ref, sin_a_ref, sin_b_ref, mixed_ref, normed_ref, q_ref, k_ref, v_ref, log_ref, vt_ref, out_ref):
    tokens = x_ref.shape[0]
    heads, groups = q_ref.shape[0], k_ref.shape[0]
    repeat = heads // groups
    per = 128 // HD
    scale = HD ** (-0.5)

    @pl.loop(0, tokens // BLOCK)
    def _(i):
        at = pl.multiple_of(i * BLOCK, BLOCK)
        rows = pl.ds(at, BLOCK)
        x = x_ref[rows, :].astype(F32)
        inverse = lax.rsqrt(jnp.mean(x * x, axis=-1, keepdims=True) + EPS)
        normed = (x * inverse * gain_ref[...]).astype(BF)
        normed_ref[rows, :] = normed
        raw = mul(normed, w_ref[...])
        tables = (cos_ref[rows, :], sin_a_ref[rows, :], sin_b_ref[rows, :])
        for h in range(0, heads, per):
            turned = rotate_lanes(raw[:, h * HD : h * HD + 128], *tables) * scale
            for u in range(per):
                q_ref[h + u, rows, :] = turned[:, u * HD : (u + 1) * HD].astype(BF)
        for g in range(0, groups, per):
            lane = (heads + g) * HD
            turned = rotate_lanes(raw[:, lane : lane + 128], *tables)
            lane = (heads + groups + g) * HD
            value = raw[:, lane : lane + 128]
            turned_value = value.T
            for u in range(per):
                k_ref[g + u, rows, :] = turned[:, u * HD : (u + 1) * HD].astype(BF)
                v_ref[g + u, rows, :] = value[:, u * HD : (u + 1) * HD].astype(BF)
                vt_ref[g + u, :, rows] = turned_value[u * HD : (u + 1) * HD].astype(BF)

    keep = causal(BLOCK)

    @pl.loop(0, heads)
    def _(h):
        g = h // repeat
        for i in range(tokens // BLOCK):
            start, stop = i * BLOCK, (i + 1) * BLOCK
            query = q_ref[h, start:stop, :]
            parts = [jnp.where(keep, mul(k_ref[g, start:stop, :], query, NT), MASKED)]
            if i:
                parts.append(mul(k_ref[g, :start, :], query, NT))
            peak = jnp.max(parts[0], axis=0, keepdims=True)
            for part in parts[1:]:
                peak = jnp.maximum(peak, jnp.max(part, axis=0, keepdims=True))
            weights = [jnp.exp(part - peak) for part in parts]
            total = sum(jnp.sum(w, axis=0, keepdims=True) for w in weights)
            shrink = 1.0 / total
            mixed = mul(vt_ref[g, :, start:stop], (weights[0] * shrink).astype(BF))
            if i:
                mixed += mul(vt_ref[g, :, :start], (weights[1] * shrink).astype(BF))
            out_ref[h, :, start:stop] = mixed
            log_ref[h, :, start:stop] = peak + jnp.log(total)

    for i in range(tokens // BLOCK):
        start, stop = i * BLOCK, (i + 1) * BLOCK
        for h in range(0, heads, per):
            pair = jnp.concatenate([out_ref[h + u, :, start:stop] for u in range(per)], axis=0)
            mixed_ref[start:stop, h * HD : h * HD + 128] = pair.T.astype(BF)


def attend(x, gain, weight, tables, heads, groups):
    tokens, width = x.shape
    return pl.pallas_call(
        attend_kernel,
        out_shape=[
            jax.ShapeDtypeStruct((tokens, heads * HD), BF),
            jax.ShapeDtypeStruct((tokens, width), BF),
            jax.ShapeDtypeStruct((heads, tokens, HD), BF),
            jax.ShapeDtypeStruct((groups, tokens, HD), BF),
            jax.ShapeDtypeStruct((groups, tokens, HD), BF),
            jax.ShapeDtypeStruct((heads, 1, tokens), F32),
        ],
        scratch_shapes=[pltpu.VMEM((groups, HD, tokens), BF), pltpu.VMEM((heads, HD, tokens), F32)],
        compiler_params=pltpu.CompilerParams(vmem_limit_bytes=48 << 20),
        cost_estimate=takes(20),
    )(x, gain[None], weight, *tables)


def attend_back_kernel(grad_ref, q_ref, k_ref, v_ref, log_ref, cos_ref, sin_a_ref, sin_b_ref, out_ref, do_ref, kt_ref, dq_ref, dk_ref, dv_ref):
    tokens = grad_ref.shape[0]
    heads, groups = q_ref.shape[0], k_ref.shape[0]
    repeat = heads // groups
    per = 128 // HD
    scale = HD ** (-0.5)
    dk_ref[...] = jnp.zeros_like(dk_ref)
    dv_ref[...] = jnp.zeros_like(dv_ref)

    @pl.loop(0, tokens // BLOCK)
    def _(i):
        rows = pl.ds(pl.multiple_of(i * BLOCK, BLOCK), BLOCK)
        for h in range(heads):
            do_ref[h, rows, :] = grad_ref[rows, h * HD : (h + 1) * HD]
        for g in range(groups):
            kt_ref[g, :, rows] = k_ref[g, rows, :].astype(F32).T.astype(BF)

    keep = causal(BLOCK)

    @pl.loop(0, heads)
    def _(h):
        g = h // repeat
        for i in range(tokens // BLOCK):
            start, stop = i * BLOCK, (i + 1) * BLOCK
            query = q_ref[h, start:stop, :]
            grads = do_ref[h, start:stop, :]
            log_total = log_ref[h, :, start:stop]
            spans = [(start, stop)] + ([(0, start)] if i else [])
            probs, grad_probs = [], []
            for lo, hi in spans:
                scores = mul(k_ref[g, lo:hi, :], query, NT)
                if hi == stop:
                    scores = jnp.where(keep, scores, MASKED)
                probs.append(jnp.exp(scores - log_total))
                grad_probs.append(mul(v_ref[g, lo:hi, :], grads, NT))
            inner = sum(jnp.sum(p * d, axis=0, keepdims=True) for p, d in zip(probs, grad_probs))
            dq = None
            for (lo, hi), p, d in zip(spans, probs, grad_probs):
                ds = (p * (d - inner)).astype(BF)
                dk_ref[g, lo:hi, :] += mul(ds, query)
                dv_ref[g, lo:hi, :] += mul(p.astype(BF), grads)
                term = mul(kt_ref[g, :, lo:hi], ds)
                dq = term if dq is None else dq + term
            dq_ref[h, :, start:stop] = dq * scale

    @pl.loop(0, tokens // BLOCK)
    def _(i):
        rows = pl.ds(pl.multiple_of(i * BLOCK, BLOCK), BLOCK)
        tables = (cos_ref[rows, :], -sin_a_ref[rows, :], -sin_b_ref[rows, :])
        for h in range(0, heads, per):
            pair = jnp.concatenate([dq_ref[h + u, :, rows] for u in range(per)], axis=0).T
            out_ref[rows, h * HD : h * HD + 128] = rotate_lanes(pair, *tables).astype(BF)
        for g in range(0, groups, per):
            pair = jnp.concatenate([dk_ref[g + u, rows, :] for u in range(per)], axis=1)
            lane = (heads + g) * HD
            out_ref[rows, lane : lane + 128] = rotate_lanes(pair, *tables).astype(BF)
            pair = jnp.concatenate([dv_ref[g + u, rows, :] for u in range(per)], axis=1)
            lane = (heads + groups + g) * HD
            out_ref[rows, lane : lane + 128] = pair.astype(BF)


def attend_back(grad_mixed, q, k, v, logs, tables):
    heads, tokens, _ = q.shape
    groups = k.shape[0]
    return pl.pallas_call(
        attend_back_kernel,
        out_shape=jax.ShapeDtypeStruct((tokens, (heads + 2 * groups) * HD), BF),
        scratch_shapes=[
            pltpu.VMEM((heads, tokens, HD), BF),
            pltpu.VMEM((groups, HD, tokens), BF),
            pltpu.VMEM((heads, HD, tokens), F32),
            pltpu.VMEM((groups, tokens, HD), F32),
            pltpu.VMEM((groups, tokens, HD), F32),
        ],
        compiler_params=pltpu.CompilerParams(vmem_limit_bytes=48 << 20),
        cost_estimate=takes(20),
    )(grad_mixed, q, k, v, logs, *tables)


def place_rule(at, s, count, right, left, use):
    if s == 0:
        use(right[0])
        return

    @pl.when(at >= s)
    def _():
        use(right[s])

    @pl.when(at < s)
    def _():
        use(left[count - s])


def expert_kernel(order_ref, *refs, top, count):
    rows_refs, extra_refs, router_ref = refs[:2], refs[2:4], refs[4]
    own_ref = refs[5]
    right = [own_ref] + list(refs[6 : 5 + count])
    left = [own_ref] + list(refs[5 + count : 4 + 2 * count])
    outs = refs[4 + 2 * count :]
    out_refs, gin_refs, term_refs = outs[:2], outs[2:4], outs[4 : 4 + count]
    gu_ref, down_ref, agu, adown = outs[4 + count :]
    step = pl.program_id(0)
    steps = pl.num_programs(0)
    hidden_width, width = down_ref.shape
    part = hidden_width // count
    own = order_ref[2 * steps]
    experts = order_ref[2 * steps + 1]
    at = order_ref[2 * steps + 2]

    def spans(s):
        return (
            (gu_ref, agu, pl.ds(s * part, part)),
            (gu_ref, agu, pl.ds(hidden_width + s * part, part)),
            (down_ref, adown, pl.ds(s * part, part)),
        )

    @pl.when(step == 0)
    def _():
        agu[...] = jnp.zeros_like(agu)
        adown[...] = jnp.zeros_like(adown)
        for s in range(count):

            def keep(source, s=s):
                for j, (to_ref, _, span) in enumerate(spans(s)):
                    to_ref[span, :] = source[pl.ds(j * part, part), :]

            place_rule(at, s, count, right, left, keep)

    near = step < steps // 2
    rows = jnp.where(near, rows_refs[0][...], rows_refs[1][...])
    extra = jnp.concatenate([ref[...] for ref in extra_refs], axis=0)
    grads32 = extra[:, :width].astype(F32)
    named = extra[:, width:].astype(F32)

    lane = lax.broadcasted_iota(jnp.int32, (rows.shape[0], LANES), 1)
    lane32 = lane.astype(F32)
    chosen = lane32 == named[:, 0:1]
    for k in range(1, top):
        chosen = chosen | (lane32 == named[:, k : k + 1])
    logits = jnp.where(chosen, mul(rows, router_ref[...]), MASKED)
    weights = jnp.where(chosen, jnp.exp(logits - jnp.max(logits, axis=-1, keepdims=True)), 0.0)
    mine = jnp.sum(jnp.where(lane == own, weights, 0.0), axis=-1, keepdims=True)
    gate = mine / jnp.sum(weights, axis=-1, keepdims=True)

    both = mul(rows, gu_ref[...], NT)
    gate_vals = both[:, :hidden_width]
    up_vals = both[:, hidden_width:]
    sigma = jax.nn.sigmoid(gate_vals)
    active = gate_vals * sigma
    hidden = (active * up_vals).astype(BF)
    grad_out = (gate * grads32).astype(BF)
    grad_hidden = mul(grad_out, down_ref[...], NT)
    expert_out = mul(hidden, down_ref[...])
    combined = (gate * expert_out).astype(BF)
    score = jnp.sum(grads32 * expert_out, axis=-1, keepdims=True)
    high = score.astype(BF).astype(F32)
    scores = jnp.where(lane == own, high, jnp.where(lane == own + experts, score - high, 0.0)).astype(BF)
    grad_gate_vals = (grad_hidden * up_vals * sigma * (1.0 + gate_vals * (1.0 - sigma))).astype(BF)
    grad_up_vals = (grad_hidden * active).astype(BF)
    grad_both = jnp.concatenate([grad_gate_vals, grad_up_vals], axis=1)
    grad_in = mul(grad_both, gu_ref[...]).astype(BF)
    agu[...] += mul(grad_both, rows, TN)
    adown[...] += mul(hidden, grad_out, TN)
    for far in range(2):

        @pl.when(near if far == 0 else step >= steps // 2)
        def _():
            out_refs[far][...] = combined
            gin_refs[far][:, :width] = grad_in
            gin_refs[far][:, width:] = scores

    @pl.when(step == steps - 1)
    def _():
        for s in range(count):
            for j, (_, sums, span) in enumerate(spans(s)):
                term_refs[s][pl.ds(j * part, part), :] = sums[span, :].astype(BF)


def run_experts(order, near, far, extra, router, right, left, top):
    total, width = 2 * near.shape[0], near.shape[1]
    steps = total // BLOCK
    half_steps = steps // 2
    wide = extra.shape[1]
    count = len(right)
    part = right[0].shape[0] // 3
    hidden = count * part
    term = pl.BlockSpec((3 * part, width), lambda i, o: (0, 0))

    def by_set(lanes):
        return [
            pl.BlockSpec((BLOCK, lanes), lambda i, o: (jnp.minimum(i, half_steps - 1), 0)),
            pl.BlockSpec((BLOCK, lanes), lambda i, o: (jnp.maximum(i - half_steps, 0), 0)),
        ]

    half, half_wide = by_set(width), by_set(wide)
    weights = right + left[1:]
    return pl.pallas_call(
        functools.partial(expert_kernel, top=top, count=count),
        grid_spec=pltpu.PrefetchScalarGridSpec(
            num_scalar_prefetch=1,
            grid=(steps,),
            in_specs=[
                *by_set(width),
                pl.BlockSpec((BLOCK // 2, wide), lambda i, o: (o[2 * i], 0)),
                pl.BlockSpec((BLOCK // 2, wide), lambda i, o: (o[2 * i + 1], 0)),
                pl.BlockSpec((width, LANES), lambda i, o: (0, 0)),
            ]
            + [term] * len(weights),
            out_specs=half + half_wide + [term] * count,
            scratch_shapes=[
                pltpu.VMEM((2 * hidden, width), BF),
                pltpu.VMEM((hidden, width), BF),
                pltpu.VMEM((2 * hidden, width), F32),
                pltpu.VMEM((hidden, width), F32),
            ],
        ),
        out_shape=[jax.ShapeDtypeStruct((total // 2, width), BF)] * 2
        + [jax.ShapeDtypeStruct((total // 2, wide), BF)] * 2
        + [jax.ShapeDtypeStruct((3 * part, width), BF)] * count,
        compiler_params=pltpu.CompilerParams(vmem_limit_bytes=58 << 20),
        cost_estimate=takes(5 * steps),
    )(order, near, far, extra, extra, router, *weights)


def join(*values):
    return lax.optimization_barrier(values)


def swap(x, bit):
    return lax.ppermute(x, "ep", [(i, i ^ bit) for i in range(lax.axis_size("ep"))])


def turn(x, by):
    n = lax.axis_size("tp")
    return lax.ppermute(x, "tp", [(i, (i + by) % n) for i in range(n)])


def gather_slots(x):
    n = lax.axis_size("ep")
    if n != 8:
        whole = lax.all_gather(x, "ep")
        return [whole[k] for k in range(n)]
    first = [x] + [swap(x, k) for k in (2, 4, 6)]
    second = [swap(v, 1) for v in first]
    return [v for pair in zip(first, second) for v in pair]


def set_halves():
    n = lax.axis_size("ep")
    if n != 8:
        return jnp.arange(2 * n, dtype=jnp.int32)
    near = jnp.array([0, 2, 4, 6, 0, 4, 2, 6], jnp.int32)
    device = jnp.bitwise_xor(lax.axis_index("ep").astype(jnp.int32), jnp.concatenate([near, near + 1]))
    return 2 * device + jnp.array([0, 0, 0, 0, 1, 1, 1, 1] * 2, jnp.int32)


def gather_near(x):
    half = x.shape[0] // 2
    return swap(x[:half], 2), swap(x[half:], 4)


def gather_more(x, got):
    half = x.shape[0] // 2
    first, second = join(
        jnp.concatenate([x[:half], got[0]], axis=0), jnp.concatenate([x[half:], got[1]], axis=0)
    )
    return (first, second), (swap(first, 4), swap(second, 2))


def gather_last(sums, got):
    return jnp.concatenate([sums[0], got[0], sums[1], got[1]], axis=0)


def gather_whole(x):
    whole = lax.all_gather(x, "ep", tiled=True)
    return whole[: whole.shape[0] // 2], whole[whole.shape[0] // 2 :]


def add(a, b):
    return (a.astype(F32) + b.astype(F32)).astype(BF)


def sum_cores(near, far, other):
    rows = near.shape[0] // 4
    return join(*[add(near[j * rows : (j + 1) * rows], other[j * rows : (j + 1) * rows]) for j in range(4)])


def halves_home(sums):
    half = sums[0].shape[0] // 2
    return swap(sums[0][half:], 2), swap(sums[1][half:], 4)


def whole_home(sums, got):
    half = sums[0].shape[0] // 2
    return jnp.concatenate([s[:half].astype(F32) + g.astype(F32) for s, g in zip(sums, got)], axis=0)


def scatter_whole(near, far):
    n = lax.axis_size("ep")
    terms = jnp.concatenate([near, far], axis=0).reshape(n, -1, near.shape[1])
    return lax.psum_scatter(terms, "ep", scatter_dimension=0, tiled=False)


def slot_devices():
    n = lax.axis_size("ep")
    order = jnp.arange(n, dtype=jnp.int32)
    return jnp.bitwise_xor(order, lax.axis_index("ep")) if n == 8 else order


def in_device_order(blocks, shape, put):
    order = slot_devices()
    out = jnp.zeros(shape, blocks[0].dtype)
    for k, block in enumerate(blocks):
        out = put(out, block, order[k])
    return out


def step_both(right, left, low=0, high=None):
    n = lax.axis_size("tp")
    pairs = [(i, i + 1) for i in range(low, n - 1 if high is None else high)]
    return (
        lax.ppermute(right, "tp", pairs),
        lax.ppermute(left, "tp", [(n - 1 - i, n - 1 - j) for i, j in pairs]),
    )


def body(
    inputs,
    routes,
    norm_gain,
    query_weight,
    key_weight,
    value_weight,
    output_weight,
    mixer_gain,
    router_weight,
    gate_weight,
    up_weight,
    down_weight,
    cotangent,
):
    tokens, width = inputs.shape
    experts = router_weight.shape[1]
    top = routes.shape[1]
    n_ep = lax.axis_size("ep")
    n_tp = lax.axis_size("tp")
    ep_at = lax.axis_index("ep").astype(jnp.int32)
    tp_at = lax.axis_index("tp").astype(jnp.int32)
    quarter = tokens // n_tp
    heads_width = query_weight.shape[1]
    groups_width = key_weight.shape[1]

    def mine(x):
        return lax.dynamic_slice_in_dim(x, tp_at * quarter, quarter, 0)

    part = output_weight.shape[0] // n_ep
    output_part = lax.dynamic_slice_in_dim(output_weight, ep_at * part, part, 0)
    output_parts = [output_part] + [turn(output_part, -s) for s in range(1, n_tp)]

    routes_mine = mine(routes)
    grad_top_mine = mine(cotangent)
    named = jnp.pad(routes_mine.astype(BF), ((0, 0), (0, LANES - top)), constant_values=-1.0)
    extra = jnp.concatenate([grad_top_mine, named], axis=1)
    extra_all = lax.all_gather(extra, "ep", tiled=True)

    expert_part = jnp.concatenate([gate_weight[0].T, up_weight[0].T, down_weight[0]], axis=0)
    qkv_weight = jnp.concatenate([query_weight, key_weight, value_weight], axis=1)
    tables = rotary_lanes(tokens)
    expert_part, output_parts, qkv_weight, tables = join(expert_part, output_parts, qkv_weight, tables)
    output_part = jnp.concatenate(output_parts, axis=0)
    step = step_both(expert_part, expert_part)
    if n_ep == 8:
        got = gather_near(output_part)
    mixed, normed, query, key, value, logs = attend(
        inputs, norm_gain, qkv_weight, tables, heads_width // HD, groups_width // HD
    )
    if n_ep == 8:
        mixed, got, step = join(mixed, got, step)
    else:
        mixed, step = join(mixed, step)
    steps = [step]

    mixed_mine = lax.all_to_all(mixed, "tp", split_axis=0, concat_axis=1, tiled=True)
    if n_ep == 8:
        held, got = gather_more(output_part, got)
        mixed_mine, held, got, extra_all = join(mixed_mine, held, got, extra_all)
        near = gather_last(held, got)
        far = swap(near, 1)
    else:
        near, far = gather_whole(output_part)
    steps[0], mixed_mine = join(steps[0], mixed_mine)
    steps.append(step_both(*steps[0], 1))
    halves = set_halves()
    output_whole = jnp.zeros((n_tp, n_ep, part, width), BF)
    for blocks, first in ((near, 0), (far, n_ep)):
        blocks = blocks.reshape(n_ep, n_tp // 2, part, width)
        for k in range(n_ep):
            device, half = lax.div(halves[first + k], 2), lax.rem(halves[first + k], 2)
            for u in range(n_tp // 2):
                place = lax.rem(tp_at + half * (n_tp // 2) + u, n_tp)
                output_whole = lax.dynamic_update_slice(
                    output_whole, blocks[k, u][None, None], (place, device, 0, 0)
                )
    output_whole = output_whole.reshape(n_tp * heads_width, width)

    branch = mul(mixed_mine, output_whole)
    inputs_mine = mine(inputs).astype(F32)
    attended = inputs_mine + branch
    inverse_two = lax.rsqrt(jnp.mean(attended * attended, axis=-1, keepdims=True) + EPS)
    unit_two = attended * inverse_two
    routed_in = (unit_two * mixer_gain).astype(BF)
    logits = mul(routed_in, router_weight)
    ids = jnp.arange(experts, dtype=jnp.int32)
    chosen = jnp.any(routes_mine[:, :, None] == ids[None, None, :], axis=1)
    logits = jnp.where(chosen, logits, MASKED)
    weights = jnp.where(chosen, jnp.exp(logits - jnp.max(logits, axis=-1, keepdims=True)), 0.0)
    gates = weights / jnp.sum(weights, axis=-1, keepdims=True)

    if n_ep == 8:
        got = gather_near(routed_in)
        got, steps[-1], gates = join(got, steps[-1], gates)
        for t in range(2, n_tp - 1):
            steps.append(step_both(*steps[-1], t))
        held, got = gather_more(routed_in, got)
        held, got = join(held, got)
        near = gather_last(held, got)
        far = swap(near, 1)
    else:
        near, far = gather_whole(routed_in)
        for t in range(2, n_tp - 1):
            steps.append(step_both(*steps[-1], t))
    near, far, steps[-1] = join(near, far, steps[-1])
    right = [expert_part] + [v[0] for v in steps]
    left = [expert_part] + [v[1] for v in steps]
    router = jnp.pad(router_weight, ((0, 0), (0, LANES - experts)))
    order = jnp.concatenate(
        [halves, ep_at[None], jnp.full((1,), experts, jnp.int32), tp_at[None]]
    )
    out_near, out_far, gin_near, gin_far, *terms = run_experts(
        order, near, far, extra_all, router, right, left, top
    )
    if n_ep == 8:
        gin = sum_cores(gin_near, gin_far, swap(gin_far, 1))
        gin, terms, out_far = join(gin, terms, out_far)
        go = step_both(terms[1], terms[n_tp - 1], 0, 1)
        got = (swap(gin[1], 4), swap(gin[3], 2))
        out = swap(out_far, 1)
        got, out = join(got, out)
        gin = add(gin[0], got[0]), add(gin[2], got[1])
        out = sum_cores(out_near, out_far, out)
        gin, out = join(gin, out)
        got = halves_home(gin)
        out_got = (swap(out[1], 4), swap(out[3], 2))
        got, go = join(got, go)
        grad_in = whole_home(gin, got)
    else:
        go = step_both(terms[1], terms[n_tp - 1], 0, 1)
        grad_in = scatter_whole(gin_near, gin_far).astype(F32)
    grad_gates = grad_in[:, width : width + experts] + grad_in[:, width + experts : width + 2 * experts]
    inner_gate = jnp.sum(gates * grad_gates, axis=-1, keepdims=True)
    grad_logits = (gates * (grad_gates - inner_gate)).astype(BF)
    grad_routed = grad_in[:, :width] + mul(grad_logits, router_weight, NT)
    grad_top = grad_top_mine.astype(F32)
    scaled_two = grad_routed * mixer_gain
    grad_attended = grad_top + inverse_two * (
        scaled_two - unit_two * jnp.mean(scaled_two * unit_two, axis=-1, keepdims=True)
    )
    grad_branch = grad_attended.astype(BF)
    grad_mixed = mul(grad_branch, output_whole, NT).astype(BF)
    for t in range(2, n_tp - 1):
        go = step_both(add(terms[t], go[0]), add(terms[n_tp - t], go[1]), 0, t)

    if n_ep == 8:
        grad_mixed, out_got = join(grad_mixed, out_got)
    grad_mixed = lax.all_to_all(grad_mixed, "tp", split_axis=1, concat_axis=0, tiled=True)
    if n_ep == 8:
        out = join(add(out[0], out_got[0]), add(out[2], out_got[1]))
        out_got = halves_home(out)
    grad_router = mul(routed_in, grad_logits, TN)
    grad_mixer = jnp.sum(grad_routed * unit_two, axis=0)
    few = -(-(1 + experts) // n_ep)
    pad = 16 * (few // 16 + 1)
    small = jnp.concatenate([grad_mixer[None], grad_router.T], axis=0).astype(BF)
    small = jnp.pad(small, ((0, few * n_ep - 1 - experts), (0, 0))).reshape(n_ep, few, width)
    small = jnp.pad(small, ((0, 0), (0, pad - few), (0, 0)))
    grad_output = mul(mixed_mine, grad_branch, TN).astype(BF)
    grad_output = grad_output.reshape(n_tp, n_ep, part, width).transpose(1, 0, 2, 3)
    grad_output = jnp.concatenate([grad_output.reshape(n_ep, n_tp * part, width), small], axis=1)
    if n_ep == 8:
        core, chip = lax.rem(ep_at, 2), lax.div(ep_at, 2)
        grad_output = grad_output.reshape((n_ep // 2, 2) + grad_output.shape[1:])
        other_output = lax.dynamic_index_in_dim(grad_output, 1 - core, 1, False)
        grad_output = lax.dynamic_index_in_dim(grad_output, core, 1, False)
        grad_mixed, out_got, go, other_output, grad_output = join(
            grad_mixed, out_got, go, other_output, grad_output
        )
        out = whole_home(out, out_got)
        other_output = swap(other_output, 1)
    else:
        out = scatter_whole(out_near, out_far).astype(F32)
    result_mine = (attended + out).astype(BF)

    result_mine, grad_mixed = join(result_mine, grad_mixed)
    result_steps = [step_both(result_mine, result_mine)]
    grad_qkv = attend_back(grad_mixed, query, key, value, logs, tables)
    if n_ep == 8:
        grad_qkv, result_steps[0], other_output = join(grad_qkv, result_steps[0], other_output)
    else:
        grad_qkv, result_steps[0] = join(grad_qkv, result_steps[0])

    grad_normed = mul(grad_qkv, qkv_weight, NT).astype(BF).reshape(n_tp, quarter, width)
    grad_qkv_w = mul(normed, grad_qkv, TN).astype(BF)

    def block(j):
        return lax.dynamic_index_in_dim(grad_normed, lax.rem(tp_at + j + n_tp, n_tp), 0, False)

    sent = None
    for t in range(1, n_tp):
        give = [block(n_tp - t), block(t - n_tp)]
        if sent is not None:
            give = [add(give[0], sent[0]), add(give[1], sent[1])]
        sent = step_both(*give, 0, t)
        if t < n_tp - 1:
            result_steps.append(step_both(*result_steps[-1], t))
            if t == 1:
                sent, result_steps[-1], grad_qkv_w = join(sent, result_steps[-1], grad_qkv_w)
                grad_qkv_w = lax.psum(grad_qkv_w, "ep")
                if n_ep == 8:
                    grad_output = add(grad_output, other_output)
            else:
                last = add(terms[n_tp - 1], go[0]), add(terms[1], go[1])
                sent, result_steps[-1], grad_output, last = join(sent, result_steps[-1], grad_output, last)
    if n_ep == 8:

        def chip_block(j):
            return lax.dynamic_index_in_dim(grad_output, jnp.bitwise_xor(chip, j), 0, False)

        got = [swap(chip_block(j), 2 * j) for j in (1, 2, 3)]
        grad_output = chip_block(0)
    else:
        got = []
        grad_output = lax.psum_scatter(grad_output, "ep", scatter_dimension=0, tiled=False)
    sent, last = join(sent, last)
    go = step_both(*last, 0, n_tp - 1)
    grad_normed = block(0).astype(F32) + sent[0].astype(F32) + sent[1].astype(F32)
    inverse_one = lax.rsqrt(jnp.mean(inputs_mine * inputs_mine, axis=-1, keepdims=True) + EPS)
    unit_one = inputs_mine * inverse_one
    scaled_one = grad_normed * norm_gain
    grad_inputs = grad_attended + inverse_one * (
        scaled_one - unit_one * jnp.mean(scaled_one * unit_one, axis=-1, keepdims=True)
    )
    grad_inputs = grad_inputs.astype(BF)
    grad_norm = jnp.sum(grad_normed * unit_one, axis=0)

    input_steps = [step_both(grad_inputs, grad_inputs)]
    got, input_steps[0] = join(got, input_steps[0])
    grad_output = sum([grad_output.astype(F32)] + [v.astype(F32) for v in got])
    grad_output = grad_output.at[-1].set(grad_norm).astype(BF)
    pieces = [
        jnp.concatenate([grad_output[j * part : (j + 1) * part], grad_output[n_tp * part :]], axis=0)
        for j in range(n_tp)
    ]
    pieces = jnp.stack(pieces)

    def piece(j):
        return lax.dynamic_index_in_dim(pieces, lax.rem(tp_at + j, n_tp), 0, False)

    got = [turn(piece(s), s) for s in range(1, n_tp)]
    input_steps.append(step_both(*input_steps[-1], 1))
    got, input_steps[-1] = join(got, input_steps[-1])
    grad_output = (piece(0).astype(F32) + sum(v.astype(F32) for v in got)).astype(BF)
    got = gather_slots(grad_output)
    for t in range(2, n_tp - 1):
        input_steps.append(step_both(*input_steps[-1], t))
    input_steps[-1], grad_qkv_w = join(input_steps[-1], grad_qkv_w)
    grad_output = in_device_order(
        got,
        (n_ep, part + pad, width),
        lambda out, block, at: lax.dynamic_update_index_in_dim(out, block, at, 0),
    )
    small = grad_output[:, part : part + few].reshape(n_ep * few, width)[: 1 + experts].astype(F32)
    grad_norm = jnp.sum(grad_output[:, -1].astype(F32), axis=0)
    grad_output = grad_output[:, :part].reshape(heads_width, width).astype(F32)
    grad_qkv_w = grad_qkv_w.astype(F32)
    grad_expert = terms[0].astype(F32) + go[0].astype(F32) + go[1].astype(F32)
    hidden_part = gate_weight.shape[2]
    grad_gate_w = grad_expert[:hidden_part].T
    grad_up_w = grad_expert[hidden_part : 2 * hidden_part].T
    grad_down_w = grad_expert[2 * hidden_part :]

    def spread(own, steps):
        out = jnp.zeros((tokens, width), BF)
        for t, step in enumerate(steps):
            for got, place in zip(step, (tp_at - t - 1, tp_at + t + 1)):
                place = jnp.where((place >= 0) & (place < n_tp), place, tp_at)
                out = lax.dynamic_update_slice(out, got, (place * quarter, 0))
        return lax.dynamic_update_slice(out, own, (tp_at * quarter, 0))

    result = spread(result_mine, result_steps)
    grad_inputs = spread(grad_inputs, input_steps)
    return (
        result,
        grad_inputs,
        grad_norm,
        grad_qkv_w[:, :heads_width],
        grad_qkv_w[:, heads_width : heads_width + groups_width],
        grad_qkv_w[:, heads_width + groups_width :],
        grad_output,
        small[0],
        small[1:].T,
        grad_gate_w[None],
        grad_up_w[None],
        grad_down_w[None],
    )


def solution(mesh):
    placed = (
        P("ep", None),
        P("ep", None),
        P(),
        P(None, "tp"),
        P(None, "tp"),
        P(None, "tp"),
        P("tp", None),
        P(),
        P(),
        P("ep", None, "tp"),
        P("ep", None, "tp"),
        P("ep", "tp", None),
        P("ep", None),
    )
    return jax.shard_map(
        body,
        mesh=mesh,
        in_specs=placed,
        out_specs=(
            P("ep", None),
            P("ep", None),
            P(),
            P(None, "tp"),
            P(None, "tp"),
            P(None, "tp"),
            P("tp", None),
            P(),
            P(),
            P("ep", None, "tp"),
            P("ep", None, "tp"),
            P("ep", "tp", None),
        ),
        check_vma=False,
    )
```

time: 694 us -> 621 us (0.89)
  waiting for transfers between devices: 298 us -> 212 us
  between operations: 30.7 us -> 62.3 us
  starting transfers between devices: 132 us -> 110 us
  matrix products: 22.8 us -> 15.2 us
    all_gather x2 -> x0, waiting for transfers between devices: 55.3 us -> none  [the longest x1 55.3 us: body(): result = lax.all_gather(result_mine, 'tp', tiled=True)]
    ppermute x33 -> x31, waiting for transfers between devices: 95.8 us -> 68.2 us  [swap(): lax.ppermute(x, 'ep', [(i, i ^ bit) for i in range(lax.axis_size('ep'))])]
    ppermute x23 -> x30, starting transfers between devices: 76.4 us -> 55.1 us  [the longest x15 35.2 us: step_both(): lax.ppermute(right, 'tp', pairs)]
    ppermute x15 -> x6, waiting for transfers between devices: 34.9 us -> 14.8 us  [turn(): return lax.ppermute(x, 'tp', [(i, (i + by) % n) for i in range(n)])]
    dynamic_update_slice x7 -> x46, local copies, waits for them, and re-layouts: 0.31 us -> 18.9 us  [the longest x12 17.4 us: spread(): out = lax.dynamic_update_slice(out, got, (place * quarter, 0))]
    all_to_all x0 -> x2, waiting for transfers between devices: none -> 17.8 us  [the longest x1 17.8 us: body(): lax.all_to_all(grad_mixed, 'tp', split_axis=1, concat_axis=0, tiled=True)]
    unnamed x149 -> x160, local copies, waits for them, and re-layouts: 33.3 us -> 19.3 us
    ppermute x15 -> x6, starting transfers between devices: 33.7 us -> 21.5 us  [turn(): return lax.ppermute(x, 'tp', [(i, (i + by) % n) for i in range(n)])]
  transfers between devices with their start and end apart: 75 -> 71, of which waited for: 32 -> 29; matrix products, arithmetic and copies ran while one was open for 18% -> 17% of each run, Pallas kernels for 12% -> 7%
where the time goes in v3:
time: 621 us; the launch traced here: 611 us
  waiting for transfers between devices  212 us (34%)
  starting transfers between devices  110 us (18%)
  Pallas kernels  86.5 us (14%)
  local copies, waits for them, and re-layouts  65.2 us (10%)
  between operations  62.3 us (10%)
  other arithmetic  59.8 us (10%)
  matrix products  15.2 us (2%)
    ppermute x15, waiting for transfers between devices, step_both(): lax.ppermute(left, 'tp', [(n - 1 - i, n - 1 - j) for i, j in pairs])  83.6 us
    ppermute x31, waiting for transfers between devices, swap(): lax.ppermute(x, 'ep', [(i, i ^ bit) for i in range(lax.axis_size('ep'))])  68.2 us
    pallas_call x1, Pallas kernels, run_experts(): pl.pallas_call(functools.partial(expert_kernel, top=top, count=count), gr...  45.5 us
    ppermute x15, starting transfers between devices, step_both(): lax.ppermute(right, 'tp', pairs)  35.2 us
    ppermute x15, waiting for transfers between devices, step_both(): lax.ppermute(right, 'tp', pairs)  27.1 us
    ppermute x31, starting transfers between devices, swap(): lax.ppermute(x, 'ep', [(i, i ^ bit) for i in range(lax.axis_size('ep'))])  26.6 us
    convert_element_type x12, other arithmetic, add(): return (a.astype(F32) + b.astype(F32)).astype(BF)  24.6 us
    ppermute x6, starting transfers between devices, turn(): return lax.ppermute(x, 'tp', [(i, (i + by) % n) for i in range(n)])  21.5 us
  transfers between devices with their start and end apart: 71, of which 29 were waited for; matrix products, arithmetic and copies ran while one was open for 17% of the time, Pallas kernels for 7%

profile of v3, /device:TPU:0, one launch (start us, length us, event | category | flops | bytes accessed | tf_op | source)
XLA Modules:
  0.0 610.9 jit_solution(9576487720284401367)
XLA Ops:
  10.5 5.1 collective-permute-start
  19.0 3.2 pad_maximum_fusion.w_ref
  22.3 5.7 collective-permute-done.1
  28.1 2.8 collective-permute-start.5
  35.5 20.0 %shard_map.238 = (bf16[1024,384]{1,0:T(8,128)(2,1)S(1)}, bf16[1024,1536]{1,0:T(8,128)(2,1)}, bf16[6,1024,64]{2,1,0:T(8,128)(2,1)S(1)}, bf16[2,1024,64]{2,1,0:T(8...) custom-call(bf16[1024,1536]{1,0:T(8,128)(2,1)} %x_ref.1, ...), custom_call_target="tpu_custom_call" | custom-call | flops 23000000512 | tf_op jit(solution)/shard_map/pallas_call | solution.py:114
  56.6 3.8 collective-permute-done.6.refs_9_
  62.6 3.6 all-to-all-start
  66.3 2.4 pad_maximum_fusion.5
  113.3 3.2 multiply_reduce_fusion.2
  119.4 23.7 %collective-permute-done.13.refs_10_ = bf16[384,1536]{1,0:T(8,128)(2,1)} collective-permute-done((bf16[384,1536]{1,0:T(8,128)(2,1)S(1)}, bf16[384,1536]{1,0:T(8,128)(2,1)}, u32[]{:S(2)}, u32[]{:S(2)}) %collective-permute-start.13) | collective-permute-done | bytes 1179680 | tf_op jit(solution)/shard_map/ppermute | solution.py:452
  144.3 18.1 %collective-permute-done.14 = bf16[256,1536]{1,0:T(8,128)(2,1)S(1)} collective-permute-done((bf16[256,1536]{1,0:T(8,128)(2,1)S(1)}, bf16[256,1536]{1,0:T(8,128)(2,1)S(1)}, u32[]{:S(2)}, u32[]{:S(2)}) %collective-permute-start.14) | collective-permute-done | bytes 786464 | tf_op jit(solution)/shard_map/ppermute | solution.py:359
  172.7 26.0 %collective-permute-done.18.refs_11_ = bf16[384,1536]{1,0:T(8,128)(2,1)} collective-permute-done((bf16[384,1536]{1,0:T(8,128)(2,1)}, bf16[384,1536]{1,0:T(8,128)(2,1)}, u32[]{:S(2)}, u32[]{:S(2)}) %collective-permute-start.18) | collective-permute-done | bytes 1179680 | tf_op jit(solution)/shard_map/ppermute | solution.py:452
  198.6 45.5 %shard_map.239 = (bf16[1024,1536]{1,0:T(8,128)(2,1)}, bf16[1024,1536]{1,0:T(8,128)(2,1)}, bf16[1024,1664]{1,0:T(8,128)(2,1)}, bf16[1024,1664]{1,0:T(8,128)(2,1)}...) custom-call(s32[19]{0:T(128)} %pad_add_fusion.order_ref, ...), custom_call_target="tpu_custom_call" | custom-call | flops 46000001024 | tf_op jit(solution)/shard_map/pallas_call | solution.py:326
  244.2 6.2 %collective-permute-done.19 = bf16[1024,1664]{1,0:T(8,128)(2,1)S(1)} collective-permute-done((bf16[1024,1664]{1,0:T(8,128)(2,1)}, bf16[1024,1664]{1,0:T(8,128)(2,1)S(1)}, u32[]{:S(2)}, u32[]{:S(2)}) %collective-permute-start.19) | collective-permute-done | bytes 3407904 | tf_op jit(solution)/shard_map/ppermute | solution.py:359
  250.5 2.9 add_convert_fusion.5
  255.6 2.5 collective-permute-start.25
  258.1 2.2 collective-permute-start.26
  260.3 14.5 %collective-permute-done.20 = bf16[256,1664]{1,0:T(8,128)(2,1)S(1)} collective-permute-done((bf16[256,1664]{1,0:T(8,128)(2,1)S(1)}, bf16[256,1664]{1,0:T(8,128)(2,1)S(1)}, u32[]{:S(2)}, u32[]{:S(2)}) %collective-permute-start.20) | collective-permute-done | bytes 852000 | tf_op jit(solution)/shard_map/ppermute | solution.py:359
  276.0 2.3 add_convert_fusion.11
  306.8 2.6 multiply_add_fusion
  309.5 4.2 fusion.5
  315.0 2.5 copy.56
  317.6 2.5 collective-permute-start.31
  324.9 3.5 all-to-all-start.1
  333.2 4.3 fusion.1
  337.5 3.4 collective-permute-done.29
  341.7 4.1 collective-permute-done.31
  345.7 17.8 %all-to-all-done.1 = bf16[256,4,384]{2,0,1:T(8,128)(2,1)S(1)} async-done(((bf16[256,4,384]{2,0,1:T(8,128)(2,1)}), bf16[256,4,384]{2,0,1:T(8,128)(2,1)S(1)}, u32[]{:S(2)}, u32[]{:S(2)}) %all-to-all-start.1) | async-done | bytes 786464 | tf_op jit(solution)/shard_map/all_to_all | solution.py:604
  366.4 2.2 collective-permute-start.33
  370.1 21.1 %shard_map.240 = bf16[1024,640]{1,0:T(8,128)(2,1)S(1)} custom-call(bf16[1024,384]{1,0:T(8,128)(2,1)S(1)} %bitcast.154, bf16[6,1024,64]{2,1,0:T(8,128)(2,1)} %copy-done.2, bf16[2,1024,64]{2,1,0:T(8,128)(2,1)S(1)} %get-tuple-element.243.k_ref, bf16[2,1024,64]{2,1,0:T(8,128)(2,1)S(1)} %get-tuple-element.244.v_ref, ...), custom_call_target="tpu_custom_call" | custom-call | flops 23000000512 | tf_op jit(solution)/shard_map/pallas_call | solution.py:194
  391.2 2.9 convolution_convert_fusion.1
  397.0 4.8 collective-permute-start.36
  404.6 2.9 add_convert_fusion.1
  407.5 3.9 convolution_convert_fusion.2
  411.4 7.9 %collective-permute-done.36 = bf16[256,1536]{1,0:T(8,128)(2,1)S(1)} collective-permute-done((bf16[256,1536]{1,0:T(8,128)(2,1)}, bf16[256,1536]{1,0:T(8,128)(2,1)S(1)}, u32[]{:S(2)}, u32[]{:S(2)}) %collective-permute-start.36) | collective-permute-done | bytes 786464 | tf_op jit(solution)/shard_map/ppermute | solution.py:451
  419.3 5.5 collective-permute-done.39
  427.6 2.3 collective-permute-start.40
  432.7 3.0 add_convert_fusion.2
  435.7 2.2 add_convert_fusion
  437.9 7.7 %collective-permute-done.40 = bf16[256,1536]{1,0:T(8,128)(2,1)S(1)} collective-permute-done((bf16[256,1536]{1,0:T(8,128)(2,1)S(1)}, bf16[256,1536]{1,0:T(8,128)(2,1)S(1)}, u32[]{:S(2)}, u32[]{:S(2)}) %collective-permute-start.40) | collective-permute-done | bytes 786464 | tf_op jit(solution)/shard_map/ppermute | solution.py:451
  445.6 5.8 collective-permute-done.43
  457.8 2.1 constant_dynamic-update-slice_fusion.13
  459.9 2.1 constant_dynamic-update-slice_fusion.12
  463.0 2.3 constant_dynamic-update-slice_fusion.10
  465.3 4.1 collective-permute-done.47
  469.4 4.1 collective-permute-done.48
  473.4 2.2 fusion.16
  475.7 2.3 fusion.15
  478.0 3.8 collective-permute-start.49
  484.5 2.3 collective-permute-start.46
  489.6 14.3 %collective-permute-done.44 = bf16[208,1536]{1,0:T(8,128)(2,1)S(1)} collective-permute-done((bf16[208,1536]{1,0:T(8,128)(2,1)S(1)}, bf16[208,1536]{1,0:T(8,128)(2,1)S(1)}, u32[]{:S(2)}, u32[]{:S(2)}) %collective-permute-start.44) | collective-permute-done | bytes 639008 | tf_op jit(solution)/shard_map/ppermute | solution.py:359
  503.9 5.6 collective-permute-start.65
  510.8 4.6 collective-permute-done.46
  516.9 2.4 collective-permute-start.51
  524.9 3.4 collective-permute-done.65
  528.3 13.0 %collective-permute-start.52 = (bf16[64,1536]{1,0:T(8,128)(2,1)}, bf16[64,1536]{1,0:T(8,128)(2,1)}, u32[]{:S(2)}, u32[]{:S(2)}) collective-permute-start(bf16[64,1536]{1,0:T(8,128)(2,1)} %get-tuple-element.357), channel_id=1, source_target_pairs={{0,2},{1,3},{2,0},{3,1},{4,6},{5,7},{6,4},{7,5},{8,10},{9,11},{10,... | collective-permute-start | bytes 589832 | tf_op jit(solution)/shard_map/ppermute | solution.py:364
  541.3 3.5 collective-permute-done.66
  548.2 2.3 copy.57
  551.6 9.1 %collective-permute-done.52 = bf16[64,1536]{1,0:T(8,128)(2,1)} collective-permute-done((bf16[64,1536]{1,0:T(8,128)(2,1)}, bf16[64,1536]{1,0:T(8,128)(2,1)}, u32[]{:S(2)}, u32[]{:S(2)}) %collective-permute-start.52) | collective-permute-done | bytes 196640 | tf_op jit(solution)/shard_map/ppermute | solution.py:364
  562.2 4.9 collective-permute-start.59
  569.3 2.1 constant_dynamic-update-slice_fusion.4
  574.9 3.4 collective-permute-done.61
  583.9 11.2 %collective-permute-done.57 = bf16[256,1536]{1,0:T(8,128)(2,1)S(1)} collective-permute-done((bf16[256,1536]{1,0:T(8,128)(2,1)}, bf16[256,1536]{1,0:T(8,128)(2,1)S(1)}, u32[]{:S(2)}, u32[]{:S(2)}) %collective-permute-start.57) | collective-permute-done | bytes 786464 | tf_op jit(solution)/shard_map/ppermute | solution.py:452
  595.1 3.1 slice.495
  (403 shorter events, 129.9 us)
Async XLA Ops:
  7.2 96.5 %all-gather.2.cloned.1.call-start = ((), (), s32[]{:S(2)}) async-start(), calls=%async_computation.2 | async-start | bytes 7667712 | tf_op jit(solution)/shard_map/all_gather | solution.py:493
  10.5 11.8 %collective-permute-start = (bf16[48,1536]{1,0:T(8,128)(2,1)S(1)}, bf16[48,1536]{1,0:T(8,128)(2,1)S(1)}, u32[]{:S(2)}, u32[]{:S(2)}) collective-permute-start(bf16[48,1536]{1,0:T(8,128)(2,1)S(1)} %constant_dynamic-slice_fusion.2), channel_id=1, source_target_pairs={{0,3},{1,0},{2,1},{3,2},{4,7},{5,4},{6,5},{7,6},{8,11},{9,8},{10,9... | collective-permute-start | bytes 442376 | tf_op jit(solution)/shard_map/ppermute | solution.py:364
  15.6 12.5 %collective-permute-start.1 = (bf16[48,1536]{1,0:T(8,128)(2,1)S(1)}, bf16[48,1536]{1,0:T(8,128)(2,1)S(1)}, u32[]{:S(2)}, u32[]{:S(2)}) collective-permute-start(bf16[48,1536]{1,0:T(8,128)(2,1)S(1)} %constant_dynamic-slice_fusion.2), channel_id=1, source_target_pairs={{0,2},{1,3},{2,0},{3,1},{4,6},{5,7},{6,4},{7,5},{8,10},{9,11},{10,... | collective-permute-start | bytes 442376 | tf_op jit(solution)/shard_map/ppermute | solution.py:364
  15.6 12.5 %collective-permute-start.2 = (bf16[48,1536]{1,0:T(8,128)(2,1)S(1)}, bf16[48,1536]{1,0:T(8,128)(2,1)S(1)}, u32[]{:S(2)}, u32[]{:S(2)}) collective-permute-start(bf16[48,1536]{1,0:T(8,128)(2,1)S(1)} %constant_dynamic-slice_fusion.2), channel_id=1, source_target_pairs={{0,1},{1,2},{2,3},{3,0},{4,5},{5,6},{6,7},{7,4},{8,9},{9,10},{10,1... | collective-permute-start | bytes 442376 | tf_op jit(solution)/shard_map/ppermute | solution.py:364
  28.1 28.5 %collective-permute-start.5 = (bf16[384,1536]{1,0:T(8,128)(2,1)S(1)}, bf16[384,1536]{1,0:T(8,128)(2,1)S(1)}, u32[]{:S(2)}, u32[]{:S(2)}) collective-permute-start(bf16[384,1536]{1,0:T(8,128)(2,1)S(1)} %pad_maximum_fusion.1.refs_5_), channel_id=1, source_target_pairs={{0,1},{1,2},{2,3},{4,5},{5,6},{6,7},{8,9},{9,10},{10,11},{12,13},{... | collective-permute-start | bytes 3538952 | tf_op jit(solution)/shard_map/ppermute | solution.py:451
  30.9 29.5 %collective-permute-start.6 = (bf16[384,1536]{1,0:T(8,128)(2,1)S(1)}, bf16[384,1536]{1,0:T(8,128)(2,1)S(1)}, u32[]{:S(2)}, u32[]{:S(2)}) collective-permute-start(bf16[384,1536]{1,0:T(8,128)(2,1)S(1)} %pad_maximum_fusion.1.refs_5_), channel_id=1, source_target_pairs={{3,2},{2,1},{1,0},{7,6},{6,5},{5,4},{11,10},{10,9},{9,8},{15,14},{... | collective-permute-start | bytes 3538952 | tf_op jit(solution)/shard_map/ppermute | solution.py:452
  32.3 24.3 %collective-permute-start.4 = (bf16[96,1536]{1,0:T(8,128)(2,1)S(1)}, bf16[96,1536]{1,0:T(8,128)(2,1)S(1)}, u32[]{:S(2)}, u32[]{:S(2)}) collective-permute-start(bf16[96,1536]{1,0:T(8,128)(2,1)S(1)} %pad_maximum_fusion.11), channel_id=1, source_target_pairs={{0,16},{4,20},{8,24},{12,28},{16,0},{20,4},{24,8},{28,12},{1,17},{... | collective-permute-start | bytes 884744 | tf_op jit(solution)/shard_map/ppermute | solution.py:359
  33.9 22.7 %collective-permute-start.3 = (bf16[96,1536]{1,0:T(8,128)(2,1)S(1)}, bf16[96,1536]{1,0:T(8,128)(2,1)S(1)}, u32[]{:S(2)}, u32[]{:S(2)}) collective-permute-start(bf16[96,1536]{1,0:T(8,128)(2,1)S(1)} %pad_maximum_fusion.10), channel_id=1, source_target_pairs={{0,8},{4,12},{8,0},{12,4},{16,24},{20,28},{24,16},{28,20},{1,9},{5... | collective-permute-start | bytes 884744 | tf_op jit(solution)/shard_map/ppermute | solution.py:359
  62.6 41.0 %all-to-all-start = ((bf16[4,256,384]{1,2,0:T(8,128)(2,1)}), bf16[4,256,384]{1,2,0:T(8,128)(2,1)S(1)}, u32[]{:S(2)}, u32[]{:S(2)}) async-start(bf16[4,256,384]{1,2,0:T(8,128)(2,1)} %copy.48), calls=%async_computation | async-start | bytes 1572864 | tf_op jit(solution)/shard_map/all_to_all | solution.py:512
  68.6 35.0 %collective-permute-start.7 = (bf16[192,1536]{1,0:T(8,128)(2,1)}, bf16[192,1536]{1,0:T(8,128)(2,1)}, u32[]{:S(2)}, u32[]{:S(2)}) collective-permute-start(bf16[192,1536]{1,0:T(8,128)(2,1)} %get-tuple-element.174), channel_id=1, source_target_pairs={{0,16},{4,20},{8,24},{12,28},{16,0},{20,4},{24,8},{28,12},{1,17},{... | collective-permute-start | bytes 1769480 | tf_op jit(solution)/shard_map/ppermute | solution.py:359
  70.1 33.5 %collective-permute-start.8 = (bf16[192,1536]{1,0:T(8,128)(2,1)}, bf16[192,1536]{1,0:T(8,128)(2,1)}, u32[]{:S(2)}, u32[]{:S(2)}) collective-permute-start(bf16[192,1536]{1,0:T(8,128)(2,1)} %get-tuple-element.176), channel_id=1, source_target_pairs={{0,8},{4,12},{8,0},{12,4},{16,24},{20,28},{24,16},{28,20},{1,9},{5... | collective-permute-start | bytes 1769480 | tf_op jit(solution)/shard_map/ppermute | solution.py:359
  108.3 11.1 %collective-permute-start.12 = (bf16[384,1536]{1,0:T(8,128)(2,1)S(1)}, bf16[384,1536]{1,0:T(8,128)(2,1)}, u32[]{:S(2)}, u32[]{:S(2)}) collective-permute-start(bf16[384,1536]{1,0:T(8,128)(2,1)S(1)} %copy-done.68), channel_id=1, source_target_pairs={{1,2},{2,3},{5,6},{6,7},{9,10},{10,11},{13,14},{14,15},{17,18},{18... | collective-permute-start | bytes 3538952 | tf_op jit(solution)/shard_map/ppermute | solution.py:451
  110.1 33.0 %collective-permute-start.13 = (bf16[384,1536]{1,0:T(8,128)(2,1)S(1)}, bf16[384,1536]{1,0:T(8,128)(2,1)}, u32[]{:S(2)}, u32[]{:S(2)}) collective-permute-start(bf16[384,1536]{1,0:T(8,128)(2,1)S(1)} %copy-done.70), channel_id=1, source_target_pairs={{2,1},{1,0},{6,5},{5,4},{10,9},{9,8},{14,13},{13,12},{18,17},{17,1... | collective-permute-start | bytes 3538952 | tf_op jit(solution)/shard_map/ppermute | solution.py:452
  116.9 26.2 %collective-permute-start.10 = (bf16[128,1536]{1,0:T(8,128)(2,1)S(1)}, bf16[128,1536]{1,0:T(8,128)(2,1)S(1)}, u32[]{:S(2)}, u32[]{:S(2)}) collective-permute-start(bf16[128,1536]{1,0:T(8,128)(2,1)S(1)} %get-tuple-element.360), channel_id=1, source_target_pairs={{0,8},{4,12},{8,0},{12,4},{16,24},{20,28},{24,16},{28,20},{1,9},{5... | collective-permute-start | bytes 1179656 | tf_op jit(solution)/shard_map/ppermute | solution.py:359
  117.5 25.6 %collective-permute-start.11 = (bf16[128,1536]{1,0:T(8,128)(2,1)S(1)}, bf16[128,1536]{1,0:T(8,128)(2,1)S(1)}, u32[]{:S(2)}, u32[]{:S(2)}) collective-permute-start(bf16[128,1536]{1,0:T(8,128)(2,1)S(1)} %get-tuple-element.359), channel_id=1, source_target_pairs={{0,16},{4,20},{8,24},{12,28},{16,0},{20,4},{24,8},{28,12},{1,17},{... | collective-permute-start | bytes 1179656 | tf_op jit(solution)/shard_map/ppermute | solution.py:359
  143.2 19.2 %collective-permute-start.14 = (bf16[256,1536]{1,0:T(8,128)(2,1)S(1)}, bf16[256,1536]{1,0:T(8,128)(2,1)S(1)}, u32[]{:S(2)}, u32[]{:S(2)}) collective-permute-start(bf16[256,1536]{1,0:T(8,128)(2,1)S(1)} %pad_maximum_fusion.2), channel_id=1, source_target_pairs={{0,16},{4,20},{8,24},{12,28},{16,0},{20,4},{24,8},{28,12},{1,17},{... | collective-permute-start | bytes 2359304 | tf_op jit(solution)/shard_map/ppermute | solution.py:359
  143.8 18.9 %collective-permute-start.15 = (bf16[256,1536]{1,0:T(8,128)(2,1)S(1)}, bf16[256,1536]{1,0:T(8,128)(2,1)S(1)}, u32[]{:S(2)}, u32[]{:S(2)}) collective-permute-start(bf16[256,1536]{1,0:T(8,128)(2,1)S(1)} %pad_maximum_fusion.3), channel_id=1, source_target_pairs={{0,8},{4,12},{8,0},{12,4},{16,24},{20,28},{24,16},{28,20},{1,9},{5... | collective-permute-start | bytes 2359304 | tf_op jit(solution)/shard_map/ppermute | solution.py:359
  166.4 32.3 %collective-permute-start.16 = (bf16[1024,1536]{1,0:T(8,128)(2,1)}, bf16[1024,1536]{1,0:T(8,128)(2,1)}, u32[]{:S(2)}, u32[]{:S(2)}) collective-permute-start(bf16[1024,1536]{1,0:T(8,128)(2,1)} %constant_dynamic-update-slice_fusion.18.refs_0_), channel_id=1, source_target_pairs={{0,4},{4,0},{8,12},{12,8},{16,20},{20,16},{24,28},{28,24},{1,5},{5... | collective-permute-start | bytes 9437192 | tf_op jit(solution)/shard_map/ppermute | solution.py:359
  168.1 30.6 %collective-permute-start.18 = (bf16[384,1536]{1,0:T(8,128)(2,1)}, bf16[384,1536]{1,0:T(8,128)(2,1)}, u32[]{:S(2)}, u32[]{:S(2)}) collective-permute-start(bf16[384,1536]{1,0:T(8,128)(2,1)} %collective-permute-done.13.refs_10_), channel_id=1, source_target_pairs={{1,0},{5,4},{9,8},{13,12},{17,16},{21,20},{25,24},{29,28}} | collective-permute-start | bytes 3538952 | tf_op jit(solution)/shard_map/ppermute | solution.py:452
  253.4 22.7 %collective-permute-start.22 = (bf16[1024,1536]{1,0:T(8,128)(2,1)S(1)}, bf16[1024,1536]{1,0:T(8,128)(2,1)S(1)}, u32[]{:S(2)}, u32[]{:S(2)}) collective-permute-start(bf16[1024,1536]{1,0:T(8,128)(2,1)S(1)} %copy-done.66), channel_id=1, source_target_pairs={{0,4},{4,0},{8,12},{12,8},{16,20},{20,16},{24,28},{28,24},{1,5},{5... | collective-permute-start | bytes 9437192 | tf_op jit(solution)/shard_map/ppermute | solution.py:359
  253.6 21.2 %collective-permute-start.20 = (bf16[256,1664]{1,0:T(8,128)(2,1)S(1)}, bf16[256,1664]{1,0:T(8,128)(2,1)S(1)}, u32[]{:S(2)}, u32[]{:S(2)}) collective-permute-start(bf16[256,1664]{1,0:T(8,128)(2,1)S(1)} %get-tuple-element.207), channel_id=1, source_target_pairs={{0,16},{4,20},{8,24},{12,28},{16,0},{20,4},{24,8},{28,12},{1,17},{... | collective-permute-start | bytes 2555912 | tf_op jit(solution)/shard_map/ppermute | solution.py:359
  255.1 20.9 %collective-permute-start.21 = (bf16[256,1664]{1,0:T(8,128)(2,1)S(1)}, bf16[256,1664]{1,0:T(8,128)(2,1)S(1)}, u32[]{:S(2)}, u32[]{:S(2)}) collective-permute-start(bf16[256,1664]{1,0:T(8,128)(2,1)S(1)} %get-tuple-element.208), channel_id=1, source_target_pairs={{0,8},{4,12},{8,0},{12,4},{16,24},{20,28},{24,16},{28,20},{1,9},{5... | collective-permute-start | bytes 2555912 | tf_op jit(solution)/shard_map/ppermute | solution.py:359
  255.6 44.8 %collective-permute-start.25 = (bf16[384,1536]{1,0:T(8,128)(2,1)}, bf16[384,1536]{1,0:T(8,128)(2,1)}, u32[]{:S(2)}, u32[]{:S(2)}) collective-permute-start(bf16[384,1536]{1,0:T(8,128)(2,1)} %get-tuple-element.222), channel_id=1, source_target_pairs={{0,1},{4,5},{8,9},{12,13},{16,17},{20,21},{24,25},{28,29}} | collective-permute-start | bytes 3538952 | tf_op jit(solution)/shard_map/ppermute | solution.py:451
  258.1 43.9 %collective-permute-start.26 = (bf16[384,1536]{1,0:T(8,128)(2,1)}, bf16[384,1536]{1,0:T(8,128)(2,1)}, u32[]{:S(2)}, u32[]{:S(2)}) collective-permute-start(bf16[384,1536]{1,0:T(8,128)(2,1)} %get-tuple-element.223), channel_id=1, source_target_pairs={{3,2},{7,6},{11,10},{15,14},{19,18},{23,22},{27,26},{31,30}} | collective-permute-start | bytes 3538952 | tf_op jit(solution)/shard_map/ppermute | solution.py:452
  279.6 22.3 %collective-permute-start.23 = (bf16[128,1664]{1,0:T(8,128)(2,1)}, bf16[128,1664]{1,0:T(8,128)(2,1)}, u32[]{:S(2)}, u32[]{:S(2)}) collective-permute-start(bf16[128,1664]{1,0:T(8,128)(2,1)} %slice.414), channel_id=1, source_target_pairs={{0,8},{4,12},{8,0},{12,4},{16,24},{20,28},{24,16},{28,20},{1,9},{5... | collective-permute-start | bytes 1277960 | tf_op jit(solution)/shard_map/ppermute | solution.py:359
  280.9 21.0 %collective-permute-start.24 = (bf16[128,1664]{1,0:T(8,128)(2,1)}, bf16[128,1664]{1,0:T(8,128)(2,1)}, u32[]{:S(2)}, u32[]{:S(2)}) collective-permute-start(bf16[128,1664]{1,0:T(8,128)(2,1)} %slice.415), channel_id=1, source_target_pairs={{0,16},{4,20},{8,24},{12,28},{16,0},{20,4},{24,8},{28,12},{1,17},{... | collective-permute-start | bytes 1277960 | tf_op jit(solution)/shard_map/ppermute | solution.py:359
  298.9 25.1 %collective-permute-start.27 = (bf16[256,1536]{1,0:T(8,128)(2,1)}, bf16[256,1536]{1,0:T(8,128)(2,1)}, u32[]{:S(2)}, u32[]{:S(2)}) collective-permute-start(bf16[256,1536]{1,0:T(8,128)(2,1)} %get-tuple-element.227), channel_id=1, source_target_pairs={{0,16},{4,20},{8,24},{12,28},{16,0},{20,4},{24,8},{28,12},{1,17},{... | collective-permute-start | bytes 2359304 | tf_op jit(solution)/shard_map/ppermute | solution.py:359
  300.4 23.5 %collective-permute-start.28 = (bf16[256,1536]{1,0:T(8,128)(2,1)}, bf16[256,1536]{1,0:T(8,128)(2,1)}, u32[]{:S(2)}, u32[]{:S(2)}) collective-permute-start(bf16[256,1536]{1,0:T(8,128)(2,1)} %get-tuple-element.228), channel_id=1, source_target_pairs={{0,8},{4,12},{8,0},{12,4},{16,24},{20,28},{24,16},{28,20},{1,9},{5... | collective-permute-start | bytes 2359304 | tf_op jit(solution)/shard_map/ppermute | solution.py:359
  317.6 28.2 %collective-permute-start.31 = (bf16[384,1536]{1,0:T(8,128)(2,1)}, bf16[384,1536]{1,0:T(8,128)(2,1)}, u32[]{:S(2)}, u32[]{:S(2)}) collective-permute-start(bf16[384,1536]{1,0:T(8,128)(2,1)} %get-tuple-element.355), channel_id=1, source_target_pairs={{0,1},{1,2},{4,5},{5,6},{8,9},{9,10},{12,13},{13,14},{16,17},{17,1... | collective-permute-start | bytes 3538952 | tf_op jit(solution)/shard_map/ppermute | solution.py:451
  320.0 25.7 %collective-permute-start.32 = (bf16[384,1536]{1,0:T(8,128)(2,1)}, bf16[384,1536]{1,0:T(8,128)(2,1)}, u32[]{:S(2)}, u32[]{:S(2)}) collective-permute-start(bf16[384,1536]{1,0:T(8,128)(2,1)} %get-tuple-element.354), channel_id=1, source_target_pairs={{3,2},{2,1},{7,6},{6,5},{11,10},{10,9},{15,14},{14,13},{19,18},{18... | collective-permute-start | bytes 3538952 | tf_op jit(solution)/shard_map/ppermute | solution.py:452
  324.9 38.6 %all-to-all-start.1 = ((bf16[256,4,384]{2,0,1:T(8,128)(2,1)}), bf16[256,4,384]{2,0,1:T(8,128)(2,1)S(1)}, u32[]{:S(2)}, u32[]{:S(2)}) async-start(bf16[256,4,384]{2,0,1:T(8,128)(2,1)} %bitcast.185), calls=%async_computation.1 | async-start | bytes 1572864 | tf_op jit(solution)/shard_map/all_to_all | solution.py:604
  328.4 255.5 %all-reduce.6.cloned.1.call-start = ((), (), s32[]{:S(2)}) async-start(), calls=%async_computation.3 | async-start | bytes 3932160 | tf_op jit(solution)/shard_map/psum | solution.py:656
  331.8 9.0 %collective-permute-start.29 = (bf16[128,1536]{1,0:T(8,128)(2,1)S(1)}, bf16[128,1536]{1,0:T(8,128)(2,1)S(1)}, u32[]{:S(2)}, u32[]{:S(2)}) collective-permute-start(bf16[128,1536]{1,0:T(8,128)(2,1)S(1)} %slice.421), channel_id=1, source_target_pairs={{0,8},{4,12},{8,0},{12,4},{16,24},{20,28},{24,16},{28,20},{1,9},{5... | collective-permute-start | bytes 1179656 | tf_op jit(solution)/shard_map/ppermute | solution.py:359
  366.1 25.1 %collective-permute-start.35 = (bf16[4,208,1536]{2,1,0:T(8,128)(2,1)}, bf16[4,208,1536]{2,1,0:T(8,128)(2,1)S(1)}, u32[]{:S(2)}, u32[]{:S(2)}) collective-permute-start(bf16[4,208,1536]{2,1,0:T(8,128)(2,1)} %get-tuple-element.247), channel_id=1, source_target_pairs={{0,4},{4,0},{8,12},{12,8},{16,20},{20,16},{24,28},{28,24},{1,5},{5... | collective-permute-start | bytes 7667720 | tf_op jit(solution)/shard_map/ppermute | solution.py:359
  366.4 24.7 %collective-permute-start.33 = (bf16[256,1536]{1,0:T(8,128)(2,1)S(1)}, bf16[256,1536]{1,0:T(8,128)(2,1)}, u32[]{:S(2)}, u32[]{:S(2)}) collective-permute-start(bf16[256,1536]{1,0:T(8,128)(2,1)S(1)} %fusion.18), channel_id=1, source_target_pairs={{0,1},{1,2},{2,3},{4,5},{5,6},{6,7},{8,9},{9,10},{10,11},{12,13},{... | collective-permute-start | bytes 2359304 | tf_op jit(solution)/shard_map/ppermute | solution.py:451
  368.6 22.6 %collective-permute-start.34 = (bf16[256,1536]{1,0:T(8,128)(2,1)S(1)}, bf16[256,1536]{1,0:T(8,128)(2,1)}, u32[]{:S(2)}, u32[]{:S(2)}) collective-permute-start(bf16[256,1536]{1,0:T(8,128)(2,1)S(1)} %fusion.18), channel_id=1, source_target_pairs={{3,2},{2,1},{1,0},{7,6},{6,5},{5,4},{11,10},{10,9},{9,8},{15,14},{... | collective-permute-start | bytes 2359304 | tf_op jit(solution)/shard_map/ppermute | solution.py:452
  397.0 22.3 %collective-permute-start.36 = (bf16[256,1536]{1,0:T(8,128)(2,1)}, bf16[256,1536]{1,0:T(8,128)(2,1)S(1)}, u32[]{:S(2)}, u32[]{:S(2)}) collective-permute-start(bf16[256,1536]{1,0:T(8,128)(2,1)} %get-tuple-element.345), channel_id=1, source_target_pairs={{0,1},{4,5},{8,9},{12,13},{16,17},{20,21},{24,25},{28,29}} | collective-permute-start | bytes 2359304 | tf_op jit(solution)/shard_map/ppermute | solution.py:451
  401.9 17.4 %collective-permute-start.37 = (bf16[256,1536]{1,0:T(8,128)(2,1)}, bf16[256,1536]{1,0:T(8,128)(2,1)S(1)}, u32[]{:S(2)}, u32[]{:S(2)}) collective-permute-start(bf16[256,1536]{1,0:T(8,128)(2,1)} %get-tuple-element.344), channel_id=1, source_target_pairs={{3,2},{7,6},{11,10},{15,14},{19,18},{23,22},{27,26},{31,30}} | collective-permute-start | bytes 2359304 | tf_op jit(solution)/shard_map/ppermute | solution.py:452
  402.6 16.7 %collective-permute-start.38 = (bf16[256,1536]{1,0:T(8,128)(2,1)}, bf16[256,1536]{1,0:T(8,128)(2,1)S(1)}, u32[]{:S(2)}, u32[]{:S(2)}) collective-permute-start(bf16[256,1536]{1,0:T(8,128)(2,1)} %collective-permute-done.33), channel_id=1, source_target_pairs={{1,2},{2,3},{5,6},{6,7},{9,10},{10,11},{13,14},{14,15},{17,18},{18... | collective-permute-start | bytes 2359304 | tf_op jit(solution)/shard_map/ppermute | solution.py:451
  403.3 21.5 %collective-permute-start.39 = (bf16[256,1536]{1,0:T(8,128)(2,1)}, bf16[256,1536]{1,0:T(8,128)(2,1)S(1)}, u32[]{:S(2)}, u32[]{:S(2)}) collective-permute-start(bf16[256,1536]{1,0:T(8,128)(2,1)} %collective-permute-done.34), channel_id=1, source_target_pairs={{2,1},{1,0},{6,5},{5,4},{10,9},{9,8},{14,13},{13,12},{18,17},{17,1... | collective-permute-start | bytes 2359304 | tf_op jit(solution)/shard_map/ppermute | solution.py:452
  427.6 18.0 %collective-permute-start.40 = (bf16[256,1536]{1,0:T(8,128)(2,1)S(1)}, bf16[256,1536]{1,0:T(8,128)(2,1)S(1)}, u32[]{:S(2)}, u32[]{:S(2)}) collective-permute-start(bf16[256,1536]{1,0:T(8,128)(2,1)S(1)} %get-tuple-element.343), channel_id=1, source_target_pairs={{0,1},{1,2},{4,5},{5,6},{8,9},{9,10},{12,13},{13,14},{16,17},{17,1... | collective-permute-start | bytes 2359304 | tf_op jit(solution)/shard_map/ppermute | solution.py:451
  430.0 15.6 %collective-permute-start.41 = (bf16[256,1536]{1,0:T(8,128)(2,1)S(1)}, bf16[256,1536]{1,0:T(8,128)(2,1)S(1)}, u32[]{:S(2)}, u32[]{:S(2)}) collective-permute-start(bf16[256,1536]{1,0:T(8,128)(2,1)S(1)} %get-tuple-element.342), channel_id=1, source_target_pairs={{3,2},{2,1},{7,6},{6,5},{11,10},{10,9},{15,14},{14,13},{19,18},{18... | collective-permute-start | bytes 2359304 | tf_op jit(solution)/shard_map/ppermute | solution.py:452
  430.7 14.9 %collective-permute-start.42 = (bf16[256,1536]{1,0:T(8,128)(2,1)S(1)}, bf16[256,1536]{1,0:T(8,128)(2,1)S(1)}, u32[]{:S(2)}, u32[]{:S(2)}) collective-permute-start(bf16[256,1536]{1,0:T(8,128)(2,1)S(1)} %collective-permute-done.38), channel_id=1, source_target_pairs={{2,3},{6,7},{10,11},{14,15},{18,19},{22,23},{26,27},{30,31}} | collective-permute-start | bytes 2359304 | tf_op jit(solution)/shard_map/ppermute | solution.py:451
  431.4 20.0 %collective-permute-start.43 = (bf16[256,1536]{1,0:T(8,128)(2,1)}, bf16[256,1536]{1,0:T(8,128)(2,1)S(1)}, u32[]{:S(2)}, u32[]{:S(2)}) collective-permute-start(bf16[256,1536]{1,0:T(8,128)(2,1)} %copy-done.48), channel_id=1, source_target_pairs={{1,0},{5,4},{9,8},{13,12},{17,16},{21,20},{25,24},{29,28}} | collective-permute-start | bytes 2359304 | tf_op jit(solution)/shard_map/ppermute | solution.py:452
  453.0 16.4 %collective-permute-start.47 = (bf16[256,1536]{1,0:T(8,128)(2,1)}, bf16[256,1536]{1,0:T(8,128)(2,1)S(1)}, u32[]{:S(2)}, u32[]{:S(2)}) collective-permute-start(bf16[256,1536]{1,0:T(8,128)(2,1)} %get-tuple-element.341), channel_id=1, source_target_pairs={{0,1},{1,2},{2,3},{4,5},{5,6},{6,7},{8,9},{9,10},{10,11},{12,13},{... | collective-permute-start | bytes 2359304 | tf_op jit(solution)/shard_map/ppermute | solution.py:451
  454.6 18.8 %collective-permute-start.48 = (bf16[256,1536]{1,0:T(8,128)(2,1)}, bf16[256,1536]{1,0:T(8,128)(2,1)S(1)}, u32[]{:S(2)}, u32[]{:S(2)}) collective-permute-start(bf16[256,1536]{1,0:T(8,128)(2,1)} %get-tuple-element.340), channel_id=1, source_target_pairs={{3,2},{2,1},{1,0},{7,6},{6,5},{5,4},{11,10},{10,9},{9,8},{15,14},{... | collective-permute-start | bytes 2359304 | tf_op jit(solution)/shard_map/ppermute | solution.py:452
  478.0 37.4 %collective-permute-start.49 = (bf16[256,1536]{1,0:T(8,128)(2,1)S(1)}, bf16[256,1536]{1,0:T(8,128)(2,1)}, u32[]{:S(2)}, u32[]{:S(2)}) collective-permute-start(bf16[256,1536]{1,0:T(8,128)(2,1)S(1)} %fusion.15), channel_id=1, source_target_pairs={{0,1},{1,2},{2,3},{4,5},{5,6},{6,7},{8,9},{9,10},{10,11},{12,13},{... | collective-permute-start | bytes 2359304 | tf_op jit(solution)/shard_map/ppermute | solution.py:451
  481.8 33.6 %collective-permute-start.50 = (bf16[256,1536]{1,0:T(8,128)(2,1)S(1)}, bf16[256,1536]{1,0:T(8,128)(2,1)}, u32[]{:S(2)}, u32[]{:S(2)}) collective-permute-start(bf16[256,1536]{1,0:T(8,128)(2,1)S(1)} %fusion.15), channel_id=1, source_target_pairs={{3,2},{2,1},{1,0},{7,6},{6,5},{5,4},{11,10},{10,9},{9,8},{15,14},{... | collective-permute-start | bytes 2359304 | tf_op jit(solution)/shard_map/ppermute | solution.py:452
  483.2 20.7 %collective-permute-start.44 = (bf16[208,1536]{1,0:T(8,128)(2,1)S(1)}, bf16[208,1536]{1,0:T(8,128)(2,1)S(1)}, u32[]{:S(2)}, u32[]{:S(2)}) collective-permute-start(bf16[208,1536]{1,0:T(8,128)(2,1)S(1)} %get-tuple-element.348), channel_id=1, source_target_pairs={{0,8},{4,12},{8,0},{12,4},{16,24},{20,28},{24,16},{28,20},{1,9},{5... | collective-permute-start | bytes 1916936 | tf_op jit(solution)/shard_map/ppermute | solution.py:359
  483.8 25.7 %collective-permute-start.45 = (bf16[208,1536]{1,0:T(8,128)(2,1)S(1)}, bf16[208,1536]{1,0:T(8,128)(2,1)S(1)}, u32[]{:S(2)}, u32[]{:S(2)}) collective-permute-start(bf16[208,1536]{1,0:T(8,128)(2,1)S(1)} %get-tuple-element.347), channel_id=1, source_target_pairs={{0,16},{4,20},{8,24},{12,28},{16,0},{20,4},{24,8},{28,12},{1,17},{... | collective-permute-start | bytes 1916936 | tf_op jit(solution)/shard_map/ppermute | solution.py:359
  484.5 30.9 %collective-permute-start.46 = (bf16[208,1536]{1,0:T(8,128)(2,1)S(1)}, bf16[208,1536]{1,0:T(8,128)(2,1)S(1)}, u32[]{:S(2)}, u32[]{:S(2)}) collective-permute-start(bf16[208,1536]{1,0:T(8,128)(2,1)S(1)} %get-tuple-element.346), channel_id=1, source_target_pairs={{0,24},{4,28},{8,16},{12,20},{16,8},{20,12},{24,0},{28,4},{1,25},{... | collective-permute-start | bytes 1916936 | tf_op jit(solution)/shard_map/ppermute | solution.py:359
  503.9 24.4 %collective-permute-start.65 = (bf16[384,1536]{1,0:T(8,128)(2,1)}, bf16[384,1536]{1,0:T(8,128)(2,1)}, u32[]{:S(2)}, u32[]{:S(2)}) collective-permute-start(bf16[384,1536]{1,0:T(8,128)(2,1)} %add_convert_fusion.2), channel_id=1, source_target_pairs={{0,1},{1,2},{2,3},{4,5},{5,6},{6,7},{8,9},{9,10},{10,11},{12,13},{... | collective-permute-start | bytes 3538952 | tf_op jit(solution)/shard_map/ppermute | solution.py:451
  509.5 35.3 %collective-permute-start.66 = (bf16[384,1536]{1,0:T(8,128)(2,1)}, bf16[384,1536]{1,0:T(8,128)(2,1)}, u32[]{:S(2)}, u32[]{:S(2)}) collective-permute-start(bf16[384,1536]{1,0:T(8,128)(2,1)} %add_convert_fusion.1), channel_id=1, source_target_pairs={{3,2},{2,1},{1,0},{7,6},{6,5},{5,4},{11,10},{10,9},{9,8},{15,14},{... | collective-permute-start | bytes 3538952 | tf_op jit(solution)/shard_map/ppermute | solution.py:452
  516.9 34.7 %collective-permute-start.51 = (bf16[64,1536]{1,0:T(8,128)(2,1)}, bf16[64,1536]{1,0:T(8,128)(2,1)}, u32[]{:S(2)}, u32[]{:S(2)}) collective-permute-start(bf16[64,1536]{1,0:T(8,128)(2,1)} %get-tuple-element.358), channel_id=1, source_target_pairs={{0,1},{1,2},{2,3},{3,0},{4,5},{5,6},{6,7},{7,4},{8,9},{9,10},{10,1... | collective-permute-start | bytes 589832 | tf_op jit(solution)/shard_map/ppermute | solution.py:364
  519.3 41.4 %collective-permute-start.54 = (bf16[256,1536]{1,0:T(8,128)(2,1)}, bf16[256,1536]{1,0:T(8,128)(2,1)}, u32[]{:S(2)}, u32[]{:S(2)}) collective-permute-start(bf16[256,1536]{1,0:T(8,128)(2,1)} %collective-permute-done.49), channel_id=1, source_target_pairs={{1,2},{2,3},{5,6},{6,7},{9,10},{10,11},{13,14},{14,15},{17,18},{18... | collective-permute-start | bytes 2359304 | tf_op jit(solution)/shard_map/ppermute | solution.py:451
  520.8 39.9 %collective-permute-start.55 = (bf16[256,1536]{1,0:T(8,128)(2,1)}, bf16[256,1536]{1,0:T(8,128)(2,1)}, u32[]{:S(2)}, u32[]{:S(2)}) collective-permute-start(bf16[256,1536]{1,0:T(8,128)(2,1)} %collective-permute-done.50), channel_id=1, source_target_pairs={{2,1},{1,0},{6,5},{5,4},{10,9},{9,8},{14,13},{13,12},{18,17},{17,1... | collective-permute-start | bytes 2359304 | tf_op jit(solution)/shard_map/ppermute | solution.py:452
  528.3 32.4 %collective-permute-start.52 = (bf16[64,1536]{1,0:T(8,128)(2,1)}, bf16[64,1536]{1,0:T(8,128)(2,1)}, u32[]{:S(2)}, u32[]{:S(2)}) collective-permute-start(bf16[64,1536]{1,0:T(8,128)(2,1)} %get-tuple-element.357), channel_id=1, source_target_pairs={{0,2},{1,3},{2,0},{3,1},{4,6},{5,7},{6,4},{7,5},{8,10},{9,11},{10,... | collective-permute-start | bytes 589832 | tf_op jit(solution)/shard_map/ppermute | solution.py:364
  544.8 15.9 %collective-permute-start.53 = (bf16[64,1536]{1,0:T(8,128)(2,1)S(1)}, bf16[64,1536]{1,0:T(8,128)(2,1)}, u32[]{:S(2)}, u32[]{:S(2)}) collective-permute-start(bf16[64,1536]{1,0:T(8,128)(2,1)S(1)} %get-tuple-element.356), channel_id=1, source_target_pairs={{0,3},{1,0},{2,1},{3,2},{4,7},{5,4},{6,5},{7,6},{8,11},{9,8},{10,9... | collective-permute-start | bytes 589832 | tf_op jit(solution)/shard_map/ppermute | solution.py:364
  562.1 11.3 %collective-permute-start.58 = (bf16[64,1536]{1,0:T(8,128)(2,1)S(1)}, bf16[64,1536]{1,0:T(8,128)(2,1)S(1)}, u32[]{:S(2)}, u32[]{:S(2)}) collective-permute-start(bf16[64,1536]{1,0:T(8,128)(2,1)S(1)} %get-tuple-element.327), channel_id=1, source_target_pairs={{0,4},{4,0},{8,12},{12,8},{16,20},{20,16},{24,28},{28,24},{1,5},{5... | collective-permute-start | bytes 589832 | tf_op jit(solution)/shard_map/ppermute | solution.py:359
  562.2 12.5 %collective-permute-start.59 = (bf16[64,1536]{1,0:T(8,128)(2,1)S(1)}, bf16[64,1536]{1,0:T(8,128)(2,1)S(1)}, u32[]{:S(2)}, u32[]{:S(2)}) collective-permute-start(bf16[64,1536]{1,0:T(8,128)(2,1)S(1)} %get-tuple-element.327), channel_id=1, source_target_pairs={{0,8},{4,12},{8,0},{12,4},{16,24},{20,28},{24,16},{28,20},{1,9},{5... | collective-permute-start | bytes 589832 | tf_op jit(solution)/shard_map/ppermute | solution.py:359
  567.1 11.2 %collective-permute-start.61 = (bf16[64,1536]{1,0:T(8,128)(2,1)S(1)}, bf16[64,1536]{1,0:T(8,128)(2,1)S(1)}, u32[]{:S(2)}, u32[]{:S(2)}) collective-permute-start(bf16[64,1536]{1,0:T(8,128)(2,1)S(1)} %get-tuple-element.327), channel_id=1, source_target_pairs={{0,16},{4,20},{8,24},{12,28},{16,0},{20,4},{24,8},{28,12},{1,17},{... | collective-permute-start | bytes 589832 | tf_op jit(solution)/shard_map/ppermute | solution.py:359
  567.8 10.5 %collective-permute-start.63 = (bf16[64,1536]{1,0:T(8,128)(2,1)S(1)}, bf16[64,1536]{1,0:T(8,128)(2,1)S(1)}, u32[]{:S(2)}, u32[]{:S(2)}) collective-permute-start(bf16[64,1536]{1,0:T(8,128)(2,1)S(1)} %get-tuple-element.327), channel_id=1, source_target_pairs={{0,24},{4,28},{8,16},{12,20},{16,8},{20,12},{24,0},{28,4},{1,25},{... | collective-permute-start | bytes 589832 | tf_op jit(solution)/shard_map/ppermute | solution.py:359
  568.6 15.3 %collective-permute-start.56 = (bf16[256,1536]{1,0:T(8,128)(2,1)}, bf16[256,1536]{1,0:T(8,128)(2,1)S(1)}, u32[]{:S(2)}, u32[]{:S(2)}) collective-permute-start(bf16[256,1536]{1,0:T(8,128)(2,1)} %collective-permute-done.54), channel_id=1, source_target_pairs={{2,3},{6,7},{10,11},{14,15},{18,19},{22,23},{26,27},{30,31}} | collective-permute-start | bytes 2359304 | tf_op jit(solution)/shard_map/ppermute | solution.py:451
  573.5 21.6 %collective-permute-start.57 = (bf16[256,1536]{1,0:T(8,128)(2,1)}, bf16[256,1536]{1,0:T(8,128)(2,1)S(1)}, u32[]{:S(2)}, u32[]{:S(2)}) collective-permute-start(bf16[256,1536]{1,0:T(8,128)(2,1)} %collective-permute-done.55), channel_id=1, source_target_pairs={{1,0},{5,4},{9,8},{13,12},{17,16},{21,20},{25,24},{29,28}} | collective-permute-start | bytes 2359304 | tf_op jit(solution)/shard_map/ppermute | solution.py:452
  (81 other events, 610.2 us)
Sparse Core Ops, SparseCore 0:
  10.6 50.8 all-gather.1
  462.1 72.8 all-reduce.5

commit v4 on v3

v4 whole, which is shorter than its diff:
```python
import functools

import jax
import jax.numpy as jnp
from jax import lax
from jax.experimental import pallas as pl
from jax.experimental.pallas import tpu as pltpu
from jax.sharding import PartitionSpec as P

HD = 64
LEN = 1024
EPS = 1e-06
MASKED = -1e30
BF = jnp.bfloat16
F32 = jnp.float32
BLOCK = 256
LANES = 128
NT = (((1,), (1,)), ((), ()))
TN = (((0,), (0,)), ((), ()))


def takes(us):
    return pl.CostEstimate(flops=int(us * 1.15e9), bytes_accessed=0, transcendentals=0)


def mul(a, b, dims=(((1,), (0,)), ((), ()))):
    return lax.dot_general(a, b, dims, preferred_element_type=F32)


def rotate_lanes(y, cos, sin_a, sin_b):
    return y * cos + pltpu.roll(y, 128 - HD // 2, 1) * sin_a + pltpu.roll(y, HD // 2, 1) * sin_b


def rotary_lanes(tokens):
    positions = (jnp.arange(tokens) % LEN).astype(F32)
    lane = jnp.arange(128)
    freqs = 10000.0 ** (-(lane % (HD // 2)).astype(F32) * 2.0 / HD)
    angles = positions[:, None] * freqs[None, :]
    cos, sin = jnp.cos(angles), jnp.sin(angles)
    first = (lane % HD < HD // 2)[None, :]
    return cos, jnp.where(first, -sin, 0.0), jnp.where(first, 0.0, sin)


def causal(block):
    key_at = lax.broadcasted_iota(jnp.int32, (block, block), 0)
    query_at = lax.broadcasted_iota(jnp.int32, (block, block), 1)
    return key_at <= query_at


def attend_kernel(at_ref, x_ref, gain_ref, wq_ref, wk_ref, wv_ref, cos_ref, sin_a_ref, sin_b_ref, *refs):
    pieces, (normed_ref, q_ref, k_ref, v_ref, w_ref, log_ref, vt_ref, out_ref) = refs[:-8], refs[-8:]
    tokens = x_ref.shape[0]
    heads, groups = q_ref.shape[0], k_ref.shape[0]
    repeat = heads // groups
    per = 128 // HD
    scale = HD ** (-0.5)
    w_ref[...] = jnp.concatenate([wq_ref[...], wk_ref[...], wv_ref[...]], axis=1)

    @pl.loop(0, tokens // BLOCK)
    def _(i):
        at = pl.multiple_of(i * BLOCK, BLOCK)
        rows = pl.ds(at, BLOCK)
        x = x_ref[rows, :].astype(F32)
        inverse = lax.rsqrt(jnp.mean(x * x, axis=-1, keepdims=True) + EPS)
        normed = (x * inverse * gain_ref[...]).astype(BF)
        normed_ref[rows, :] = normed
        raw = mul(normed, w_ref[...])
        tables = (cos_ref[rows, :], sin_a_ref[rows, :], sin_b_ref[rows, :])
        for h in range(0, heads, per):
            turned = rotate_lanes(raw[:, h * HD : h * HD + 128], *tables) * scale
            for u in range(per):
                q_ref[h + u, rows, :] = turned[:, u * HD : (u + 1) * HD].astype(BF)
        for g in range(0, groups, per):
            lane = (heads + g) * HD
            turned = rotate_lanes(raw[:, lane : lane + 128], *tables)
            lane = (heads + groups + g) * HD
            value = raw[:, lane : lane + 128]
            turned_value = value.T
            for u in range(per):
                k_ref[g + u, rows, :] = turned[:, u * HD : (u + 1) * HD].astype(BF)
                v_ref[g + u, rows, :] = value[:, u * HD : (u + 1) * HD].astype(BF)
                vt_ref[g + u, :, rows] = turned_value[u * HD : (u + 1) * HD].astype(BF)

    keep = causal(BLOCK)

    @pl.loop(0, heads)
    def _(h):
        g = h // repeat
        for i in range(tokens // BLOCK):
            start, stop = i * BLOCK, (i + 1) * BLOCK
            query = q_ref[h, start:stop, :]
            parts = [jnp.where(keep, mul(k_ref[g, start:stop, :], query, NT), MASKED)]
            if i:
                parts.append(mul(k_ref[g, :start, :], query, NT))
            peak = jnp.max(parts[0], axis=0, keepdims=True)
            for part in parts[1:]:
                peak = jnp.maximum(peak, jnp.max(part, axis=0, keepdims=True))
            weights = [jnp.exp(part - peak) for part in parts]
            total = sum(jnp.sum(w, axis=0, keepdims=True) for w in weights)
            shrink = 1.0 / total
            mixed = mul(vt_ref[g, :, start:stop], (weights[0] * shrink).astype(BF))
            if i:
                mixed += mul(vt_ref[g, :, :start], (weights[1] * shrink).astype(BF))
            out_ref[h, :, start:stop] = mixed
            log_ref[h, :, start:stop] = peak + jnp.log(total)

    for s, piece_ref in enumerate(pieces):
        span = pl.ds(pl.multiple_of(lax.rem(at_ref[0] + s, len(pieces)) * BLOCK, BLOCK), BLOCK)
        for h in range(0, heads, per):
            pair = jnp.concatenate([out_ref[h + u, :, span] for u in range(per)], axis=0)
            piece_ref[:, h * HD : h * HD + 128] = pair.T.astype(BF)


VMEM = pl.BlockSpec(memory_space=pltpu.VMEM)
SMEM = pl.BlockSpec(memory_space=pltpu.SMEM)


def attend(x, gain, weights, tables, heads, groups, at):
    tokens, width = x.shape
    count = tokens // BLOCK
    return pl.pallas_call(
        attend_kernel,
        in_specs=[SMEM] + [VMEM] * 8,
        out_shape=[jax.ShapeDtypeStruct((BLOCK, heads * HD), BF)] * count
        + [
            jax.ShapeDtypeStruct((tokens, width), BF),
            jax.ShapeDtypeStruct((heads, tokens, HD), BF),
            jax.ShapeDtypeStruct((groups, tokens, HD), BF),
            jax.ShapeDtypeStruct((groups, tokens, HD), BF),
            jax.ShapeDtypeStruct((width, (heads + 2 * groups) * HD), BF),
            jax.ShapeDtypeStruct((heads, 1, tokens), F32),
        ],
        scratch_shapes=[pltpu.VMEM((groups, HD, tokens), BF), pltpu.VMEM((heads, HD, tokens), F32)],
        compiler_params=pltpu.CompilerParams(vmem_limit_bytes=48 << 20),
        cost_estimate=takes(20),
    )(at[None], x, gain[None], *weights, *tables)


def attend_back_kernel(at_ref, q_ref, k_ref, v_ref, log_ref, cos_ref, sin_a_ref, sin_b_ref, *refs):
    do_ref, kt_ref, dq_ref, dk_ref, dv_ref = refs[-5:]
    out_ref = refs[-6]
    grad_refs = refs[:-6]
    count = len(grad_refs)
    tokens = q_ref.shape[1]
    heads, groups = q_ref.shape[0], k_ref.shape[0]
    repeat = heads // groups
    per = 128 // HD
    scale = HD ** (-0.5)
    dk_ref[...] = jnp.zeros_like(dk_ref)
    dv_ref[...] = jnp.zeros_like(dv_ref)

    def span_of(s):
        return pl.ds(pl.multiple_of(lax.rem(at_ref[0] + s, count) * BLOCK, BLOCK), BLOCK)

    for s, grad_ref in enumerate(grad_refs):
        for h in range(heads):
            do_ref[h, span_of(s), :] = grad_ref[:, h * HD : (h + 1) * HD]

    @pl.loop(0, tokens // BLOCK)
    def _(i):
        rows = pl.ds(pl.multiple_of(i * BLOCK, BLOCK), BLOCK)
        for g in range(groups):
            kt_ref[g, :, rows] = k_ref[g, rows, :].astype(F32).T.astype(BF)

    keep = causal(BLOCK)

    @pl.loop(0, heads)
    def _(h):
        g = h // repeat
        for i in range(tokens // BLOCK):
            start, stop = i * BLOCK, (i + 1) * BLOCK
            query = q_ref[h, start:stop, :]
            grads = do_ref[h, start:stop, :]
            log_total = log_ref[h, :, start:stop]
            spans = [(start, stop)] + ([(0, start)] if i else [])
            probs, grad_probs = [], []
            for lo, hi in spans:
                scores = mul(k_ref[g, lo:hi, :], query, NT)
                if hi == stop:
                    scores = jnp.where(keep, scores, MASKED)
                probs.append(jnp.exp(scores - log_total))
                grad_probs.append(mul(v_ref[g, lo:hi, :], grads, NT))
            inner = sum(jnp.sum(p * d, axis=0, keepdims=True) for p, d in zip(probs, grad_probs))
            dq = None
            for (lo, hi), p, d in zip(spans, probs, grad_probs):
                ds = (p * (d - inner)).astype(BF)
                dk_ref[g, lo:hi, :] += mul(ds, query)
                dv_ref[g, lo:hi, :] += mul(p.astype(BF), grads)
                term = mul(kt_ref[g, :, lo:hi], ds)
                dq = term if dq is None else dq + term
            dq_ref[h, :, start:stop] = dq * scale

    @pl.loop(0, tokens // BLOCK)
    def _(i):
        rows = pl.ds(pl.multiple_of(i * BLOCK, BLOCK), BLOCK)
        tables = (cos_ref[rows, :], -sin_a_ref[rows, :], -sin_b_ref[rows, :])
        for h in range(0, heads, per):
            pair = jnp.concatenate([dq_ref[h + u, :, rows] for u in range(per)], axis=0).T
            out_ref[rows, h * HD : h * HD + 128] = rotate_lanes(pair, *tables).astype(BF)
        for g in range(0, groups, per):
            pair = jnp.concatenate([dk_ref[g + u, rows, :] for u in range(per)], axis=1)
            lane = (heads + g) * HD
            out_ref[rows, lane : lane + 128] = rotate_lanes(pair, *tables).astype(BF)
            pair = jnp.concatenate([dv_ref[g + u, rows, :] for u in range(per)], axis=1)
            lane = (heads + groups + g) * HD
            out_ref[rows, lane : lane + 128] = pair.astype(BF)


def attend_back(grad_pieces, q, k, v, logs, tables, at):
    heads, tokens, _ = q.shape
    groups = k.shape[0]
    count = len(grad_pieces)
    lanes = (heads + 2 * groups) * HD
    return pl.pallas_call(
        attend_back_kernel,
        in_specs=[SMEM] + [VMEM] * (7 + count),
        out_shape=jax.ShapeDtypeStruct((tokens, lanes), BF),
        scratch_shapes=[
            pltpu.VMEM((heads, tokens, HD), BF),
            pltpu.VMEM((groups, HD, tokens), BF),
            pltpu.VMEM((heads, HD, tokens), F32),
            pltpu.VMEM((groups, tokens, HD), F32),
            pltpu.VMEM((groups, tokens, HD), F32),
        ],
        compiler_params=pltpu.CompilerParams(vmem_limit_bytes=48 << 20),
        cost_estimate=takes(20),
    )(at[None], q, k, v, logs, *tables, *grad_pieces)


def expert_kernel(order_ref, near_ref, far_ref, extra_near_ref, extra_far_ref, router_ref, parts_ref, *refs, top, count):
    out_refs, gin_refs, terms_ref = refs[:2], refs[2:4], refs[4]
    weights_ref, sums_ref = refs[5:]
    step = pl.program_id(0)
    steps = pl.num_programs(0)
    hidden_width, width = weights_ref.shape[0] // 3, weights_ref.shape[1]
    gate_up = slice(0, 2 * hidden_width)
    down = slice(2 * hidden_width, 3 * hidden_width)
    own = order_ref[0]
    experts = order_ref[1]
    part = hidden_width // count
    spans = [
        (pl.ds((3 * s + j) * part, part), pl.ds(j * hidden_width + s * part, part))
        for s in range(count)
        for j in range(3)
    ]

    @pl.when(step == 0)
    def _():
        sums_ref[...] = jnp.zeros_like(sums_ref)
        for there, here in spans:
            weights_ref[here, :] = parts_ref[there, :]

    near = step < steps // 2
    rows = jnp.where(near, near_ref[...], far_ref[...])
    extra = jnp.where(near, extra_near_ref[...], extra_far_ref[...])
    grads32 = extra[:, :width].astype(F32)
    named = extra[:, width:].astype(F32)

    lane = lax.broadcasted_iota(jnp.int32, (rows.shape[0], LANES), 1)
    lane32 = lane.astype(F32)
    chosen = lane32 == named[:, 0:1]
    for k in range(1, top):
        chosen = chosen | (lane32 == named[:, k : k + 1])
    logits = jnp.where(chosen, mul(rows, router_ref[...]), MASKED)
    weights = jnp.where(chosen, jnp.exp(logits - jnp.max(logits, axis=-1, keepdims=True)), 0.0)
    mine = jnp.sum(jnp.where(lane == own, weights, 0.0), axis=-1, keepdims=True)
    gate = mine / jnp.sum(weights, axis=-1, keepdims=True)

    both = mul(rows, weights_ref[gate_up, :], NT)
    gate_vals = both[:, :hidden_width]
    up_vals = both[:, hidden_width:]
    sigma = jax.nn.sigmoid(gate_vals)
    active = gate_vals * sigma
    hidden = (active * up_vals).astype(BF)
    grad_out = (gate * grads32).astype(BF)
    grad_hidden = mul(grad_out, weights_ref[down, :], NT)
    expert_out = mul(hidden, weights_ref[down, :])
    combined = (gate * expert_out).astype(BF)
    score = jnp.sum(grads32 * expert_out, axis=-1, keepdims=True)
    high = score.astype(BF).astype(F32)
    scores = jnp.where(lane == own, high, jnp.where(lane == own + experts, score - high, 0.0)).astype(BF)
    grad_gate_vals = (grad_hidden * up_vals * sigma * (1.0 + gate_vals * (1.0 - sigma))).astype(BF)
    grad_up_vals = (grad_hidden * active).astype(BF)
    grad_both = jnp.concatenate([grad_gate_vals, grad_up_vals], axis=1)
    grad_in = mul(grad_both, weights_ref[gate_up, :]).astype(BF)
    sums_ref[gate_up, :] += mul(grad_both, rows, TN)
    sums_ref[down, :] += mul(hidden, grad_out, TN)
    for far in range(2):

        @pl.when(near if far == 0 else step >= steps // 2)
        def _():
            out_refs[far][...] = combined
            gin_refs[far][:, :width] = grad_in
            gin_refs[far][:, width:] = scores

    @pl.when(step == steps - 1)
    def _():
        for there, here in spans:
            terms_ref[there, :] = sums_ref[here, :].astype(BF)


def run_experts(order, near, far, extra_near, extra_far, router, parts, top, count):
    total, width = 2 * near.shape[0], near.shape[1]
    steps = total // BLOCK
    half_steps = steps // 2
    wide = extra_near.shape[1]
    hidden = parts.shape[0] // 3

    def by_set(lanes):
        return [
            pl.BlockSpec((BLOCK, lanes), lambda i, o: (jnp.minimum(i, half_steps - 1), 0)),
            pl.BlockSpec((BLOCK, lanes), lambda i, o: (jnp.maximum(i - half_steps, 0), 0)),
        ]

    half, half_wide = by_set(width), by_set(wide)
    whole = pl.BlockSpec((3 * hidden, width), lambda i, o: (0, 0), pipeline_mode=pl.Buffered(1))
    return pl.pallas_call(
        functools.partial(expert_kernel, top=top, count=count),
        grid_spec=pltpu.PrefetchScalarGridSpec(
            num_scalar_prefetch=1,
            grid=(steps,),
            in_specs=[
                *by_set(width),
                *by_set(wide),
                pl.BlockSpec((width, LANES), lambda i, o: (0, 0)),
                whole,
            ],
            out_specs=half + half_wide + [whole],
            scratch_shapes=[
                pltpu.VMEM((3 * hidden, width), BF),
                pltpu.VMEM((3 * hidden, width), F32),
            ],
        ),
        out_shape=[jax.ShapeDtypeStruct((total // 2, width), BF)] * 2
        + [jax.ShapeDtypeStruct((total // 2, wide), BF)] * 2
        + [jax.ShapeDtypeStruct((3 * hidden, width), BF)],
        compiler_params=pltpu.CompilerParams(vmem_limit_bytes=58 << 20),
        cost_estimate=takes(5 * steps),
    )(order, near, far, extra_near, extra_far, router, parts)


def set_rows_kernel(order_ref, near_ref, far_ref, out_ref, small_ref, norm_ref, *, part, few_rows):
    rows, width = near_ref.shape[0] // 4, near_ref.shape[1]
    norm = jnp.zeros((1, width), F32)
    for k in range(8):
        source = near_ref if k < 4 else far_ref
        block = source[(k % 4) * rows : (k % 4 + 1) * rows, :].astype(F32)
        device = order_ref[k]
        out_ref[pl.ds(pl.multiple_of(device * part, 8), part), :] = block[:part]
        small_ref[pl.ds(pl.multiple_of(device * few_rows, 8), few_rows), :] = block[part : part + few_rows]
        norm += block[rows - 1 :]
    norm_ref[...] = norm


def set_rows(order, near, far, part, few_rows):
    width = near.shape[1]
    return pl.pallas_call(
        functools.partial(set_rows_kernel, part=part, few_rows=few_rows),
        in_specs=[SMEM, VMEM, VMEM],
        out_shape=[
            jax.ShapeDtypeStruct((8 * part, width), F32),
            jax.ShapeDtypeStruct((8 * few_rows, width), F32),
            jax.ShapeDtypeStruct((1, width), F32),
        ],
        compiler_params=pltpu.CompilerParams(vmem_limit_bytes=32 << 20),
        cost_estimate=takes(3),
    )(order, near, far)


def join(*values):
    return lax.optimization_barrier(values)


def add(a, b):
    return (a.astype(F32) + b.astype(F32)).astype(BF)


def swap(x, bit):
    return lax.ppermute(x, "ep", [(i, i ^ bit) for i in range(lax.axis_size("ep"))])


def turn(x, by):
    n = lax.axis_size("tp")
    return lax.ppermute(x, "tp", [(i, (i + by) % n) for i in range(n)])


def step_both(right, left, low=0, high=None):
    n = lax.axis_size("tp")
    pairs = [(i, i + 1) for i in range(low, n - 1 if high is None else high)]
    mirror = [(n - 1 - i, n - 1 - j) for i, j in pairs]
    return lax.ppermute(right, "tp", pairs), lax.ppermute(left, "tp", mirror)


def step_ends(right, left, low, high):
    n = lax.axis_size("tp")
    at = lax.axis_index("tp")
    pairs = [(i, i + 1) for i in range(low, high)]
    give = jnp.where((at >= low) & (at < high), right, left)
    return lax.ppermute(give, "tp", pairs + [(n - 1 - i, n - 1 - j) for i, j in pairs])


def by_side(got, low, high):
    at = lax.axis_index("tp")
    ahead = (at > low) & (at <= high)
    return jnp.where(ahead, got, 0), jnp.where(ahead, 0, got)


def gather_first(x):
    half = x.shape[0] // 2
    return swap(x[:half], 2), swap(x[half:], 4)


def gather_second(x, got):
    half = x.shape[0] // 2
    first, second = join(
        jnp.concatenate([x[:half], got[0]], axis=0), jnp.concatenate([x[half:], got[1]], axis=0)
    )
    return (first, second), (swap(first, 4), swap(second, 2))


def gather_near(held, got):
    return jnp.concatenate([held[0], got[0], held[1], got[1]], axis=0)


def gather_halves():
    n = lax.axis_size("ep")
    if n != 8:
        return [(jnp.int32(k // 2), k % 2) for k in range(2 * n)]
    at = lax.axis_index("ep").astype(jnp.int32)
    near = [(0, 0), (2, 0), (4, 0), (6, 0), (0, 1), (4, 1), (2, 1), (6, 1)]
    return [(jnp.bitwise_xor(at, k + core), half) for core in (0, 1) for k, half in near]


def gather_whole(x):
    whole = lax.all_gather(x, "ep", tiled=True)
    return whole[: whole.shape[0] // 2], whole[whole.shape[0] // 2 :]


def sum_cores(near, far):
    rows = near.shape[0] // 4
    return join(*[add(near[j * rows : (j + 1) * rows], far[j * rows : (j + 1) * rows]) for j in range(4)])


def sum_first(sums):
    return swap(sums[1], 4), swap(sums[3], 2)


def sum_second(sums, got):
    first, second = join(add(sums[0], got[0]), add(sums[2], got[1]))
    half = first.shape[0] // 2
    return (first, second), (swap(first[half:], 2), swap(second[half:], 4))


def sum_last(sums, got):
    half = sums[0].shape[0] // 2
    return jnp.concatenate([s[:half].astype(F32) + g.astype(F32) for s, g in zip(sums, got)], axis=0)


def sum_whole(near, far):
    n = lax.axis_size("ep")
    terms = jnp.concatenate([near, far], axis=0).reshape(n, -1, near.shape[1])
    return lax.psum_scatter(terms, "ep", scatter_dimension=0, tiled=False).astype(F32)


def spread(own, steps, last):
    n = lax.axis_size("tp")
    at = lax.axis_index("tp").astype(jnp.int32)
    rows, width = own.shape
    out = jnp.zeros((n * rows, width), BF)
    for t, step in enumerate(steps):
        for got, place in zip(step, (at - t - 1, at + t + 1)):
            place = jnp.where((place >= 0) & (place < n), place, at)
            out = lax.dynamic_update_slice(out, got, (place * rows, 0))
    place = jnp.where(at == n - 1, 0, jnp.where(at == 0, n - 1, at))
    out = lax.dynamic_update_slice(out, last, (place * rows, 0))
    return lax.dynamic_update_slice(out, own, (at * rows, 0))


def body(
    inputs,
    routes,
    norm_gain,
    query_weight,
    key_weight,
    value_weight,
    output_weight,
    mixer_gain,
    router_weight,
    gate_weight,
    up_weight,
    down_weight,
    cotangent,
):
    tokens, width = inputs.shape
    experts = router_weight.shape[1]
    top = routes.shape[1]
    n_ep = lax.axis_size("ep")
    n_tp = lax.axis_size("tp")
    fine = n_ep == 8
    ep_at = lax.axis_index("ep").astype(jnp.int32)
    tp_at = lax.axis_index("tp").astype(jnp.int32)
    quarter = tokens // n_tp
    heads_width = query_weight.shape[1]
    groups_width = key_weight.shape[1]

    def mine(x):
        return lax.dynamic_slice_in_dim(x, tp_at * quarter, quarter, 0)

    part = output_weight.shape[0] // n_ep
    output_part = lax.dynamic_slice_in_dim(output_weight, ep_at * part, part, 0)
    output_parts = [output_part] + [turn(output_part, -s) for s in range(1, n_tp)]

    hidden_part = gate_weight.shape[2]
    expert_part = jnp.concatenate([gate_weight[0].T, up_weight[0].T, down_weight[0]], axis=0)
    expert_parts = lax.all_gather(expert_part, "tp", tiled=True)

    routes_mine = mine(routes)
    grad_top_mine = mine(cotangent)
    named = jnp.pad(routes_mine.astype(BF), ((0, 0), (0, LANES - top)), constant_values=-1.0)
    extra = jnp.concatenate([grad_top_mine, named], axis=1)
    tables = rotary_lanes(tokens)
    if fine:
        extra_got = gather_first(extra)
        output_parts, extra_got, tables = join(output_parts, extra_got, tables)
        output_part = jnp.concatenate(output_parts, axis=0)
        output_got = gather_first(output_part)
        extra_held, extra_got = gather_second(extra, extra_got)
    else:
        output_part = jnp.concatenate(output_parts, axis=0)
        extra_near, extra_far = gather_whole(extra)

    *mixed, normed, query, key, value, qkv_weight, logs = attend(
        inputs,
        norm_gain,
        (query_weight, key_weight, value_weight),
        tables,
        heads_width // HD,
        groups_width // HD,
        tp_at,
    )
    if fine:
        mixed, output_got, extra_held, extra_got = join(mixed, output_got, extra_held, extra_got)

    mixed = [mixed[0]] + [turn(mixed[s], s) for s in range(1, n_tp)]
    if fine:
        output_held, output_got = gather_second(output_part, output_got)
        extra_near = gather_near(extra_held, extra_got)
        mixed, output_held, output_got, extra_near = join(mixed, output_held, output_got, extra_near)
        near = gather_near(output_held, output_got)
        far = swap(near, 1)
        extra_far = swap(extra_near, 1)
    else:
        near, far = gather_whole(output_part)
    halves = gather_halves()
    output_whole = jnp.zeros((n_tp, n_ep, part, width), BF)
    for j, blocks in enumerate((near, far)):
        blocks = blocks.reshape(n_ep, n_tp // 2, part, width)
        for k in range(n_ep):
            device, half = halves[j * n_ep + k]
            for u in range(n_tp // 2):
                place = (n_tp - half * (n_tp // 2) - u) % n_tp
                output_whole = lax.dynamic_update_slice(
                    output_whole, blocks[k, u][None, None], (place, device, 0, 0)
                )
    output_whole = output_whole.reshape(n_tp * heads_width, width)

    mixed_mine = jnp.concatenate(mixed, axis=1)
    branch = mul(mixed_mine, output_whole)
    inputs_mine = mine(inputs).astype(F32)
    attended = inputs_mine + branch
    inverse_two = lax.rsqrt(jnp.mean(attended * attended, axis=-1, keepdims=True) + EPS)
    unit_two = attended * inverse_two
    routed_in = (unit_two * mixer_gain).astype(BF)
    logits = mul(routed_in, router_weight)
    ids = jnp.arange(experts, dtype=jnp.int32)
    chosen = jnp.any(routes_mine[:, :, None] == ids[None, None, :], axis=1)
    logits = jnp.where(chosen, logits, MASKED)
    weights = jnp.where(chosen, jnp.exp(logits - jnp.max(logits, axis=-1, keepdims=True)), 0.0)
    gates = weights / jnp.sum(weights, axis=-1, keepdims=True)

    router = jnp.pad(router_weight, ((0, 0), (0, LANES - experts)))
    order = jnp.concatenate([ep_at[None], jnp.full((1,), experts, jnp.int32)])
    if fine:
        got = gather_first(routed_in)
        got, gates, router, order = join(got, gates, router, order)
        held, got = gather_second(routed_in, got)
        held, got = join(held, got)
        near = gather_near(held, got)
        far = swap(near, 1)
    else:
        near, far = gather_whole(routed_in)
    out_near, out_far, gin_near, gin_far, terms = run_experts(
        order, near, far, extra_near, extra_far, router, expert_parts, top, n_tp
    )

    grad_expert = lax.psum_scatter(terms, "tp", scatter_dimension=0, tiled=True)

    if fine:
        gin = sum_cores(gin_near, swap(gin_far, 1))
        got = sum_first(gin)
        out_far, gin = join(out_far, gin)
        out_far = swap(out_far, 1)
        got, out_far = join(got, out_far)
        gin, got = sum_second(gin, got)
        out = sum_cores(out_near, out_far)
        out_got = sum_first(out)
        gin, got = join(gin, got)
        grad_in = sum_last(gin, got)
    else:
        grad_in = sum_whole(gin_near, gin_far)
    grad_gates = grad_in[:, width : width + experts] + grad_in[:, width + experts : width + 2 * experts]
    inner_gate = jnp.sum(gates * grad_gates, axis=-1, keepdims=True)
    grad_logits = (gates * (grad_gates - inner_gate)).astype(BF)
    grad_routed = grad_in[:, :width] + mul(grad_logits, router_weight, NT)
    grad_top = grad_top_mine.astype(F32)
    scaled_two = grad_routed * mixer_gain
    grad_attended = grad_top + inverse_two * (
        scaled_two - unit_two * jnp.mean(scaled_two * unit_two, axis=-1, keepdims=True)
    )
    grad_branch = grad_attended.astype(BF)
    grad_mixed = mul(grad_branch, output_whole, NT).astype(BF)
    grad_mixed = [grad_mixed[:, s * heads_width : (s + 1) * heads_width] for s in range(n_tp)]

    if fine:
        grad_mixed, out_got = join(grad_mixed, out_got)
    grad_mixed = [grad_mixed[0]] + [turn(grad_mixed[s], -s) for s in range(1, n_tp)]
    if fine:
        out, out_got = sum_second(out, out_got)

    few = -(-(1 + experts) // n_ep)
    pad = 16 * (few // 16 + 1)
    small_rows = -(-few // 8) * 8
    grad_router = mul(routed_in, grad_logits, TN)
    grad_mixer = jnp.sum(grad_routed * unit_two, axis=0)
    small = jnp.concatenate([grad_mixer[None], grad_router.T], axis=0).astype(BF)
    small = jnp.pad(small, ((0, few * n_ep - 1 - experts), (0, 0))).reshape(n_ep, few, width)
    small = jnp.pad(small, ((0, 0), (0, pad - few), (0, 0)))
    grad_output = mul(mixed_mine, grad_branch, TN).astype(BF)
    grad_output = grad_output.reshape(n_tp, n_ep, part, width).transpose(1, 0, 2, 3)
    grad_output = jnp.concatenate([grad_output.reshape(n_ep, n_tp * part, width), small], axis=1)
    if fine:
        core, chip = lax.rem(ep_at, 2), lax.div(ep_at, 2)
        grad_output = grad_output.reshape((n_ep // 2, 2) + grad_output.shape[1:])
        other_output = lax.dynamic_index_in_dim(grad_output, 1 - core, 1, False)
        grad_output = lax.dynamic_index_in_dim(grad_output, core, 1, False)
        grad_mixed, out, out_got, other_output, grad_output = join(
            grad_mixed, out, out_got, other_output, grad_output
        )
        out = sum_last(out, out_got)
        other_output = swap(other_output, 1)
    else:
        out = sum_whole(out_near, out_far)
    result_mine = (attended + out).astype(BF)

    result_mine, grad_mixed = join(result_mine, grad_mixed)
    result_steps = [step_both(result_mine, result_mine)]
    grad_qkv = attend_back(grad_mixed, query, key, value, logs, tables, tp_at)
    if fine:
        grad_qkv, result_steps[0], other_output = join(grad_qkv, result_steps[0], other_output)
    else:
        grad_qkv, result_steps[0] = join(grad_qkv, result_steps[0])

    grad_normed = mul(grad_qkv, qkv_weight, NT).astype(BF).reshape(n_tp, quarter, width)
    grad_qkv_w = mul(normed, grad_qkv, TN).astype(BF)
    if fine:
        grad_output = add(grad_output, other_output)

    def block(j):
        return lax.dynamic_index_in_dim(grad_normed, lax.rem(tp_at + j + n_tp, n_tp), 0, False)

    def chip_half(j, half):
        rows = grad_output.shape[1] // 2
        chip_rows = lax.dynamic_index_in_dim(grad_output, jnp.bitwise_xor(chip, j), 0, False)
        return chip_rows[half * rows : (half + 1) * rows]

    if fine:
        sums = join(
            *[
                jnp.concatenate([chip_half(a, half), chip_half(c, half)], axis=0)
                for half, places in ((0, ((0, 1), (2, 3))), (1, ((0, 2), (1, 3))))
                for a, c in places
            ]
        )
        got = sum_first(sums)
    result_steps.append(step_both(*result_steps[-1], 1))
    sent = step_ends(block(n_tp - 1), block(1 - n_tp), 0, 1)
    if fine:
        sent, result_steps[-1], got, grad_qkv_w, grad_expert = join(
            sent, result_steps[-1], got, grad_qkv_w, grad_expert
        )
        sums, got = sum_second(sums, got)
    else:
        sent, result_steps[-1], grad_qkv_w, grad_expert = join(
            sent, result_steps[-1], grad_qkv_w, grad_expert
        )
    grad_qkv_w = lax.psum(grad_qkv_w, "ep")
    sent = by_side(sent, 0, 1)
    result_last = None
    for t in range(2, n_tp):
        sent = step_both(add(block(n_tp - t), sent[0]), add(block(t - n_tp), sent[1]), 0, t)
        if t < n_tp - 1:
            result_last = step_ends(*result_steps[-1], t, n_tp - 1)
            if fine:
                sent, result_last, got, sums = join(sent, result_last, got, sums)
                grad_output = sum_last(sums, got).astype(BF)
            else:
                sent, result_last = join(sent, result_last)
                grad_output = lax.psum_scatter(grad_output, "ep", scatter_dimension=0, tiled=False)
            pieces = [
                jnp.concatenate([grad_output[s * part : (s + 1) * part], grad_output[n_tp * part :][:small_rows]], axis=0)
                for s in range(n_tp)
            ]
    got = [turn(pieces[s], -s) for s in range(1, n_tp)]
    sent, result_steps, result_last = join(sent, result_steps, result_last)
    grad_normed = block(0).astype(F32) + sent[0].astype(F32) + sent[1].astype(F32)
    inverse_one = lax.rsqrt(jnp.mean(inputs_mine * inputs_mine, axis=-1, keepdims=True) + EPS)
    unit_one = inputs_mine * inverse_one
    scaled_one = grad_normed * norm_gain
    grad_inputs = grad_attended + inverse_one * (
        scaled_one - unit_one * jnp.mean(scaled_one * unit_one, axis=-1, keepdims=True)
    )
    grad_inputs = grad_inputs.astype(BF)
    grad_norm = jnp.sum(grad_normed * unit_one, axis=0)
    used = -(-(part + small_rows + 1) // 32) * 32

    grad_inputs, grad_norm = join(grad_inputs, grad_norm)
    input_steps = [step_both(grad_inputs, grad_inputs)]
    grad_norm = grad_norm[None]
    norm_got = [turn(grad_norm, s) for s in range(1, n_tp)]
    got, norm_got, input_steps[0] = join(got, norm_got, input_steps[0])
    grad_norm = (grad_norm + sum(norm_got))[0]
    grad_output = (pieces[0].astype(F32) + sum(v.astype(F32) for v in got)).astype(BF)
    grad_output = jnp.pad(grad_output, ((0, used - grad_output.shape[0]), (0, 0)))
    grad_output = grad_output.at[used - 1].set(grad_norm.astype(BF))
    if fine:
        got = [swap(grad_output, k) for k in (2, 4, 6)]
    grad_expert = grad_expert.reshape(3, -1, width).astype(F32)
    grad_gate_w, grad_up_w, grad_down_w = grad_expert[0].T, grad_expert[1].T, grad_expert[2]
    for t in range(1, n_tp - 2):
        input_steps.append(step_both(*input_steps[-1], t))
    if fine:
        got, input_steps[-1], grad_gate_w, grad_up_w, grad_down_w = join(
            got, input_steps[-1], grad_gate_w, grad_up_w, grad_down_w
        )
        near = jnp.concatenate([grad_output] + got, axis=0)
        far = swap(near, 1)
        far, grad_qkv_w = join(far, grad_qkv_w)
        devices = jnp.stack([jnp.bitwise_xor(ep_at, jnp.int32(k)) for k in (0, 2, 4, 6, 1, 3, 5, 7)])
        grad_output, small, grad_norm = set_rows(devices, near, far, part, small_rows)
        small = small.reshape(n_ep, small_rows, width)
        grad_norm = grad_norm[0]
    else:
        gathered = lax.all_gather(grad_output, "ep")
        small = gathered[:, part : part + small_rows].astype(F32)
        grad_norm = jnp.sum(gathered[:, used - 1].astype(F32), axis=0)
        grad_output = gathered[:, :part].reshape(heads_width, width).astype(F32)
    small = small[:, :few].reshape(n_ep * few, width)[: 1 + experts]
    result = spread(result_mine, result_steps, result_last)
    input_last = step_ends(*input_steps[-1], n_tp - 2, n_tp - 1)
    grad_qkv_w = grad_qkv_w.astype(F32)
    qkv_grads = (
        grad_qkv_w[:, :heads_width],
        grad_qkv_w[:, heads_width : heads_width + groups_width],
        grad_qkv_w[:, heads_width + groups_width :],
    )
    grad_norm, small, grad_output, input_last, qkv_grads, result = join(
        grad_norm, small, grad_output, input_last, qkv_grads, result
    )
    grad_inputs = spread(grad_inputs, input_steps, input_last)
    return (
        result,
        grad_inputs,
        grad_norm,
        *qkv_grads,
        grad_output,
        small[0],
        small[1:].T,
        grad_gate_w[None],
        grad_up_w[None],
        grad_down_w[None],
    )


def solution(mesh):
    placed = (
        P("ep", None),
        P("ep", None),
        P(),
        P(None, "tp"),
        P(None, "tp"),
        P(None, "tp"),
        P("tp", None),
        P(),
        P(),
        P("ep", None, "tp"),
        P("ep", None, "tp"),
        P("ep", "tp", None),
        P("ep", None),
    )
    return jax.shard_map(
        body,
        mesh=mesh,
        in_specs=placed,
        out_specs=(
            P("ep", None),
            P("ep", None),
            P(),
            P(None, "tp"),
            P(None, "tp"),
            P(None, "tp"),
            P("tp", None),
            P(),
            P(),
            P("ep", None, "tp"),
            P("ep", None, "tp"),
            P("ep", "tp", None),
        ),
        check_vma=False,
    )
```

time: 621 us -> 525 us (0.85)
  between operations: 62.3 us -> 15.6 us
  waiting for transfers between devices: 212 us -> 173 us
  other arithmetic: 59.8 us -> 51.2 us
  local copies, waits for them, and re-layouts: 65.2 us -> 57.6 us
    ppermute x30 -> x15, waiting for transfers between devices: 111 us -> 34.6 us  [the longest x3 17.3 us: step_ends(): lax.ppermute(give, 'tp', pairs + [(n - 1 - i, n - 1 - j) for i, j in pairs])]
    ppermute x6 -> x15, waiting for transfers between devices: 14.8 us -> 51.4 us  [turn(): return lax.ppermute(x, 'tp', [(i, (i + by) % n) for i in range(n)])]
    ppermute x6 -> x15, starting transfers between devices: 21.5 us -> 43.2 us  [turn(): return lax.ppermute(x, 'tp', [(i, (i + by) % n) for i in range(n)])]
    ppermute x31 -> x34, waiting for transfers between devices: 68.2 us -> 87.3 us  [swap(): lax.ppermute(x, 'ep', [(i, i ^ bit) for i in range(lax.axis_size('ep'))])]
    all_to_all x2 -> x0, waiting for transfers between devices: 17.8 us -> none  [the longest x1 17.8 us: body(): lax.all_to_all(grad_mixed, 'tp', split_axis=1, concat_axis=0, tiled=True)]
    ppermute x30 -> x15, starting transfers between devices: 55.1 us -> 38.3 us  [the longest x12 31.1 us: step_both(): return (lax.ppermute(right, 'tp', pairs), lax.ppermute(left, 'tp', mirror))]
    all_to_all x2 -> x0, starting transfers between devices: 7.12 us -> none  [the longest x1 3.63 us: body(): lax.all_to_all(mixed, 'tp', split_axis=0, concat_axis=1, tiled=True)]
    add x7 -> x4, other arithmetic: 7.39 us -> 0.36 us  [sum_last(): s[:half].astype(F32) + g.astype(F32)]
  transfers between devices with their start and end apart: 71 -> 67, of which waited for: 29 -> 32; matrix products, arithmetic and copies ran while one was open for 17% -> 21% of each run, Pallas kernels for 7% -> 9%
where the time goes in v4:
time: 525 us; the launch traced here: 518 us
  waiting for transfers between devices  173 us (33%)
  starting transfers between devices  112 us (21%)
  Pallas kernels  88.8 us (17%)
  local copies, waits for them, and re-layouts  57.6 us (11%)
  other arithmetic  51.2 us (10%)
  matrix products  19.1 us (4%)
  between operations  15.6 us (3%)
    ppermute x34, waiting for transfers between devices, swap(): lax.ppermute(x, 'ep', [(i, i ^ bit) for i in range(lax.axis_size('ep'))])  87.3 us
    ppermute x15, waiting for transfers between devices, turn(): return lax.ppermute(x, 'tp', [(i, (i + by) % n) for i in range(n)])  51.4 us
    pallas_call x1, Pallas kernels, run_experts(): pl.pallas_call(functools.partial(expert_kernel, top=top, count=count), gr...  44.3 us
    ppermute x15, starting transfers between devices, turn(): return lax.ppermute(x, 'tp', [(i, (i + by) % n) for i in range(n)])  43.2 us
    ppermute x12, starting transfers between devices, step_both(): return (lax.ppermute(right, 'tp', pairs), lax.ppermute(left, 'tp', mirror))  31.1 us
    ppermute x34, starting transfers between devices, swap(): lax.ppermute(x, 'ep', [(i, i ^ bit) for i in range(lax.axis_size('ep'))])  30 us
    convert_element_type x11, other arithmetic, add(): return (a.astype(F32) + b.astype(F32)).astype(BF)  23 us
    pallas_call x1, Pallas kernels, attend(): pl.pallas_call(attend_kernel, in_specs=[SMEM] + [VMEM] * 8, out_shape=[ja...  21.5 us
  transfers between devices with their start and end apart: 67, of which 32 were waited for; matrix products, arithmetic and copies ran while one was open for 21% of the time, Pallas kernels for 9%

profile of v4, /device:TPU:0, one launch (start us, length us, event | category | flops | bytes accessed | tf_op | source)
XLA Modules:
  0.0 517.9 jit_solution(1407882624353072481)
XLA Ops:
  8.5 5.1 collective-permute-start
  23.5 1.9 fusion.23
  26.1 1.6 collective-permute-done.3
  34.7 21.5 %shard_map.220 = (bf16[256,384]{1,0:T(8,128)(2,1)S(1)}, bf16[256,384]{1,0:T(8,128)(2,1)S(1)}, bf16[256,384]{1,0:T(8,128)(2,1)S(1)}, bf16[256,384]{1,0:T(8,128)(2...) custom-call(s32[1]{0:T(128)} %bitcast.8.at_ref, ...), custom_call_target="tpu_custom_call" | custom-call | flops 23000000512 | tf_op jit(solution)/shard_map/pallas_call | solution.py:121
  61.4 1.8 pad.23.router_ref
  63.8 2.5 collective-permute-start.9
  67.4 1.7 collective-permute-start.11
  69.2 2.2 pad_maximum_fusion.extra_near_ref
  71.4 6.2 %collective-permute-done.9 = bf16[256,384]{1,0:T(8,128)(2,1)S(1)} collective-permute-done((bf16[256,384]{1,0:T(8,128)(2,1)S(1)}, bf16[256,384]{1,0:T(8,128)(2,1)S(1)}, u32[]{:S(2)}, u32[]{:S(2)}) %collective-permute-start.9) | collective-permute-done | bytes 196640 | tf_op jit(solution)/shard_map/ppermute | solution.py:384
  77.5 12.5 %collective-permute-done.10 = bf16[256,384]{1,0:T(8,128)(2,1)S(1)} collective-permute-done((bf16[256,384]{1,0:T(8,128)(2,1)S(1)}, bf16[256,384]{1,0:T(8,128)(2,1)S(1)}, u32[]{:S(2)}, u32[]{:S(2)}) %collective-permute-start.10) | collective-permute-done | bytes 196640 | tf_op jit(solution)/shard_map/ppermute | solution.py:384
  96.7 3.5 collective-permute-done.14
  100.6 3.2 multiply_reduce_fusion.2
  106.9 8.4 %collective-permute-done.15 = bf16[128,1536]{1,0:T(8,128)(2,1)S(1)} collective-permute-done((bf16[128,1536]{1,0:T(8,128)(2,1)S(1)}, bf16[128,1536]{1,0:T(8,128)(2,1)S(1)}, u32[]{:S(2)}, u32[]{:S(2)}) %collective-permute-start.15) | collective-permute-done | bytes 393248 | tf_op jit(solution)/shard_map/ppermute | solution.py:379
  117.8 17.5 %collective-permute-done.17 = bf16[256,1536]{1,0:T(8,128)(2,1)S(1)} collective-permute-done((bf16[256,1536]{1,0:T(8,128)(2,1)S(1)}, bf16[256,1536]{1,0:T(8,128)(2,1)S(1)}, u32[]{:S(2)}, u32[]{:S(2)}) %collective-permute-start.17) | collective-permute-done | bytes 786464 | tf_op jit(solution)/shard_map/ppermute | solution.py:379
  139.2 6.0 %collective-permute-done.19.far_ref = bf16[1024,1536]{1,0:T(8,128)(2,1)} collective-permute-done((bf16[1024,1536]{1,0:T(8,128)(2,1)}, bf16[1024,1536]{1,0:T(8,128)(2,1)}, u32[]{:S(2)}, u32[]{:S(2)}) %collective-permute-start.19) | collective-permute-done | bytes 3145760 | tf_op jit(solution)/shard_map/ppermute | solution.py:379
  145.2 44.3 %shard_map.221 = (bf16[1024,1536]{1,0:T(8,128)(2,1)}, bf16[1024,1536]{1,0:T(8,128)(2,1)}, bf16[1024,1664]{1,0:T(8,128)(2,1)}, bf16[1024,1664]{1,0:T(8,128)(2,1)}, bf16[1536,1536]{1,0:T(8,128)(2,1)}) custom-call(s32[2]{0:T(128)} %pad_add_fusion.order_ref, bf16[1024,1536]{1,0:T(8,128)(2,1)} %constant_dynamic-update-slice_fusion.8.near_ref, ...), custom_call_target="tpu_custom_call" | custom-call | flops 46000001024 | tf_op jit(solution)/shard_map/pallas_call | solution.py:317
  189.7 6.1 %collective-permute-done.21 = bf16[1024,1664]{1,0:T(8,128)(2,1)S(1)} collective-permute-done((bf16[1024,1664]{1,0:T(8,128)(2,1)}, bf16[1024,1664]{1,0:T(8,128)(2,1)S(1)}, u32[]{:S(2)}, u32[]{:S(2)}) %collective-permute-start.21) | collective-permute-done | bytes 3407904 | tf_op jit(solution)/shard_map/ppermute | solution.py:379
  195.8 4.3 add_convert_fusion.3
  204.3 17.4 %collective-permute-done.22 = bf16[256,1664]{1,0:T(8,128)(2,1)} collective-permute-done((bf16[256,1664]{1,0:T(8,128)(2,1)}, bf16[256,1664]{1,0:T(8,128)(2,1)}, u32[]{:S(2)}, u32[]{:S(2)}) %collective-permute-start.22) | collective-permute-done | bytes 852000 | tf_op jit(solution)/shard_map/ppermute | solution.py:379
  223.0 1.8 add_convert_fusion.2
  224.8 1.6 add_convert_fusion.1
  227.5 4.1 add_convert_fusion.9
  231.6 1.8 collective-permute-start.27
  234.8 4.5 collective-permute-done.25
  242.5 1.7 multiply_add_fusion
  245.6 2.5 copy.48
  248.2 4.4 convolution_convert_fusion.3
  252.7 1.9 collective-permute-done.27
  254.6 17.8 %collective-permute-start.29 = (bf16[256,384]{1,0:T(8,128)(2,1)S(1)}, bf16[256,384]{1,0:T(8,128)(2,1)S(1)}, u32[]{:S(2)}, u32[]{:S(2)}) collective-permute-start(bf16[256,384]{1,0:T(8,128)(2,1)S(1)} %get-tuple-element.261), channel_id=1, source_target_pairs={{0,3},{1,0},{2,1},{3,2},{4,7},{5,4},{6,5},{7,6},{8,11},{9,8},{10,9... | collective-permute-start | bytes 589832 | tf_op jit(solution)/shard_map/ppermute | solution.py:384
  278.4 3.7 collective-permute-done.29.refs_1_
  282.1 26.8 %collective-permute-done.30.refs_2_ = bf16[256,384]{1,0:T(8,128)(2,1)S(1)} collective-permute-done((bf16[256,384]{1,0:T(8,128)(2,1)S(1)}, bf16[256,384]{1,0:T(8,128)(2,1)S(1)}, u32[]{:S(2)}, u32[]{:S(2)}) %collective-permute-start.30) | collective-permute-done | bytes 196640 | tf_op jit(solution)/shard_map/ppermute | solution.py:384
  309.5 4.6 collective-permute-start.34
  315.5 20.9 %shard_map.222 = bf16[1024,640]{1,0:T(8,128)(2,1)S(1)} custom-call(s32[1]{0:T(128)} %bitcast.8.at_ref, bf16[6,1024,64]{2,1,0:T(8,128)(2,1)} %get-tuple-element.190.q_ref, bf16[2,1024,64]{2,1,0:T(8,128)(2,1)S(1)} %get-tuple-element.191.k_ref, bf16[2,1024,64]{2,1,0:T(8,128)(2,1)S(1)} %copy-done.6, f32[6,1,1024]{2,1,0:T(1,128)S(1)} %get-tuple-element.193.log_ref, ...), custom_call_target="tpu_custom_call" | custom-call | flops 23000000512 | tf_op jit(solution)/shard_map/pallas_call | solution.py:214
  336.5 2.9 convolution_convert_fusion.1
  339.4 1.7 copy-done.12
  342.0 4.6 collective-permute-start.37
  348.6 2.4 add_convert_fusion
  357.0 5.8 %convolution_convert_fusion.2 = bf16[1536,640]{1,0:T(8,128)(2,1)} fusion(bf16[1024,1536]{1,0:T(8,128)(2,1)} %get-tuple-element.292, bf16[1024,640]{1,0:T(8,128)(2,1)S(1)} %shard_map.222), kind=kOutput, calls=%fused_computation.8 | convolution fusion | flops 2014248960 | bytes 6422528 | tf_op jit(solution)/shard_map/dot_general | solution.py:27
  362.8 8.2 %collective-permute-done.40 = bf16[208,1536]{1,0:T(8,128)(2,1)} collective-permute-done((bf16[208,1536]{1,0:T(8,128)(2,1)}, bf16[208,1536]{1,0:T(8,128)(2,1)}, u32[]{:S(2)}, u32[]{:S(2)}) %collective-permute-start.40) | collective-permute-done | bytes 639008 | tf_op jit(solution)/shard_map/ppermute | solution.py:379
  372.4 1.6 convert_element_type.428
  374.1 2.0 slice.499
  377.6 5.7 %collective-permute-start.42 = (bf16[256,1536]{1,0:T(8,128)(2,1)}, bf16[256,1536]{1,0:T(8,128)(2,1)}, u32[]{:S(2)}, u32[]{:S(2)}) collective-permute-start(bf16[256,1536]{1,0:T(8,128)(2,1)} %get-tuple-element.403), channel_id=1, source_target_pairs={{0,1},{1,2},{4,5},{5,6},{8,9},{9,10},{12,13},{13,14},{16,17},{17,1... | collective-permute-start | bytes 2359304 | tf_op jit(solution)/shard_map/ppermute | solution.py:391
  384.9 2.1 broadcast_select_fusion.1
  395.9 2.9 collective-permute-done.45
  398.8 2.1 collective-permute-done.46
  400.9 5.9 %collective-permute-done.44 = bf16[256,1536]{1,0:T(8,128)(2,1)} collective-permute-done((bf16[256,1536]{1,0:T(8,128)(2,1)}, bf16[256,1536]{1,0:T(8,128)(2,1)}, u32[]{:S(2)}, u32[]{:S(2)}) %collective-permute-start.44) | collective-permute-done | bytes 786464 | tf_op jit(solution)/shard_map/ppermute | solution.py:399
  408.0 1.9 fusion.17
  413.9 6.1 %collective-permute-start.47 = (bf16[56,1536]{1,0:T(8,128)(2,1)S(1)}, bf16[56,1536]{1,0:T(8,128)(2,1)S(1)}, u32[]{:S(2)}, u32[]{:S(2)}) collective-permute-start(bf16[56,1536]{1,0:T(8,128)(2,1)S(1)} %get-tuple-element.432), channel_id=1, source_target_pairs={{0,3},{1,0},{2,1},{3,2},{4,7},{5,4},{6,5},{7,6},{8,11},{9,8},{10,9... | collective-permute-start | bytes 516104 | tf_op jit(solution)/shard_map/ppermute | solution.py:384
  420.9 8.5 %collective-permute-done.50 = bf16[256,1536]{1,0:T(8,128)(2,1)S(1)} collective-permute-done((bf16[256,1536]{1,0:T(8,128)(2,1)S(1)}, bf16[256,1536]{1,0:T(8,128)(2,1)S(1)}, u32[]{:S(2)}, u32[]{:S(2)}) %collective-permute-start.50) | collective-permute-done | bytes 786464 | tf_op jit(solution)/shard_map/ppermute | solution.py:391
  429.4 2.7 collective-permute-done.51
  433.6 9.7 %collective-permute-start.55 = (bf16[256,1536]{1,0:T(8,128)(2,1)S(1)}, bf16[256,1536]{1,0:T(8,128)(2,1)S(1)}, u32[]{:S(2)}, u32[]{:S(2)}) collective-permute-start(bf16[256,1536]{1,0:T(8,128)(2,1)S(1)} %fusion.13), channel_id=1, source_target_pairs={{0,1},{1,2},{2,3},{4,5},{5,6},{6,7},{8,9},{9,10},{10,11},{12,13},{... | collective-permute-start | bytes 2359304 | tf_op jit(solution)/shard_map/ppermute | solution.py:391
  444.6 1.9 broadcast.161.clone.1
  446.5 2.1 constant_dynamic-update-slice_fusion.23
  448.5 2.1 constant_dynamic-update-slice_fusion.22
  451.5 2.1 constant_dynamic-update-slice_fusion.20
  453.6 2.1 constant_dynamic-update-slice_fusion.19
  455.7 2.6 collective-permute-start.52
  459.5 2.6 collective-permute-start.54
  469.5 1.9 broadcast.161.clone
  475.4 6.0 %collective-permute-done.61 = bf16[256,1536]{1,0:T(8,128)(2,1)S(1)} collective-permute-done((bf16[256,1536]{1,0:T(8,128)(2,1)S(1)}, bf16[256,1536]{1,0:T(8,128)(2,1)S(1)}, u32[]{:S(2)}, u32[]{:S(2)}) %collective-permute-start.61) | collective-permute-done | bytes 786464 | tf_op jit(solution)/shard_map/ppermute | solution.py:391
  488.4 2.1 shard_map.223
  490.6 3.0 slice.502
  495.5 11.4 %collective-permute-done.63 = bf16[256,1536]{1,0:T(8,128)(2,1)} collective-permute-done((bf16[256,1536]{1,0:T(8,128)(2,1)}, bf16[256,1536]{1,0:T(8,128)(2,1)}, u32[]{:S(2)}, u32[]{:S(2)}) %collective-permute-start.63) | collective-permute-done | bytes 786464 | tf_op jit(solution)/shard_map/ppermute | solution.py:399
  508.1 2.1 constant_dynamic-update-slice_fusion.13
  (369 shorter events, 118.0 us)
Async XLA Ops:
  7.2 132.0 %all-gather.2.cloned.1.call-start = ((), (), s32[]{:S(2)}) async-start(), calls=%async_computation.1 | async-start | bytes 5898240 | tf_op jit(solution)/shard_map/all_gather | solution.py:515
  8.5 17.0 %collective-permute-start = (bf16[48,1536]{1,0:T(8,128)(2,1)S(1)}, bf16[48,1536]{1,0:T(8,128)(2,1)S(1)}, u32[]{:S(2)}, u32[]{:S(2)}) collective-permute-start(bf16[48,1536]{1,0:T(8,128)(2,1)S(1)} %constant_dynamic-slice_fusion.2), channel_id=1, source_target_pairs={{0,3},{1,0},{2,1},{3,2},{4,7},{5,4},{6,5},{7,6},{8,11},{9,8},{10,9... | collective-permute-start | bytes 442376 | tf_op jit(solution)/shard_map/ppermute | solution.py:384
  13.6 12.5 %collective-permute-start.1 = (bf16[48,1536]{1,0:T(8,128)(2,1)S(1)}, bf16[48,1536]{1,0:T(8,128)(2,1)S(1)}, u32[]{:S(2)}, u32[]{:S(2)}) collective-permute-start(bf16[48,1536]{1,0:T(8,128)(2,1)S(1)} %constant_dynamic-slice_fusion.2), channel_id=1, source_target_pairs={{0,2},{1,3},{2,0},{3,1},{4,6},{5,7},{6,4},{7,5},{8,10},{9,11},{10,... | collective-permute-start | bytes 442376 | tf_op jit(solution)/shard_map/ppermute | solution.py:384
  13.6 12.5 %collective-permute-start.2 = (bf16[48,1536]{1,0:T(8,128)(2,1)S(1)}, bf16[48,1536]{1,0:T(8,128)(2,1)S(1)}, u32[]{:S(2)}, u32[]{:S(2)}) collective-permute-start(bf16[48,1536]{1,0:T(8,128)(2,1)S(1)} %constant_dynamic-slice_fusion.2), channel_id=1, source_target_pairs={{0,1},{1,2},{2,3},{3,0},{4,5},{5,6},{6,7},{7,4},{8,9},{9,10},{10,1... | collective-permute-start | bytes 442376 | tf_op jit(solution)/shard_map/ppermute | solution.py:384
  16.8 10.9 %collective-permute-start.3 = (bf16[128,1664]{1,0:T(8,128)(2,1)S(1)}, bf16[128,1664]{1,0:T(8,128)(2,1)}, u32[]{:S(2)}, u32[]{:S(2)}) collective-permute-start(bf16[128,1664]{1,0:T(8,128)(2,1)S(1)} %get-tuple-element.419), channel_id=1, source_target_pairs={{0,8},{4,12},{8,0},{12,4},{16,24},{20,28},{24,16},{28,20},{1,9},{5... | collective-permute-start | bytes 1277960 | tf_op jit(solution)/shard_map/ppermute | solution.py:379
  18.4 10.5 %collective-permute-start.4 = (bf16[128,1664]{1,0:T(8,128)(2,1)S(1)}, bf16[128,1664]{1,0:T(8,128)(2,1)}, u32[]{:S(2)}, u32[]{:S(2)}) collective-permute-start(bf16[128,1664]{1,0:T(8,128)(2,1)S(1)} %get-tuple-element.418), channel_id=1, source_target_pairs={{0,16},{4,20},{8,24},{12,28},{16,0},{20,4},{24,8},{28,12},{1,17},{... | collective-permute-start | bytes 1277960 | tf_op jit(solution)/shard_map/ppermute | solution.py:379
  23.4 339.4 %reduce-scatter.2.cloned.1.call-start = ((), (), s32[]{:S(2)}) async-start(), calls=%async_computation.2 | async-start | bytes 5898240 | tf_op jit(solution)/shard_map/reduce_scatter | solution.py:596
  28.9 27.2 %collective-permute-start.5 = (bf16[96,1536]{1,0:T(8,128)(2,1)S(1)}, bf16[96,1536]{1,0:T(8,128)(2,1)S(1)}, u32[]{:S(2)}, u32[]{:S(2)}) collective-permute-start(bf16[96,1536]{1,0:T(8,128)(2,1)S(1)} %pad_maximum_fusion.13), channel_id=1, source_target_pairs={{0,8},{4,12},{8,0},{12,4},{16,24},{20,28},{24,16},{28,20},{1,9},{5... | collective-permute-start | bytes 884744 | tf_op jit(solution)/shard_map/ppermute | solution.py:379
  29.5 26.6 %collective-permute-start.6 = (bf16[96,1536]{1,0:T(8,128)(2,1)S(1)}, bf16[96,1536]{1,0:T(8,128)(2,1)S(1)}, u32[]{:S(2)}, u32[]{:S(2)}) collective-permute-start(bf16[96,1536]{1,0:T(8,128)(2,1)S(1)} %pad_maximum_fusion.14), channel_id=1, source_target_pairs={{0,16},{4,20},{8,24},{12,28},{16,0},{20,4},{24,8},{28,12},{1,17},{... | collective-permute-start | bytes 884744 | tf_op jit(solution)/shard_map/ppermute | solution.py:379
  32.5 23.7 %collective-permute-start.7 = (bf16[256,1664]{1,0:T(8,128)(2,1)S(1)}, bf16[256,1664]{1,0:T(8,128)(2,1)S(1)}, u32[]{:S(2)}, u32[]{:S(2)}) collective-permute-start(bf16[256,1664]{1,0:T(8,128)(2,1)S(1)} %get-tuple-element.214), channel_id=1, source_target_pairs={{0,16},{4,20},{8,24},{12,28},{16,0},{20,4},{24,8},{28,12},{1,17},{... | collective-permute-start | bytes 2555912 | tf_op jit(solution)/shard_map/ppermute | solution.py:379
  33.1 23.1 %collective-permute-start.8 = (bf16[256,1664]{1,0:T(8,128)(2,1)S(1)}, bf16[256,1664]{1,0:T(8,128)(2,1)S(1)}, u32[]{:S(2)}, u32[]{:S(2)}) collective-permute-start(bf16[256,1664]{1,0:T(8,128)(2,1)S(1)} %get-tuple-element.216), channel_id=1, source_target_pairs={{0,8},{4,12},{8,0},{12,4},{16,24},{20,28},{24,16},{28,20},{1,9},{5... | collective-permute-start | bytes 2555912 | tf_op jit(solution)/shard_map/ppermute | solution.py:379
  58.2 32.8 %collective-permute-start.12 = (bf16[192,1536]{1,0:T(8,128)(2,1)}, bf16[192,1536]{1,0:T(8,128)(2,1)}, u32[]{:S(2)}, u32[]{:S(2)}) collective-permute-start(bf16[192,1536]{1,0:T(8,128)(2,1)} %pad_maximum_fusion.11), channel_id=1, source_target_pairs={{0,16},{4,20},{8,24},{12,28},{16,0},{20,4},{24,8},{28,12},{1,17},{... | collective-permute-start | bytes 1769480 | tf_op jit(solution)/shard_map/ppermute | solution.py:379
  59.7 31.4 %collective-permute-start.13 = (bf16[192,1536]{1,0:T(8,128)(2,1)}, bf16[192,1536]{1,0:T(8,128)(2,1)}, u32[]{:S(2)}, u32[]{:S(2)}) collective-permute-start(bf16[192,1536]{1,0:T(8,128)(2,1)} %pad_maximum_fusion.12), channel_id=1, source_target_pairs={{0,8},{4,12},{8,0},{12,4},{16,24},{20,28},{24,16},{28,20},{1,9},{5... | collective-permute-start | bytes 1769480 | tf_op jit(solution)/shard_map/ppermute | solution.py:379
  63.8 13.7 %collective-permute-start.9 = (bf16[256,384]{1,0:T(8,128)(2,1)S(1)}, bf16[256,384]{1,0:T(8,128)(2,1)S(1)}, u32[]{:S(2)}, u32[]{:S(2)}) collective-permute-start(bf16[256,384]{1,0:T(8,128)(2,1)S(1)} %get-tuple-element.207), channel_id=1, source_target_pairs={{0,1},{1,2},{2,3},{3,0},{4,5},{5,6},{6,7},{7,4},{8,9},{9,10},{10,1... | collective-permute-start | bytes 589832 | tf_op jit(solution)/shard_map/ppermute | solution.py:384
  66.3 23.8 %collective-permute-start.10 = (bf16[256,384]{1,0:T(8,128)(2,1)S(1)}, bf16[256,384]{1,0:T(8,128)(2,1)S(1)}, u32[]{:S(2)}, u32[]{:S(2)}) collective-permute-start(bf16[256,384]{1,0:T(8,128)(2,1)S(1)} %get-tuple-element.208), channel_id=1, source_target_pairs={{0,2},{1,3},{2,0},{3,1},{4,6},{5,7},{6,4},{7,5},{8,10},{9,11},{10,... | collective-permute-start | bytes 589832 | tf_op jit(solution)/shard_map/ppermute | solution.py:384
  67.4 23.6 %collective-permute-start.11 = (bf16[256,384]{1,0:T(8,128)(2,1)S(1)}, bf16[256,384]{1,0:T(8,128)(2,1)S(1)}, u32[]{:S(2)}, u32[]{:S(2)}) collective-permute-start(bf16[256,384]{1,0:T(8,128)(2,1)S(1)} %get-tuple-element.209), channel_id=1, source_target_pairs={{0,3},{1,0},{2,1},{3,2},{4,7},{5,4},{6,5},{7,6},{8,11},{9,8},{10,9... | collective-permute-start | bytes 589832 | tf_op jit(solution)/shard_map/ppermute | solution.py:384
  104.1 11.2 %collective-permute-start.15 = (bf16[128,1536]{1,0:T(8,128)(2,1)S(1)}, bf16[128,1536]{1,0:T(8,128)(2,1)S(1)}, u32[]{:S(2)}, u32[]{:S(2)}) collective-permute-start(bf16[128,1536]{1,0:T(8,128)(2,1)S(1)} %get-tuple-element.427), channel_id=1, source_target_pairs={{0,8},{4,12},{8,0},{12,4},{16,24},{20,28},{24,16},{28,20},{1,9},{5... | collective-permute-start | bytes 1179656 | tf_op jit(solution)/shard_map/ppermute | solution.py:379
  105.6 10.9 %collective-permute-start.16 = (bf16[128,1536]{1,0:T(8,128)(2,1)S(1)}, bf16[128,1536]{1,0:T(8,128)(2,1)S(1)}, u32[]{:S(2)}, u32[]{:S(2)}) collective-permute-start(bf16[128,1536]{1,0:T(8,128)(2,1)S(1)} %get-tuple-element.426), channel_id=1, source_target_pairs={{0,16},{4,20},{8,24},{12,28},{16,0},{20,4},{24,8},{28,12},{1,17},{... | collective-permute-start | bytes 1179656 | tf_op jit(solution)/shard_map/ppermute | solution.py:379
  116.6 18.6 %collective-permute-start.17 = (bf16[256,1536]{1,0:T(8,128)(2,1)S(1)}, bf16[256,1536]{1,0:T(8,128)(2,1)S(1)}, u32[]{:S(2)}, u32[]{:S(2)}) collective-permute-start(bf16[256,1536]{1,0:T(8,128)(2,1)S(1)} %pad_maximum_fusion.4), channel_id=1, source_target_pairs={{0,16},{4,20},{8,24},{12,28},{16,0},{20,4},{24,8},{28,12},{1,17},{... | collective-permute-start | bytes 2359304 | tf_op jit(solution)/shard_map/ppermute | solution.py:379
  117.2 18.3 %collective-permute-start.18 = (bf16[256,1536]{1,0:T(8,128)(2,1)S(1)}, bf16[256,1536]{1,0:T(8,128)(2,1)S(1)}, u32[]{:S(2)}, u32[]{:S(2)}) collective-permute-start(bf16[256,1536]{1,0:T(8,128)(2,1)S(1)} %pad_maximum_fusion.5), channel_id=1, source_target_pairs={{0,8},{4,12},{8,0},{12,4},{16,24},{20,28},{24,16},{28,20},{1,9},{5... | collective-permute-start | bytes 2359304 | tf_op jit(solution)/shard_map/ppermute | solution.py:379
  117.8 21.4 %collective-permute-start.20 = (bf16[1024,1664]{1,0:T(8,128)(2,1)S(1)}, bf16[1024,1664]{1,0:T(8,128)(2,1)}, u32[]{:S(2)}, u32[]{:S(2)}) collective-permute-start(bf16[1024,1664]{1,0:T(8,128)(2,1)S(1)} %pad_maximum_fusion.extra_near_ref), channel_id=1, source_target_pairs={{0,4},{4,0},{8,12},{12,8},{16,20},{20,16},{24,28},{28,24},{1,5},{5... | collective-permute-start | bytes 10223624 | tf_op jit(solution)/shard_map/ppermute | solution.py:379
  139.2 6.0 %collective-permute-start.19 = (bf16[1024,1536]{1,0:T(8,128)(2,1)}, bf16[1024,1536]{1,0:T(8,128)(2,1)}, u32[]{:S(2)}, u32[]{:S(2)}) collective-permute-start(bf16[1024,1536]{1,0:T(8,128)(2,1)} %constant_dynamic-update-slice_fusion.8.near_ref), channel_id=1, source_target_pairs={{0,4},{4,0},{8,12},{12,8},{16,20},{20,16},{24,28},{28,24},{1,5},{5... | collective-permute-start | bytes 9437192 | tf_op jit(solution)/shard_map/ppermute | solution.py:379
  189.5 6.3 %collective-permute-start.21 = (bf16[1024,1664]{1,0:T(8,128)(2,1)}, bf16[1024,1664]{1,0:T(8,128)(2,1)S(1)}, u32[]{:S(2)}, u32[]{:S(2)}) collective-permute-start(bf16[1024,1664]{1,0:T(8,128)(2,1)} %get-tuple-element.239), channel_id=1, source_target_pairs={{0,4},{4,0},{8,12},{12,8},{16,20},{20,16},{24,28},{28,24},{1,5},{5... | collective-permute-start | bytes 10223624 | tf_op jit(solution)/shard_map/ppermute | solution.py:379
  200.1 22.9 %collective-permute-start.24 = (bf16[1024,1536]{1,0:T(8,128)(2,1)}, bf16[1024,1536]{1,0:T(8,128)(2,1)}, u32[]{:S(2)}, u32[]{:S(2)}) collective-permute-start(bf16[1024,1536]{1,0:T(8,128)(2,1)} %get-tuple-element.245), channel_id=1, source_target_pairs={{0,4},{4,0},{8,12},{12,8},{16,20},{20,16},{24,28},{28,24},{1,5},{5... | collective-permute-start | bytes 9437192 | tf_op jit(solution)/shard_map/ppermute | solution.py:379
  200.2 21.5 %collective-permute-start.22 = (bf16[256,1664]{1,0:T(8,128)(2,1)}, bf16[256,1664]{1,0:T(8,128)(2,1)}, u32[]{:S(2)}, u32[]{:S(2)}) collective-permute-start(bf16[256,1664]{1,0:T(8,128)(2,1)} %get-tuple-element.241), channel_id=1, source_target_pairs={{0,16},{4,20},{8,24},{12,28},{16,0},{20,4},{24,8},{28,12},{1,17},{... | collective-permute-start | bytes 2555912 | tf_op jit(solution)/shard_map/ppermute | solution.py:379
  201.8 21.2 %collective-permute-start.23 = (bf16[256,1664]{1,0:T(8,128)(2,1)}, bf16[256,1664]{1,0:T(8,128)(2,1)}, u32[]{:S(2)}, u32[]{:S(2)}) collective-permute-start(bf16[256,1664]{1,0:T(8,128)(2,1)} %get-tuple-element.243), channel_id=1, source_target_pairs={{0,8},{4,12},{8,0},{12,4},{16,24},{20,28},{24,16},{28,20},{1,9},{5... | collective-permute-start | bytes 2555912 | tf_op jit(solution)/shard_map/ppermute | solution.py:379
  203.8 284.6 %all-reduce.7.cloned.1.call-start = ((), (), s32[]{:S(2)}) async-start(), calls=%async_computation.3 | async-start | bytes 3932160 | tf_op jit(solution)/shard_map/psum | solution.py:696
  226.5 12.8 %collective-permute-start.25 = (bf16[128,1664]{1,0:T(8,128)(2,1)S(1)}, bf16[128,1664]{1,0:T(8,128)(2,1)S(1)}, u32[]{:S(2)}, u32[]{:S(2)}) collective-permute-start(bf16[128,1664]{1,0:T(8,128)(2,1)S(1)} %slice.389), channel_id=1, source_target_pairs={{0,8},{4,12},{8,0},{12,4},{16,24},{20,28},{24,16},{28,20},{1,9},{5... | collective-permute-start | bytes 1277960 | tf_op jit(solution)/shard_map/ppermute | solution.py:379
  227.2 12.8 %collective-permute-start.26 = (bf16[128,1664]{1,0:T(8,128)(2,1)S(1)}, bf16[128,1664]{1,0:T(8,128)(2,1)S(1)}, u32[]{:S(2)}, u32[]{:S(2)}) collective-permute-start(bf16[128,1664]{1,0:T(8,128)(2,1)S(1)} %slice.390), channel_id=1, source_target_pairs={{0,16},{4,20},{8,24},{12,28},{16,0},{20,4},{24,8},{28,12},{1,17},{... | collective-permute-start | bytes 1277960 | tf_op jit(solution)/shard_map/ppermute | solution.py:379
  231.6 23.1 %collective-permute-start.27 = (bf16[256,1536]{1,0:T(8,128)(2,1)}, bf16[256,1536]{1,0:T(8,128)(2,1)}, u32[]{:S(2)}, u32[]{:S(2)}) collective-permute-start(bf16[256,1536]{1,0:T(8,128)(2,1)} %get-tuple-element.258), channel_id=1, source_target_pairs={{0,16},{4,20},{8,24},{12,28},{16,0},{20,4},{24,8},{28,12},{1,17},{... | collective-permute-start | bytes 2359304 | tf_op jit(solution)/shard_map/ppermute | solution.py:379
  233.3 21.3 %collective-permute-start.28 = (bf16[256,1536]{1,0:T(8,128)(2,1)}, bf16[256,1536]{1,0:T(8,128)(2,1)}, u32[]{:S(2)}, u32[]{:S(2)}) collective-permute-start(bf16[256,1536]{1,0:T(8,128)(2,1)} %get-tuple-element.259), channel_id=1, source_target_pairs={{0,8},{4,12},{8,0},{12,4},{16,24},{20,28},{24,16},{28,20},{1,9},{5... | collective-permute-start | bytes 2359304 | tf_op jit(solution)/shard_map/ppermute | solution.py:379
  254.6 27.5 %collective-permute-start.29 = (bf16[256,384]{1,0:T(8,128)(2,1)S(1)}, bf16[256,384]{1,0:T(8,128)(2,1)S(1)}, u32[]{:S(2)}, u32[]{:S(2)}) collective-permute-start(bf16[256,384]{1,0:T(8,128)(2,1)S(1)} %get-tuple-element.261), channel_id=1, source_target_pairs={{0,3},{1,0},{2,1},{3,2},{4,7},{5,4},{6,5},{7,6},{8,11},{9,8},{10,9... | collective-permute-start | bytes 589832 | tf_op jit(solution)/shard_map/ppermute | solution.py:384
  272.4 36.5 %collective-permute-start.30 = (bf16[256,384]{1,0:T(8,128)(2,1)S(1)}, bf16[256,384]{1,0:T(8,128)(2,1)S(1)}, u32[]{:S(2)}, u32[]{:S(2)}) collective-permute-start(bf16[256,384]{1,0:T(8,128)(2,1)S(1)} %get-tuple-element.262), channel_id=1, source_target_pairs={{0,2},{1,3},{2,0},{3,1},{4,6},{5,7},{6,4},{7,5},{8,10},{9,11},{10,... | collective-permute-start | bytes 589832 | tf_op jit(solution)/shard_map/ppermute | solution.py:384
  272.4 36.5 %collective-permute-start.31 = (bf16[256,384]{1,0:T(8,128)(2,1)S(1)}, bf16[256,384]{1,0:T(8,128)(2,1)S(1)}, u32[]{:S(2)}, u32[]{:S(2)}) collective-permute-start(bf16[256,384]{1,0:T(8,128)(2,1)S(1)} %get-tuple-element.263), channel_id=1, source_target_pairs={{0,1},{1,2},{2,3},{3,0},{4,5},{5,6},{6,7},{7,4},{8,9},{9,10},{10,1... | collective-permute-start | bytes 589832 | tf_op jit(solution)/shard_map/ppermute | solution.py:384
  275.7 33.2 %collective-permute-start.32 = (bf16[128,1536]{1,0:T(8,128)(2,1)S(1)}, bf16[128,1536]{1,0:T(8,128)(2,1)S(1)}, u32[]{:S(2)}, u32[]{:S(2)}) collective-permute-start(bf16[128,1536]{1,0:T(8,128)(2,1)S(1)} %slice.408), channel_id=1, source_target_pairs={{0,8},{4,12},{8,0},{12,4},{16,24},{20,28},{24,16},{28,20},{1,9},{5... | collective-permute-start | bytes 1179656 | tf_op jit(solution)/shard_map/ppermute | solution.py:379
  277.2 31.7 %collective-permute-start.33 = (bf16[128,1536]{1,0:T(8,128)(2,1)S(1)}, bf16[128,1536]{1,0:T(8,128)(2,1)S(1)}, u32[]{:S(2)}, u32[]{:S(2)}) collective-permute-start(bf16[128,1536]{1,0:T(8,128)(2,1)S(1)} %slice.409), channel_id=1, source_target_pairs={{0,16},{4,20},{8,24},{12,28},{16,0},{20,4},{24,8},{28,12},{1,17},{... | collective-permute-start | bytes 1179656 | tf_op jit(solution)/shard_map/ppermute | solution.py:379
  308.9 27.6 %collective-permute-start.36 = (bf16[4,208,1536]{2,1,0:T(8,128)(2,1)S(1)}, bf16[4,208,1536]{2,1,0:T(8,128)(2,1)}, u32[]{:S(2)}, u32[]{:S(2)}) collective-permute-start(bf16[4,208,1536]{2,1,0:T(8,128)(2,1)S(1)} %get-tuple-element.283), channel_id=1, source_target_pairs={{0,4},{4,0},{8,12},{12,8},{16,20},{20,16},{24,28},{28,24},{1,5},{5... | collective-permute-start | bytes 7667720 | tf_op jit(solution)/shard_map/ppermute | solution.py:379
  309.5 27.0 %collective-permute-start.34 = (bf16[256,1536]{1,0:T(8,128)(2,1)S(1)}, bf16[256,1536]{1,0:T(8,128)(2,1)}, u32[]{:S(2)}, u32[]{:S(2)}) collective-permute-start(bf16[256,1536]{1,0:T(8,128)(2,1)S(1)} %fusion.16), channel_id=1, source_target_pairs={{0,1},{1,2},{2,3},{4,5},{5,6},{6,7},{8,9},{9,10},{10,11},{12,13},{... | collective-permute-start | bytes 2359304 | tf_op jit(solution)/shard_map/ppermute | solution.py:391
  314.0 22.4 %collective-permute-start.35 = (bf16[256,1536]{1,0:T(8,128)(2,1)S(1)}, bf16[256,1536]{1,0:T(8,128)(2,1)}, u32[]{:S(2)}, u32[]{:S(2)}) collective-permute-start(bf16[256,1536]{1,0:T(8,128)(2,1)S(1)} %fusion.16), channel_id=1, source_target_pairs={{3,2},{2,1},{1,0},{7,6},{6,5},{5,4},{11,10},{10,9},{9,8},{15,14},{... | collective-permute-start | bytes 2359304 | tf_op jit(solution)/shard_map/ppermute | solution.py:391
  342.0 29.5 %collective-permute-start.37 = (bf16[256,1536]{1,0:T(8,128)(2,1)}, bf16[256,1536]{1,0:T(8,128)(2,1)S(1)}, u32[]{:S(2)}, u32[]{:S(2)}) collective-permute-start(bf16[256,1536]{1,0:T(8,128)(2,1)} %select_bitcast_fusion), channel_id=1, source_target_pairs={{0,1},{3,2},{4,5},{7,6},{8,9},{11,10},{12,13},{15,14},{16,17},{19,... | collective-permute-start | bytes 2359304 | tf_op jit(solution)/shard_map/ppermute | solution.py:399
  346.6 24.9 %collective-permute-start.38 = (bf16[256,1536]{1,0:T(8,128)(2,1)}, bf16[256,1536]{1,0:T(8,128)(2,1)S(1)}, u32[]{:S(2)}, u32[]{:S(2)}) collective-permute-start(bf16[256,1536]{1,0:T(8,128)(2,1)} %collective-permute-done.34), channel_id=1, source_target_pairs={{1,2},{2,3},{5,6},{6,7},{9,10},{10,11},{13,14},{14,15},{17,18},{18... | collective-permute-start | bytes 2359304 | tf_op jit(solution)/shard_map/ppermute | solution.py:391
  347.3 25.1 %collective-permute-start.39 = (bf16[256,1536]{1,0:T(8,128)(2,1)}, bf16[256,1536]{1,0:T(8,128)(2,1)}, u32[]{:S(2)}, u32[]{:S(2)}) collective-permute-start(bf16[256,1536]{1,0:T(8,128)(2,1)} %collective-permute-done.35), channel_id=1, source_target_pairs={{2,1},{1,0},{6,5},{5,4},{10,9},{9,8},{14,13},{13,12},{18,17},{17,1... | collective-permute-start | bytes 2359304 | tf_op jit(solution)/shard_map/ppermute | solution.py:391
  354.8 16.2 %collective-permute-start.40 = (bf16[208,1536]{1,0:T(8,128)(2,1)}, bf16[208,1536]{1,0:T(8,128)(2,1)}, u32[]{:S(2)}, u32[]{:S(2)}) collective-permute-start(bf16[208,1536]{1,0:T(8,128)(2,1)} %pad_maximum_fusion.8), channel_id=1, source_target_pairs={{0,16},{4,20},{8,24},{12,28},{16,0},{20,4},{24,8},{28,12},{1,17},{... | collective-permute-start | bytes 1916936 | tf_op jit(solution)/shard_map/ppermute | solution.py:379
  355.5 16.0 %collective-permute-start.41 = (bf16[208,1536]{1,0:T(8,128)(2,1)}, bf16[208,1536]{1,0:T(8,128)(2,1)}, u32[]{:S(2)}, u32[]{:S(2)}) collective-permute-start(bf16[208,1536]{1,0:T(8,128)(2,1)} %pad_maximum_fusion.10), channel_id=1, source_target_pairs={{0,8},{4,12},{8,0},{12,4},{16,24},{20,28},{24,16},{28,20},{1,9},{5... | collective-permute-start | bytes 1916936 | tf_op jit(solution)/shard_map/ppermute | solution.py:379
  377.6 23.3 %collective-permute-start.42 = (bf16[256,1536]{1,0:T(8,128)(2,1)}, bf16[256,1536]{1,0:T(8,128)(2,1)}, u32[]{:S(2)}, u32[]{:S(2)}) collective-permute-start(bf16[256,1536]{1,0:T(8,128)(2,1)} %get-tuple-element.403), channel_id=1, source_target_pairs={{0,1},{1,2},{4,5},{5,6},{8,9},{9,10},{12,13},{13,14},{16,17},{17,1... | collective-permute-start | bytes 2359304 | tf_op jit(solution)/shard_map/ppermute | solution.py:391
  383.3 17.6 %collective-permute-start.43 = (bf16[256,1536]{1,0:T(8,128)(2,1)}, bf16[256,1536]{1,0:T(8,128)(2,1)}, u32[]{:S(2)}, u32[]{:S(2)}) collective-permute-start(bf16[256,1536]{1,0:T(8,128)(2,1)} %get-tuple-element.402), channel_id=1, source_target_pairs={{3,2},{2,1},{7,6},{6,5},{11,10},{10,9},{15,14},{14,13},{19,18},{18... | collective-permute-start | bytes 2359304 | tf_op jit(solution)/shard_map/ppermute | solution.py:391
  387.0 19.8 %collective-permute-start.44 = (bf16[256,1536]{1,0:T(8,128)(2,1)}, bf16[256,1536]{1,0:T(8,128)(2,1)}, u32[]{:S(2)}, u32[]{:S(2)}) collective-permute-start(bf16[256,1536]{1,0:T(8,128)(2,1)} %broadcast_select_fusion.1), channel_id=1, source_target_pairs={{2,3},{1,0},{6,7},{5,4},{10,11},{9,8},{14,15},{13,12},{18,19},{17,... | collective-permute-start | bytes 2359304 | tf_op jit(solution)/shard_map/ppermute | solution.py:399
  391.0 7.8 %collective-permute-start.45 = (bf16[104,1536]{1,0:T(8,128)(2,1)S(1)}, bf16[104,1536]{1,0:T(8,128)(2,1)}, u32[]{:S(2)}, u32[]{:S(2)}) collective-permute-start(bf16[104,1536]{1,0:T(8,128)(2,1)S(1)} %slice.428), channel_id=1, source_target_pairs={{0,8},{4,12},{8,0},{12,4},{16,24},{20,28},{24,16},{28,20},{1,9},{5... | collective-permute-start | bytes 958472 | tf_op jit(solution)/shard_map/ppermute | solution.py:379
  393.2 7.6 %collective-permute-start.46 = (bf16[104,1536]{1,0:T(8,128)(2,1)}, bf16[104,1536]{1,0:T(8,128)(2,1)}, u32[]{:S(2)}, u32[]{:S(2)}) collective-permute-start(bf16[104,1536]{1,0:T(8,128)(2,1)} %slice.429), channel_id=1, source_target_pairs={{0,16},{4,20},{8,24},{12,28},{16,0},{20,4},{24,8},{28,12},{1,17},{... | collective-permute-start | bytes 958472 | tf_op jit(solution)/shard_map/ppermute | solution.py:379
  409.9 19.5 %collective-permute-start.50 = (bf16[256,1536]{1,0:T(8,128)(2,1)S(1)}, bf16[256,1536]{1,0:T(8,128)(2,1)S(1)}, u32[]{:S(2)}, u32[]{:S(2)}) collective-permute-start(bf16[256,1536]{1,0:T(8,128)(2,1)S(1)} %get-tuple-element.405), channel_id=1, source_target_pairs={{0,1},{1,2},{2,3},{4,5},{5,6},{6,7},{8,9},{9,10},{10,11},{12,13},{... | collective-permute-start | bytes 2359304 | tf_op jit(solution)/shard_map/ppermute | solution.py:391
  411.4 20.6 %collective-permute-start.51 = (bf16[256,1536]{1,0:T(8,128)(2,1)S(1)}, bf16[256,1536]{1,0:T(8,128)(2,1)S(1)}, u32[]{:S(2)}, u32[]{:S(2)}) collective-permute-start(bf16[256,1536]{1,0:T(8,128)(2,1)S(1)} %get-tuple-element.404), channel_id=1, source_target_pairs={{3,2},{2,1},{1,0},{7,6},{6,5},{5,4},{11,10},{10,9},{9,8},{15,14},{... | collective-permute-start | bytes 2359304 | tf_op jit(solution)/shard_map/ppermute | solution.py:391
  413.9 41.8 %collective-permute-start.47 = (bf16[56,1536]{1,0:T(8,128)(2,1)S(1)}, bf16[56,1536]{1,0:T(8,128)(2,1)S(1)}, u32[]{:S(2)}, u32[]{:S(2)}) collective-permute-start(bf16[56,1536]{1,0:T(8,128)(2,1)S(1)} %get-tuple-element.432), channel_id=1, source_target_pairs={{0,3},{1,0},{2,1},{3,2},{4,7},{5,4},{6,5},{7,6},{8,11},{9,8},{10,9... | collective-permute-start | bytes 516104 | tf_op jit(solution)/shard_map/ppermute | solution.py:384
  420.0 38.3 %collective-permute-start.48 = (bf16[56,1536]{1,0:T(8,128)(2,1)S(1)}, bf16[56,1536]{1,0:T(8,128)(2,1)S(1)}, u32[]{:S(2)}, u32[]{:S(2)}) collective-permute-start(bf16[56,1536]{1,0:T(8,128)(2,1)S(1)} %get-tuple-element.431), channel_id=1, source_target_pairs={{0,2},{1,3},{2,0},{3,1},{4,6},{5,7},{6,4},{7,5},{8,10},{9,11},{10,... | collective-permute-start | bytes 516104 | tf_op jit(solution)/shard_map/ppermute | solution.py:384
  420.0 39.5 %collective-permute-start.49 = (bf16[56,1536]{1,0:T(8,128)(2,1)S(1)}, bf16[56,1536]{1,0:T(8,128)(2,1)S(1)}, u32[]{:S(2)}, u32[]{:S(2)}) collective-permute-start(bf16[56,1536]{1,0:T(8,128)(2,1)S(1)} %get-tuple-element.430), channel_id=1, source_target_pairs={{0,1},{1,2},{2,3},{3,0},{4,5},{5,6},{6,7},{7,4},{8,9},{9,10},{10,1... | collective-permute-start | bytes 516104 | tf_op jit(solution)/shard_map/ppermute | solution.py:384
  433.6 30.1 %collective-permute-start.55 = (bf16[256,1536]{1,0:T(8,128)(2,1)S(1)}, bf16[256,1536]{1,0:T(8,128)(2,1)S(1)}, u32[]{:S(2)}, u32[]{:S(2)}) collective-permute-start(bf16[256,1536]{1,0:T(8,128)(2,1)S(1)} %fusion.13), channel_id=1, source_target_pairs={{0,1},{1,2},{2,3},{4,5},{5,6},{6,7},{8,9},{9,10},{10,11},{12,13},{... | collective-permute-start | bytes 2359304 | tf_op jit(solution)/shard_map/ppermute | solution.py:391
  443.3 20.4 %collective-permute-start.56 = (bf16[256,1536]{1,0:T(8,128)(2,1)S(1)}, bf16[256,1536]{1,0:T(8,128)(2,1)S(1)}, u32[]{:S(2)}, u32[]{:S(2)}) collective-permute-start(bf16[256,1536]{1,0:T(8,128)(2,1)S(1)} %fusion.13), channel_id=1, source_target_pairs={{3,2},{2,1},{1,0},{7,6},{6,5},{5,4},{11,10},{10,9},{9,8},{15,14},{... | collective-permute-start | bytes 2359304 | tf_op jit(solution)/shard_map/ppermute | solution.py:391
  455.7 7.4 %collective-permute-start.52 = (f32[1,1536]{1,0:T(1,128)S(1)}, f32[1,1536]{1,0:T(1,128)S(1)}, u32[]{:S(2)}, u32[]{:S(2)}) collective-permute-start(f32[1,1536]{1,0:T(1,128)S(1)} %broadcast_in_dim.86), channel_id=1, source_target_pairs={{0,1},{1,2},{2,3},{3,0},{4,5},{5,6},{6,7},{7,4},{8,9},{9,10},{10,1... | collective-permute-start | bytes 18440 | tf_op jit(solution)/shard_map/ppermute | solution.py:384
  463.7 11.6 %collective-permute-start.60 = (bf16[256,1536]{1,0:T(8,128)(2,1)S(1)}, bf16[256,1536]{1,0:T(8,128)(2,1)S(1)}, u32[]{:S(2)}, u32[]{:S(2)}) collective-permute-start(bf16[256,1536]{1,0:T(8,128)(2,1)S(1)} %collective-permute-done.55), channel_id=1, source_target_pairs={{1,2},{2,3},{5,6},{6,7},{9,10},{10,11},{13,14},{14,15},{17,18},{18... | collective-permute-start | bytes 2359304 | tf_op jit(solution)/shard_map/ppermute | solution.py:391
  464.4 17.0 %collective-permute-start.61 = (bf16[256,1536]{1,0:T(8,128)(2,1)S(1)}, bf16[256,1536]{1,0:T(8,128)(2,1)S(1)}, u32[]{:S(2)}, u32[]{:S(2)}) collective-permute-start(bf16[256,1536]{1,0:T(8,128)(2,1)S(1)} %collective-permute-done.56), channel_id=1, source_target_pairs={{2,1},{1,0},{6,5},{5,4},{10,9},{9,8},{14,13},{13,12},{18,17},{17,1... | collective-permute-start | bytes 2359304 | tf_op jit(solution)/shard_map/ppermute | solution.py:391
  466.0 7.3 %collective-permute-start.57 = (bf16[64,1536]{1,0:T(8,128)(2,1)S(1)}, bf16[64,1536]{1,0:T(8,128)(2,1)S(1)}, u32[]{:S(2)}, u32[]{:S(2)}) collective-permute-start(bf16[64,1536]{1,0:T(8,128)(2,1)S(1)} %scatter.4), channel_id=1, source_target_pairs={{0,8},{4,12},{8,0},{12,4},{16,24},{20,28},{24,16},{28,20},{1,9},{5... | collective-permute-start | bytes 589832 | tf_op jit(solution)/shard_map/ppermute | solution.py:379
  467.4 6.7 %collective-permute-start.58 = (bf16[64,1536]{1,0:T(8,128)(2,1)S(1)}, bf16[64,1536]{1,0:T(8,128)(2,1)S(1)}, u32[]{:S(2)}, u32[]{:S(2)}) collective-permute-start(bf16[64,1536]{1,0:T(8,128)(2,1)S(1)} %scatter.4), channel_id=1, source_target_pairs={{0,16},{4,20},{8,24},{12,28},{16,0},{20,4},{24,8},{28,12},{1,17},{... | collective-permute-start | bytes 589832 | tf_op jit(solution)/shard_map/ppermute | solution.py:379
  468.8 6.6 %collective-permute-start.59 = (bf16[64,1536]{1,0:T(8,128)(2,1)S(1)}, bf16[64,1536]{1,0:T(8,128)(2,1)S(1)}, u32[]{:S(2)}, u32[]{:S(2)}) collective-permute-start(bf16[64,1536]{1,0:T(8,128)(2,1)S(1)} %scatter.4), channel_id=1, source_target_pairs={{0,24},{4,28},{8,16},{12,20},{16,8},{20,12},{24,0},{28,4},{1,25},{... | collective-permute-start | bytes 589832 | tf_op jit(solution)/shard_map/ppermute | solution.py:379
  482.4 6.0 %collective-permute-start.62 = (bf16[256,1536]{1,0:T(8,128)(2,1)S(1)}, bf16[256,1536]{1,0:T(8,128)(2,1)S(1)}, u32[]{:S(2)}, u32[]{:S(2)}) collective-permute-start(bf16[256,1536]{1,0:T(8,128)(2,1)S(1)} %pad_maximum_fusion.6.near_ref), channel_id=1, source_target_pairs={{0,4},{4,0},{8,12},{12,8},{16,20},{20,16},{24,28},{28,24},{1,5},{5... | collective-permute-start | bytes 2359304 | tf_op jit(solution)/shard_map/ppermute | solution.py:379
  484.8 22.1 %collective-permute-start.63 = (bf16[256,1536]{1,0:T(8,128)(2,1)}, bf16[256,1536]{1,0:T(8,128)(2,1)}, u32[]{:S(2)}, u32[]{:S(2)}) collective-permute-start(bf16[256,1536]{1,0:T(8,128)(2,1)} %get-tuple-element.421), channel_id=1, source_target_pairs={{2,3},{1,0},{6,7},{5,4},{10,11},{9,8},{14,15},{13,12},{18,19},{17,... | collective-permute-start | bytes 2359304 | tf_op jit(solution)/shard_map/ppermute | solution.py:399
  (64 other events, 744.0 us)
Sparse Core Ops, SparseCore 0:
  23.5 104.6 all-gather.1
  203.9 112.3 reduce-scatter.1
  394.7 62.0 all-reduce.6

commit v5 on v4

--- a/solution.py
+++ b/solution.py
@@ -2,6 +2,7 @@
 
 import jax
 import jax.numpy as jnp
+import numpy as np
 from jax import lax
 from jax.experimental import pallas as pl
 from jax.experimental.pallas import tpu as pltpu
@@ -27,18 +28,18 @@
     return lax.dot_general(a, b, dims, preferred_element_type=F32)
 
 
-def rotate_lanes(y, cos, sin_a, sin_b):
-    return y * cos + pltpu.roll(y, 128 - HD // 2, 1) * sin_a + pltpu.roll(y, HD // 2, 1) * sin_b
+def rotate_lanes(y, cos, sin):
+    half = HD // 2
+    first = lax.broadcasted_iota(jnp.int32, y.shape, 1) % HD < half
+    return y * cos + jnp.where(first, pltpu.roll(y, 128 - half, 1), pltpu.roll(y, half, 1)) * sin
 
 
 def rotary_lanes(tokens):
-    positions = (jnp.arange(tokens) % LEN).astype(F32)
-    lane = jnp.arange(128)
-    freqs = 10000.0 ** (-(lane % (HD // 2)).astype(F32) * 2.0 / HD)
-    angles = positions[:, None] * freqs[None, :]
-    cos, sin = jnp.cos(angles), jnp.sin(angles)
-    first = (lane % HD < HD // 2)[None, :]
-    return cos, jnp.where(first, -sin, 0.0), jnp.where(first, 0.0, sin)
+    lane = np.arange(128)
+    freqs = np.float32(10000.0) ** (-(lane % (HD // 2)).astype(np.float32) * np.float32(2.0 / HD))
+    angles = (np.arange(tokens) % LEN).astype(np.float32)[:, None] * freqs[None, :].astype(np.float32)
+    sign = np.where(lane % HD < HD // 2, np.float32(-1.0), np.float32(1.0))
+    return jnp.asarray(np.cos(angles), F32), jnp.asarray(np.sin(angles) * sign, F32)
 
 
 def causal(block):
@@ -47,8 +48,8 @@
     return key_at <= query_at
 
 
-def attend_kernel(at_ref, x_ref, gain_ref, wq_ref, wk_ref, wv_ref, cos_ref, sin_a_ref, sin_b_ref, *refs):
-    pieces, (normed_ref, q_ref, k_ref, v_ref, w_ref, log_ref, vt_ref, out_ref) = refs[:-8], refs[-8:]
+def attend_kernel(at_ref, x_ref, gain_ref, wq_ref, wk_ref, wv_ref, cos_ref, sin_ref, *refs):
+    pieces, (q_ref, k_ref, v_ref, log_ref, w_ref, vt_ref, out_ref) = refs[:-7], refs[-7:]
     tokens = x_ref.shape[0]
     heads, groups = q_ref.shape[0], k_ref.shape[0]
     repeat = heads // groups
@@ -63,9 +64,8 @@
         x = x_ref[rows, :].astype(F32)
         inverse = lax.rsqrt(jnp.mean(x * x, axis=-1, keepdims=True) + EPS)
         normed = (x * inverse * gain_ref[...]).astype(BF)
-        normed_ref[rows, :] = normed
         raw = mul(normed, w_ref[...])
-        tables = (cos_ref[rows, :], sin_a_ref[rows, :], sin_b_ref[rows, :])
+        tables = (cos_ref[rows, :], sin_ref[rows, :])
         for h in range(0, heads, per):
             turned = rotate_lanes(raw[:, h * HD : h * HD + 128], *tables) * scale
             for u in range(per):
@@ -120,32 +120,35 @@
     count = tokens // BLOCK
     return pl.pallas_call(
         attend_kernel,
-        in_specs=[SMEM] + [VMEM] * 8,
+        in_specs=[SMEM] + [VMEM] * 7,
         out_shape=[jax.ShapeDtypeStruct((BLOCK, heads * HD), BF)] * count
         + [
-            jax.ShapeDtypeStruct((tokens, width), BF),
             jax.ShapeDtypeStruct((heads, tokens, HD), BF),
             jax.ShapeDtypeStruct((groups, tokens, HD), BF),
             jax.ShapeDtypeStruct((groups, tokens, HD), BF),
-            jax.ShapeDtypeStruct((width, (heads + 2 * groups) * HD), BF),
             jax.ShapeDtypeStruct((heads, 1, tokens), F32),
         ],
-        scratch_shapes=[pltpu.VMEM((groups, HD, tokens), BF), pltpu.VMEM((heads, HD, tokens), F32)],
+        scratch_shapes=[
+            pltpu.VMEM((width, (heads + 2 * groups) * HD), BF),
+            pltpu.VMEM((groups, HD, tokens), BF),
+            pltpu.VMEM((heads, HD, tokens), F32),
+        ],
         compiler_params=pltpu.CompilerParams(vmem_limit_bytes=48 << 20),
         cost_estimate=takes(20),
     )(at[None], x, gain[None], *weights, *tables)
 
 
-def attend_back_kernel(at_ref, q_ref, k_ref, v_ref, log_ref, cos_ref, sin_a_ref, sin_b_ref, *refs):
-    do_ref, kt_ref, dq_ref, dk_ref, dv_ref = refs[-5:]
-    out_ref = refs[-6]
-    grad_refs = refs[:-6]
-    count = len(grad_refs)
+def attend_back_kernel(at_ref, q_ref, k_ref, v_ref, log_ref, cos_ref, sin_ref, wq_ref, wk_ref, wv_ref, *refs):
+    w_ref, do_ref, kt_ref, dq_ref, dk_ref, dv_ref = refs[-6:]
+    out_ref, end_ref = refs[-8:-6]
+    count = (len(refs) - 8) // 2
+    grad_refs, block_refs = refs[:count], refs[count:-8]
     tokens = q_ref.shape[1]
     heads, groups = q_ref.shape[0], k_ref.shape[0]
     repeat = heads // groups
     per = 128 // HD
     scale = HD ** (-0.5)
+    w_ref[...] = jnp.concatenate([wq_ref[...], wk_ref[...], wv_ref[...]], axis=1)
     dk_ref[...] = jnp.zeros_like(dk_ref)
     dv_ref[...] = jnp.zeros_like(dv_ref)
 
@@ -193,7 +196,7 @@
     @pl.loop(0, tokens // BLOCK)
     def _(i):
         rows = pl.ds(pl.multiple_of(i * BLOCK, BLOCK), BLOCK)
-        tables = (cos_ref[rows, :], -sin_a_ref[rows, :], -sin_b_ref[rows, :])
+        tables = (cos_ref[rows, :], -sin_ref[rows, :])
         for h in range(0, heads, per):
             pair = jnp.concatenate([dq_ref[h + u, :, rows] for u in range(per)], axis=0).T
             out_ref[rows, h * HD : h * HD + 128] = rotate_lanes(pair, *tables).astype(BF)
@@ -206,16 +209,31 @@
             out_ref[rows, lane : lane + 128] = pair.astype(BF)
 
 
-def attend_back(grad_pieces, q, k, v, logs, tables, at):
+    for s, block_ref in enumerate(block_refs):
+        block_ref[...] = mul(out_ref[span_of(s), :], w_ref[...], NT).astype(BF)
+
+    @pl.when(at_ref[0] < count // 2)
+    def _():
+        end_ref[...] = block_refs[count - 1][...]
+
+    @pl.when(at_ref[0] >= count // 2)
+    def _():
+        end_ref[...] = block_refs[1][...]
+
+
+def attend_back(grad_pieces, q, k, v, logs, tables, weights, at):
     heads, tokens, _ = q.shape
     groups = k.shape[0]
     count = len(grad_pieces)
     lanes = (heads + 2 * groups) * HD
+    width = weights[0].shape[0]
+    block = jax.ShapeDtypeStruct((BLOCK, width), BF)
     return pl.pallas_call(
         attend_back_kernel,
-        in_specs=[SMEM] + [VMEM] * (7 + count),
-        out_shape=jax.ShapeDtypeStruct((tokens, lanes), BF),
+        in_specs=[SMEM] + [VMEM] * (9 + count),
+        out_shape=[block] * count + [jax.ShapeDtypeStruct((tokens, lanes), BF), block],
         scratch_shapes=[
+            pltpu.VMEM((width, lanes), BF),
             pltpu.VMEM((heads, tokens, HD), BF),
             pltpu.VMEM((groups, HD, tokens), BF),
             pltpu.VMEM((heads, HD, tokens), F32),
@@ -224,7 +242,23 @@
         ],
         compiler_params=pltpu.CompilerParams(vmem_limit_bytes=48 << 20),
         cost_estimate=takes(20),
-    )(at[None], q, k, v, logs, *tables, *grad_pieces)
+    )(at[None], q, k, v, logs, *tables, *weights, *grad_pieces)
+
+
+def pack_kernel(gate_ref, up_ref, down_ref, out_ref):
+    part = down_ref.shape[0]
+    out_ref[:part, :] = gate_ref[...].astype(F32).T.astype(BF)
+    out_ref[part : 2 * part, :] = up_ref[...].astype(F32).T.astype(BF)
+    out_ref[2 * part :, :] = down_ref[...]
+
+
+def pack(gate, up, down):
+    return pl.pallas_call(
+        pack_kernel,
+        out_shape=jax.ShapeDtypeStruct((3 * down.shape[0], down.shape[1]), BF),
+        compiler_params=pltpu.CompilerParams(vmem_limit_bytes=32 << 20),
+        cost_estimate=takes(3),
+    )(gate, up, down)
 
 
 def expert_kernel(order_ref, near_ref, far_ref, extra_near_ref, extra_far_ref, router_ref, parts_ref, *refs, top, count):
@@ -395,7 +429,7 @@
     n = lax.axis_size("tp")
     at = lax.axis_index("tp")
     pairs = [(i, i + 1) for i in range(low, high)]
-    give = jnp.where((at >= low) & (at < high), right, left)
+    give = right if right is left else jnp.where((at >= low) & (at < high), right, left)
     return lax.ppermute(give, "tp", pairs + [(n - 1 - i, n - 1 - j) for i, j in pairs])
 
 
@@ -511,7 +545,7 @@
     output_parts = [output_part] + [turn(output_part, -s) for s in range(1, n_tp)]
 
     hidden_part = gate_weight.shape[2]
-    expert_part = jnp.concatenate([gate_weight[0].T, up_weight[0].T, down_weight[0]], axis=0)
+    expert_part = pack(gate_weight[0], up_weight[0], down_weight[0])
     expert_parts = lax.all_gather(expert_part, "tp", tiled=True)
 
     routes_mine = mine(routes)
@@ -519,36 +553,35 @@
     named = jnp.pad(routes_mine.astype(BF), ((0, 0), (0, LANES - top)), constant_values=-1.0)
     extra = jnp.concatenate([grad_top_mine, named], axis=1)
     tables = rotary_lanes(tokens)
+    qkv_weights = (query_weight, key_weight, value_weight)
     if fine:
         extra_got = gather_first(extra)
-        output_parts, extra_got, tables = join(output_parts, extra_got, tables)
+        output_parts, qkv_weights, expert_part = join(output_parts, qkv_weights, expert_part)
         output_part = jnp.concatenate(output_parts, axis=0)
         output_got = gather_first(output_part)
-        extra_held, extra_got = gather_second(extra, extra_got)
     else:
         output_part = jnp.concatenate(output_parts, axis=0)
         extra_near, extra_far = gather_whole(extra)
 
-    *mixed, normed, query, key, value, qkv_weight, logs = attend(
+    *mixed, query, key, value, logs = attend(
         inputs,
         norm_gain,
-        (query_weight, key_weight, value_weight),
+        qkv_weights,
         tables,
         heads_width // HD,
         groups_width // HD,
         tp_at,
     )
     if fine:
-        mixed, output_got, extra_held, extra_got = join(mixed, output_got, extra_held, extra_got)
+        mixed, output_got, extra_got = join(mixed, output_got, extra_got)
 
     mixed = [mixed[0]] + [turn(mixed[s], s) for s in range(1, n_tp)]
     if fine:
         output_held, output_got = gather_second(output_part, output_got)
-        extra_near = gather_near(extra_held, extra_got)
-        mixed, output_held, output_got, extra_near = join(mixed, output_held, output_got, extra_near)
+        mixed, output_held, output_got = join(mixed, output_held, output_got)
         near = gather_near(output_held, output_got)
         far = swap(near, 1)
-        extra_far = swap(extra_near, 1)
+        extra_held, extra_got = gather_second(extra, extra_got)
     else:
         near, far = gather_whole(output_part)
     halves = gather_halves()
@@ -582,7 +615,11 @@
     order = jnp.concatenate([ep_at[None], jnp.full((1,), experts, jnp.int32)])
     if fine:
         got = gather_first(routed_in)
-        got, gates, router, order = join(got, gates, router, order)
+        got, gates, router, order, extra_held, extra_got = join(
+            got, gates, router, order, extra_held, extra_got
+        )
+        extra_near = gather_near(extra_held, extra_got)
+        extra_far = swap(extra_near, 1)
         held, got = gather_second(routed_in, got)
         held, got = join(held, got)
         near = gather_near(held, got)
@@ -654,19 +691,20 @@
 
     result_mine, grad_mixed = join(result_mine, grad_mixed)
     result_steps = [step_both(result_mine, result_mine)]
-    grad_qkv = attend_back(grad_mixed, query, key, value, logs, tables, tp_at)
-    if fine:
-        grad_qkv, result_steps[0], other_output = join(grad_qkv, result_steps[0], other_output)
+    *blocks, grad_qkv, end_block = attend_back(grad_mixed, query, key, value, logs, tables, qkv_weights, tp_at)
+    if fine:
+        blocks, grad_qkv, end_block, result_steps[0], other_output = join(
+            blocks, grad_qkv, end_block, result_steps[0], other_output
+        )
     else:
-        grad_qkv, result_steps[0] = join(grad_qkv, result_steps[0])
-
-    grad_normed = mul(grad_qkv, qkv_weight, NT).astype(BF).reshape(n_tp, quarter, width)
+        blocks, grad_qkv, end_block, result_steps[0] = join(blocks, grad_qkv, end_block, result_steps[0])
+
+    inputs32 = inputs.astype(F32)
+    normed = inputs32 * lax.rsqrt(jnp.mean(inputs32 * inputs32, axis=-1, keepdims=True) + EPS)
+    normed = (normed * norm_gain).astype(BF)
     grad_qkv_w = mul(normed, grad_qkv, TN).astype(BF)
     if fine:
         grad_output = add(grad_output, other_output)
-
-    def block(j):
-        return lax.dynamic_index_in_dim(grad_normed, lax.rem(tp_at + j + n_tp, n_tp), 0, False)
 
     def chip_half(j, half):
         rows = grad_output.shape[1] // 2
@@ -683,7 +721,7 @@
         )
         got = sum_first(sums)
     result_steps.append(step_both(*result_steps[-1], 1))
-    sent = step_ends(block(n_tp - 1), block(1 - n_tp), 0, 1)
+    sent = step_ends(end_block, end_block, 0, 1)
     if fine:
         sent, result_steps[-1], got, grad_qkv_w, grad_expert = join(
             sent, result_steps[-1], got, grad_qkv_w, grad_expert
@@ -697,7 +735,7 @@
     sent = by_side(sent, 0, 1)
     result_last = None
     for t in range(2, n_tp):
-        sent = step_both(add(block(n_tp - t), sent[0]), add(block(t - n_tp), sent[1]), 0, t)
+        sent = step_both(add(blocks[n_tp - t], sent[0]), add(blocks[t], sent[1]), 0, t)
         if t < n_tp - 1:
             result_last = step_ends(*result_steps[-1], t, n_tp - 1)
             if fine:
@@ -712,7 +750,7 @@
             ]
     got = [turn(pieces[s], -s) for s in range(1, n_tp)]
     sent, result_steps, result_last = join(sent, result_steps, result_last)
-    grad_normed = block(0).astype(F32) + sent[0].astype(F32) + sent[1].astype(F32)
+    grad_normed = blocks[0].astype(F32) + sent[0].astype(F32) + sent[1].astype(F32)
     inverse_one = lax.rsqrt(jnp.mean(inputs_mine * inputs_mine, axis=-1, keepdims=True) + EPS)
     unit_one = inputs_mine * inverse_one
     scaled_one = grad_normed * norm_gain

time: 525 us -> 518 us (0.987)
  starting transfers between devices: 112 us -> 99 us
  waiting for transfers between devices: 173 us -> 181 us
    all_gather x1, waiting for transfers between devices: 0.01 us -> 25.7 us  [body(): expert_parts = lax.all_gather(expert_part, 'tp', tiled=True)]
    ppermute x15, starting transfers between devices: 43.2 us -> 27.2 us  [turn(): return lax.ppermute(x, 'tp', [(i, (i + by) % n) for i in range(n)])]
    ppermute x34, waiting for transfers between devices: 87.3 us -> 71.7 us  [swap(): lax.ppermute(x, 'ep', [(i, i ^ bit) for i in range(lax.axis_size('ep'))])]
    pallas_call x2 -> x3, Pallas kernels: 42.4 us -> 46.5 us  [the longest x1 25.5 us: attend_back(): pl.pallas_call(attend_back_kernel, in_specs=[SMEM] + [VMEM] * (9 + count)...]
    unnamed x137 -> x134, local copies, waits for them, and re-layouts: 18.1 us -> 14.9 us
    dot_general x8 -> x7, matrix products: 19.1 us -> 16.2 us  [mul(): return lax.dot_general(a, b, dims, preferred_element_type=F32)]
    convert_element_type x11 -> x12, other arithmetic: 23 us -> 22.4 us  [add(): return (a.astype(F32) + b.astype(F32)).astype(BF)]
  transfers between devices with their start and end apart: 67 -> 67, of which waited for: 32 -> 28; matrix products, arithmetic and copies ran while one was open for 21% -> 20% of each run, Pallas kernels for 9% -> 10%
where the time goes in v5:
time: 518 us; the launch traced here: 509 us
  waiting for transfers between devices  181 us (35%)
  starting transfers between devices  99 us (19%)
  Pallas kernels  93.2 us (18%)
  local copies, waits for them, and re-layouts  54.7 us (11%)
  other arithmetic  49.4 us (10%)
  matrix products  16.2 us (3%)
  between operations  15.6 us (3%)
    ppermute x34, waiting for transfers between devices, swap(): lax.ppermute(x, 'ep', [(i, i ^ bit) for i in range(lax.axis_size('ep'))])  71.7 us
    ppermute x15, waiting for transfers between devices, turn(): return lax.ppermute(x, 'tp', [(i, (i + by) % n) for i in range(n)])  49.5 us
    pallas_call x1, Pallas kernels, run_experts(): pl.pallas_call(functools.partial(expert_kernel, top=top, count=count), gr...  44.6 us
    ppermute x34, starting transfers between devices, swap(): lax.ppermute(x, 'ep', [(i, i ^ bit) for i in range(lax.axis_size('ep'))])  32.5 us
    ppermute x12, starting transfers between devices, step_both(): return (lax.ppermute(right, 'tp', pairs), lax.ppermute(left, 'tp', mirror))  30.5 us
    ppermute x15, starting transfers between devices, turn(): return lax.ppermute(x, 'tp', [(i, (i + by) % n) for i in range(n)])  27.2 us
    all_gather x1, waiting for transfers between devices, body(): expert_parts = lax.all_gather(expert_part, 'tp', tiled=True)  25.7 us
    pallas_call x1, Pallas kernels, attend_back(): pl.pallas_call(attend_back_kernel, in_specs=[SMEM] + [VMEM] * (9 + count)...  25.5 us
  transfers between devices with their start and end apart: 67, of which 28 were waited for; matrix products, arithmetic and copies ran while one was open for 20% of the time, Pallas kernels for 10%

profile of v5, /device:TPU:0, one launch (start us, length us, event | category | flops | bytes accessed | tf_op | source)
XLA Modules:
  0.0 508.7 jit_solution(3356064650607329234)
XLA Ops:
  8.5 5.1 %collective-permute-start = (bf16[48,1536]{1,0:T(8,128)(2,1)S(1)}, bf16[48,1536]{1,0:T(8,128)(2,1)S(1)}, u32[]{:S(2)}, u32[]{:S(2)}) collective-permute-start(bf16[48,1536]{1,0:T(8,128)(2,1)S(1)} %constant_dynamic-slice_fusion.2), channel_id=1, source_target_pairs={{0,3},{1,0},{2,1},{3,2},{4,7},{5,4},{6,5},{7,6},{8,11},{9,8},{10,9... | collective-permute-start | bytes 442376 | tf_op jit(solution)/shard_map/ppermute | solution.py:418
  22.2 3.9 collective-permute-done.1
  30.4 19.7 %shard_map.239 = (bf16[256,384]{1,0:T(8,128)(2,1)S(1)}, bf16[256,384]{1,0:T(8,128)(2,1)S(1)}, bf16[256,384]{1,0:T(8,128)(2,1)S(1)}, bf16[256,384]{1,0:T(8,128)(2...) custom-call(s32[1]{0:T(128)} %bitcast.8.at_ref, ...), custom_call_target="tpu_custom_call" | custom-call | flops 23000000512 | tf_op jit(solution)/shard_map/pallas_call | solution.py:121
  55.8 1.9 collective-permute-start.8
  57.7 2.9 collective-permute-start.9
  60.6 1.7 pad_maximum_fusion
  62.4 2.3 collective-permute-done.7
  66.1 10.3 %collective-permute-done.8 = bf16[256,384]{1,0:T(8,128)(2,1)S(1)} collective-permute-done((bf16[256,384]{1,0:T(8,128)(2,1)S(1)}, bf16[256,384]{1,0:T(8,128)(2,1)S(1)}, u32[]{:S(2)}, u32[]{:S(2)}) %collective-permute-start.8) | collective-permute-done | bytes 196640 | tf_op jit(solution)/shard_map/ppermute | solution.py:418
  80.3 3.5 collective-permute-done.12
  84.2 3.2 multiply_reduce_fusion.2
  90.7 7.6 %collective-permute-done.16 = bf16[256,1664]{1,0:T(8,128)(2,1)S(1)} collective-permute-done((bf16[256,1664]{1,0:T(8,128)(2,1)S(1)}, bf16[256,1664]{1,0:T(8,128)(2,1)S(1)}, u32[]{:S(2)}, u32[]{:S(2)}) %collective-permute-start.16) | collective-permute-done | bytes 852000 | tf_op jit(solution)/shard_map/ppermute | solution.py:413
  98.3 5.0 collective-permute-done.13
  103.4 1.8 collective-permute-start.17
  110.7 9.1 %collective-permute-done.17 = bf16[256,1536]{1,0:T(8,128)(2,1)S(1)} collective-permute-done((bf16[256,1536]{1,0:T(8,128)(2,1)S(1)}, bf16[256,1536]{1,0:T(8,128)(2,1)S(1)}, u32[]{:S(2)}, u32[]{:S(2)}) %collective-permute-start.17) | collective-permute-done | bytes 786464 | tf_op jit(solution)/shard_map/ppermute | solution.py:413
  124.8 25.7 %all-gather.2.cloned.1.call-done.parts_ref = bf16[1536,1536]{1,0:T(8,128)(2,1)} async-done(((bf16[384,1536]{1,0:T(8,128)(2,1)}), bf16[1536,1536]{1,0:T(8,128)(2,1)}) %all-gather.2.cloned.1.call-update) | async-done | bytes 4718608 | tf_op jit(solution)/shard_map/all_gather | solution.py:549
  150.5 44.6 %shard_map.240 = (bf16[1024,1536]{1,0:T(8,128)(2,1)}, bf16[1024,1536]{1,0:T(8,128)(2,1)}, bf16[1024,1664]{1,0:T(8,128)(2,1)}, bf16[1024,1664]{1,0:T(8,128)(2,1)}, bf16[1536,1536]{1,0:T(8,128)(2,1)}) custom-call(s32[2]{0:T(128)} %pad_add_fusion.order_ref, bf16[1024,1536]{1,0:T(8,128)(2,1)} %constant_dynamic-update-slice_fusion.8.near_ref, ...), custom_call_target="tpu_custom_call" | custom-call | flops 46000001024 | tf_op jit(solution)/shard_map/pallas_call | solution.py:351
  195.2 6.2 %collective-permute-done.21 = bf16[1024,1664]{1,0:T(8,128)(2,1)S(1)} collective-permute-done((bf16[1024,1664]{1,0:T(8,128)(2,1)}, bf16[1024,1664]{1,0:T(8,128)(2,1)S(1)}, u32[]{:S(2)}, u32[]{:S(2)}) %collective-permute-start.21) | collective-permute-done | bytes 3407904 | tf_op jit(solution)/shard_map/ppermute | solution.py:413
  201.5 3.9 add_convert_fusion.3
  209.9 2.6 fusion
  213.0 14.1 %collective-permute-done.22 = bf16[256,1664]{1,0:T(8,128)(2,1)} collective-permute-done((bf16[256,1664]{1,0:T(8,128)(2,1)}, bf16[256,1664]{1,0:T(8,128)(2,1)}, u32[]{:S(2)}, u32[]{:S(2)}) %collective-permute-start.22) | collective-permute-done | bytes 852000 | tf_op jit(solution)/shard_map/ppermute | solution.py:413
  233.4 4.1 add_convert_fusion.11
  239.6 4.5 collective-permute-done.25
  246.8 1.7 multiply_add_fusion
  250.3 2.5 copy.44
  252.9 3.9 convolution_convert_fusion.2
  256.9 3.6 collective-permute-done.27
  260.5 2.3 collective-permute-start.29
  269.1 6.1 %collective-permute-done.29.refs_1_ = bf16[256,384]{1,0:T(8,128)(2,1)S(1)} collective-permute-done((bf16[256,384]{1,0:T(8,128)(2,1)S(1)}, bf16[256,384]{1,0:T(8,128)(2,1)S(1)}, u32[]{:S(2)}, u32[]{:S(2)}) %collective-permute-start.29) | collective-permute-done | bytes 196640 | tf_op jit(solution)/shard_map/ppermute | solution.py:418
  275.2 25.3 %collective-permute-done.30.refs_2_ = bf16[256,384]{1,0:T(8,128)(2,1)S(1)} collective-permute-done((bf16[256,384]{1,0:T(8,128)(2,1)S(1)}, bf16[256,384]{1,0:T(8,128)(2,1)S(1)}, u32[]{:S(2)}, u32[]{:S(2)}) %collective-permute-start.30) | collective-permute-done | bytes 196640 | tf_op jit(solution)/shard_map/ppermute | solution.py:418
  301.2 3.8 collective-permute-start.34
  306.6 25.5 %shard_map.241 = (bf16[256,1536]{1,0:T(8,128)(2,1)S(1)}, bf16[256,1536]{1,0:T(8,128)(2,1)S(1)}, bf16[256,1536]{1,0:T(8,128)(2,1)S(1)}, bf16[256,1536]{1,0:T(8,12...) custom-call(s32[1]{0:T(128)} %bitcast.8.at_ref, bf16[6,1024,64]{2,1,0:T(8,128)(2,1)} %get-tuple-element.198.q_ref, ...), custom_call_target="tpu_custom_call" | custom-call | flops 23000000512 | tf_op jit(solution)/shard_map/pallas_call | solution.py:231
  332.1 5.5 %collective-permute-start.37 = (bf16[256,1536]{1,0:T(8,128)(2,1)}, bf16[256,1536]{1,0:T(8,128)(2,1)}, u32[]{:S(2)}, u32[]{:S(2)}) collective-permute-start(bf16[256,1536]{1,0:T(8,128)(2,1)} %get-tuple-element.298), channel_id=1, source_target_pairs={{0,1},{3,2},{4,5},{7,6},{8,9},{11,10},{12,13},{15,14},{16,17},{19,... | collective-permute-start | bytes 2359304 | tf_op jit(solution)/shard_map/ppermute | solution.py:433
  346.3 6.4 %convolution_convert_fusion.1 = bf16[1536,640]{1,0:T(8,128)(2,1)} fusion(bf16[1024,640]{1,0:T(8,128)(2,1)} %get-tuple-element.305, bf16[1024,1536]{1,0:T(8,128)(2,1)} %x_ref.1, f32[1536]{0:T(1024)S(1)} %copy-done.56, f32[1024]{0:T(1024)S(1)} %add_rsqrt_fusion), kind=kOutput, calls=%fused_computation.11 | convolution fusion | flops 2020540416 | bytes 6432768 | tf_op jit(solution)/shard_map/dot_general | solution.py:28
  352.6 7.7 %collective-permute-done.40 = bf16[208,1536]{1,0:T(8,128)(2,1)} collective-permute-done((bf16[208,1536]{1,0:T(8,128)(2,1)}, bf16[208,1536]{1,0:T(8,128)(2,1)}, u32[]{:S(2)}, u32[]{:S(2)}) %collective-permute-start.40) | collective-permute-done | bytes 639008 | tf_op jit(solution)/shard_map/ppermute | solution.py:413
  360.9 3.0 convert_element_type.385
  364.8 2.7 fusion.15
  367.5 5.3 %collective-permute-start.42 = (bf16[256,1536]{1,0:T(8,128)(2,1)}, bf16[256,1536]{1,0:T(8,128)(2,1)}, u32[]{:S(2)}, u32[]{:S(2)}) collective-permute-start(bf16[256,1536]{1,0:T(8,128)(2,1)} %get-tuple-element.431), channel_id=1, source_target_pairs={{0,1},{1,2},{4,5},{5,6},{8,9},{9,10},{12,13},{13,14},{16,17},{17,1... | collective-permute-start | bytes 2359304 | tf_op jit(solution)/shard_map/ppermute | solution.py:425
  374.4 2.1 broadcast_select_fusion.1
  383.6 2.6 slice_bitcast_fusion
  386.3 2.1 collective-permute-done.45
  388.3 1.9 collective-permute-done.46
  390.2 5.8 %collective-permute-done.44 = bf16[256,1536]{1,0:T(8,128)(2,1)} collective-permute-done((bf16[256,1536]{1,0:T(8,128)(2,1)}, bf16[256,1536]{1,0:T(8,128)(2,1)}, u32[]{:S(2)}, u32[]{:S(2)}) %collective-permute-start.44) | collective-permute-done | bytes 786464 | tf_op jit(solution)/shard_map/ppermute | solution.py:433
  398.6 1.7 collective-permute-start.50
  404.1 6.8 %collective-permute-start.47 = (bf16[56,1536]{1,0:T(8,128)(2,1)S(1)}, bf16[56,1536]{1,0:T(8,128)(2,1)S(1)}, u32[]{:S(2)}, u32[]{:S(2)}) collective-permute-start(bf16[56,1536]{1,0:T(8,128)(2,1)S(1)} %get-tuple-element.446), channel_id=1, source_target_pairs={{0,3},{1,0},{2,1},{3,2},{4,7},{5,4},{6,5},{7,6},{8,11},{9,8},{10,9... | collective-permute-start | bytes 516104 | tf_op jit(solution)/shard_map/ppermute | solution.py:418
  411.5 6.7 %collective-permute-done.50 = bf16[256,1536]{1,0:T(8,128)(2,1)S(1)} collective-permute-done((bf16[256,1536]{1,0:T(8,128)(2,1)S(1)}, bf16[256,1536]{1,0:T(8,128)(2,1)S(1)}, u32[]{:S(2)}, u32[]{:S(2)}) %collective-permute-start.50) | collective-permute-done | bytes 786464 | tf_op jit(solution)/shard_map/ppermute | solution.py:425
  418.3 4.5 collective-permute-done.51
  424.3 10.1 %collective-permute-start.55 = (bf16[256,1536]{1,0:T(8,128)(2,1)S(1)}, bf16[256,1536]{1,0:T(8,128)(2,1)S(1)}, u32[]{:S(2)}, u32[]{:S(2)}) collective-permute-start(bf16[256,1536]{1,0:T(8,128)(2,1)S(1)} %fusion.21), channel_id=1, source_target_pairs={{0,1},{1,2},{2,3},{4,5},{5,6},{6,7},{8,9},{9,10},{10,11},{12,13},{... | collective-permute-start | bytes 2359304 | tf_op jit(solution)/shard_map/ppermute | solution.py:425
  435.7 1.9 broadcast.86.clone.1
  437.5 2.1 constant_dynamic-update-slice_fusion.27
  439.6 2.1 constant_dynamic-update-slice_fusion.26
  442.6 2.1 constant_dynamic-update-slice_fusion.24
  444.7 2.1 constant_dynamic-update-slice_fusion.23
  446.8 2.6 collective-permute-start.52
  449.4 2.4 collective-permute-start.54
  452.8 1.7 collective-permute-done.53
  460.3 1.9 broadcast.86.clone
  464.0 1.7 collective-permute-done.58
  465.8 6.2 %collective-permute-done.61 = bf16[256,1536]{1,0:T(8,128)(2,1)} collective-permute-done((bf16[256,1536]{1,0:T(8,128)(2,1)S(1)}, bf16[256,1536]{1,0:T(8,128)(2,1)}, u32[]{:S(2)}, u32[]{:S(2)}) %collective-permute-start.61) | collective-permute-done | bytes 786464 | tf_op jit(solution)/shard_map/ppermute | solution.py:425
  473.0 2.5 constant_dynamic-update-slice_fusion.18
  476.9 2.3 copy.45
  480.3 2.1 shard_map.242
  482.5 3.0 slice.502
  487.4 10.3 %collective-permute-done.63 = bf16[256,1536]{1,0:T(8,128)(2,1)} collective-permute-done((bf16[256,1536]{1,0:T(8,128)(2,1)}, bf16[256,1536]{1,0:T(8,128)(2,1)}, u32[]{:S(2)}, u32[]{:S(2)}) %collective-permute-start.63) | collective-permute-done | bytes 786464 | tf_op jit(solution)/shard_map/ppermute | solution.py:433
  498.9 2.1 constant_dynamic-update-slice_fusion.17
  (362 shorter events, 110.7 us)
Async XLA Ops:
  7.2 143.3 %all-gather.2.cloned.1.call-start = ((), (), s32[]{:S(2)}) async-start(), calls=%async_computation.1 | async-start | bytes 5898240 | tf_op jit(solution)/shard_map/all_gather | solution.py:549
  8.5 13.7 %collective-permute-start = (bf16[48,1536]{1,0:T(8,128)(2,1)S(1)}, bf16[48,1536]{1,0:T(8,128)(2,1)S(1)}, u32[]{:S(2)}, u32[]{:S(2)}) collective-permute-start(bf16[48,1536]{1,0:T(8,128)(2,1)S(1)} %constant_dynamic-slice_fusion.2), channel_id=1, source_target_pairs={{0,3},{1,0},{2,1},{3,2},{4,7},{5,4},{6,5},{7,6},{8,11},{9,8},{10,9... | collective-permute-start | bytes 442376 | tf_op jit(solution)/shard_map/ppermute | solution.py:418
  13.6 12.5 %collective-permute-start.1 = (bf16[48,1536]{1,0:T(8,128)(2,1)S(1)}, bf16[48,1536]{1,0:T(8,128)(2,1)S(1)}, u32[]{:S(2)}, u32[]{:S(2)}) collective-permute-start(bf16[48,1536]{1,0:T(8,128)(2,1)S(1)} %constant_dynamic-slice_fusion.2), channel_id=1, source_target_pairs={{0,2},{1,3},{2,0},{3,1},{4,6},{5,7},{6,4},{7,5},{8,10},{9,11},{10,... | collective-permute-start | bytes 442376 | tf_op jit(solution)/shard_map/ppermute | solution.py:418
  13.6 12.5 %collective-permute-start.2 = (bf16[48,1536]{1,0:T(8,128)(2,1)S(1)}, bf16[48,1536]{1,0:T(8,128)(2,1)S(1)}, u32[]{:S(2)}, u32[]{:S(2)}) collective-permute-start(bf16[48,1536]{1,0:T(8,128)(2,1)S(1)} %constant_dynamic-slice_fusion.2), channel_id=1, source_target_pairs={{0,1},{1,2},{2,3},{3,0},{4,5},{5,6},{6,7},{7,4},{8,9},{9,10},{10,1... | collective-permute-start | bytes 442376 | tf_op jit(solution)/shard_map/ppermute | solution.py:418
  17.8 33.9 %collective-permute-start.5 = (bf16[128,1664]{1,0:T(8,128)(2,1)}, bf16[128,1664]{1,0:T(8,128)(2,1)}, u32[]{:S(2)}, u32[]{:S(2)}) collective-permute-start(bf16[128,1664]{1,0:T(8,128)(2,1)} %get-tuple-element.433), channel_id=1, source_target_pairs={{0,8},{4,12},{8,0},{12,4},{16,24},{20,28},{24,16},{28,20},{1,9},{5... | collective-permute-start | bytes 1277960 | tf_op jit(solution)/shard_map/ppermute | solution.py:413
  19.3 32.4 %collective-permute-start.6 = (bf16[128,1664]{1,0:T(8,128)(2,1)}, bf16[128,1664]{1,0:T(8,128)(2,1)}, u32[]{:S(2)}, u32[]{:S(2)}) collective-permute-start(bf16[128,1664]{1,0:T(8,128)(2,1)} %get-tuple-element.432), channel_id=1, source_target_pairs={{0,16},{4,20},{8,24},{12,28},{16,0},{20,4},{24,8},{28,12},{1,17},{... | collective-permute-start | bytes 1277960 | tf_op jit(solution)/shard_map/ppermute | solution.py:413
  26.1 25.6 %collective-permute-start.3 = (bf16[96,1536]{1,0:T(8,128)(2,1)S(1)}, bf16[96,1536]{1,0:T(8,128)(2,1)S(1)}, u32[]{:S(2)}, u32[]{:S(2)}) collective-permute-start(bf16[96,1536]{1,0:T(8,128)(2,1)S(1)} %pad_maximum_fusion.11), channel_id=1, source_target_pairs={{0,8},{4,12},{8,0},{12,4},{16,24},{20,28},{24,16},{28,20},{1,9},{5... | collective-permute-start | bytes 884744 | tf_op jit(solution)/shard_map/ppermute | solution.py:413
  27.7 24.0 %collective-permute-start.4 = (bf16[96,1536]{1,0:T(8,128)(2,1)S(1)}, bf16[96,1536]{1,0:T(8,128)(2,1)S(1)}, u32[]{:S(2)}, u32[]{:S(2)}) collective-permute-start(bf16[96,1536]{1,0:T(8,128)(2,1)S(1)} %pad_maximum_fusion.12), channel_id=1, source_target_pairs={{0,16},{4,20},{8,24},{12,28},{16,0},{20,4},{24,8},{28,12},{1,17},{... | collective-permute-start | bytes 884744 | tf_op jit(solution)/shard_map/ppermute | solution.py:413
  51.8 26.1 %collective-permute-start.10 = (bf16[192,1536]{1,0:T(8,128)(2,1)S(1)}, bf16[192,1536]{1,0:T(8,128)(2,1)}, u32[]{:S(2)}, u32[]{:S(2)}) collective-permute-start(bf16[192,1536]{1,0:T(8,128)(2,1)S(1)} %get-tuple-element.222), channel_id=1, source_target_pairs={{0,16},{4,20},{8,24},{12,28},{16,0},{20,4},{24,8},{28,12},{1,17},{... | collective-permute-start | bytes 1769480 | tf_op jit(solution)/shard_map/ppermute | solution.py:413
  52.4 25.5 %collective-permute-start.11 = (bf16[192,1536]{1,0:T(8,128)(2,1)S(1)}, bf16[192,1536]{1,0:T(8,128)(2,1)S(1)}, u32[]{:S(2)}, u32[]{:S(2)}) collective-permute-start(bf16[192,1536]{1,0:T(8,128)(2,1)S(1)} %get-tuple-element.224), channel_id=1, source_target_pairs={{0,8},{4,12},{8,0},{12,4},{16,24},{20,28},{24,16},{28,20},{1,9},{5... | collective-permute-start | bytes 1769480 | tf_op jit(solution)/shard_map/ppermute | solution.py:413
  53.0 299.7 %reduce-scatter.2.cloned.1.call-start = ((), (), s32[]{:S(2)}) async-start(), calls=%async_computation.2 | async-start | bytes 5898240 | tf_op jit(solution)/shard_map/reduce_scatter | solution.py:633
  54.9 9.7 %collective-permute-start.7 = (bf16[256,384]{1,0:T(8,128)(2,1)S(1)}, bf16[256,384]{1,0:T(8,128)(2,1)S(1)}, u32[]{:S(2)}, u32[]{:S(2)}) collective-permute-start(bf16[256,384]{1,0:T(8,128)(2,1)S(1)} %get-tuple-element.211), channel_id=1, source_target_pairs={{0,1},{1,2},{2,3},{3,0},{4,5},{5,6},{6,7},{7,4},{8,9},{9,10},{10,1... | collective-permute-start | bytes 589832 | tf_op jit(solution)/shard_map/ppermute | solution.py:418
  55.8 20.6 %collective-permute-start.8 = (bf16[256,384]{1,0:T(8,128)(2,1)S(1)}, bf16[256,384]{1,0:T(8,128)(2,1)S(1)}, u32[]{:S(2)}, u32[]{:S(2)}) collective-permute-start(bf16[256,384]{1,0:T(8,128)(2,1)S(1)} %get-tuple-element.212), channel_id=1, source_target_pairs={{0,2},{1,3},{2,0},{3,1},{4,6},{5,7},{6,4},{7,5},{8,10},{9,11},{10,... | collective-permute-start | bytes 589832 | tf_op jit(solution)/shard_map/ppermute | solution.py:418
  57.7 20.2 %collective-permute-start.9 = (bf16[256,384]{1,0:T(8,128)(2,1)S(1)}, bf16[256,384]{1,0:T(8,128)(2,1)S(1)}, u32[]{:S(2)}, u32[]{:S(2)}) collective-permute-start(bf16[256,384]{1,0:T(8,128)(2,1)S(1)} %get-tuple-element.213), channel_id=1, source_target_pairs={{0,3},{1,0},{2,1},{3,2},{4,7},{5,4},{6,5},{7,6},{8,11},{9,8},{10,9... | collective-permute-start | bytes 589832 | tf_op jit(solution)/shard_map/ppermute | solution.py:418
  64.6 26.0 %collective-permute-start.15 = (bf16[256,1664]{1,0:T(8,128)(2,1)S(1)}, bf16[256,1664]{1,0:T(8,128)(2,1)S(1)}, u32[]{:S(2)}, u32[]{:S(2)}) collective-permute-start(bf16[256,1664]{1,0:T(8,128)(2,1)S(1)} %get-tuple-element.239), channel_id=1, source_target_pairs={{0,16},{4,20},{8,24},{12,28},{16,0},{20,4},{24,8},{28,12},{1,17},{... | collective-permute-start | bytes 2555912 | tf_op jit(solution)/shard_map/ppermute | solution.py:413
  76.4 21.9 %collective-permute-start.16 = (bf16[256,1664]{1,0:T(8,128)(2,1)S(1)}, bf16[256,1664]{1,0:T(8,128)(2,1)S(1)}, u32[]{:S(2)}, u32[]{:S(2)}) collective-permute-start(bf16[256,1664]{1,0:T(8,128)(2,1)S(1)} %get-tuple-element.241), channel_id=1, source_target_pairs={{0,8},{4,12},{8,0},{12,4},{16,24},{20,28},{24,16},{28,20},{1,9},{5... | collective-permute-start | bytes 2555912 | tf_op jit(solution)/shard_map/ppermute | solution.py:413
  87.8 15.5 %collective-permute-start.13 = (bf16[128,1536]{1,0:T(8,128)(2,1)S(1)}, bf16[128,1536]{1,0:T(8,128)(2,1)S(1)}, u32[]{:S(2)}, u32[]{:S(2)}) collective-permute-start(bf16[128,1536]{1,0:T(8,128)(2,1)S(1)} %get-tuple-element.441), channel_id=1, source_target_pairs={{0,8},{4,12},{8,0},{12,4},{16,24},{20,28},{24,16},{28,20},{1,9},{5... | collective-permute-start | bytes 1179656 | tf_op jit(solution)/shard_map/ppermute | solution.py:413
  88.4 14.9 %collective-permute-start.14 = (bf16[128,1536]{1,0:T(8,128)(2,1)S(1)}, bf16[128,1536]{1,0:T(8,128)(2,1)S(1)}, u32[]{:S(2)}, u32[]{:S(2)}) collective-permute-start(bf16[128,1536]{1,0:T(8,128)(2,1)S(1)} %get-tuple-element.440), channel_id=1, source_target_pairs={{0,16},{4,20},{8,24},{12,28},{16,0},{20,4},{24,8},{28,12},{1,17},{... | collective-permute-start | bytes 1179656 | tf_op jit(solution)/shard_map/ppermute | solution.py:413
  103.4 16.3 %collective-permute-start.17 = (bf16[256,1536]{1,0:T(8,128)(2,1)S(1)}, bf16[256,1536]{1,0:T(8,128)(2,1)S(1)}, u32[]{:S(2)}, u32[]{:S(2)}) collective-permute-start(bf16[256,1536]{1,0:T(8,128)(2,1)S(1)} %pad_maximum_fusion.2), channel_id=1, source_target_pairs={{0,16},{4,20},{8,24},{12,28},{16,0},{20,4},{24,8},{28,12},{1,17},{... | collective-permute-start | bytes 2359304 | tf_op jit(solution)/shard_map/ppermute | solution.py:413
  105.2 15.9 %collective-permute-start.18 = (bf16[256,1536]{1,0:T(8,128)(2,1)S(1)}, bf16[256,1536]{1,0:T(8,128)(2,1)S(1)}, u32[]{:S(2)}, u32[]{:S(2)}) collective-permute-start(bf16[256,1536]{1,0:T(8,128)(2,1)S(1)} %pad_maximum_fusion.3), channel_id=1, source_target_pairs={{0,8},{4,12},{8,0},{12,4},{16,24},{20,28},{24,16},{28,20},{1,9},{5... | collective-permute-start | bytes 2359304 | tf_op jit(solution)/shard_map/ppermute | solution.py:413
  110.7 39.9 %collective-permute-start.20 = (bf16[1024,1664]{1,0:T(8,128)(2,1)}, bf16[1024,1664]{1,0:T(8,128)(2,1)}, u32[]{:S(2)}, u32[]{:S(2)}) collective-permute-start(bf16[1024,1664]{1,0:T(8,128)(2,1)} %constant_dynamic-update-slice_fusion.12.extra_near_ref), channel_id=1, source_target_pairs={{0,4},{4,0},{8,12},{12,8},{16,20},{20,16},{24,28},{28,24},{1,5},{5... | collective-permute-start | bytes 10223624 | tf_op jit(solution)/shard_map/ppermute | solution.py:413
  124.8 25.8 %collective-permute-start.19 = (bf16[1024,1536]{1,0:T(8,128)(2,1)}, bf16[1024,1536]{1,0:T(8,128)(2,1)}, u32[]{:S(2)}, u32[]{:S(2)}) collective-permute-start(bf16[1024,1536]{1,0:T(8,128)(2,1)} %constant_dynamic-update-slice_fusion.8.near_ref), channel_id=1, source_target_pairs={{0,4},{4,0},{8,12},{12,8},{16,20},{20,16},{24,28},{28,24},{1,5},{5... | collective-permute-start | bytes 9437192 | tf_op jit(solution)/shard_map/ppermute | solution.py:413
  195.2 6.3 %collective-permute-start.21 = (bf16[1024,1664]{1,0:T(8,128)(2,1)}, bf16[1024,1664]{1,0:T(8,128)(2,1)S(1)}, u32[]{:S(2)}, u32[]{:S(2)}) collective-permute-start(bf16[1024,1664]{1,0:T(8,128)(2,1)} %get-tuple-element.246), channel_id=1, source_target_pairs={{0,4},{4,0},{8,12},{12,8},{16,20},{20,16},{24,28},{28,24},{1,5},{5... | collective-permute-start | bytes 10223624 | tf_op jit(solution)/shard_map/ppermute | solution.py:413
  205.4 22.9 %collective-permute-start.24 = (bf16[1024,1536]{1,0:T(8,128)(2,1)}, bf16[1024,1536]{1,0:T(8,128)(2,1)}, u32[]{:S(2)}, u32[]{:S(2)}) collective-permute-start(bf16[1024,1536]{1,0:T(8,128)(2,1)} %get-tuple-element.252), channel_id=1, source_target_pairs={{0,4},{4,0},{8,12},{12,8},{16,20},{20,16},{24,28},{28,24},{1,5},{5... | collective-permute-start | bytes 9437192 | tf_op jit(solution)/shard_map/ppermute | solution.py:413
  205.5 21.5 %collective-permute-start.22 = (bf16[256,1664]{1,0:T(8,128)(2,1)}, bf16[256,1664]{1,0:T(8,128)(2,1)}, u32[]{:S(2)}, u32[]{:S(2)}) collective-permute-start(bf16[256,1664]{1,0:T(8,128)(2,1)} %get-tuple-element.248), channel_id=1, source_target_pairs={{0,16},{4,20},{8,24},{12,28},{16,0},{20,4},{24,8},{28,12},{1,17},{... | collective-permute-start | bytes 2555912 | tf_op jit(solution)/shard_map/ppermute | solution.py:413
  207.1 21.2 %collective-permute-start.23 = (bf16[256,1664]{1,0:T(8,128)(2,1)}, bf16[256,1664]{1,0:T(8,128)(2,1)}, u32[]{:S(2)}, u32[]{:S(2)}) collective-permute-start(bf16[256,1664]{1,0:T(8,128)(2,1)} %get-tuple-element.250), channel_id=1, source_target_pairs={{0,8},{4,12},{8,0},{12,4},{16,24},{20,28},{24,16},{28,20},{1,9},{5... | collective-permute-start | bytes 2555912 | tf_op jit(solution)/shard_map/ppermute | solution.py:413
  212.5 267.7 %all-reduce.7.cloned.1.call-start = ((), (), s32[]{:S(2)}) async-start(), calls=%async_computation.3 | async-start | bytes 3932160 | tf_op jit(solution)/shard_map/psum | solution.py:734
  231.2 12.8 %collective-permute-start.25 = (bf16[128,1664]{1,0:T(8,128)(2,1)S(1)}, bf16[128,1664]{1,0:T(8,128)(2,1)S(1)}, u32[]{:S(2)}, u32[]{:S(2)}) collective-permute-start(bf16[128,1664]{1,0:T(8,128)(2,1)S(1)} %slice.389), channel_id=1, source_target_pairs={{0,8},{4,12},{8,0},{12,4},{16,24},{20,28},{24,16},{28,20},{1,9},{5... | collective-permute-start | bytes 1277960 | tf_op jit(solution)/shard_map/ppermute | solution.py:413
  232.8 12.8 %collective-permute-start.26 = (bf16[128,1664]{1,0:T(8,128)(2,1)S(1)}, bf16[128,1664]{1,0:T(8,128)(2,1)S(1)}, u32[]{:S(2)}, u32[]{:S(2)}) collective-permute-start(bf16[128,1664]{1,0:T(8,128)(2,1)S(1)} %slice.390), channel_id=1, source_target_pairs={{0,16},{4,20},{8,24},{12,28},{16,0},{20,4},{24,8},{28,12},{1,17},{... | collective-permute-start | bytes 1277960 | tf_op jit(solution)/shard_map/ppermute | solution.py:413
  237.5 23.1 %collective-permute-start.27 = (bf16[256,1536]{1,0:T(8,128)(2,1)}, bf16[256,1536]{1,0:T(8,128)(2,1)}, u32[]{:S(2)}, u32[]{:S(2)}) collective-permute-start(bf16[256,1536]{1,0:T(8,128)(2,1)} %get-tuple-element.265), channel_id=1, source_target_pairs={{0,16},{4,20},{8,24},{12,28},{16,0},{20,4},{24,8},{28,12},{1,17},{... | collective-permute-start | bytes 2359304 | tf_op jit(solution)/shard_map/ppermute | solution.py:413
  239.0 21.5 %collective-permute-start.28 = (bf16[256,1536]{1,0:T(8,128)(2,1)}, bf16[256,1536]{1,0:T(8,128)(2,1)}, u32[]{:S(2)}, u32[]{:S(2)}) collective-permute-start(bf16[256,1536]{1,0:T(8,128)(2,1)} %get-tuple-element.266), channel_id=1, source_target_pairs={{0,8},{4,12},{8,0},{12,4},{16,24},{20,28},{24,16},{28,20},{1,9},{5... | collective-permute-start | bytes 2359304 | tf_op jit(solution)/shard_map/ppermute | solution.py:413
  260.5 14.7 %collective-permute-start.29 = (bf16[256,384]{1,0:T(8,128)(2,1)S(1)}, bf16[256,384]{1,0:T(8,128)(2,1)S(1)}, u32[]{:S(2)}, u32[]{:S(2)}) collective-permute-start(bf16[256,384]{1,0:T(8,128)(2,1)S(1)} %get-tuple-element.268), channel_id=1, source_target_pairs={{0,3},{1,0},{2,1},{3,2},{4,7},{5,4},{6,5},{7,6},{8,11},{9,8},{10,9... | collective-permute-start | bytes 589832 | tf_op jit(solution)/shard_map/ppermute | solution.py:418
  262.9 37.7 %collective-permute-start.30 = (bf16[256,384]{1,0:T(8,128)(2,1)S(1)}, bf16[256,384]{1,0:T(8,128)(2,1)S(1)}, u32[]{:S(2)}, u32[]{:S(2)}) collective-permute-start(bf16[256,384]{1,0:T(8,128)(2,1)S(1)} %get-tuple-element.269), channel_id=1, source_target_pairs={{0,2},{1,3},{2,0},{3,1},{4,6},{5,7},{6,4},{7,5},{8,10},{9,11},{10,... | collective-permute-start | bytes 589832 | tf_op jit(solution)/shard_map/ppermute | solution.py:418
  262.9 37.7 %collective-permute-start.31 = (bf16[256,384]{1,0:T(8,128)(2,1)S(1)}, bf16[256,384]{1,0:T(8,128)(2,1)S(1)}, u32[]{:S(2)}, u32[]{:S(2)}) collective-permute-start(bf16[256,384]{1,0:T(8,128)(2,1)S(1)} %get-tuple-element.270), channel_id=1, source_target_pairs={{0,1},{1,2},{2,3},{3,0},{4,5},{5,6},{6,7},{7,4},{8,9},{9,10},{10,1... | collective-permute-start | bytes 589832 | tf_op jit(solution)/shard_map/ppermute | solution.py:418
  266.1 34.4 %collective-permute-start.32 = (bf16[128,1536]{1,0:T(8,128)(2,1)S(1)}, bf16[128,1536]{1,0:T(8,128)(2,1)S(1)}, u32[]{:S(2)}, u32[]{:S(2)}) collective-permute-start(bf16[128,1536]{1,0:T(8,128)(2,1)S(1)} %slice.408), channel_id=1, source_target_pairs={{0,8},{4,12},{8,0},{12,4},{16,24},{20,28},{24,16},{28,20},{1,9},{5... | collective-permute-start | bytes 1179656 | tf_op jit(solution)/shard_map/ppermute | solution.py:413
  266.8 33.7 %collective-permute-start.33 = (bf16[128,1536]{1,0:T(8,128)(2,1)S(1)}, bf16[128,1536]{1,0:T(8,128)(2,1)S(1)}, u32[]{:S(2)}, u32[]{:S(2)}) collective-permute-start(bf16[128,1536]{1,0:T(8,128)(2,1)S(1)} %slice.409), channel_id=1, source_target_pairs={{0,16},{4,20},{8,24},{12,28},{16,0},{20,4},{24,8},{28,12},{1,17},{... | collective-permute-start | bytes 1179656 | tf_op jit(solution)/shard_map/ppermute | solution.py:413
  300.5 31.6 %collective-permute-start.36 = (bf16[4,208,1536]{2,1,0:T(8,128)(2,1)}, bf16[4,208,1536]{2,1,0:T(8,128)(2,1)S(1)}, u32[]{:S(2)}, u32[]{:S(2)}) collective-permute-start(bf16[4,208,1536]{2,1,0:T(8,128)(2,1)} %get-tuple-element.296), channel_id=1, source_target_pairs={{0,4},{4,0},{8,12},{12,8},{16,20},{20,16},{24,28},{28,24},{1,5},{5... | collective-permute-start | bytes 7667720 | tf_op jit(solution)/shard_map/ppermute | solution.py:413
  301.2 30.9 %collective-permute-start.34 = (bf16[256,1536]{1,0:T(8,128)(2,1)S(1)}, bf16[256,1536]{1,0:T(8,128)(2,1)}, u32[]{:S(2)}, u32[]{:S(2)}) collective-permute-start(bf16[256,1536]{1,0:T(8,128)(2,1)S(1)} %fusion.24), channel_id=1, source_target_pairs={{0,1},{1,2},{2,3},{4,5},{5,6},{6,7},{8,9},{9,10},{10,11},{12,13},{... | collective-permute-start | bytes 2359304 | tf_op jit(solution)/shard_map/ppermute | solution.py:425
  305.0 27.1 %collective-permute-start.35 = (bf16[256,1536]{1,0:T(8,128)(2,1)S(1)}, bf16[256,1536]{1,0:T(8,128)(2,1)}, u32[]{:S(2)}, u32[]{:S(2)}) collective-permute-start(bf16[256,1536]{1,0:T(8,128)(2,1)S(1)} %fusion.24), channel_id=1, source_target_pairs={{3,2},{2,1},{1,0},{7,6},{6,5},{5,4},{11,10},{10,9},{9,8},{15,14},{... | collective-permute-start | bytes 2359304 | tf_op jit(solution)/shard_map/ppermute | solution.py:425
  332.1 28.8 %collective-permute-start.37 = (bf16[256,1536]{1,0:T(8,128)(2,1)}, bf16[256,1536]{1,0:T(8,128)(2,1)}, u32[]{:S(2)}, u32[]{:S(2)}) collective-permute-start(bf16[256,1536]{1,0:T(8,128)(2,1)} %get-tuple-element.298), channel_id=1, source_target_pairs={{0,1},{3,2},{4,5},{7,6},{8,9},{11,10},{12,13},{15,14},{16,17},{19,... | collective-permute-start | bytes 2359304 | tf_op jit(solution)/shard_map/ppermute | solution.py:433
  337.6 23.3 %collective-permute-start.38 = (bf16[256,1536]{1,0:T(8,128)(2,1)}, bf16[256,1536]{1,0:T(8,128)(2,1)S(1)}, u32[]{:S(2)}, u32[]{:S(2)}) collective-permute-start(bf16[256,1536]{1,0:T(8,128)(2,1)} %collective-permute-done.34), channel_id=1, source_target_pairs={{1,2},{2,3},{5,6},{6,7},{9,10},{10,11},{13,14},{14,15},{17,18},{18... | collective-permute-start | bytes 2359304 | tf_op jit(solution)/shard_map/ppermute | solution.py:425
  338.3 22.6 %collective-permute-start.39 = (bf16[256,1536]{1,0:T(8,128)(2,1)}, bf16[256,1536]{1,0:T(8,128)(2,1)}, u32[]{:S(2)}, u32[]{:S(2)}) collective-permute-start(bf16[256,1536]{1,0:T(8,128)(2,1)} %collective-permute-done.35), channel_id=1, source_target_pairs={{2,1},{1,0},{6,5},{5,4},{10,9},{9,8},{14,13},{13,12},{18,17},{17,1... | collective-permute-start | bytes 2359304 | tf_op jit(solution)/shard_map/ppermute | solution.py:425
  344.1 16.3 %collective-permute-start.40 = (bf16[208,1536]{1,0:T(8,128)(2,1)}, bf16[208,1536]{1,0:T(8,128)(2,1)}, u32[]{:S(2)}, u32[]{:S(2)}) collective-permute-start(bf16[208,1536]{1,0:T(8,128)(2,1)} %pad_maximum_fusion.6), channel_id=1, source_target_pairs={{0,16},{4,20},{8,24},{12,28},{16,0},{20,4},{24,8},{28,12},{1,17},{... | collective-permute-start | bytes 1916936 | tf_op jit(solution)/shard_map/ppermute | solution.py:413
  344.8 16.0 %collective-permute-start.41 = (bf16[208,1536]{1,0:T(8,128)(2,1)}, bf16[208,1536]{1,0:T(8,128)(2,1)}, u32[]{:S(2)}, u32[]{:S(2)}) collective-permute-start(bf16[208,1536]{1,0:T(8,128)(2,1)} %pad_maximum_fusion.8), channel_id=1, source_target_pairs={{0,8},{4,12},{8,0},{12,4},{16,24},{20,28},{24,16},{28,20},{1,9},{5... | collective-permute-start | bytes 1916936 | tf_op jit(solution)/shard_map/ppermute | solution.py:413
  367.5 22.7 %collective-permute-start.42 = (bf16[256,1536]{1,0:T(8,128)(2,1)}, bf16[256,1536]{1,0:T(8,128)(2,1)}, u32[]{:S(2)}, u32[]{:S(2)}) collective-permute-start(bf16[256,1536]{1,0:T(8,128)(2,1)} %get-tuple-element.431), channel_id=1, source_target_pairs={{0,1},{1,2},{4,5},{5,6},{8,9},{9,10},{12,13},{13,14},{16,17},{17,1... | collective-permute-start | bytes 2359304 | tf_op jit(solution)/shard_map/ppermute | solution.py:425
  372.8 17.4 %collective-permute-start.43 = (bf16[256,1536]{1,0:T(8,128)(2,1)}, bf16[256,1536]{1,0:T(8,128)(2,1)}, u32[]{:S(2)}, u32[]{:S(2)}) collective-permute-start(bf16[256,1536]{1,0:T(8,128)(2,1)} %get-tuple-element.430), channel_id=1, source_target_pairs={{3,2},{2,1},{7,6},{6,5},{11,10},{10,9},{15,14},{14,13},{19,18},{18... | collective-permute-start | bytes 2359304 | tf_op jit(solution)/shard_map/ppermute | solution.py:425
  376.5 19.6 %collective-permute-start.44 = (bf16[256,1536]{1,0:T(8,128)(2,1)}, bf16[256,1536]{1,0:T(8,128)(2,1)}, u32[]{:S(2)}, u32[]{:S(2)}) collective-permute-start(bf16[256,1536]{1,0:T(8,128)(2,1)} %broadcast_select_fusion.1), channel_id=1, source_target_pairs={{2,3},{1,0},{6,7},{5,4},{10,11},{9,8},{14,15},{13,12},{18,19},{17,... | collective-permute-start | bytes 2359304 | tf_op jit(solution)/shard_map/ppermute | solution.py:433
  380.8 7.6 %collective-permute-start.45 = (bf16[104,1536]{1,0:T(8,128)(2,1)S(1)}, bf16[104,1536]{1,0:T(8,128)(2,1)}, u32[]{:S(2)}, u32[]{:S(2)}) collective-permute-start(bf16[104,1536]{1,0:T(8,128)(2,1)S(1)} %slice.428), channel_id=1, source_target_pairs={{0,8},{4,12},{8,0},{12,4},{16,24},{20,28},{24,16},{28,20},{1,9},{5... | collective-permute-start | bytes 958472 | tf_op jit(solution)/shard_map/ppermute | solution.py:413
  382.9 7.4 %collective-permute-start.46 = (bf16[104,1536]{1,0:T(8,128)(2,1)}, bf16[104,1536]{1,0:T(8,128)(2,1)}, u32[]{:S(2)}, u32[]{:S(2)}) collective-permute-start(bf16[104,1536]{1,0:T(8,128)(2,1)} %slice.429), channel_id=1, source_target_pairs={{0,16},{4,20},{8,24},{12,28},{16,0},{20,4},{24,8},{28,12},{1,17},{... | collective-permute-start | bytes 958472 | tf_op jit(solution)/shard_map/ppermute | solution.py:413
  398.6 19.7 %collective-permute-start.50 = (bf16[256,1536]{1,0:T(8,128)(2,1)S(1)}, bf16[256,1536]{1,0:T(8,128)(2,1)S(1)}, u32[]{:S(2)}, u32[]{:S(2)}) collective-permute-start(bf16[256,1536]{1,0:T(8,128)(2,1)S(1)} %add_convert_fusion.8), channel_id=1, source_target_pairs={{0,1},{1,2},{2,3},{4,5},{5,6},{6,7},{8,9},{9,10},{10,11},{12,13},{... | collective-permute-start | bytes 2359304 | tf_op jit(solution)/shard_map/ppermute | solution.py:425
  401.7 21.1 %collective-permute-start.51 = (bf16[256,1536]{1,0:T(8,128)(2,1)S(1)}, bf16[256,1536]{1,0:T(8,128)(2,1)S(1)}, u32[]{:S(2)}, u32[]{:S(2)}) collective-permute-start(bf16[256,1536]{1,0:T(8,128)(2,1)S(1)} %add_convert_fusion.7), channel_id=1, source_target_pairs={{3,2},{2,1},{1,0},{7,6},{6,5},{5,4},{11,10},{10,9},{9,8},{15,14},{... | collective-permute-start | bytes 2359304 | tf_op jit(solution)/shard_map/ppermute | solution.py:425
  404.1 42.6 %collective-permute-start.47 = (bf16[56,1536]{1,0:T(8,128)(2,1)S(1)}, bf16[56,1536]{1,0:T(8,128)(2,1)S(1)}, u32[]{:S(2)}, u32[]{:S(2)}) collective-permute-start(bf16[56,1536]{1,0:T(8,128)(2,1)S(1)} %get-tuple-element.446), channel_id=1, source_target_pairs={{0,3},{1,0},{2,1},{3,2},{4,7},{5,4},{6,5},{7,6},{8,11},{9,8},{10,9... | collective-permute-start | bytes 516104 | tf_op jit(solution)/shard_map/ppermute | solution.py:418
  410.9 38.5 %collective-permute-start.48 = (bf16[56,1536]{1,0:T(8,128)(2,1)S(1)}, bf16[56,1536]{1,0:T(8,128)(2,1)S(1)}, u32[]{:S(2)}, u32[]{:S(2)}) collective-permute-start(bf16[56,1536]{1,0:T(8,128)(2,1)S(1)} %get-tuple-element.445), channel_id=1, source_target_pairs={{0,2},{1,3},{2,0},{3,1},{4,6},{5,7},{6,4},{7,5},{8,10},{9,11},{10,... | collective-permute-start | bytes 516104 | tf_op jit(solution)/shard_map/ppermute | solution.py:418
  410.9 38.5 %collective-permute-start.49 = (bf16[56,1536]{1,0:T(8,128)(2,1)S(1)}, bf16[56,1536]{1,0:T(8,128)(2,1)S(1)}, u32[]{:S(2)}, u32[]{:S(2)}) collective-permute-start(bf16[56,1536]{1,0:T(8,128)(2,1)S(1)} %get-tuple-element.444), channel_id=1, source_target_pairs={{0,1},{1,2},{2,3},{3,0},{4,5},{5,6},{6,7},{7,4},{8,9},{9,10},{10,1... | collective-permute-start | bytes 516104 | tf_op jit(solution)/shard_map/ppermute | solution.py:418
  424.3 30.1 %collective-permute-start.55 = (bf16[256,1536]{1,0:T(8,128)(2,1)S(1)}, bf16[256,1536]{1,0:T(8,128)(2,1)S(1)}, u32[]{:S(2)}, u32[]{:S(2)}) collective-permute-start(bf16[256,1536]{1,0:T(8,128)(2,1)S(1)} %fusion.21), channel_id=1, source_target_pairs={{0,1},{1,2},{2,3},{4,5},{5,6},{6,7},{8,9},{9,10},{10,11},{12,13},{... | collective-permute-start | bytes 2359304 | tf_op jit(solution)/shard_map/ppermute | solution.py:425
  434.4 20.1 %collective-permute-start.56 = (bf16[256,1536]{1,0:T(8,128)(2,1)S(1)}, bf16[256,1536]{1,0:T(8,128)(2,1)S(1)}, u32[]{:S(2)}, u32[]{:S(2)}) collective-permute-start(bf16[256,1536]{1,0:T(8,128)(2,1)S(1)} %fusion.21), channel_id=1, source_target_pairs={{3,2},{2,1},{1,0},{7,6},{6,5},{5,4},{11,10},{10,9},{9,8},{15,14},{... | collective-permute-start | bytes 2359304 | tf_op jit(solution)/shard_map/ppermute | solution.py:425
  446.8 6.0 %collective-permute-start.52 = (f32[1,1536]{1,0:T(1,128)S(1)}, f32[1,1536]{1,0:T(1,128)S(1)}, u32[]{:S(2)}, u32[]{:S(2)}) collective-permute-start(f32[1,1536]{1,0:T(1,128)S(1)} %broadcast_in_dim.61), channel_id=1, source_target_pairs={{0,1},{1,2},{2,3},{3,0},{4,5},{5,6},{6,7},{7,4},{8,9},{9,10},{10,1... | collective-permute-start | bytes 18440 | tf_op jit(solution)/shard_map/ppermute | solution.py:418
  454.4 11.3 %collective-permute-start.60 = (bf16[256,1536]{1,0:T(8,128)(2,1)S(1)}, bf16[256,1536]{1,0:T(8,128)(2,1)S(1)}, u32[]{:S(2)}, u32[]{:S(2)}) collective-permute-start(bf16[256,1536]{1,0:T(8,128)(2,1)S(1)} %collective-permute-done.55), channel_id=1, source_target_pairs={{1,2},{2,3},{5,6},{6,7},{9,10},{10,11},{13,14},{14,15},{17,18},{18... | collective-permute-start | bytes 2359304 | tf_op jit(solution)/shard_map/ppermute | solution.py:425
  455.2 16.8 %collective-permute-start.61 = (bf16[256,1536]{1,0:T(8,128)(2,1)S(1)}, bf16[256,1536]{1,0:T(8,128)(2,1)}, u32[]{:S(2)}, u32[]{:S(2)}) collective-permute-start(bf16[256,1536]{1,0:T(8,128)(2,1)S(1)} %collective-permute-done.56), channel_id=1, source_target_pairs={{2,1},{1,0},{6,5},{5,4},{10,9},{9,8},{14,13},{13,12},{18,17},{17,1... | collective-permute-start | bytes 2359304 | tf_op jit(solution)/shard_map/ppermute | solution.py:425
  456.7 7.3 %collective-permute-start.57 = (bf16[64,1536]{1,0:T(8,128)(2,1)S(1)}, bf16[64,1536]{1,0:T(8,128)(2,1)S(1)}, u32[]{:S(2)}, u32[]{:S(2)}) collective-permute-start(bf16[64,1536]{1,0:T(8,128)(2,1)S(1)} %scatter.4), channel_id=1, source_target_pairs={{0,8},{4,12},{8,0},{12,4},{16,24},{20,28},{24,16},{28,20},{1,9},{5... | collective-permute-start | bytes 589832 | tf_op jit(solution)/shard_map/ppermute | solution.py:413
  458.0 7.8 %collective-permute-start.58 = (bf16[64,1536]{1,0:T(8,128)(2,1)S(1)}, bf16[64,1536]{1,0:T(8,128)(2,1)S(1)}, u32[]{:S(2)}, u32[]{:S(2)}) collective-permute-start(bf16[64,1536]{1,0:T(8,128)(2,1)S(1)} %scatter.4), channel_id=1, source_target_pairs={{0,16},{4,20},{8,24},{12,28},{16,0},{20,4},{24,8},{28,12},{1,17},{... | collective-permute-start | bytes 589832 | tf_op jit(solution)/shard_map/ppermute | solution.py:413
  458.8 7.0 %collective-permute-start.59 = (bf16[64,1536]{1,0:T(8,128)(2,1)S(1)}, bf16[64,1536]{1,0:T(8,128)(2,1)S(1)}, u32[]{:S(2)}, u32[]{:S(2)}) collective-permute-start(bf16[64,1536]{1,0:T(8,128)(2,1)S(1)} %scatter.4), channel_id=1, source_target_pairs={{0,24},{4,28},{8,16},{12,20},{16,8},{20,12},{24,0},{28,4},{1,25},{... | collective-permute-start | bytes 589832 | tf_op jit(solution)/shard_map/ppermute | solution.py:413
  472.0 8.3 %collective-permute-start.62 = (bf16[256,1536]{1,0:T(8,128)(2,1)S(1)}, bf16[256,1536]{1,0:T(8,128)(2,1)S(1)}, u32[]{:S(2)}, u32[]{:S(2)}) collective-permute-start(bf16[256,1536]{1,0:T(8,128)(2,1)S(1)} %pad_maximum_fusion.4.near_ref), channel_id=1, source_target_pairs={{0,4},{4,0},{8,12},{12,8},{16,20},{20,16},{24,28},{28,24},{1,5},{5... | collective-permute-start | bytes 2359304 | tf_op jit(solution)/shard_map/ppermute | solution.py:413
  475.6 22.1 %collective-permute-start.63 = (bf16[256,1536]{1,0:T(8,128)(2,1)}, bf16[256,1536]{1,0:T(8,128)(2,1)}, u32[]{:S(2)}, u32[]{:S(2)}) collective-permute-start(bf16[256,1536]{1,0:T(8,128)(2,1)} %get-tuple-element.435), channel_id=1, source_target_pairs={{2,3},{1,0},{6,7},{5,4},{10,11},{9,8},{14,15},{13,12},{18,19},{17,... | collective-permute-start | bytes 2359304 | tf_op jit(solution)/shard_map/ppermute | solution.py:433
  (62 other events, 535.3 us)
Sparse Core Ops, SparseCore 0:
  53.1 97.4 all-gather.1
  212.7 95.9 reduce-scatter.1
  383.7 63.3 all-reduce.6

commit v6 on v5

--- a/solution.py
+++ b/solution.py
@@ -262,8 +262,8 @@
 
 
 def expert_kernel(order_ref, near_ref, far_ref, extra_near_ref, extra_far_ref, router_ref, parts_ref, *refs, top, count):
-    out_refs, gin_refs, terms_ref = refs[:2], refs[2:4], refs[4]
-    weights_ref, sums_ref = refs[5:]
+    out_refs, gin_refs, terms_ref = refs[:2], refs[2:5], refs[5]
+    weights_ref, sums_ref = refs[6:]
     step = pl.program_id(0)
     steps = pl.num_programs(0)
     hidden_width, width = weights_ref.shape[0] // 3, weights_ref.shape[1]
@@ -319,13 +319,20 @@
     grad_in = mul(grad_both, weights_ref[gate_up, :]).astype(BF)
     sums_ref[gate_up, :] += mul(grad_both, rows, TN)
     sums_ref[down, :] += mul(hidden, grad_out, TN)
-    for far in range(2):
-
-        @pl.when(near if far == 0 else step >= steps // 2)
+    far_step = step - steps // 2
+    for k, now in enumerate((near, jnp.logical_not(near))):
+
+        @pl.when(now)
         def _():
-            out_refs[far][...] = combined
-            gin_refs[far][:, :width] = grad_in
-            gin_refs[far][:, width:] = scores
+            out_refs[k][...] = combined
+
+    even = lax.rem(step, 2) == 0
+    for k, now in enumerate((near, (far_step >= 0) & even, (far_step >= 0) & jnp.logical_not(even))):
+
+        @pl.when(now)
+        def _():
+            gin_refs[k][:, :width] = grad_in
+            gin_refs[k][:, width:] = scores
 
     @pl.when(step == steps - 1)
     def _():
@@ -346,7 +353,9 @@
             pl.BlockSpec((BLOCK, lanes), lambda i, o: (jnp.maximum(i - half_steps, 0), 0)),
         ]
 
-    half, half_wide = by_set(width), by_set(wide)
+    half = by_set(width)
+    far_pair = pl.BlockSpec((BLOCK, wide), lambda i, o: (jnp.maximum(i - half_steps, 0) // 2, 0))
+    half_wide = [by_set(wide)[0], far_pair, far_pair]
     whole = pl.BlockSpec((3 * hidden, width), lambda i, o: (0, 0), pipeline_mode=pl.Buffered(1))
     return pl.pallas_call(
         functools.partial(expert_kernel, top=top, count=count),
@@ -366,7 +375,8 @@
             ],
         ),
         out_shape=[jax.ShapeDtypeStruct((total // 2, width), BF)] * 2
-        + [jax.ShapeDtypeStruct((total // 2, wide), BF)] * 2
+        + [jax.ShapeDtypeStruct((total // 2, wide), BF)]
+        + [jax.ShapeDtypeStruct((total // 4, wide), BF)] * 2
         + [jax.ShapeDtypeStruct((3 * hidden, width), BF)],
         compiler_params=pltpu.CompilerParams(vmem_limit_bytes=58 << 20),
         cost_estimate=takes(5 * steps),
@@ -626,25 +636,33 @@
         far = swap(near, 1)
     else:
         near, far = gather_whole(routed_in)
-    out_near, out_far, gin_near, gin_far, terms = run_experts(
+    out_near, out_far, gin_near, gin_even, gin_odd, terms = run_experts(
         order, near, far, extra_near, extra_far, router, expert_parts, top, n_tp
     )
 
     grad_expert = lax.psum_scatter(terms, "tp", scatter_dimension=0, tiled=True)
 
     if fine:
-        gin = sum_cores(gin_near, swap(gin_far, 1))
-        got = sum_first(gin)
-        out_far, gin = join(out_far, gin)
+        gin_near = [gin_near[j * quarter : (j + 1) * quarter] for j in range(4)]
+        other = swap(gin_odd, 1)
+        gin = join(add(gin_near[1], other[:quarter]), add(gin_near[3], other[quarter:]))
+        got = (swap(gin[0], 4), swap(gin[1], 2))
+        out_far, gin_even, gin = join(out_far, gin_even, gin)
+        gin_even = swap(gin_even, 1)
         out_far = swap(out_far, 1)
-        got, out_far = join(got, out_far)
-        gin, got = sum_second(gin, got)
+        got, out_far, gin_even = join(got, out_far, gin_even)
+        gin = join(
+            add(gin_near[0].astype(F32) + gin_even[:quarter].astype(F32), got[0]),
+            add(gin_near[2].astype(F32) + gin_even[quarter:].astype(F32), got[1]),
+        )
+        got = [swap(g[quarter // 2 :], bit) for g, bit in zip(gin, (2, 4))]
         out = sum_cores(out_near, out_far)
         out_got = sum_first(out)
         gin, got = join(gin, got)
         grad_in = sum_last(gin, got)
     else:
-        grad_in = sum_whole(gin_near, gin_far)
+        gin_far = jnp.stack([v.reshape(-1, quarter, v.shape[1]) for v in (gin_even, gin_odd)], axis=1)
+        grad_in = sum_whole(gin_near, gin_far.reshape(gin_near.shape))
     grad_gates = grad_in[:, width : width + experts] + grad_in[:, width + experts : width + 2 * experts]
     inner_gate = jnp.sum(gates * grad_gates, axis=-1, keepdims=True)
     grad_logits = (gates * (grad_gates - inner_gate)).astype(BF)
@@ -658,8 +676,7 @@
     grad_mixed = mul(grad_branch, output_whole, NT).astype(BF)
     grad_mixed = [grad_mixed[:, s * heads_width : (s + 1) * heads_width] for s in range(n_tp)]
 
-    if fine:
-        grad_mixed, out_got = join(grad_mixed, out_got)
+    grad_mixed, grad_branch = join(grad_mixed, grad_branch)
     grad_mixed = [grad_mixed[0]] + [turn(grad_mixed[s], -s) for s in range(1, n_tp)]
     if fine:
         out, out_got = sum_second(out, out_got)
@@ -693,8 +710,8 @@
     result_steps = [step_both(result_mine, result_mine)]
     *blocks, grad_qkv, end_block = attend_back(grad_mixed, query, key, value, logs, tables, qkv_weights, tp_at)
     if fine:
-        blocks, grad_qkv, end_block, result_steps[0], other_output = join(
-            blocks, grad_qkv, end_block, result_steps[0], other_output
+        blocks, grad_qkv, end_block, result_steps[0], other_output, grad_expert, inputs = join(
+            blocks, grad_qkv, end_block, result_steps[0], other_output, grad_expert, inputs
         )
     else:
         blocks, grad_qkv, end_block, result_steps[0] = join(blocks, grad_qkv, end_block, result_steps[0])
@@ -703,30 +720,29 @@
     normed = inputs32 * lax.rsqrt(jnp.mean(inputs32 * inputs32, axis=-1, keepdims=True) + EPS)
     normed = (normed * norm_gain).astype(BF)
     grad_qkv_w = mul(normed, grad_qkv, TN).astype(BF)
-    if fine:
-        grad_output = add(grad_output, other_output)
-
-    def chip_half(j, half):
+
+    def chip_halves(half, *places):
         rows = grad_output.shape[1] // 2
-        chip_rows = lax.dynamic_index_in_dim(grad_output, jnp.bitwise_xor(chip, j), 0, False)
-        return chip_rows[half * rows : (half + 1) * rows]
-
-    if fine:
-        sums = join(
-            *[
-                jnp.concatenate([chip_half(a, half), chip_half(c, half)], axis=0)
-                for half, places in ((0, ((0, 1), (2, 3))), (1, ((0, 2), (1, 3))))
-                for a, c in places
-            ]
-        )
-        got = sum_first(sums)
+        picked = []
+        for j in places:
+            chip_at = (jnp.bitwise_xor(chip, j), half * rows, 0)
+            size = (1, rows, width)
+            picked.append(
+                add(
+                    lax.dynamic_slice(grad_output, chip_at, size)[0],
+                    lax.dynamic_slice(other_output, chip_at, size)[0],
+                )
+            )
+        return jnp.concatenate(picked, axis=0)
+
+    if fine:
+        got = join(chip_halves(0, 2, 3), chip_halves(1, 1, 3))
+        got = (swap(got[0], 4), swap(got[1], 2))
     result_steps.append(step_both(*result_steps[-1], 1))
     sent = step_ends(end_block, end_block, 0, 1)
     if fine:
-        sent, result_steps[-1], got, grad_qkv_w, grad_expert = join(
-            sent, result_steps[-1], got, grad_qkv_w, grad_expert
-        )
-        sums, got = sum_second(sums, got)
+        sent, result_steps[-1], got, grad_qkv_w = join(sent, result_steps[-1], got, grad_qkv_w)
+        sums, got = sum_second((chip_halves(0, 0, 1), None, chip_halves(1, 0, 2)), got)
     else:
         sent, result_steps[-1], grad_qkv_w, grad_expert = join(
             sent, result_steps[-1], grad_qkv_w, grad_expert
@@ -751,6 +767,7 @@
     got = [turn(pieces[s], -s) for s in range(1, n_tp)]
     sent, result_steps, result_last = join(sent, result_steps, result_last)
     grad_normed = blocks[0].astype(F32) + sent[0].astype(F32) + sent[1].astype(F32)
+    inputs_mine = mine(inputs).astype(F32)
     inverse_one = lax.rsqrt(jnp.mean(inputs_mine * inputs_mine, axis=-1, keepdims=True) + EPS)
     unit_one = inputs_mine * inverse_one
     scaled_one = grad_normed * norm_gain

time: 518 us -> 506 us (0.977)
    unnamed x134 -> x164, local copies, waits for them, and re-layouts: 14.9 us -> 19.6 us
    ppermute x34 -> x35, waiting for transfers between devices: 71.7 us -> 67.1 us  [swap(): lax.ppermute(x, 'ep', [(i, i ^ bit) for i in range(lax.axis_size('ep'))])]
    convert_element_type x12 -> x11, other arithmetic: 22.4 us -> 25.7 us  [add(): return (a.astype(F32) + b.astype(F32)).astype(BF)]
    ppermute x34 -> x35, starting transfers between devices: 32.5 us -> 31.2 us  [swap(): lax.ppermute(x, 'ep', [(i, i ^ bit) for i in range(lax.axis_size('ep'))])]
  transfers between devices with their start and end apart: 67 -> 68, of which waited for: 28 -> 27; matrix products, arithmetic and copies ran while one was open for 20% -> 19% of each run, Pallas kernels for 10% -> 10%
where the time goes in v6:
time: 506 us; the launch traced here: 500 us
  waiting for transfers between devices  180 us (36%)
  starting transfers between devices  96.8 us (19%)
  Pallas kernels  93.5 us (18%)
  local copies, waits for them, and re-layouts  53.5 us (11%)
  other arithmetic  49.4 us (10%)
  between operations  15.7 us (3%)
  matrix products  11.6 us (2%)
    ppermute x35, waiting for transfers between devices, swap(): lax.ppermute(x, 'ep', [(i, i ^ bit) for i in range(lax.axis_size('ep'))])  67.1 us
    ppermute x15, waiting for transfers between devices, turn(): return lax.ppermute(x, 'tp', [(i, (i + by) % n) for i in range(n)])  50.5 us
    pallas_call x1, Pallas kernels, run_experts(): pl.pallas_call(functools.partial(expert_kernel, top=top, count=count), gr...  44.9 us
    ppermute x35, starting transfers between devices, swap(): lax.ppermute(x, 'ep', [(i, i ^ bit) for i in range(lax.axis_size('ep'))])  31.2 us
    ppermute x12, starting transfers between devices, step_both(): return (lax.ppermute(right, 'tp', pairs), lax.ppermute(left, 'tp', mirror))  29 us
    ppermute x15, starting transfers between devices, turn(): return lax.ppermute(x, 'tp', [(i, (i + by) % n) for i in range(n)])  27.9 us
    convert_element_type x11, other arithmetic, add(): return (a.astype(F32) + b.astype(F32)).astype(BF)  25.7 us
    pallas_call x1, Pallas kernels, attend_back(): pl.pallas_call(attend_back_kernel, in_specs=[SMEM] + [VMEM] * (9 + count)...  25.5 us
  transfers between devices with their start and end apart: 68, of which 27 were waited for; matrix products, arithmetic and copies ran while one was open for 19% of the time, Pallas kernels for 10%

profile of v6, /device:TPU:0, one launch (start us, length us, event | category | flops | bytes accessed | tf_op | source)
XLA Modules:
  0.0 500.1 jit_solution(13430436973915292577)
XLA Ops:
  8.5 5.1 %collective-permute-start = (bf16[48,1536]{1,0:T(8,128)(2,1)S(1)}, bf16[48,1536]{1,0:T(8,128)(2,1)S(1)}, u32[]{:S(2)}, u32[]{:S(2)}) collective-permute-start(bf16[48,1536]{1,0:T(8,128)(2,1)S(1)} %constant_dynamic-slice_fusion.2), channel_id=1, source_target_pairs={{0,3},{1,0},{2,1},{3,2},{4,7},{5,4},{6,5},{7,6},{8,11},{9,8},{10,9... | collective-permute-start | bytes 442376 | tf_op jit(solution)/shard_map/ppermute | solution.py:428
  22.2 3.9 collective-permute-done.1
  26.1 1.6 collective-permute-start.3
  27.7 1.6 collective-permute-start.4
  30.3 19.7 %shard_map.239 = (bf16[256,384]{1,0:T(8,128)(2,1)S(1)}, bf16[256,384]{1,0:T(8,128)(2,1)S(1)}, bf16[256,384]{1,0:T(8,128)(2,1)S(1)}, bf16[256,384]{1,0:T(8,128)(2...) custom-call(s32[1]{0:T(128)} %bitcast.8.at_ref, ...), custom_call_target="tpu_custom_call" | custom-call | flops 23000000512 | tf_op jit(solution)/shard_map/pallas_call | solution.py:121
  55.8 1.9 collective-permute-start.8
  57.7 3.1 collective-permute-start.9
  60.8 1.7 pad_maximum_fusion
  62.6 2.1 collective-permute-done.7
  66.2 10.3 %collective-permute-done.8 = bf16[256,384]{1,0:T(8,128)(2,1)S(1)} collective-permute-done((bf16[256,384]{1,0:T(8,128)(2,1)S(1)}, bf16[256,384]{1,0:T(8,128)(2,1)S(1)}, u32[]{:S(2)}, u32[]{:S(2)}) %collective-permute-start.8) | collective-permute-done | bytes 196640 | tf_op jit(solution)/shard_map/ppermute | solution.py:428
  81.4 3.5 collective-permute-done.12
  85.3 3.2 multiply_reduce_fusion.2
  91.7 6.6 %collective-permute-done.16 = bf16[256,1664]{1,0:T(8,128)(2,1)S(1)} collective-permute-done((bf16[256,1664]{1,0:T(8,128)(2,1)S(1)}, bf16[256,1664]{1,0:T(8,128)(2,1)S(1)}, u32[]{:S(2)}, u32[]{:S(2)}) %collective-permute-start.16) | collective-permute-done | bytes 852000 | tf_op jit(solution)/shard_map/ppermute | solution.py:423
  98.3 5.1 %collective-permute-done.13 = bf16[128,1536]{1,0:T(8,128)(2,1)S(1)} collective-permute-done((bf16[128,1536]{1,0:T(8,128)(2,1)S(1)}, bf16[128,1536]{1,0:T(8,128)(2,1)S(1)}, u32[]{:S(2)}, u32[]{:S(2)}) %collective-permute-start.13) | collective-permute-done | bytes 393248 | tf_op jit(solution)/shard_map/ppermute | solution.py:423
  103.6 1.7 collective-permute-start.17
  110.7 9.3 %collective-permute-done.17 = bf16[256,1536]{1,0:T(8,128)(2,1)S(1)} collective-permute-done((bf16[256,1536]{1,0:T(8,128)(2,1)S(1)}, bf16[256,1536]{1,0:T(8,128)(2,1)S(1)}, u32[]{:S(2)}, u32[]{:S(2)}) %collective-permute-start.17) | collective-permute-done | bytes 786464 | tf_op jit(solution)/shard_map/ppermute | solution.py:423
  125.1 25.5 %all-gather.2.cloned.1.call-done.parts_ref = bf16[1536,1536]{1,0:T(8,128)(2,1)} async-done(((bf16[384,1536]{1,0:T(8,128)(2,1)}), bf16[1536,1536]{1,0:T(8,128)(2,1)}) %all-gather.2.cloned.1.call-update) | async-done | bytes 4718608 | tf_op jit(solution)/shard_map/all_gather | solution.py:559
  150.6 44.9 %shard_map.240 = (bf16[1024,1536]{1,0:T(8,128)(2,1)}, bf16[1024,1536]{1,0:T(8,128)(2,1)}, bf16[1024,1664]{1,0:T(8,128)(2,1)}, bf16[512,1664]{1,0:T(8,128)(2,1)},...) custom-call(s32[2]{0:T(128)} %pad_add_fusion.order_ref, ...), custom_call_target="tpu_custom_call" | custom-call | flops 46000001024 | tf_op jit(solution)/shard_map/pallas_call | solution.py:360
  195.6 3.8 collective-permute-done.21
  199.4 3.0 add_convert_fusion.2
  206.2 17.9 %collective-permute-done.22 = bf16[256,1664]{1,0:T(8,128)(2,1)} collective-permute-done((bf16[256,1664]{1,0:T(8,128)(2,1)}, bf16[256,1664]{1,0:T(8,128)(2,1)}, u32[]{:S(2)}, u32[]{:S(2)}) %collective-permute-start.22) | collective-permute-done | bytes 852000 | tf_op jit(solution)/shard_map/ppermute | solution.py:423
  225.4 3.3 add_convert_fusion
  230.9 4.1 add_convert_fusion.8
  234.9 1.5 collective-permute-start.31
  237.1 4.5 collective-permute-done.26
  241.6 1.6 collective-permute-done.27
  245.4 1.6 fusion.44
  249.4 2.4 collective-permute-start.28
  254.0 2.6 copy.44
  258.2 1.7 add_convert_fusion.7
  262.5 1.6 fusion.7
  264.1 24.8 %collective-permute-done.29.refs_2_ = bf16[256,384]{1,0:T(8,128)(2,1)S(1)} collective-permute-done((bf16[256,384]{1,0:T(8,128)(2,1)}, bf16[256,384]{1,0:T(8,128)(2,1)S(1)}, u32[]{:S(2)}, u32[]{:S(2)}) %collective-permute-start.29) | collective-permute-done | bytes 196640 | tf_op jit(solution)/shard_map/ppermute | solution.py:428
  289.7 2.6 collective-permute-start.35
  292.3 1.7 collective-permute-start.36
  295.9 25.5 %shard_map.241 = (bf16[256,1536]{1,0:T(8,128)(2,1)S(1)}, bf16[256,1536]{1,0:T(8,128)(2,1)S(1)}, bf16[256,1536]{1,0:T(8,128)(2,1)S(1)}, bf16[256,1536]{1,0:T(8,12...) custom-call(s32[1]{0:T(128)} %bitcast.8.at_ref, bf16[6,1024,64]{2,1,0:T(8,128)(2,1)} %get-tuple-element.195.q_ref, ...), custom_call_target="tpu_custom_call" | custom-call | flops 23000000512 | tf_op jit(solution)/shard_map/pallas_call | solution.py:231
  323.2 5.8 %collective-permute-start.38 = (bf16[256,1536]{1,0:T(8,128)(2,1)}, bf16[256,1536]{1,0:T(8,128)(2,1)}, u32[]{:S(2)}, u32[]{:S(2)}) collective-permute-start(bf16[256,1536]{1,0:T(8,128)(2,1)} %get-tuple-element.294), channel_id=1, source_target_pairs={{0,1},{3,2},{4,5},{7,6},{8,9},{11,10},{12,13},{15,14},{16,17},{19,... | collective-permute-start | bytes 2359304 | tf_op jit(solution)/shard_map/ppermute | solution.py:443
  331.0 4.2 fusion.33
  338.6 1.7 convert_element_type.505
  340.3 4.3 convolution_convert_fusion.1
  344.6 8.9 %collective-permute-done.41 = bf16[208,1536]{1,0:T(8,128)(2,1)} collective-permute-done((bf16[208,1536]{1,0:T(8,128)(2,1)}, bf16[208,1536]{1,0:T(8,128)(2,1)}, u32[]{:S(2)}, u32[]{:S(2)}) %collective-permute-start.41) | collective-permute-done | bytes 639008 | tf_op jit(solution)/shard_map/ppermute | solution.py:423
  354.0 2.7 fusion.15
  356.6 5.3 %collective-permute-start.43 = (bf16[256,1536]{1,0:T(8,128)(2,1)}, bf16[256,1536]{1,0:T(8,128)(2,1)}, u32[]{:S(2)}, u32[]{:S(2)}) collective-permute-start(bf16[256,1536]{1,0:T(8,128)(2,1)} %get-tuple-element.425), channel_id=1, source_target_pairs={{0,1},{1,2},{4,5},{5,6},{8,9},{9,10},{12,13},{13,14},{16,17},{17,1... | collective-permute-start | bytes 2359304 | tf_op jit(solution)/shard_map/ppermute | solution.py:435
  362.0 1.5 collective-permute-start.44
  363.5 2.1 broadcast_select_fusion.1
  370.9 1.7 collective-permute-start.47
  378.8 6.5 %collective-permute-done.45 = bf16[256,1536]{1,0:T(8,128)(2,1)} collective-permute-done((bf16[256,1536]{1,0:T(8,128)(2,1)}, bf16[256,1536]{1,0:T(8,128)(2,1)}, u32[]{:S(2)}, u32[]{:S(2)}) %collective-permute-start.45) | collective-permute-done | bytes 786464 | tf_op jit(solution)/shard_map/ppermute | solution.py:443
  387.9 2.0 collective-permute-start.51
  393.7 6.7 %collective-permute-start.48 = (bf16[56,1536]{1,0:T(8,128)(2,1)S(1)}, bf16[56,1536]{1,0:T(8,128)(2,1)S(1)}, u32[]{:S(2)}, u32[]{:S(2)}) collective-permute-start(bf16[56,1536]{1,0:T(8,128)(2,1)S(1)} %get-tuple-element.440), channel_id=1, source_target_pairs={{0,3},{1,0},{2,1},{3,2},{4,7},{5,4},{6,5},{7,6},{8,11},{9,8},{10,9... | collective-permute-start | bytes 516104 | tf_op jit(solution)/shard_map/ppermute | solution.py:428
  401.0 6.6 %collective-permute-done.51 = bf16[256,1536]{1,0:T(8,128)(2,1)S(1)} collective-permute-done((bf16[256,1536]{1,0:T(8,128)(2,1)S(1)}, bf16[256,1536]{1,0:T(8,128)(2,1)S(1)}, u32[]{:S(2)}, u32[]{:S(2)}) %collective-permute-start.51) | collective-permute-done | bytes 786464 | tf_op jit(solution)/shard_map/ppermute | solution.py:435
  407.6 4.5 collective-permute-done.52
  412.9 2.2 fusion.20
  415.2 9.4 %collective-permute-start.56 = (bf16[256,1536]{1,0:T(8,128)(2,1)S(1)}, bf16[256,1536]{1,0:T(8,128)(2,1)S(1)}, u32[]{:S(2)}, u32[]{:S(2)}) collective-permute-start(bf16[256,1536]{1,0:T(8,128)(2,1)S(1)} %fusion.20), channel_id=1, source_target_pairs={{0,1},{1,2},{2,3},{4,5},{5,6},{6,7},{8,9},{9,10},{10,11},{12,13},{... | collective-permute-start | bytes 2359304 | tf_op jit(solution)/shard_map/ppermute | solution.py:435
  428.9 2.7 collective-permute-start.53
  432.6 2.0 collective-permute-start.55
  434.7 6.8 %collective-permute-done.53 = f32[1,1536]{1,0:T(1,128)S(1)} collective-permute-done((f32[1,1536]{1,0:T(1,128)S(1)}, f32[1,1536]{1,0:T(1,128)S(1)}, u32[]{:S(2)}, u32[]{:S(2)}) %collective-permute-start.53) | collective-permute-done | bytes 6176 | tf_op jit(solution)/shard_map/ppermute | solution.py:428
  441.5 2.6 collective-permute-done.54
  450.0 1.9 broadcast.86.clone
  452.8 2.1 constant_dynamic-update-slice_fusion.17
  455.2 7.2 %collective-permute-done.62 = bf16[256,1536]{1,0:T(8,128)(2,1)S(1)} collective-permute-done((bf16[256,1536]{1,0:T(8,128)(2,1)}, bf16[256,1536]{1,0:T(8,128)(2,1)S(1)}, u32[]{:S(2)}, u32[]{:S(2)}) %collective-permute-start.62) | collective-permute-done | bytes 786464 | tf_op jit(solution)/shard_map/ppermute | solution.py:435
  464.4 2.5 constant_dynamic-update-slice_fusion.27
  470.6 2.1 shard_map.242
  472.8 3.0 slice.436
  477.6 11.4 %collective-permute-done.64 = bf16[256,1536]{1,0:T(8,128)(2,1)} collective-permute-done((bf16[256,1536]{1,0:T(8,128)(2,1)}, bf16[256,1536]{1,0:T(8,128)(2,1)}, u32[]{:S(2)}, u32[]{:S(2)}) %collective-permute-start.64) | collective-permute-done | bytes 786464 | tf_op jit(solution)/shard_map/ppermute | solution.py:443
  490.3 2.1 constant_dynamic-update-slice_fusion.26
  (390 shorter events, 107.0 us)
Async XLA Ops:
  7.2 143.4 %all-gather.2.cloned.1.call-start = ((), (), s32[]{:S(2)}) async-start(), calls=%async_computation.1 | async-start | bytes 5898240 | tf_op jit(solution)/shard_map/all_gather | solution.py:559
  8.5 13.7 %collective-permute-start = (bf16[48,1536]{1,0:T(8,128)(2,1)S(1)}, bf16[48,1536]{1,0:T(8,128)(2,1)S(1)}, u32[]{:S(2)}, u32[]{:S(2)}) collective-permute-start(bf16[48,1536]{1,0:T(8,128)(2,1)S(1)} %constant_dynamic-slice_fusion.2), channel_id=1, source_target_pairs={{0,3},{1,0},{2,1},{3,2},{4,7},{5,4},{6,5},{7,6},{8,11},{9,8},{10,9... | collective-permute-start | bytes 442376 | tf_op jit(solution)/shard_map/ppermute | solution.py:428
  13.6 12.5 %collective-permute-start.1 = (bf16[48,1536]{1,0:T(8,128)(2,1)S(1)}, bf16[48,1536]{1,0:T(8,128)(2,1)S(1)}, u32[]{:S(2)}, u32[]{:S(2)}) collective-permute-start(bf16[48,1536]{1,0:T(8,128)(2,1)S(1)} %constant_dynamic-slice_fusion.2), channel_id=1, source_target_pairs={{0,2},{1,3},{2,0},{3,1},{4,6},{5,7},{6,4},{7,5},{8,10},{9,11},{10,... | collective-permute-start | bytes 442376 | tf_op jit(solution)/shard_map/ppermute | solution.py:428
  13.6 12.5 %collective-permute-start.2 = (bf16[48,1536]{1,0:T(8,128)(2,1)S(1)}, bf16[48,1536]{1,0:T(8,128)(2,1)S(1)}, u32[]{:S(2)}, u32[]{:S(2)}) collective-permute-start(bf16[48,1536]{1,0:T(8,128)(2,1)S(1)} %constant_dynamic-slice_fusion.2), channel_id=1, source_target_pairs={{0,1},{1,2},{2,3},{3,0},{4,5},{5,6},{6,7},{7,4},{8,9},{9,10},{10,1... | collective-permute-start | bytes 442376 | tf_op jit(solution)/shard_map/ppermute | solution.py:428
  17.8 33.8 %collective-permute-start.5 = (bf16[128,1664]{1,0:T(8,128)(2,1)}, bf16[128,1664]{1,0:T(8,128)(2,1)}, u32[]{:S(2)}, u32[]{:S(2)}) collective-permute-start(bf16[128,1664]{1,0:T(8,128)(2,1)} %get-tuple-element.427), channel_id=1, source_target_pairs={{0,8},{4,12},{8,0},{12,4},{16,24},{20,28},{24,16},{28,20},{1,9},{5... | collective-permute-start | bytes 1277960 | tf_op jit(solution)/shard_map/ppermute | solution.py:423
  19.3 32.4 %collective-permute-start.6 = (bf16[128,1664]{1,0:T(8,128)(2,1)}, bf16[128,1664]{1,0:T(8,128)(2,1)}, u32[]{:S(2)}, u32[]{:S(2)}) collective-permute-start(bf16[128,1664]{1,0:T(8,128)(2,1)} %get-tuple-element.426), channel_id=1, source_target_pairs={{0,16},{4,20},{8,24},{12,28},{16,0},{20,4},{24,8},{28,12},{1,17},{... | collective-permute-start | bytes 1277960 | tf_op jit(solution)/shard_map/ppermute | solution.py:423
  26.1 25.6 %collective-permute-start.3 = (bf16[96,1536]{1,0:T(8,128)(2,1)S(1)}, bf16[96,1536]{1,0:T(8,128)(2,1)S(1)}, u32[]{:S(2)}, u32[]{:S(2)}) collective-permute-start(bf16[96,1536]{1,0:T(8,128)(2,1)S(1)} %pad_maximum_fusion.9), channel_id=1, source_target_pairs={{0,8},{4,12},{8,0},{12,4},{16,24},{20,28},{24,16},{28,20},{1,9},{5... | collective-permute-start | bytes 884744 | tf_op jit(solution)/shard_map/ppermute | solution.py:423
  27.7 24.0 %collective-permute-start.4 = (bf16[96,1536]{1,0:T(8,128)(2,1)S(1)}, bf16[96,1536]{1,0:T(8,128)(2,1)S(1)}, u32[]{:S(2)}, u32[]{:S(2)}) collective-permute-start(bf16[96,1536]{1,0:T(8,128)(2,1)S(1)} %pad_maximum_fusion.10), channel_id=1, source_target_pairs={{0,16},{4,20},{8,24},{12,28},{16,0},{20,4},{24,8},{28,12},{1,17},{... | collective-permute-start | bytes 884744 | tf_op jit(solution)/shard_map/ppermute | solution.py:423
  51.8 26.1 %collective-permute-start.10 = (bf16[192,1536]{1,0:T(8,128)(2,1)S(1)}, bf16[192,1536]{1,0:T(8,128)(2,1)}, u32[]{:S(2)}, u32[]{:S(2)}) collective-permute-start(bf16[192,1536]{1,0:T(8,128)(2,1)S(1)} %get-tuple-element.219), channel_id=1, source_target_pairs={{0,16},{4,20},{8,24},{12,28},{16,0},{20,4},{24,8},{28,12},{1,17},{... | collective-permute-start | bytes 1769480 | tf_op jit(solution)/shard_map/ppermute | solution.py:423
  52.4 25.6 %collective-permute-start.11 = (bf16[192,1536]{1,0:T(8,128)(2,1)S(1)}, bf16[192,1536]{1,0:T(8,128)(2,1)}, u32[]{:S(2)}, u32[]{:S(2)}) collective-permute-start(bf16[192,1536]{1,0:T(8,128)(2,1)S(1)} %get-tuple-element.221), channel_id=1, source_target_pairs={{0,8},{4,12},{8,0},{12,4},{16,24},{20,28},{24,16},{28,20},{1,9},{5... | collective-permute-start | bytes 1769480 | tf_op jit(solution)/shard_map/ppermute | solution.py:423
  52.9 270.3 %reduce-scatter.2.cloned.1.call-start = ((), (), s32[]{:S(2)}) async-start(), calls=%async_computation.2 | async-start | bytes 5898240 | tf_op jit(solution)/shard_map/reduce_scatter | solution.py:643
  55.0 9.7 %collective-permute-start.7 = (bf16[256,384]{1,0:T(8,128)(2,1)S(1)}, bf16[256,384]{1,0:T(8,128)(2,1)S(1)}, u32[]{:S(2)}, u32[]{:S(2)}) collective-permute-start(bf16[256,384]{1,0:T(8,128)(2,1)S(1)} %get-tuple-element.208), channel_id=1, source_target_pairs={{0,1},{1,2},{2,3},{3,0},{4,5},{5,6},{6,7},{7,4},{8,9},{9,10},{10,1... | collective-permute-start | bytes 589832 | tf_op jit(solution)/shard_map/ppermute | solution.py:428
  55.8 20.6 %collective-permute-start.8 = (bf16[256,384]{1,0:T(8,128)(2,1)S(1)}, bf16[256,384]{1,0:T(8,128)(2,1)S(1)}, u32[]{:S(2)}, u32[]{:S(2)}) collective-permute-start(bf16[256,384]{1,0:T(8,128)(2,1)S(1)} %get-tuple-element.209), channel_id=1, source_target_pairs={{0,2},{1,3},{2,0},{3,1},{4,6},{5,7},{6,4},{7,5},{8,10},{9,11},{10,... | collective-permute-start | bytes 589832 | tf_op jit(solution)/shard_map/ppermute | solution.py:428
  57.7 20.2 %collective-permute-start.9 = (bf16[256,384]{1,0:T(8,128)(2,1)S(1)}, bf16[256,384]{1,0:T(8,128)(2,1)S(1)}, u32[]{:S(2)}, u32[]{:S(2)}) collective-permute-start(bf16[256,384]{1,0:T(8,128)(2,1)S(1)} %get-tuple-element.210), channel_id=1, source_target_pairs={{0,3},{1,0},{2,1},{3,2},{4,7},{5,4},{6,5},{7,6},{8,11},{9,8},{10,9... | collective-permute-start | bytes 589832 | tf_op jit(solution)/shard_map/ppermute | solution.py:428
  64.6 27.1 %collective-permute-start.15 = (bf16[256,1664]{1,0:T(8,128)(2,1)S(1)}, bf16[256,1664]{1,0:T(8,128)(2,1)S(1)}, u32[]{:S(2)}, u32[]{:S(2)}) collective-permute-start(bf16[256,1664]{1,0:T(8,128)(2,1)S(1)} %get-tuple-element.236), channel_id=1, source_target_pairs={{0,16},{4,20},{8,24},{12,28},{16,0},{20,4},{24,8},{28,12},{1,17},{... | collective-permute-start | bytes 2555912 | tf_op jit(solution)/shard_map/ppermute | solution.py:423
  76.4 21.9 %collective-permute-start.16 = (bf16[256,1664]{1,0:T(8,128)(2,1)S(1)}, bf16[256,1664]{1,0:T(8,128)(2,1)S(1)}, u32[]{:S(2)}, u32[]{:S(2)}) collective-permute-start(bf16[256,1664]{1,0:T(8,128)(2,1)S(1)} %get-tuple-element.238), channel_id=1, source_target_pairs={{0,8},{4,12},{8,0},{12,4},{16,24},{20,28},{24,16},{28,20},{1,9},{5... | collective-permute-start | bytes 2555912 | tf_op jit(solution)/shard_map/ppermute | solution.py:423
  88.9 14.6 %collective-permute-start.13 = (bf16[128,1536]{1,0:T(8,128)(2,1)S(1)}, bf16[128,1536]{1,0:T(8,128)(2,1)S(1)}, u32[]{:S(2)}, u32[]{:S(2)}) collective-permute-start(bf16[128,1536]{1,0:T(8,128)(2,1)S(1)} %get-tuple-element.435), channel_id=1, source_target_pairs={{0,8},{4,12},{8,0},{12,4},{16,24},{20,28},{24,16},{28,20},{1,9},{5... | collective-permute-start | bytes 1179656 | tf_op jit(solution)/shard_map/ppermute | solution.py:423
  89.4 14.0 %collective-permute-start.14 = (bf16[128,1536]{1,0:T(8,128)(2,1)S(1)}, bf16[128,1536]{1,0:T(8,128)(2,1)S(1)}, u32[]{:S(2)}, u32[]{:S(2)}) collective-permute-start(bf16[128,1536]{1,0:T(8,128)(2,1)S(1)} %get-tuple-element.434), channel_id=1, source_target_pairs={{0,16},{4,20},{8,24},{12,28},{16,0},{20,4},{24,8},{28,12},{1,17},{... | collective-permute-start | bytes 1179656 | tf_op jit(solution)/shard_map/ppermute | solution.py:423
  103.6 16.4 %collective-permute-start.17 = (bf16[256,1536]{1,0:T(8,128)(2,1)S(1)}, bf16[256,1536]{1,0:T(8,128)(2,1)S(1)}, u32[]{:S(2)}, u32[]{:S(2)}) collective-permute-start(bf16[256,1536]{1,0:T(8,128)(2,1)S(1)} %pad_maximum_fusion.2), channel_id=1, source_target_pairs={{0,16},{4,20},{8,24},{12,28},{16,0},{20,4},{24,8},{28,12},{1,17},{... | collective-permute-start | bytes 2359304 | tf_op jit(solution)/shard_map/ppermute | solution.py:423
  105.3 16.1 %collective-permute-start.18 = (bf16[256,1536]{1,0:T(8,128)(2,1)S(1)}, bf16[256,1536]{1,0:T(8,128)(2,1)S(1)}, u32[]{:S(2)}, u32[]{:S(2)}) collective-permute-start(bf16[256,1536]{1,0:T(8,128)(2,1)S(1)} %pad_maximum_fusion.3), channel_id=1, source_target_pairs={{0,8},{4,12},{8,0},{12,4},{16,24},{20,28},{24,16},{28,20},{1,9},{5... | collective-permute-start | bytes 2359304 | tf_op jit(solution)/shard_map/ppermute | solution.py:423
  110.7 39.9 %collective-permute-start.20 = (bf16[1024,1664]{1,0:T(8,128)(2,1)}, bf16[1024,1664]{1,0:T(8,128)(2,1)}, u32[]{:S(2)}, u32[]{:S(2)}) collective-permute-start(bf16[1024,1664]{1,0:T(8,128)(2,1)} %constant_dynamic-update-slice_fusion.12.extra_near_ref), channel_id=1, source_target_pairs={{0,4},{4,0},{8,12},{12,8},{16,20},{20,16},{24,28},{28,24},{1,5},{5... | collective-permute-start | bytes 10223624 | tf_op jit(solution)/shard_map/ppermute | solution.py:423
  125.1 25.5 %collective-permute-start.19 = (bf16[1024,1536]{1,0:T(8,128)(2,1)}, bf16[1024,1536]{1,0:T(8,128)(2,1)}, u32[]{:S(2)}, u32[]{:S(2)}) collective-permute-start(bf16[1024,1536]{1,0:T(8,128)(2,1)} %constant_dynamic-update-slice_fusion.8.near_ref), channel_id=1, source_target_pairs={{0,4},{4,0},{8,12},{12,8},{16,20},{20,16},{24,28},{28,24},{1,5},{5... | collective-permute-start | bytes 9437192 | tf_op jit(solution)/shard_map/ppermute | solution.py:423
  202.4 23.1 %collective-permute-start.24 = (bf16[1024,1536]{1,0:T(8,128)(2,1)}, bf16[1024,1536]{1,0:T(8,128)(2,1)}, u32[]{:S(2)}, u32[]{:S(2)}) collective-permute-start(bf16[1024,1536]{1,0:T(8,128)(2,1)} %get-tuple-element.247), channel_id=1, source_target_pairs={{0,4},{4,0},{8,12},{12,8},{16,20},{20,16},{24,28},{28,24},{1,5},{5... | collective-permute-start | bytes 9437192 | tf_op jit(solution)/shard_map/ppermute | solution.py:423
  202.5 22.9 %collective-permute-start.25 = (bf16[512,1664]{1,0:T(8,128)(2,1)}, bf16[512,1664]{1,0:T(8,128)(2,1)}, u32[]{:S(2)}, u32[]{:S(2)}) collective-permute-start(bf16[512,1664]{1,0:T(8,128)(2,1)} %get-tuple-element.248), channel_id=1, source_target_pairs={{0,4},{4,0},{8,12},{12,8},{16,20},{20,16},{24,28},{28,24},{1,5},{5... | collective-permute-start | bytes 5111816 | tf_op jit(solution)/shard_map/ppermute | solution.py:423
  202.9 21.3 %collective-permute-start.22 = (bf16[256,1664]{1,0:T(8,128)(2,1)}, bf16[256,1664]{1,0:T(8,128)(2,1)}, u32[]{:S(2)}, u32[]{:S(2)}) collective-permute-start(bf16[256,1664]{1,0:T(8,128)(2,1)} %get-tuple-element.243), channel_id=1, source_target_pairs={{0,16},{4,20},{8,24},{12,28},{16,0},{20,4},{24,8},{28,12},{1,17},{... | collective-permute-start | bytes 2555912 | tf_op jit(solution)/shard_map/ppermute | solution.py:423
  204.4 21.0 %collective-permute-start.23 = (bf16[256,1664]{1,0:T(8,128)(2,1)}, bf16[256,1664]{1,0:T(8,128)(2,1)}, u32[]{:S(2)}, u32[]{:S(2)}) collective-permute-start(bf16[256,1664]{1,0:T(8,128)(2,1)} %get-tuple-element.244), channel_id=1, source_target_pairs={{0,8},{4,12},{8,0},{12,4},{16,24},{20,28},{24,16},{28,20},{1,9},{5... | collective-permute-start | bytes 2555912 | tf_op jit(solution)/shard_map/ppermute | solution.py:423
  206.0 264.6 %all-reduce.7.cloned.1.call-start = ((), (), s32[]{:S(2)}) async-start(), calls=%async_computation.3 | async-start | bytes 3932160 | tf_op jit(solution)/shard_map/psum | solution.py:750
  228.8 12.8 %collective-permute-start.26 = (bf16[128,1664]{1,0:T(8,128)(2,1)S(1)}, bf16[128,1664]{1,0:T(8,128)(2,1)S(1)}, u32[]{:S(2)}, u32[]{:S(2)}) collective-permute-start(bf16[128,1664]{1,0:T(8,128)(2,1)S(1)} %slice.341), channel_id=1, source_target_pairs={{0,8},{4,12},{8,0},{12,4},{16,24},{20,28},{24,16},{28,20},{1,9},{5... | collective-permute-start | bytes 1277960 | tf_op jit(solution)/shard_map/ppermute | solution.py:423
  230.4 12.8 %collective-permute-start.27 = (bf16[128,1664]{1,0:T(8,128)(2,1)S(1)}, bf16[128,1664]{1,0:T(8,128)(2,1)S(1)}, u32[]{:S(2)}, u32[]{:S(2)}) collective-permute-start(bf16[128,1664]{1,0:T(8,128)(2,1)S(1)} %slice.342), channel_id=1, source_target_pairs={{0,16},{4,20},{8,24},{12,28},{16,0},{20,4},{24,8},{28,12},{1,17},{... | collective-permute-start | bytes 1277960 | tf_op jit(solution)/shard_map/ppermute | solution.py:423
  234.9 23.2 %collective-permute-start.31 = (bf16[256,1536]{1,0:T(8,128)(2,1)}, bf16[256,1536]{1,0:T(8,128)(2,1)}, u32[]{:S(2)}, u32[]{:S(2)}) collective-permute-start(bf16[256,1536]{1,0:T(8,128)(2,1)} %get-tuple-element.266), channel_id=1, source_target_pairs={{0,16},{4,20},{8,24},{12,28},{16,0},{20,4},{24,8},{28,12},{1,17},{... | collective-permute-start | bytes 2359304 | tf_op jit(solution)/shard_map/ppermute | solution.py:423
  236.5 23.4 %collective-permute-start.32 = (bf16[256,1536]{1,0:T(8,128)(2,1)}, bf16[256,1536]{1,0:T(8,128)(2,1)}, u32[]{:S(2)}, u32[]{:S(2)}) collective-permute-start(bf16[256,1536]{1,0:T(8,128)(2,1)} %get-tuple-element.268), channel_id=1, source_target_pairs={{0,8},{4,12},{8,0},{12,4},{16,24},{20,28},{24,16},{28,20},{1,9},{5... | collective-permute-start | bytes 2359304 | tf_op jit(solution)/shard_map/ppermute | solution.py:423
  249.4 14.8 %collective-permute-start.28 = (bf16[256,384]{1,0:T(8,128)(2,1)}, bf16[256,384]{1,0:T(8,128)(2,1)S(1)}, u32[]{:S(2)}, u32[]{:S(2)}) collective-permute-start(bf16[256,384]{1,0:T(8,128)(2,1)} %get-tuple-element.260), channel_id=1, source_target_pairs={{0,3},{1,0},{2,1},{3,2},{4,7},{5,4},{6,5},{7,6},{8,11},{9,8},{10,9... | collective-permute-start | bytes 589832 | tf_op jit(solution)/shard_map/ppermute | solution.py:428
  251.7 37.3 %collective-permute-start.29 = (bf16[256,384]{1,0:T(8,128)(2,1)}, bf16[256,384]{1,0:T(8,128)(2,1)S(1)}, u32[]{:S(2)}, u32[]{:S(2)}) collective-permute-start(bf16[256,384]{1,0:T(8,128)(2,1)} %get-tuple-element.261), channel_id=1, source_target_pairs={{0,2},{1,3},{2,0},{3,1},{4,6},{5,7},{6,4},{7,5},{8,10},{9,11},{10,... | collective-permute-start | bytes 589832 | tf_op jit(solution)/shard_map/ppermute | solution.py:428
  251.7 37.3 %collective-permute-start.30 = (bf16[256,384]{1,0:T(8,128)(2,1)}, bf16[256,384]{1,0:T(8,128)(2,1)S(1)}, u32[]{:S(2)}, u32[]{:S(2)}) collective-permute-start(bf16[256,384]{1,0:T(8,128)(2,1)} %get-tuple-element.262), channel_id=1, source_target_pairs={{0,1},{1,2},{2,3},{3,0},{4,5},{5,6},{6,7},{7,4},{8,9},{9,10},{10,1... | collective-permute-start | bytes 589832 | tf_op jit(solution)/shard_map/ppermute | solution.py:428
  261.4 27.6 %collective-permute-start.33 = (bf16[128,1536]{1,0:T(8,128)(2,1)S(1)}, bf16[128,1536]{1,0:T(8,128)(2,1)S(1)}, u32[]{:S(2)}, u32[]{:S(2)}) collective-permute-start(bf16[128,1536]{1,0:T(8,128)(2,1)S(1)} %slice.360), channel_id=1, source_target_pairs={{0,8},{4,12},{8,0},{12,4},{16,24},{20,28},{24,16},{28,20},{1,9},{5... | collective-permute-start | bytes 1179656 | tf_op jit(solution)/shard_map/ppermute | solution.py:423
  262.0 27.0 %collective-permute-start.34 = (bf16[128,1536]{1,0:T(8,128)(2,1)S(1)}, bf16[128,1536]{1,0:T(8,128)(2,1)S(1)}, u32[]{:S(2)}, u32[]{:S(2)}) collective-permute-start(bf16[128,1536]{1,0:T(8,128)(2,1)S(1)} %slice.361), channel_id=1, source_target_pairs={{0,16},{4,20},{8,24},{12,28},{16,0},{20,4},{24,8},{28,12},{1,17},{... | collective-permute-start | bytes 1179656 | tf_op jit(solution)/shard_map/ppermute | solution.py:423
  289.0 34.2 %collective-permute-start.37 = (bf16[4,208,1536]{2,1,0:T(8,128)(2,1)S(1)}, bf16[4,208,1536]{2,1,0:T(8,128)(2,1)}, u32[]{:S(2)}, u32[]{:S(2)}) collective-permute-start(bf16[4,208,1536]{2,1,0:T(8,128)(2,1)S(1)} %get-tuple-element.291), channel_id=1, source_target_pairs={{0,4},{4,0},{8,12},{12,8},{16,20},{20,16},{24,28},{28,24},{1,5},{5... | collective-permute-start | bytes 7667720 | tf_op jit(solution)/shard_map/ppermute | solution.py:423
  289.7 31.7 %collective-permute-start.35 = (bf16[256,1536]{1,0:T(8,128)(2,1)S(1)}, bf16[256,1536]{1,0:T(8,128)(2,1)S(1)}, u32[]{:S(2)}, u32[]{:S(2)}) collective-permute-start(bf16[256,1536]{1,0:T(8,128)(2,1)S(1)} %fusion.24), channel_id=1, source_target_pairs={{0,1},{1,2},{2,3},{4,5},{5,6},{6,7},{8,9},{9,10},{10,11},{12,13},{... | collective-permute-start | bytes 2359304 | tf_op jit(solution)/shard_map/ppermute | solution.py:435
  292.3 29.1 %collective-permute-start.36 = (bf16[256,1536]{1,0:T(8,128)(2,1)S(1)}, bf16[256,1536]{1,0:T(8,128)(2,1)S(1)}, u32[]{:S(2)}, u32[]{:S(2)}) collective-permute-start(bf16[256,1536]{1,0:T(8,128)(2,1)S(1)} %fusion.24), channel_id=1, source_target_pairs={{3,2},{2,1},{1,0},{7,6},{6,5},{5,4},{11,10},{10,9},{9,8},{15,14},{... | collective-permute-start | bytes 2359304 | tf_op jit(solution)/shard_map/ppermute | solution.py:435
  323.2 30.8 %collective-permute-start.38 = (bf16[256,1536]{1,0:T(8,128)(2,1)}, bf16[256,1536]{1,0:T(8,128)(2,1)}, u32[]{:S(2)}, u32[]{:S(2)}) collective-permute-start(bf16[256,1536]{1,0:T(8,128)(2,1)} %get-tuple-element.294), channel_id=1, source_target_pairs={{0,1},{3,2},{4,5},{7,6},{8,9},{11,10},{12,13},{15,14},{16,17},{19,... | collective-permute-start | bytes 2359304 | tf_op jit(solution)/shard_map/ppermute | solution.py:443
  329.0 25.0 %collective-permute-start.39 = (bf16[256,1536]{1,0:T(8,128)(2,1)}, bf16[256,1536]{1,0:T(8,128)(2,1)S(1)}, u32[]{:S(2)}, u32[]{:S(2)}) collective-permute-start(bf16[256,1536]{1,0:T(8,128)(2,1)} %copy-done.53), channel_id=1, source_target_pairs={{1,2},{2,3},{5,6},{6,7},{9,10},{10,11},{13,14},{14,15},{17,18},{18... | collective-permute-start | bytes 2359304 | tf_op jit(solution)/shard_map/ppermute | solution.py:435
  329.7 24.3 %collective-permute-start.40 = (bf16[256,1536]{1,0:T(8,128)(2,1)}, bf16[256,1536]{1,0:T(8,128)(2,1)}, u32[]{:S(2)}, u32[]{:S(2)}) collective-permute-start(bf16[256,1536]{1,0:T(8,128)(2,1)} %copy-done.55), channel_id=1, source_target_pairs={{2,1},{1,0},{6,5},{5,4},{10,9},{9,8},{14,13},{13,12},{18,17},{17,1... | collective-permute-start | bytes 2359304 | tf_op jit(solution)/shard_map/ppermute | solution.py:435
  337.0 16.5 %collective-permute-start.41 = (bf16[208,1536]{1,0:T(8,128)(2,1)}, bf16[208,1536]{1,0:T(8,128)(2,1)}, u32[]{:S(2)}, u32[]{:S(2)}) collective-permute-start(bf16[208,1536]{1,0:T(8,128)(2,1)} %pad_maximum_fusion.5), channel_id=1, source_target_pairs={{0,16},{4,20},{8,24},{12,28},{16,0},{20,4},{24,8},{28,12},{1,17},{... | collective-permute-start | bytes 1916936 | tf_op jit(solution)/shard_map/ppermute | solution.py:423
  337.7 16.2 %collective-permute-start.42 = (bf16[208,1536]{1,0:T(8,128)(2,1)}, bf16[208,1536]{1,0:T(8,128)(2,1)}, u32[]{:S(2)}, u32[]{:S(2)}) collective-permute-start(bf16[208,1536]{1,0:T(8,128)(2,1)} %pad_maximum_fusion.6), channel_id=1, source_target_pairs={{0,8},{4,12},{8,0},{12,4},{16,24},{20,28},{24,16},{28,20},{1,9},{5... | collective-permute-start | bytes 1916936 | tf_op jit(solution)/shard_map/ppermute | solution.py:423
  356.6 22.2 %collective-permute-start.43 = (bf16[256,1536]{1,0:T(8,128)(2,1)}, bf16[256,1536]{1,0:T(8,128)(2,1)}, u32[]{:S(2)}, u32[]{:S(2)}) collective-permute-start(bf16[256,1536]{1,0:T(8,128)(2,1)} %get-tuple-element.425), channel_id=1, source_target_pairs={{0,1},{1,2},{4,5},{5,6},{8,9},{9,10},{12,13},{13,14},{16,17},{17,1... | collective-permute-start | bytes 2359304 | tf_op jit(solution)/shard_map/ppermute | solution.py:435
  362.0 16.9 %collective-permute-start.44 = (bf16[256,1536]{1,0:T(8,128)(2,1)}, bf16[256,1536]{1,0:T(8,128)(2,1)}, u32[]{:S(2)}, u32[]{:S(2)}) collective-permute-start(bf16[256,1536]{1,0:T(8,128)(2,1)} %get-tuple-element.424), channel_id=1, source_target_pairs={{3,2},{2,1},{7,6},{6,5},{11,10},{10,9},{15,14},{14,13},{19,18},{18... | collective-permute-start | bytes 2359304 | tf_op jit(solution)/shard_map/ppermute | solution.py:435
  365.6 19.8 %collective-permute-start.45 = (bf16[256,1536]{1,0:T(8,128)(2,1)}, bf16[256,1536]{1,0:T(8,128)(2,1)}, u32[]{:S(2)}, u32[]{:S(2)}) collective-permute-start(bf16[256,1536]{1,0:T(8,128)(2,1)} %broadcast_select_fusion.1), channel_id=1, source_target_pairs={{2,3},{1,0},{6,7},{5,4},{10,11},{9,8},{14,15},{13,12},{18,19},{17,... | collective-permute-start | bytes 2359304 | tf_op jit(solution)/shard_map/ppermute | solution.py:443
  369.6 7.8 %collective-permute-start.46 = (bf16[104,1536]{1,0:T(8,128)(2,1)S(1)}, bf16[104,1536]{1,0:T(8,128)(2,1)}, u32[]{:S(2)}, u32[]{:S(2)}) collective-permute-start(bf16[104,1536]{1,0:T(8,128)(2,1)S(1)} %slice.364), channel_id=1, source_target_pairs={{0,8},{4,12},{8,0},{12,4},{16,24},{20,28},{24,16},{28,20},{1,9},{5... | collective-permute-start | bytes 958472 | tf_op jit(solution)/shard_map/ppermute | solution.py:423
  370.9 7.9 %collective-permute-start.47 = (bf16[104,1536]{1,0:T(8,128)(2,1)}, bf16[104,1536]{1,0:T(8,128)(2,1)}, u32[]{:S(2)}, u32[]{:S(2)}) collective-permute-start(bf16[104,1536]{1,0:T(8,128)(2,1)} %slice.365), channel_id=1, source_target_pairs={{0,16},{4,20},{8,24},{12,28},{16,0},{20,4},{24,8},{28,12},{1,17},{... | collective-permute-start | bytes 958472 | tf_op jit(solution)/shard_map/ppermute | solution.py:423
  387.9 19.7 %collective-permute-start.51 = (bf16[256,1536]{1,0:T(8,128)(2,1)S(1)}, bf16[256,1536]{1,0:T(8,128)(2,1)S(1)}, u32[]{:S(2)}, u32[]{:S(2)}) collective-permute-start(bf16[256,1536]{1,0:T(8,128)(2,1)S(1)} %add_convert_fusion.5), channel_id=1, source_target_pairs={{0,1},{1,2},{2,3},{4,5},{5,6},{6,7},{8,9},{9,10},{10,11},{12,13},{... | collective-permute-start | bytes 2359304 | tf_op jit(solution)/shard_map/ppermute | solution.py:435
  391.2 20.9 %collective-permute-start.52 = (bf16[256,1536]{1,0:T(8,128)(2,1)S(1)}, bf16[256,1536]{1,0:T(8,128)(2,1)S(1)}, u32[]{:S(2)}, u32[]{:S(2)}) collective-permute-start(bf16[256,1536]{1,0:T(8,128)(2,1)S(1)} %add_convert_fusion.4), channel_id=1, source_target_pairs={{3,2},{2,1},{1,0},{7,6},{6,5},{5,4},{11,10},{10,9},{9,8},{15,14},{... | collective-permute-start | bytes 2359304 | tf_op jit(solution)/shard_map/ppermute | solution.py:435
  393.7 35.2 %collective-permute-start.48 = (bf16[56,1536]{1,0:T(8,128)(2,1)S(1)}, bf16[56,1536]{1,0:T(8,128)(2,1)S(1)}, u32[]{:S(2)}, u32[]{:S(2)}) collective-permute-start(bf16[56,1536]{1,0:T(8,128)(2,1)S(1)} %get-tuple-element.440), channel_id=1, source_target_pairs={{0,3},{1,0},{2,1},{3,2},{4,7},{5,4},{6,5},{7,6},{8,11},{9,8},{10,9... | collective-permute-start | bytes 516104 | tf_op jit(solution)/shard_map/ppermute | solution.py:428
  400.4 31.3 %collective-permute-start.49 = (bf16[56,1536]{1,0:T(8,128)(2,1)S(1)}, bf16[56,1536]{1,0:T(8,128)(2,1)S(1)}, u32[]{:S(2)}, u32[]{:S(2)}) collective-permute-start(bf16[56,1536]{1,0:T(8,128)(2,1)S(1)} %get-tuple-element.439), channel_id=1, source_target_pairs={{0,2},{1,3},{2,0},{3,1},{4,6},{5,7},{6,4},{7,5},{8,10},{9,11},{10,... | collective-permute-start | bytes 516104 | tf_op jit(solution)/shard_map/ppermute | solution.py:428
  400.4 32.3 %collective-permute-start.50 = (bf16[56,1536]{1,0:T(8,128)(2,1)S(1)}, bf16[56,1536]{1,0:T(8,128)(2,1)S(1)}, u32[]{:S(2)}, u32[]{:S(2)}) collective-permute-start(bf16[56,1536]{1,0:T(8,128)(2,1)S(1)} %get-tuple-element.438), channel_id=1, source_target_pairs={{0,1},{1,2},{2,3},{3,0},{4,5},{5,6},{6,7},{7,4},{8,9},{9,10},{10,1... | collective-permute-start | bytes 516104 | tf_op jit(solution)/shard_map/ppermute | solution.py:428
  415.2 28.9 %collective-permute-start.56 = (bf16[256,1536]{1,0:T(8,128)(2,1)S(1)}, bf16[256,1536]{1,0:T(8,128)(2,1)S(1)}, u32[]{:S(2)}, u32[]{:S(2)}) collective-permute-start(bf16[256,1536]{1,0:T(8,128)(2,1)S(1)} %fusion.20), channel_id=1, source_target_pairs={{0,1},{1,2},{2,3},{4,5},{5,6},{6,7},{8,9},{9,10},{10,11},{12,13},{... | collective-permute-start | bytes 2359304 | tf_op jit(solution)/shard_map/ppermute | solution.py:435
  424.6 19.5 %collective-permute-start.57 = (bf16[256,1536]{1,0:T(8,128)(2,1)S(1)}, bf16[256,1536]{1,0:T(8,128)(2,1)}, u32[]{:S(2)}, u32[]{:S(2)}) collective-permute-start(bf16[256,1536]{1,0:T(8,128)(2,1)S(1)} %fusion.20), channel_id=1, source_target_pairs={{3,2},{2,1},{1,0},{7,6},{6,5},{5,4},{11,10},{10,9},{9,8},{15,14},{... | collective-permute-start | bytes 2359304 | tf_op jit(solution)/shard_map/ppermute | solution.py:435
  428.9 12.6 %collective-permute-start.53 = (f32[1,1536]{1,0:T(1,128)S(1)}, f32[1,1536]{1,0:T(1,128)S(1)}, u32[]{:S(2)}, u32[]{:S(2)}) collective-permute-start(f32[1,1536]{1,0:T(1,128)S(1)} %broadcast_in_dim.61), channel_id=1, source_target_pairs={{0,1},{1,2},{2,3},{3,0},{4,5},{5,6},{6,7},{7,4},{8,9},{9,10},{10,1... | collective-permute-start | bytes 18440 | tf_op jit(solution)/shard_map/ppermute | solution.py:428
  431.6 12.5 %collective-permute-start.54 = (f32[1,1536]{1,0:T(1,128)S(1)}, f32[1,1536]{1,0:T(1,128)S(1)}, u32[]{:S(2)}, u32[]{:S(2)}) collective-permute-start(f32[1,1536]{1,0:T(1,128)S(1)} %broadcast_in_dim.61), channel_id=1, source_target_pairs={{0,2},{1,3},{2,0},{3,1},{4,6},{5,7},{6,4},{7,5},{8,10},{9,11},{10,... | collective-permute-start | bytes 18440 | tf_op jit(solution)/shard_map/ppermute | solution.py:428
  432.6 11.5 %collective-permute-start.55 = (f32[1,1536]{1,0:T(1,128)S(1)}, f32[1,1536]{1,0:T(1,128)S(1)}, u32[]{:S(2)}, u32[]{:S(2)}) collective-permute-start(f32[1,1536]{1,0:T(1,128)S(1)} %broadcast_in_dim.61), channel_id=1, source_target_pairs={{0,3},{1,0},{2,1},{3,2},{4,7},{5,4},{6,5},{7,6},{8,11},{9,8},{10,9... | collective-permute-start | bytes 18440 | tf_op jit(solution)/shard_map/ppermute | solution.py:428
  444.1 11.1 %collective-permute-start.61 = (bf16[256,1536]{1,0:T(8,128)(2,1)S(1)}, bf16[256,1536]{1,0:T(8,128)(2,1)S(1)}, u32[]{:S(2)}, u32[]{:S(2)}) collective-permute-start(bf16[256,1536]{1,0:T(8,128)(2,1)S(1)} %collective-permute-done.56), channel_id=1, source_target_pairs={{1,2},{2,3},{5,6},{6,7},{9,10},{10,11},{13,14},{14,15},{17,18},{18... | collective-permute-start | bytes 2359304 | tf_op jit(solution)/shard_map/ppermute | solution.py:435
  444.8 17.6 %collective-permute-start.62 = (bf16[256,1536]{1,0:T(8,128)(2,1)}, bf16[256,1536]{1,0:T(8,128)(2,1)S(1)}, u32[]{:S(2)}, u32[]{:S(2)}) collective-permute-start(bf16[256,1536]{1,0:T(8,128)(2,1)} %collective-permute-done.57), channel_id=1, source_target_pairs={{2,1},{1,0},{6,5},{5,4},{10,9},{9,8},{14,13},{13,12},{18,17},{17,1... | collective-permute-start | bytes 2359304 | tf_op jit(solution)/shard_map/ppermute | solution.py:435
  446.4 8.4 %collective-permute-start.58 = (bf16[64,1536]{1,0:T(8,128)(2,1)S(1)}, bf16[64,1536]{1,0:T(8,128)(2,1)S(1)}, u32[]{:S(2)}, u32[]{:S(2)}) collective-permute-start(bf16[64,1536]{1,0:T(8,128)(2,1)S(1)} %scatter.4), channel_id=1, source_target_pairs={{0,8},{4,12},{8,0},{12,4},{16,24},{20,28},{24,16},{28,20},{1,9},{5... | collective-permute-start | bytes 589832 | tf_op jit(solution)/shard_map/ppermute | solution.py:423
  447.4 7.4 %collective-permute-start.59 = (bf16[64,1536]{1,0:T(8,128)(2,1)S(1)}, bf16[64,1536]{1,0:T(8,128)(2,1)S(1)}, u32[]{:S(2)}, u32[]{:S(2)}) collective-permute-start(bf16[64,1536]{1,0:T(8,128)(2,1)S(1)} %scatter.4), channel_id=1, source_target_pairs={{0,16},{4,20},{8,24},{12,28},{16,0},{20,4},{24,8},{28,12},{1,17},{... | collective-permute-start | bytes 589832 | tf_op jit(solution)/shard_map/ppermute | solution.py:423
  467.0 22.1 %collective-permute-start.64 = (bf16[256,1536]{1,0:T(8,128)(2,1)}, bf16[256,1536]{1,0:T(8,128)(2,1)}, u32[]{:S(2)}, u32[]{:S(2)}) collective-permute-start(bf16[256,1536]{1,0:T(8,128)(2,1)} %get-tuple-element.429), channel_id=1, source_target_pairs={{2,3},{1,0},{6,7},{5,4},{10,11},{9,8},{14,15},{13,12},{18,19},{17,... | collective-permute-start | bytes 2359304 | tf_op jit(solution)/shard_map/ppermute | solution.py:443
  (78 other events, 776.5 us)
Sparse Core Ops, SparseCore 0:
  53.1 97.4 all-gather.1
  206.1 100.1 reduce-scatter.1
  376.5 63.1 all-reduce.6

commit v7 on v6

--- a/solution.py
+++ b/solution.py
@@ -98,10 +98,10 @@
             weights = [jnp.exp(part - peak) for part in parts]
             total = sum(jnp.sum(w, axis=0, keepdims=True) for w in weights)
             shrink = 1.0 / total
-            mixed = mul(vt_ref[g, :, start:stop], (weights[0] * shrink).astype(BF))
+            mixed = mul(vt_ref[g, :, start:stop], weights[0].astype(BF))
             if i:
-                mixed += mul(vt_ref[g, :, :start], (weights[1] * shrink).astype(BF))
-            out_ref[h, :, start:stop] = mixed
+                mixed += mul(vt_ref[g, :, :start], weights[1].astype(BF))
+            out_ref[h, :, start:stop] = mixed * shrink
             log_ref[h, :, start:stop] = peak + jnp.log(total)
 
     for s, piece_ref in enumerate(pieces):
@@ -383,6 +383,16 @@
     )(order, near, far, extra_near, extra_far, router, parts)
 
 
+def keep_kernel(x_ref, out_ref):
+    out_ref[...] = x_ref[...]
+
+
+def keep(x, us):
+    return pl.pallas_call(
+        keep_kernel, out_shape=jax.ShapeDtypeStruct(x.shape, x.dtype), cost_estimate=takes(us)
+    )(x)
+
+
 def set_rows_kernel(order_ref, near_ref, far_ref, out_ref, small_ref, norm_ref, *, part, few_rows):
     rows, width = near_ref.shape[0] // 4, near_ref.shape[1]
     norm = jnp.zeros((1, width), F32)
@@ -566,9 +576,7 @@
     qkv_weights = (query_weight, key_weight, value_weight)
     if fine:
         extra_got = gather_first(extra)
-        output_parts, qkv_weights, expert_part = join(output_parts, qkv_weights, expert_part)
-        output_part = jnp.concatenate(output_parts, axis=0)
-        output_got = gather_first(output_part)
+        qkv_weights, expert_part = join(qkv_weights, expert_part)
     else:
         output_part = jnp.concatenate(output_parts, axis=0)
         extra_near, extra_far = gather_whole(extra)
@@ -583,12 +591,22 @@
         tp_at,
     )
     if fine:
-        mixed, output_got, extra_got = join(mixed, output_got, extra_got)
-
-    mixed = [mixed[0]] + [turn(mixed[s], s) for s in range(1, n_tp)]
+        mixed, output_parts, extra_got = join(mixed, output_parts, extra_got)
+        output_part = jnp.concatenate(output_parts, axis=0)
+
+    router = jnp.pad(router_weight, ((0, 0), (0, LANES - experts)))
+
+    ends = [turn(mixed[s], s) for s in (1, n_tp - 1)]
+    if fine:
+        output_got = gather_first(output_part)
+        ends, output_got, mixed, router = join(ends, output_got, mixed, router)
+        router = keep(router, 20)
+    mixed = [mixed[0], ends[0]] + [turn(mixed[s], s) for s in range(2, n_tp - 1)] + [ends[1]]
     if fine:
         output_held, output_got = gather_second(output_part, output_got)
-        mixed, output_held, output_got = join(mixed, output_held, output_got)
+        mixed, output_held, output_got, router, extra, extra_got = join(
+            mixed, output_held, output_got, router, extra, extra_got
+        )
         near = gather_near(output_held, output_got)
         far = swap(near, 1)
         extra_held, extra_got = gather_second(extra, extra_got)
@@ -621,7 +639,6 @@
     weights = jnp.where(chosen, jnp.exp(logits - jnp.max(logits, axis=-1, keepdims=True)), 0.0)
     gates = weights / jnp.sum(weights, axis=-1, keepdims=True)
 
-    router = jnp.pad(router_weight, ((0, 0), (0, LANES - experts)))
     order = jnp.concatenate([ep_at[None], jnp.full((1,), experts, jnp.int32)])
     if fine:
         got = gather_first(routed_in)
@@ -647,10 +664,11 @@
         other = swap(gin_odd, 1)
         gin = join(add(gin_near[1], other[:quarter]), add(gin_near[3], other[quarter:]))
         got = (swap(gin[0], 4), swap(gin[1], 2))
-        out_far, gin_even, gin = join(out_far, gin_even, gin)
+        out_far, gin_even, gin, gates = join(out_far, gin_even, gin, gates)
+        gates = keep(gates, 20)
         gin_even = swap(gin_even, 1)
         out_far = swap(out_far, 1)
-        got, out_far, gin_even = join(got, out_far, gin_even)
+        got, out_far, gin_even, gates = join(got, out_far, gin_even, gates)
         gin = join(
             add(gin_near[0].astype(F32) + gin_even[:quarter].astype(F32), got[0]),
             add(gin_near[2].astype(F32) + gin_even[quarter:].astype(F32), got[1]),

time: 506 us -> 502 us (level)
  waiting for transfers between devices: 180 us -> 170 us
    all_gather x1, waiting for transfers between devices: 25.5 us -> 3.3 us  [body(): expert_parts = lax.all_gather(expert_part, 'tp', tiled=True)]
    ppermute x35, waiting for transfers between devices: 67.1 us -> 75.7 us  [swap(): lax.ppermute(x, 'ep', [(i, i ^ bit) for i in range(lax.axis_size('ep'))])]
    unnamed x164 -> x158, local copies, waits for them, and re-layouts: 19.6 us -> 22.4 us
  transfers between devices with their start and end apart: 68 -> 68, of which waited for: 27 -> 29; matrix products, arithmetic and copies ran while one was open for 19% -> 20% of each run, Pallas kernels for 10% -> 10%
where the time goes in v7:
time: 502 us; the launch traced here: 496 us
  waiting for transfers between devices  170 us (34%)
  Pallas kernels  95.7 us (19%)
  starting transfers between devices  93.9 us (19%)
  local copies, waits for them, and re-layouts  56.3 us (11%)
  other arithmetic  53.2 us (11%)
  between operations  15.6 us (3%)
  matrix products  11.6 us (2%)
    ppermute x35, waiting for transfers between devices, swap(): lax.ppermute(x, 'ep', [(i, i ^ bit) for i in range(lax.axis_size('ep'))])  75.7 us
    ppermute x15, waiting for transfers between devices, turn(): return lax.ppermute(x, 'tp', [(i, (i + by) % n) for i in range(n)])  55 us
    pallas_call x1, Pallas kernels, run_experts(): pl.pallas_call(functools.partial(expert_kernel, top=top, count=count), gr...  44.9 us
    ppermute x35, starting transfers between devices, swap(): lax.ppermute(x, 'ep', [(i, i ^ bit) for i in range(lax.axis_size('ep'))])  30.7 us
    ppermute x12, starting transfers between devices, step_both(): return (lax.ppermute(right, 'tp', pairs), lax.ppermute(left, 'tp', mirror))  28.7 us
    ppermute x15, starting transfers between devices, turn(): return lax.ppermute(x, 'tp', [(i, (i + by) % n) for i in range(n)])  25.8 us
    convert_element_type x11, other arithmetic, add(): return (a.astype(F32) + b.astype(F32)).astype(BF)  25.6 us
    pallas_call x1, Pallas kernels, attend_back(): pl.pallas_call(attend_back_kernel, in_specs=[SMEM] + [VMEM] * (9 + count)...  25.5 us
  transfers between devices with their start and end apart: 68, of which 29 were waited for; matrix products, arithmetic and copies ran while one was open for 20% of the time, Pallas kernels for 10%

profile of v7, /device:TPU:0, one launch (start us, length us, event | category | flops | bytes accessed | tf_op | source)
XLA Modules:
  0.0 496.1 jit_solution(8861869943064421124)
XLA Ops:
  8.5 5.1 %collective-permute-start = (bf16[48,1536]{1,0:T(8,128)(2,1)S(1)}, bf16[48,1536]{1,0:T(8,128)(2,1)}, u32[]{:S(2)}, u32[]{:S(2)}) collective-permute-start(bf16[48,1536]{1,0:T(8,128)(2,1)S(1)} %constant_dynamic-slice_fusion.2), channel_id=1, source_target_pairs={{0,3},{1,0},{2,1},{3,2},{4,7},{5,4},{6,5},{7,6},{8,11},{9,8},{10,9... | collective-permute-start | bytes 442376 | tf_op jit(solution)/shard_map/ppermute | solution.py:438
  24.0 18.5 %shard_map.239 = (bf16[256,384]{1,0:T(8,128)(2,1)S(1)}, bf16[256,384]{1,0:T(8,128)(2,1)S(1)}, bf16[256,384]{1,0:T(8,128)(2,1)S(1)}, bf16[256,384]{1,0:T(8,128)(2...) custom-call(s32[1]{0:T(128)} %bitcast.8.at_ref, ...), custom_call_target="tpu_custom_call" | custom-call | flops 23000000512 | tf_op jit(solution)/shard_map/pallas_call | solution.py:121
  47.7 2.5 collective-permute-start.5
  53.3 3.2 collective-permute-done.5
  56.6 1.9 collective-permute-done.6
  60.3 1.6 collective-permute-start.10
  63.3 1.8 shard_map.240.router_ref
  65.1 17.7 %collective-permute-done.9 = bf16[256,384]{1,0:T(8,128)(2,1)S(1)} collective-permute-done((bf16[256,384]{1,0:T(8,128)(2,1)S(1)}, bf16[256,384]{1,0:T(8,128)(2,1)S(1)}, u32[]{:S(2)}, u32[]{:S(2)}) %collective-permute-start.9) | collective-permute-done | bytes 196640 | tf_op jit(solution)/shard_map/ppermute | solution.py:438
  88.1 1.8 collective-permute-start.15
  94.2 3.2 multiply_reduce_fusion.2
  100.1 9.8 %collective-permute-done.15 = bf16[256,1664]{1,0:T(8,128)(2,1)S(1)} collective-permute-done((bf16[256,1664]{1,0:T(8,128)(2,1)S(1)}, bf16[256,1664]{1,0:T(8,128)(2,1)S(1)}, u32[]{:S(2)}, u32[]{:S(2)}) %collective-permute-start.15) | collective-permute-done | bytes 852000 | tf_op jit(solution)/shard_map/ppermute | solution.py:433
  109.9 1.8 collective-permute-done.16
  111.7 7.5 %collective-permute-done.13 = bf16[128,1536]{1,0:T(8,128)(2,1)S(1)} collective-permute-done((bf16[128,1536]{1,0:T(8,128)(2,1)S(1)}, bf16[128,1536]{1,0:T(8,128)(2,1)S(1)}, u32[]{:S(2)}, u32[]{:S(2)}) %collective-permute-start.13) | collective-permute-done | bytes 393248 | tf_op jit(solution)/shard_map/ppermute | solution.py:433
  119.9 1.6 collective-permute-start.18
  125.5 12.7 %collective-permute-done.17 = bf16[256,1536]{1,0:T(8,128)(2,1)S(1)} collective-permute-done((bf16[256,1536]{1,0:T(8,128)(2,1)S(1)}, bf16[256,1536]{1,0:T(8,128)(2,1)S(1)}, u32[]{:S(2)}, u32[]{:S(2)}) %collective-permute-start.17) | collective-permute-done | bytes 786464 | tf_op jit(solution)/shard_map/ppermute | solution.py:433
  142.3 3.3 all-gather.2.cloned.1.call-done.parts_ref
  145.6 2.7 collective-permute-done.19.far_ref
  148.3 44.9 %shard_map.241 = (bf16[1024,1536]{1,0:T(8,128)(2,1)}, bf16[1024,1536]{1,0:T(8,128)(2,1)}, bf16[1024,1664]{1,0:T(8,128)(2,1)}, bf16[512,1664]{1,0:T(8,128)(2,1)},...) custom-call(s32[2]{0:T(128)} %pad_add_fusion.order_ref, ...), custom_call_target="tpu_custom_call" | custom-call | flops 46000001024 | tf_op jit(solution)/shard_map/pallas_call | solution.py:360
  193.4 3.7 collective-permute-done.21
  197.1 3.0 add_convert_fusion.2
  203.6 1.6 shard_map.242
  205.1 17.1 %collective-permute-done.22 = bf16[256,1664]{1,0:T(8,128)(2,1)} collective-permute-done((bf16[256,1664]{1,0:T(8,128)(2,1)}, bf16[256,1664]{1,0:T(8,128)(2,1)}, u32[]{:S(2)}, u32[]{:S(2)}) %collective-permute-start.22) | collective-permute-done | bytes 852000 | tf_op jit(solution)/shard_map/ppermute | solution.py:433
  223.3 3.2 add_convert_fusion
  228.9 4.0 add_convert_fusion.8
  234.9 4.5 collective-permute-done.26
  239.4 1.6 collective-permute-done.27
  243.2 1.7 fusion.44
  250.9 2.5 copy.44
  255.9 1.7 add_convert_fusion.7
  260.5 1.6 fusion.7
  262.2 22.6 %collective-permute-done.29.refs_2_ = bf16[256,384]{1,0:T(8,128)(2,1)S(1)} collective-permute-done((bf16[256,384]{1,0:T(8,128)(2,1)}, bf16[256,384]{1,0:T(8,128)(2,1)S(1)}, u32[]{:S(2)}, u32[]{:S(2)}) %collective-permute-start.29) | collective-permute-done | bytes 196640 | tf_op jit(solution)/shard_map/ppermute | solution.py:438
  285.6 2.2 collective-permute-start.35
  287.8 1.7 collective-permute-start.36
  291.4 25.5 %shard_map.243 = (bf16[256,1536]{1,0:T(8,128)(2,1)S(1)}, bf16[256,1536]{1,0:T(8,128)(2,1)S(1)}, bf16[256,1536]{1,0:T(8,128)(2,1)S(1)}, bf16[256,1536]{1,0:T(8,12...) custom-call(s32[1]{0:T(128)} %bitcast.8.at_ref, bf16[6,1024,64]{2,1,0:T(8,128)(2,1)} %get-tuple-element.206.q_ref, ...), custom_call_target="tpu_custom_call" | custom-call | flops 23000000512 | tf_op jit(solution)/shard_map/pallas_call | solution.py:231
  318.7 5.8 %collective-permute-start.38 = (bf16[256,1536]{1,0:T(8,128)(2,1)}, bf16[256,1536]{1,0:T(8,128)(2,1)}, u32[]{:S(2)}, u32[]{:S(2)}) collective-permute-start(bf16[256,1536]{1,0:T(8,128)(2,1)} %get-tuple-element.316), channel_id=1, source_target_pairs={{0,1},{3,2},{4,5},{7,6},{8,9},{11,10},{12,13},{15,14},{16,17},{19,... | collective-permute-start | bytes 2359304 | tf_op jit(solution)/shard_map/ppermute | solution.py:453
  326.5 4.2 fusion.33
  335.6 1.7 convert_element_type.505
  337.3 4.3 convolution_convert_fusion.1
  341.6 7.4 %collective-permute-done.41 = bf16[208,1536]{1,0:T(8,128)(2,1)} collective-permute-done((bf16[208,1536]{1,0:T(8,128)(2,1)}, bf16[208,1536]{1,0:T(8,128)(2,1)}, u32[]{:S(2)}, u32[]{:S(2)}) %collective-permute-start.41) | collective-permute-done | bytes 639008 | tf_op jit(solution)/shard_map/ppermute | solution.py:433
  350.0 2.6 fusion.15
  352.6 5.3 %collective-permute-start.43 = (bf16[256,1536]{1,0:T(8,128)(2,1)}, bf16[256,1536]{1,0:T(8,128)(2,1)}, u32[]{:S(2)}, u32[]{:S(2)}) collective-permute-start(bf16[256,1536]{1,0:T(8,128)(2,1)} %get-tuple-element.447), channel_id=1, source_target_pairs={{0,1},{1,2},{4,5},{5,6},{8,9},{9,10},{12,13},{13,14},{16,17},{17,1... | collective-permute-start | bytes 2359304 | tf_op jit(solution)/shard_map/ppermute | solution.py:445
  357.9 1.6 collective-permute-start.44
  359.5 2.1 broadcast_select_fusion.1
  373.4 1.9 collective-permute-done.47
  375.2 6.1 %collective-permute-done.45 = bf16[256,1536]{1,0:T(8,128)(2,1)} collective-permute-done((bf16[256,1536]{1,0:T(8,128)(2,1)}, bf16[256,1536]{1,0:T(8,128)(2,1)}, u32[]{:S(2)}, u32[]{:S(2)}) %collective-permute-start.45) | collective-permute-done | bytes 786464 | tf_op jit(solution)/shard_map/ppermute | solution.py:453
  383.9 2.0 collective-permute-start.51
  389.7 6.7 %collective-permute-start.48 = (bf16[56,1536]{1,0:T(8,128)(2,1)S(1)}, bf16[56,1536]{1,0:T(8,128)(2,1)S(1)}, u32[]{:S(2)}, u32[]{:S(2)}) collective-permute-start(bf16[56,1536]{1,0:T(8,128)(2,1)S(1)} %get-tuple-element.464), channel_id=1, source_target_pairs={{0,3},{1,0},{2,1},{3,2},{4,7},{5,4},{6,5},{7,6},{8,11},{9,8},{10,9... | collective-permute-start | bytes 516104 | tf_op jit(solution)/shard_map/ppermute | solution.py:438
  397.0 6.6 %collective-permute-done.51 = bf16[256,1536]{1,0:T(8,128)(2,1)S(1)} collective-permute-done((bf16[256,1536]{1,0:T(8,128)(2,1)S(1)}, bf16[256,1536]{1,0:T(8,128)(2,1)S(1)}, u32[]{:S(2)}, u32[]{:S(2)}) %collective-permute-start.51) | collective-permute-done | bytes 786464 | tf_op jit(solution)/shard_map/ppermute | solution.py:445
  403.6 4.5 collective-permute-done.52
  408.9 2.2 fusion.20
  411.2 9.4 %collective-permute-start.56 = (bf16[256,1536]{1,0:T(8,128)(2,1)S(1)}, bf16[256,1536]{1,0:T(8,128)(2,1)S(1)}, u32[]{:S(2)}, u32[]{:S(2)}) collective-permute-start(bf16[256,1536]{1,0:T(8,128)(2,1)S(1)} %fusion.20), channel_id=1, source_target_pairs={{0,1},{1,2},{2,3},{4,5},{5,6},{6,7},{8,9},{9,10},{10,11},{12,13},{... | collective-permute-start | bytes 2359304 | tf_op jit(solution)/shard_map/ppermute | solution.py:445
  424.9 2.7 collective-permute-start.53
  428.6 2.0 collective-permute-start.55
  430.7 6.8 %collective-permute-done.53 = f32[1,1536]{1,0:T(1,128)S(1)} collective-permute-done((f32[1,1536]{1,0:T(1,128)S(1)}, f32[1,1536]{1,0:T(1,128)S(1)}, u32[]{:S(2)}, u32[]{:S(2)}) %collective-permute-start.53) | collective-permute-done | bytes 6176 | tf_op jit(solution)/shard_map/ppermute | solution.py:438
  437.5 2.6 collective-permute-done.54
  444.4 1.5 collective-permute-start.60
  446.0 1.9 broadcast.86.clone
  448.8 2.1 constant_dynamic-update-slice_fusion.17
  451.4 7.1 %collective-permute-done.62 = bf16[256,1536]{1,0:T(8,128)(2,1)S(1)} collective-permute-done((bf16[256,1536]{1,0:T(8,128)(2,1)}, bf16[256,1536]{1,0:T(8,128)(2,1)S(1)}, u32[]{:S(2)}, u32[]{:S(2)}) %collective-permute-start.62) | collective-permute-done | bytes 786464 | tf_op jit(solution)/shard_map/ppermute | solution.py:445
  460.5 2.6 constant_dynamic-update-slice_fusion.27
  466.6 2.1 shard_map.244
  468.9 3.0 slice.442
  473.7 11.4 %collective-permute-done.64 = bf16[256,1536]{1,0:T(8,128)(2,1)} collective-permute-done((bf16[256,1536]{1,0:T(8,128)(2,1)}, bf16[256,1536]{1,0:T(8,128)(2,1)}, u32[]{:S(2)}, u32[]{:S(2)}) %collective-permute-start.64) | collective-permute-done | bytes 786464 | tf_op jit(solution)/shard_map/ppermute | solution.py:453
  486.4 2.1 constant_dynamic-update-slice_fusion.26
  (388 shorter events, 118.4 us)
Async XLA Ops:
  7.2 138.4 %all-gather.2.cloned.1.call-start = ((), (), s32[]{:S(2)}) async-start(), calls=%async_computation.1 | async-start | bytes 5898240 | tf_op jit(solution)/shard_map/all_gather | solution.py:569
  8.5 35.7 %collective-permute-start = (bf16[48,1536]{1,0:T(8,128)(2,1)S(1)}, bf16[48,1536]{1,0:T(8,128)(2,1)}, u32[]{:S(2)}, u32[]{:S(2)}) collective-permute-start(bf16[48,1536]{1,0:T(8,128)(2,1)S(1)} %constant_dynamic-slice_fusion.2), channel_id=1, source_target_pairs={{0,3},{1,0},{2,1},{3,2},{4,7},{5,4},{6,5},{7,6},{8,11},{9,8},{10,9... | collective-permute-start | bytes 442376 | tf_op jit(solution)/shard_map/ppermute | solution.py:438
  13.6 30.6 %collective-permute-start.1 = (bf16[48,1536]{1,0:T(8,128)(2,1)S(1)}, bf16[48,1536]{1,0:T(8,128)(2,1)}, u32[]{:S(2)}, u32[]{:S(2)}) collective-permute-start(bf16[48,1536]{1,0:T(8,128)(2,1)S(1)} %constant_dynamic-slice_fusion.2), channel_id=1, source_target_pairs={{0,2},{1,3},{2,0},{3,1},{4,6},{5,7},{6,4},{7,5},{8,10},{9,11},{10,... | collective-permute-start | bytes 442376 | tf_op jit(solution)/shard_map/ppermute | solution.py:438
  13.6 30.6 %collective-permute-start.2 = (bf16[48,1536]{1,0:T(8,128)(2,1)S(1)}, bf16[48,1536]{1,0:T(8,128)(2,1)}, u32[]{:S(2)}, u32[]{:S(2)}) collective-permute-start(bf16[48,1536]{1,0:T(8,128)(2,1)S(1)} %constant_dynamic-slice_fusion.2), channel_id=1, source_target_pairs={{0,1},{1,2},{2,3},{3,0},{4,5},{5,6},{6,7},{7,4},{8,9},{9,10},{10,1... | collective-permute-start | bytes 442376 | tf_op jit(solution)/shard_map/ppermute | solution.py:438
  17.9 26.3 %collective-permute-start.3 = (bf16[128,1664]{1,0:T(8,128)(2,1)}, bf16[128,1664]{1,0:T(8,128)(2,1)}, u32[]{:S(2)}, u32[]{:S(2)}) collective-permute-start(bf16[128,1664]{1,0:T(8,128)(2,1)} %get-tuple-element.451), channel_id=1, source_target_pairs={{0,8},{4,12},{8,0},{12,4},{16,24},{20,28},{24,16},{28,20},{1,9},{5... | collective-permute-start | bytes 1277960 | tf_op jit(solution)/shard_map/ppermute | solution.py:433
  19.4 24.8 %collective-permute-start.4 = (bf16[128,1664]{1,0:T(8,128)(2,1)}, bf16[128,1664]{1,0:T(8,128)(2,1)}, u32[]{:S(2)}, u32[]{:S(2)}) collective-permute-start(bf16[128,1664]{1,0:T(8,128)(2,1)} %get-tuple-element.450), channel_id=1, source_target_pairs={{0,16},{4,20},{8,24},{12,28},{16,0},{20,4},{24,8},{28,12},{1,17},{... | collective-permute-start | bytes 1277960 | tf_op jit(solution)/shard_map/ppermute | solution.py:433
  45.1 13.4 %collective-permute-start.7 = (bf16[96,1536]{1,0:T(8,128)(2,1)S(1)}, bf16[96,1536]{1,0:T(8,128)(2,1)S(1)}, u32[]{:S(2)}, u32[]{:S(2)}) collective-permute-start(bf16[96,1536]{1,0:T(8,128)(2,1)S(1)} %pad_maximum_fusion.9), channel_id=1, source_target_pairs={{0,8},{4,12},{8,0},{12,4},{16,24},{20,28},{24,16},{28,20},{1,9},{5... | collective-permute-start | bytes 884744 | tf_op jit(solution)/shard_map/ppermute | solution.py:433
  46.7 11.8 %collective-permute-start.8 = (bf16[96,1536]{1,0:T(8,128)(2,1)S(1)}, bf16[96,1536]{1,0:T(8,128)(2,1)S(1)}, u32[]{:S(2)}, u32[]{:S(2)}) collective-permute-start(bf16[96,1536]{1,0:T(8,128)(2,1)S(1)} %pad_maximum_fusion.10), channel_id=1, source_target_pairs={{0,16},{4,20},{8,24},{12,28},{16,0},{20,4},{24,8},{28,12},{1,17},{... | collective-permute-start | bytes 884744 | tf_op jit(solution)/shard_map/ppermute | solution.py:433
  47.3 271.3 %reduce-scatter.2.cloned.1.call-start = ((), (), s32[]{:S(2)}) async-start(), calls=%async_computation.2 | async-start | bytes 5898240 | tf_op jit(solution)/shard_map/reduce_scatter | solution.py:660
  47.7 8.9 %collective-permute-start.5 = (bf16[256,384]{1,0:T(8,128)(2,1)S(1)}, bf16[256,384]{1,0:T(8,128)(2,1)}, u32[]{:S(2)}, u32[]{:S(2)}) collective-permute-start(bf16[256,384]{1,0:T(8,128)(2,1)S(1)} %get-tuple-element.214), channel_id=1, source_target_pairs={{0,1},{1,2},{2,3},{3,0},{4,5},{5,6},{6,7},{7,4},{8,9},{9,10},{10,1... | collective-permute-start | bytes 589832 | tf_op jit(solution)/shard_map/ppermute | solution.py:438
  50.2 8.3 %collective-permute-start.6 = (bf16[256,384]{1,0:T(8,128)(2,1)S(1)}, bf16[256,384]{1,0:T(8,128)(2,1)}, u32[]{:S(2)}, u32[]{:S(2)}) collective-permute-start(bf16[256,384]{1,0:T(8,128)(2,1)S(1)} %get-tuple-element.215), channel_id=1, source_target_pairs={{0,3},{1,0},{2,1},{3,2},{4,7},{5,4},{6,5},{7,6},{8,11},{9,8},{10,9... | collective-permute-start | bytes 589832 | tf_op jit(solution)/shard_map/ppermute | solution.py:438
  58.5 24.3 %collective-permute-start.9 = (bf16[256,384]{1,0:T(8,128)(2,1)S(1)}, bf16[256,384]{1,0:T(8,128)(2,1)S(1)}, u32[]{:S(2)}, u32[]{:S(2)}) collective-permute-start(bf16[256,384]{1,0:T(8,128)(2,1)S(1)} %get-tuple-element.224), channel_id=1, source_target_pairs={{0,2},{1,3},{2,0},{3,1},{4,6},{5,7},{6,4},{7,5},{8,10},{9,11},{10,... | collective-permute-start | bytes 589832 | tf_op jit(solution)/shard_map/ppermute | solution.py:438
  60.3 22.6 %collective-permute-start.10 = (bf16[192,1536]{1,0:T(8,128)(2,1)S(1)}, bf16[192,1536]{1,0:T(8,128)(2,1)}, u32[]{:S(2)}, u32[]{:S(2)}) collective-permute-start(bf16[192,1536]{1,0:T(8,128)(2,1)S(1)} %get-tuple-element.237), channel_id=1, source_target_pairs={{0,16},{4,20},{8,24},{12,28},{16,0},{20,4},{24,8},{28,12},{1,17},{... | collective-permute-start | bytes 1769480 | tf_op jit(solution)/shard_map/ppermute | solution.py:433
  61.9 21.0 %collective-permute-start.11 = (bf16[192,1536]{1,0:T(8,128)(2,1)S(1)}, bf16[192,1536]{1,0:T(8,128)(2,1)S(1)}, u32[]{:S(2)}, u32[]{:S(2)}) collective-permute-start(bf16[192,1536]{1,0:T(8,128)(2,1)S(1)} %get-tuple-element.239), channel_id=1, source_target_pairs={{0,8},{4,12},{8,0},{12,4},{16,24},{20,28},{24,16},{28,20},{1,9},{5... | collective-permute-start | bytes 1769480 | tf_op jit(solution)/shard_map/ppermute | solution.py:433
  84.1 9.4 %collective-permute-start.12 = (bf16[768,1536]{1,0:T(8,128)(2,1)S(1)}, bf16[768,1536]{1,0:T(8,128)(2,1)S(1)}, u32[]{:S(2)}, u32[]{:S(2)}) collective-permute-start(bf16[768,1536]{1,0:T(8,128)(2,1)S(1)} %constant_dynamic-update-slice_fusion.4), channel_id=1, source_target_pairs={{0,4},{4,0},{8,12},{12,8},{16,20},{20,16},{24,28},{28,24},{1,5},{5... | collective-permute-start | bytes 7077896 | tf_op jit(solution)/shard_map/ppermute | solution.py:433
  88.1 21.8 %collective-permute-start.15 = (bf16[256,1664]{1,0:T(8,128)(2,1)S(1)}, bf16[256,1664]{1,0:T(8,128)(2,1)S(1)}, u32[]{:S(2)}, u32[]{:S(2)}) collective-permute-start(bf16[256,1664]{1,0:T(8,128)(2,1)S(1)} %pad_maximum_fusion), channel_id=1, source_target_pairs={{0,16},{4,20},{8,24},{12,28},{16,0},{20,4},{24,8},{28,12},{1,17},{... | collective-permute-start | bytes 2555912 | tf_op jit(solution)/shard_map/ppermute | solution.py:433
  89.9 21.8 %collective-permute-start.16 = (bf16[256,1664]{1,0:T(8,128)(2,1)S(1)}, bf16[256,1664]{1,0:T(8,128)(2,1)S(1)}, u32[]{:S(2)}, u32[]{:S(2)}) collective-permute-start(bf16[256,1664]{1,0:T(8,128)(2,1)S(1)} %pad_maximum_fusion.1), channel_id=1, source_target_pairs={{0,8},{4,12},{8,0},{12,4},{16,24},{20,28},{24,16},{28,20},{1,9},{5... | collective-permute-start | bytes 2555912 | tf_op jit(solution)/shard_map/ppermute | solution.py:433
  97.8 21.5 %collective-permute-start.13 = (bf16[128,1536]{1,0:T(8,128)(2,1)S(1)}, bf16[128,1536]{1,0:T(8,128)(2,1)S(1)}, u32[]{:S(2)}, u32[]{:S(2)}) collective-permute-start(bf16[128,1536]{1,0:T(8,128)(2,1)S(1)} %get-tuple-element.459), channel_id=1, source_target_pairs={{0,8},{4,12},{8,0},{12,4},{16,24},{20,28},{24,16},{28,20},{1,9},{5... | collective-permute-start | bytes 1179656 | tf_op jit(solution)/shard_map/ppermute | solution.py:433
  98.4 20.8 %collective-permute-start.14 = (bf16[128,1536]{1,0:T(8,128)(2,1)S(1)}, bf16[128,1536]{1,0:T(8,128)(2,1)S(1)}, u32[]{:S(2)}, u32[]{:S(2)}) collective-permute-start(bf16[128,1536]{1,0:T(8,128)(2,1)S(1)} %get-tuple-element.458), channel_id=1, source_target_pairs={{0,16},{4,20},{8,24},{12,28},{16,0},{20,4},{24,8},{28,12},{1,17},{... | collective-permute-start | bytes 1179656 | tf_op jit(solution)/shard_map/ppermute | solution.py:433
  119.4 18.8 %collective-permute-start.17 = (bf16[256,1536]{1,0:T(8,128)(2,1)S(1)}, bf16[256,1536]{1,0:T(8,128)(2,1)S(1)}, u32[]{:S(2)}, u32[]{:S(2)}) collective-permute-start(bf16[256,1536]{1,0:T(8,128)(2,1)S(1)} %pad_maximum_fusion.2), channel_id=1, source_target_pairs={{0,16},{4,20},{8,24},{12,28},{16,0},{20,4},{24,8},{28,12},{1,17},{... | collective-permute-start | bytes 2359304 | tf_op jit(solution)/shard_map/ppermute | solution.py:433
  119.9 18.7 %collective-permute-start.18 = (bf16[256,1536]{1,0:T(8,128)(2,1)S(1)}, bf16[256,1536]{1,0:T(8,128)(2,1)S(1)}, u32[]{:S(2)}, u32[]{:S(2)}) collective-permute-start(bf16[256,1536]{1,0:T(8,128)(2,1)S(1)} %pad_maximum_fusion.3), channel_id=1, source_target_pairs={{0,8},{4,12},{8,0},{12,4},{16,24},{20,28},{24,16},{28,20},{1,9},{5... | collective-permute-start | bytes 2359304 | tf_op jit(solution)/shard_map/ppermute | solution.py:433
  125.5 20.1 %collective-permute-start.20 = (bf16[1024,1664]{1,0:T(8,128)(2,1)}, bf16[1024,1664]{1,0:T(8,128)(2,1)}, u32[]{:S(2)}, u32[]{:S(2)}) collective-permute-start(bf16[1024,1664]{1,0:T(8,128)(2,1)} %constant_dynamic-update-slice_fusion.12.extra_near_ref), channel_id=1, source_target_pairs={{0,4},{4,0},{8,12},{12,8},{16,20},{20,16},{24,28},{28,24},{1,5},{5... | collective-permute-start | bytes 10223624 | tf_op jit(solution)/shard_map/ppermute | solution.py:433
  200.1 23.3 %collective-permute-start.24 = (bf16[1024,1536]{1,0:T(8,128)(2,1)}, bf16[1024,1536]{1,0:T(8,128)(2,1)}, u32[]{:S(2)}, u32[]{:S(2)}) collective-permute-start(bf16[1024,1536]{1,0:T(8,128)(2,1)} %get-tuple-element.268), channel_id=1, source_target_pairs={{0,4},{4,0},{8,12},{12,8},{16,20},{20,16},{24,28},{28,24},{1,5},{5... | collective-permute-start | bytes 9437192 | tf_op jit(solution)/shard_map/ppermute | solution.py:433
  200.3 266.3 %all-reduce.7.cloned.1.call-start = ((), (), s32[]{:S(2)}) async-start(), calls=%async_computation.3 | async-start | bytes 3932160 | tf_op jit(solution)/shard_map/psum | solution.py:768
  200.6 21.6 %collective-permute-start.22 = (bf16[256,1664]{1,0:T(8,128)(2,1)}, bf16[256,1664]{1,0:T(8,128)(2,1)}, u32[]{:S(2)}, u32[]{:S(2)}) collective-permute-start(bf16[256,1664]{1,0:T(8,128)(2,1)} %get-tuple-element.263), channel_id=1, source_target_pairs={{0,16},{4,20},{8,24},{12,28},{16,0},{20,4},{24,8},{28,12},{1,17},{... | collective-permute-start | bytes 2555912 | tf_op jit(solution)/shard_map/ppermute | solution.py:433
  202.1 21.2 %collective-permute-start.23 = (bf16[256,1664]{1,0:T(8,128)(2,1)}, bf16[256,1664]{1,0:T(8,128)(2,1)}, u32[]{:S(2)}, u32[]{:S(2)}) collective-permute-start(bf16[256,1664]{1,0:T(8,128)(2,1)} %get-tuple-element.264), channel_id=1, source_target_pairs={{0,8},{4,12},{8,0},{12,4},{16,24},{20,28},{24,16},{28,20},{1,9},{5... | collective-permute-start | bytes 2555912 | tf_op jit(solution)/shard_map/ppermute | solution.py:433
  203.5 19.8 %collective-permute-start.25 = (bf16[512,1664]{1,0:T(8,128)(2,1)}, bf16[512,1664]{1,0:T(8,128)(2,1)}, u32[]{:S(2)}, u32[]{:S(2)}) collective-permute-start(bf16[512,1664]{1,0:T(8,128)(2,1)} %get-tuple-element.269), channel_id=1, source_target_pairs={{0,4},{4,0},{8,12},{12,8},{16,20},{20,16},{24,28},{28,24},{1,5},{5... | collective-permute-start | bytes 5111816 | tf_op jit(solution)/shard_map/ppermute | solution.py:433
  226.6 12.8 %collective-permute-start.26 = (bf16[128,1664]{1,0:T(8,128)(2,1)S(1)}, bf16[128,1664]{1,0:T(8,128)(2,1)S(1)}, u32[]{:S(2)}, u32[]{:S(2)}) collective-permute-start(bf16[128,1664]{1,0:T(8,128)(2,1)S(1)} %slice.347), channel_id=1, source_target_pairs={{0,8},{4,12},{8,0},{12,4},{16,24},{20,28},{24,16},{28,20},{1,9},{5... | collective-permute-start | bytes 1277960 | tf_op jit(solution)/shard_map/ppermute | solution.py:433
  228.2 12.8 %collective-permute-start.27 = (bf16[128,1664]{1,0:T(8,128)(2,1)S(1)}, bf16[128,1664]{1,0:T(8,128)(2,1)S(1)}, u32[]{:S(2)}, u32[]{:S(2)}) collective-permute-start(bf16[128,1664]{1,0:T(8,128)(2,1)S(1)} %slice.348), channel_id=1, source_target_pairs={{0,16},{4,20},{8,24},{12,28},{16,0},{20,4},{24,8},{28,12},{1,17},{... | collective-permute-start | bytes 1277960 | tf_op jit(solution)/shard_map/ppermute | solution.py:433
  232.9 22.9 %collective-permute-start.31 = (bf16[256,1536]{1,0:T(8,128)(2,1)}, bf16[256,1536]{1,0:T(8,128)(2,1)}, u32[]{:S(2)}, u32[]{:S(2)}) collective-permute-start(bf16[256,1536]{1,0:T(8,128)(2,1)} %get-tuple-element.288), channel_id=1, source_target_pairs={{0,16},{4,20},{8,24},{12,28},{16,0},{20,4},{24,8},{28,12},{1,17},{... | collective-permute-start | bytes 2359304 | tf_op jit(solution)/shard_map/ppermute | solution.py:433
  234.3 23.3 %collective-permute-start.32 = (bf16[256,1536]{1,0:T(8,128)(2,1)}, bf16[256,1536]{1,0:T(8,128)(2,1)}, u32[]{:S(2)}, u32[]{:S(2)}) collective-permute-start(bf16[256,1536]{1,0:T(8,128)(2,1)} %get-tuple-element.290), channel_id=1, source_target_pairs={{0,8},{4,12},{8,0},{12,4},{16,24},{20,28},{24,16},{28,20},{1,9},{5... | collective-permute-start | bytes 2359304 | tf_op jit(solution)/shard_map/ppermute | solution.py:433
  247.2 15.0 %collective-permute-start.28 = (bf16[256,384]{1,0:T(8,128)(2,1)}, bf16[256,384]{1,0:T(8,128)(2,1)S(1)}, u32[]{:S(2)}, u32[]{:S(2)}) collective-permute-start(bf16[256,384]{1,0:T(8,128)(2,1)} %get-tuple-element.282), channel_id=1, source_target_pairs={{0,3},{1,0},{2,1},{3,2},{4,7},{5,4},{6,5},{7,6},{8,11},{9,8},{10,9... | collective-permute-start | bytes 589832 | tf_op jit(solution)/shard_map/ppermute | solution.py:438
  247.9 36.9 %collective-permute-start.29 = (bf16[256,384]{1,0:T(8,128)(2,1)}, bf16[256,384]{1,0:T(8,128)(2,1)S(1)}, u32[]{:S(2)}, u32[]{:S(2)}) collective-permute-start(bf16[256,384]{1,0:T(8,128)(2,1)} %get-tuple-element.283), channel_id=1, source_target_pairs={{0,2},{1,3},{2,0},{3,1},{4,6},{5,7},{6,4},{7,5},{8,10},{9,11},{10,... | collective-permute-start | bytes 589832 | tf_op jit(solution)/shard_map/ppermute | solution.py:438
  247.9 36.9 %collective-permute-start.30 = (bf16[256,384]{1,0:T(8,128)(2,1)}, bf16[256,384]{1,0:T(8,128)(2,1)S(1)}, u32[]{:S(2)}, u32[]{:S(2)}) collective-permute-start(bf16[256,384]{1,0:T(8,128)(2,1)} %get-tuple-element.284), channel_id=1, source_target_pairs={{0,1},{1,2},{2,3},{3,0},{4,5},{5,6},{6,7},{7,4},{8,9},{9,10},{10,1... | collective-permute-start | bytes 589832 | tf_op jit(solution)/shard_map/ppermute | solution.py:438
  259.1 25.8 %collective-permute-start.33 = (bf16[128,1536]{1,0:T(8,128)(2,1)S(1)}, bf16[128,1536]{1,0:T(8,128)(2,1)S(1)}, u32[]{:S(2)}, u32[]{:S(2)}) collective-permute-start(bf16[128,1536]{1,0:T(8,128)(2,1)S(1)} %slice.366), channel_id=1, source_target_pairs={{0,8},{4,12},{8,0},{12,4},{16,24},{20,28},{24,16},{28,20},{1,9},{5... | collective-permute-start | bytes 1179656 | tf_op jit(solution)/shard_map/ppermute | solution.py:433
  259.8 25.1 %collective-permute-start.34 = (bf16[128,1536]{1,0:T(8,128)(2,1)S(1)}, bf16[128,1536]{1,0:T(8,128)(2,1)S(1)}, u32[]{:S(2)}, u32[]{:S(2)}) collective-permute-start(bf16[128,1536]{1,0:T(8,128)(2,1)S(1)} %slice.367), channel_id=1, source_target_pairs={{0,16},{4,20},{8,24},{12,28},{16,0},{20,4},{24,8},{28,12},{1,17},{... | collective-permute-start | bytes 1179656 | tf_op jit(solution)/shard_map/ppermute | solution.py:433
  284.9 33.8 %collective-permute-start.37 = (bf16[4,208,1536]{2,1,0:T(8,128)(2,1)S(1)}, bf16[4,208,1536]{2,1,0:T(8,128)(2,1)}, u32[]{:S(2)}, u32[]{:S(2)}) collective-permute-start(bf16[4,208,1536]{2,1,0:T(8,128)(2,1)S(1)} %get-tuple-element.313), channel_id=1, source_target_pairs={{0,4},{4,0},{8,12},{12,8},{16,20},{20,16},{24,28},{28,24},{1,5},{5... | collective-permute-start | bytes 7667720 | tf_op jit(solution)/shard_map/ppermute | solution.py:433
  285.6 31.3 %collective-permute-start.35 = (bf16[256,1536]{1,0:T(8,128)(2,1)S(1)}, bf16[256,1536]{1,0:T(8,128)(2,1)S(1)}, u32[]{:S(2)}, u32[]{:S(2)}) collective-permute-start(bf16[256,1536]{1,0:T(8,128)(2,1)S(1)} %fusion.24), channel_id=1, source_target_pairs={{0,1},{1,2},{2,3},{4,5},{5,6},{6,7},{8,9},{9,10},{10,11},{12,13},{... | collective-permute-start | bytes 2359304 | tf_op jit(solution)/shard_map/ppermute | solution.py:445
  287.8 29.1 %collective-permute-start.36 = (bf16[256,1536]{1,0:T(8,128)(2,1)S(1)}, bf16[256,1536]{1,0:T(8,128)(2,1)S(1)}, u32[]{:S(2)}, u32[]{:S(2)}) collective-permute-start(bf16[256,1536]{1,0:T(8,128)(2,1)S(1)} %fusion.24), channel_id=1, source_target_pairs={{3,2},{2,1},{1,0},{7,6},{6,5},{5,4},{11,10},{10,9},{9,8},{15,14},{... | collective-permute-start | bytes 2359304 | tf_op jit(solution)/shard_map/ppermute | solution.py:445
  318.7 31.3 %collective-permute-start.38 = (bf16[256,1536]{1,0:T(8,128)(2,1)}, bf16[256,1536]{1,0:T(8,128)(2,1)}, u32[]{:S(2)}, u32[]{:S(2)}) collective-permute-start(bf16[256,1536]{1,0:T(8,128)(2,1)} %get-tuple-element.316), channel_id=1, source_target_pairs={{0,1},{3,2},{4,5},{7,6},{8,9},{11,10},{12,13},{15,14},{16,17},{19,... | collective-permute-start | bytes 2359304 | tf_op jit(solution)/shard_map/ppermute | solution.py:453
  324.5 25.5 %collective-permute-start.39 = (bf16[256,1536]{1,0:T(8,128)(2,1)}, bf16[256,1536]{1,0:T(8,128)(2,1)S(1)}, u32[]{:S(2)}, u32[]{:S(2)}) collective-permute-start(bf16[256,1536]{1,0:T(8,128)(2,1)} %copy-done.55), channel_id=1, source_target_pairs={{1,2},{2,3},{5,6},{6,7},{9,10},{10,11},{13,14},{14,15},{17,18},{18... | collective-permute-start | bytes 2359304 | tf_op jit(solution)/shard_map/ppermute | solution.py:445
  325.2 24.8 %collective-permute-start.40 = (bf16[256,1536]{1,0:T(8,128)(2,1)}, bf16[256,1536]{1,0:T(8,128)(2,1)}, u32[]{:S(2)}, u32[]{:S(2)}) collective-permute-start(bf16[256,1536]{1,0:T(8,128)(2,1)} %copy-done.57), channel_id=1, source_target_pairs={{2,1},{1,0},{6,5},{5,4},{10,9},{9,8},{14,13},{13,12},{18,17},{17,1... | collective-permute-start | bytes 2359304 | tf_op jit(solution)/shard_map/ppermute | solution.py:445
  332.4 16.5 %collective-permute-start.41 = (bf16[208,1536]{1,0:T(8,128)(2,1)}, bf16[208,1536]{1,0:T(8,128)(2,1)}, u32[]{:S(2)}, u32[]{:S(2)}) collective-permute-start(bf16[208,1536]{1,0:T(8,128)(2,1)} %pad_maximum_fusion.5), channel_id=1, source_target_pairs={{0,16},{4,20},{8,24},{12,28},{16,0},{20,4},{24,8},{28,12},{1,17},{... | collective-permute-start | bytes 1916936 | tf_op jit(solution)/shard_map/ppermute | solution.py:433
  333.7 16.2 %collective-permute-start.42 = (bf16[208,1536]{1,0:T(8,128)(2,1)}, bf16[208,1536]{1,0:T(8,128)(2,1)}, u32[]{:S(2)}, u32[]{:S(2)}) collective-permute-start(bf16[208,1536]{1,0:T(8,128)(2,1)} %pad_maximum_fusion.6), channel_id=1, source_target_pairs={{0,8},{4,12},{8,0},{12,4},{16,24},{20,28},{24,16},{28,20},{1,9},{5... | collective-permute-start | bytes 1916936 | tf_op jit(solution)/shard_map/ppermute | solution.py:433
  352.6 22.6 %collective-permute-start.43 = (bf16[256,1536]{1,0:T(8,128)(2,1)}, bf16[256,1536]{1,0:T(8,128)(2,1)}, u32[]{:S(2)}, u32[]{:S(2)}) collective-permute-start(bf16[256,1536]{1,0:T(8,128)(2,1)} %get-tuple-element.447), channel_id=1, source_target_pairs={{0,1},{1,2},{4,5},{5,6},{8,9},{9,10},{12,13},{13,14},{16,17},{17,1... | collective-permute-start | bytes 2359304 | tf_op jit(solution)/shard_map/ppermute | solution.py:445
  357.9 17.3 %collective-permute-start.44 = (bf16[256,1536]{1,0:T(8,128)(2,1)}, bf16[256,1536]{1,0:T(8,128)(2,1)}, u32[]{:S(2)}, u32[]{:S(2)}) collective-permute-start(bf16[256,1536]{1,0:T(8,128)(2,1)} %get-tuple-element.446), channel_id=1, source_target_pairs={{3,2},{2,1},{7,6},{6,5},{11,10},{10,9},{15,14},{14,13},{19,18},{18... | collective-permute-start | bytes 2359304 | tf_op jit(solution)/shard_map/ppermute | solution.py:445
  361.6 19.8 %collective-permute-start.45 = (bf16[256,1536]{1,0:T(8,128)(2,1)}, bf16[256,1536]{1,0:T(8,128)(2,1)}, u32[]{:S(2)}, u32[]{:S(2)}) collective-permute-start(bf16[256,1536]{1,0:T(8,128)(2,1)} %broadcast_select_fusion.1), channel_id=1, source_target_pairs={{2,3},{1,0},{6,7},{5,4},{10,11},{9,8},{14,15},{13,12},{18,19},{17,... | collective-permute-start | bytes 2359304 | tf_op jit(solution)/shard_map/ppermute | solution.py:453
  365.6 7.8 %collective-permute-start.46 = (bf16[104,1536]{1,0:T(8,128)(2,1)S(1)}, bf16[104,1536]{1,0:T(8,128)(2,1)}, u32[]{:S(2)}, u32[]{:S(2)}) collective-permute-start(bf16[104,1536]{1,0:T(8,128)(2,1)S(1)} %slice.370), channel_id=1, source_target_pairs={{0,8},{4,12},{8,0},{12,4},{16,24},{20,28},{24,16},{28,20},{1,9},{5... | collective-permute-start | bytes 958472 | tf_op jit(solution)/shard_map/ppermute | solution.py:433
  367.6 7.6 %collective-permute-start.47 = (bf16[104,1536]{1,0:T(8,128)(2,1)}, bf16[104,1536]{1,0:T(8,128)(2,1)}, u32[]{:S(2)}, u32[]{:S(2)}) collective-permute-start(bf16[104,1536]{1,0:T(8,128)(2,1)} %slice.371), channel_id=1, source_target_pairs={{0,16},{4,20},{8,24},{12,28},{16,0},{20,4},{24,8},{28,12},{1,17},{... | collective-permute-start | bytes 958472 | tf_op jit(solution)/shard_map/ppermute | solution.py:433
  383.9 19.7 %collective-permute-start.51 = (bf16[256,1536]{1,0:T(8,128)(2,1)S(1)}, bf16[256,1536]{1,0:T(8,128)(2,1)S(1)}, u32[]{:S(2)}, u32[]{:S(2)}) collective-permute-start(bf16[256,1536]{1,0:T(8,128)(2,1)S(1)} %add_convert_fusion.5), channel_id=1, source_target_pairs={{0,1},{1,2},{2,3},{4,5},{5,6},{6,7},{8,9},{9,10},{10,11},{12,13},{... | collective-permute-start | bytes 2359304 | tf_op jit(solution)/shard_map/ppermute | solution.py:445
  387.2 20.9 %collective-permute-start.52 = (bf16[256,1536]{1,0:T(8,128)(2,1)S(1)}, bf16[256,1536]{1,0:T(8,128)(2,1)S(1)}, u32[]{:S(2)}, u32[]{:S(2)}) collective-permute-start(bf16[256,1536]{1,0:T(8,128)(2,1)S(1)} %add_convert_fusion.4), channel_id=1, source_target_pairs={{3,2},{2,1},{1,0},{7,6},{6,5},{5,4},{11,10},{10,9},{9,8},{15,14},{... | collective-permute-start | bytes 2359304 | tf_op jit(solution)/shard_map/ppermute | solution.py:445
  389.7 35.3 %collective-permute-start.48 = (bf16[56,1536]{1,0:T(8,128)(2,1)S(1)}, bf16[56,1536]{1,0:T(8,128)(2,1)S(1)}, u32[]{:S(2)}, u32[]{:S(2)}) collective-permute-start(bf16[56,1536]{1,0:T(8,128)(2,1)S(1)} %get-tuple-element.464), channel_id=1, source_target_pairs={{0,3},{1,0},{2,1},{3,2},{4,7},{5,4},{6,5},{7,6},{8,11},{9,8},{10,9... | collective-permute-start | bytes 516104 | tf_op jit(solution)/shard_map/ppermute | solution.py:438
  396.4 31.3 %collective-permute-start.49 = (bf16[56,1536]{1,0:T(8,128)(2,1)S(1)}, bf16[56,1536]{1,0:T(8,128)(2,1)S(1)}, u32[]{:S(2)}, u32[]{:S(2)}) collective-permute-start(bf16[56,1536]{1,0:T(8,128)(2,1)S(1)} %get-tuple-element.463), channel_id=1, source_target_pairs={{0,2},{1,3},{2,0},{3,1},{4,6},{5,7},{6,4},{7,5},{8,10},{9,11},{10,... | collective-permute-start | bytes 516104 | tf_op jit(solution)/shard_map/ppermute | solution.py:438
  396.4 32.3 %collective-permute-start.50 = (bf16[56,1536]{1,0:T(8,128)(2,1)S(1)}, bf16[56,1536]{1,0:T(8,128)(2,1)S(1)}, u32[]{:S(2)}, u32[]{:S(2)}) collective-permute-start(bf16[56,1536]{1,0:T(8,128)(2,1)S(1)} %get-tuple-element.462), channel_id=1, source_target_pairs={{0,1},{1,2},{2,3},{3,0},{4,5},{5,6},{6,7},{7,4},{8,9},{9,10},{10,1... | collective-permute-start | bytes 516104 | tf_op jit(solution)/shard_map/ppermute | solution.py:438
  411.2 29.0 %collective-permute-start.56 = (bf16[256,1536]{1,0:T(8,128)(2,1)S(1)}, bf16[256,1536]{1,0:T(8,128)(2,1)S(1)}, u32[]{:S(2)}, u32[]{:S(2)}) collective-permute-start(bf16[256,1536]{1,0:T(8,128)(2,1)S(1)} %fusion.20), channel_id=1, source_target_pairs={{0,1},{1,2},{2,3},{4,5},{5,6},{6,7},{8,9},{9,10},{10,11},{12,13},{... | collective-permute-start | bytes 2359304 | tf_op jit(solution)/shard_map/ppermute | solution.py:445
  420.6 19.6 %collective-permute-start.57 = (bf16[256,1536]{1,0:T(8,128)(2,1)S(1)}, bf16[256,1536]{1,0:T(8,128)(2,1)}, u32[]{:S(2)}, u32[]{:S(2)}) collective-permute-start(bf16[256,1536]{1,0:T(8,128)(2,1)S(1)} %fusion.20), channel_id=1, source_target_pairs={{3,2},{2,1},{1,0},{7,6},{6,5},{5,4},{11,10},{10,9},{9,8},{15,14},{... | collective-permute-start | bytes 2359304 | tf_op jit(solution)/shard_map/ppermute | solution.py:445
  424.9 12.6 %collective-permute-start.53 = (f32[1,1536]{1,0:T(1,128)S(1)}, f32[1,1536]{1,0:T(1,128)S(1)}, u32[]{:S(2)}, u32[]{:S(2)}) collective-permute-start(f32[1,1536]{1,0:T(1,128)S(1)} %broadcast_in_dim.61), channel_id=1, source_target_pairs={{0,1},{1,2},{2,3},{3,0},{4,5},{5,6},{6,7},{7,4},{8,9},{9,10},{10,1... | collective-permute-start | bytes 18440 | tf_op jit(solution)/shard_map/ppermute | solution.py:438
  427.6 12.5 %collective-permute-start.54 = (f32[1,1536]{1,0:T(1,128)S(1)}, f32[1,1536]{1,0:T(1,128)S(1)}, u32[]{:S(2)}, u32[]{:S(2)}) collective-permute-start(f32[1,1536]{1,0:T(1,128)S(1)} %broadcast_in_dim.61), channel_id=1, source_target_pairs={{0,2},{1,3},{2,0},{3,1},{4,6},{5,7},{6,4},{7,5},{8,10},{9,11},{10,... | collective-permute-start | bytes 18440 | tf_op jit(solution)/shard_map/ppermute | solution.py:438
  428.6 11.5 %collective-permute-start.55 = (f32[1,1536]{1,0:T(1,128)S(1)}, f32[1,1536]{1,0:T(1,128)S(1)}, u32[]{:S(2)}, u32[]{:S(2)}) collective-permute-start(f32[1,1536]{1,0:T(1,128)S(1)} %broadcast_in_dim.61), channel_id=1, source_target_pairs={{0,3},{1,0},{2,1},{3,2},{4,7},{5,4},{6,5},{7,6},{8,11},{9,8},{10,9... | collective-permute-start | bytes 18440 | tf_op jit(solution)/shard_map/ppermute | solution.py:438
  440.2 11.2 %collective-permute-start.61 = (bf16[256,1536]{1,0:T(8,128)(2,1)S(1)}, bf16[256,1536]{1,0:T(8,128)(2,1)S(1)}, u32[]{:S(2)}, u32[]{:S(2)}) collective-permute-start(bf16[256,1536]{1,0:T(8,128)(2,1)S(1)} %collective-permute-done.56), channel_id=1, source_target_pairs={{1,2},{2,3},{5,6},{6,7},{9,10},{10,11},{13,14},{14,15},{17,18},{18... | collective-permute-start | bytes 2359304 | tf_op jit(solution)/shard_map/ppermute | solution.py:445
  440.9 17.6 %collective-permute-start.62 = (bf16[256,1536]{1,0:T(8,128)(2,1)}, bf16[256,1536]{1,0:T(8,128)(2,1)S(1)}, u32[]{:S(2)}, u32[]{:S(2)}) collective-permute-start(bf16[256,1536]{1,0:T(8,128)(2,1)} %collective-permute-done.57), channel_id=1, source_target_pairs={{2,1},{1,0},{6,5},{5,4},{10,9},{9,8},{14,13},{13,12},{18,17},{17,1... | collective-permute-start | bytes 2359304 | tf_op jit(solution)/shard_map/ppermute | solution.py:445
  442.4 8.4 %collective-permute-start.58 = (bf16[64,1536]{1,0:T(8,128)(2,1)S(1)}, bf16[64,1536]{1,0:T(8,128)(2,1)S(1)}, u32[]{:S(2)}, u32[]{:S(2)}) collective-permute-start(bf16[64,1536]{1,0:T(8,128)(2,1)S(1)} %scatter.4), channel_id=1, source_target_pairs={{0,8},{4,12},{8,0},{12,4},{16,24},{20,28},{24,16},{28,20},{1,9},{5... | collective-permute-start | bytes 589832 | tf_op jit(solution)/shard_map/ppermute | solution.py:433
  443.6 7.8 %collective-permute-start.59 = (bf16[64,1536]{1,0:T(8,128)(2,1)S(1)}, bf16[64,1536]{1,0:T(8,128)(2,1)S(1)}, u32[]{:S(2)}, u32[]{:S(2)}) collective-permute-start(bf16[64,1536]{1,0:T(8,128)(2,1)S(1)} %scatter.4), channel_id=1, source_target_pairs={{0,16},{4,20},{8,24},{12,28},{16,0},{20,4},{24,8},{28,12},{1,17},{... | collective-permute-start | bytes 589832 | tf_op jit(solution)/shard_map/ppermute | solution.py:433
  463.0 22.1 %collective-permute-start.64 = (bf16[256,1536]{1,0:T(8,128)(2,1)}, bf16[256,1536]{1,0:T(8,128)(2,1)}, u32[]{:S(2)}, u32[]{:S(2)}) collective-permute-start(bf16[256,1536]{1,0:T(8,128)(2,1)} %get-tuple-element.453), channel_id=1, source_target_pairs={{2,3},{1,0},{6,7},{5,4},{10,11},{9,8},{14,15},{13,12},{18,19},{17,... | collective-permute-start | bytes 2359304 | tf_op jit(solution)/shard_map/ppermute | solution.py:453
  (75 other events, 695.6 us)
Sparse Core Ops, SparseCore 0:
  47.5 98.0 all-gather.1
  200.4 99.2 reduce-scatter.1
  372.3 63.4 all-reduce.6

commit v8 on v7

--- a/solution.py
+++ b/solution.py
@@ -649,7 +649,7 @@
         extra_far = swap(extra_near, 1)
         held, got = gather_second(routed_in, got)
         held, got = join(held, got)
-        near = gather_near(held, got)
+        (near,) = join(gather_near(held, got))
         far = swap(near, 1)
     else:
         near, far = gather_whole(routed_in)

time: 502 us -> 500 us (level)
    unnamed x158 -> x155, local copies, waits for them, and re-layouts: 22.4 us -> 19.6 us
where the time goes in v8:
time: 500 us; the launch traced here: 494 us
  waiting for transfers between devices  170 us (34%)
  Pallas kernels  95.7 us (19%)
  starting transfers between devices  93.9 us (19%)
  other arithmetic  55 us (11%)
  local copies, waits for them, and re-layouts  52.5 us (10%)
  between operations  15.6 us (3%)
  matrix products  11.6 us (2%)
    ppermute x35, waiting for transfers between devices, swap(): lax.ppermute(x, 'ep', [(i, i ^ bit) for i in range(lax.axis_size('ep'))])  73.7 us
    ppermute x15, waiting for transfers between devices, turn(): return lax.ppermute(x, 'tp', [(i, (i + by) % n) for i in range(n)])  55 us
    pallas_call x1, Pallas kernels, run_experts(): pl.pallas_call(functools.partial(expert_kernel, top=top, count=count), gr...  44.9 us
    ppermute x35, starting transfers between devices, swap(): lax.ppermute(x, 'ep', [(i, i ^ bit) for i in range(lax.axis_size('ep'))])  30.7 us
    ppermute x12, starting transfers between devices, step_both(): return (lax.ppermute(right, 'tp', pairs), lax.ppermute(left, 'tp', mirror))  28.7 us
    ppermute x15, starting transfers between devices, turn(): return lax.ppermute(x, 'tp', [(i, (i + by) % n) for i in range(n)])  25.9 us
    convert_element_type x11, other arithmetic, add(): return (a.astype(F32) + b.astype(F32)).astype(BF)  25.6 us
    pallas_call x1, Pallas kernels, attend_back(): pl.pallas_call(attend_back_kernel, in_specs=[SMEM] + [VMEM] * (9 + count)...  25.5 us
  transfers between devices with their start and end apart: 68, of which 29 were waited for; matrix products, arithmetic and copies ran while one was open for 20% of the time, Pallas kernels for 10%

profile of v8, /device:TPU:0, one launch (start us, length us, event | category | flops | bytes accessed | tf_op | source)
XLA Modules:
  0.0 494.1 jit_solution(5575540106298956795)
XLA Ops:
  8.5 5.1 %collective-permute-start = (bf16[48,1536]{1,0:T(8,128)(2,1)S(1)}, bf16[48,1536]{1,0:T(8,128)(2,1)}, u32[]{:S(2)}, u32[]{:S(2)}) collective-permute-start(bf16[48,1536]{1,0:T(8,128)(2,1)S(1)} %constant_dynamic-slice_fusion.2), channel_id=1, source_target_pairs={{0,3},{1,0},{2,1},{3,2},{4,7},{5,4},{6,5},{7,6},{8,11},{9,8},{10,9... | collective-permute-start | bytes 442376 | tf_op jit(solution)/shard_map/ppermute | solution.py:438
  24.0 18.5 %shard_map.239 = (bf16[256,384]{1,0:T(8,128)(2,1)S(1)}, bf16[256,384]{1,0:T(8,128)(2,1)S(1)}, bf16[256,384]{1,0:T(8,128)(2,1)S(1)}, bf16[256,384]{1,0:T(8,128)(2...) custom-call(s32[1]{0:T(128)} %bitcast.8.at_ref, ...), custom_call_target="tpu_custom_call" | custom-call | flops 23000000512 | tf_op jit(solution)/shard_map/pallas_call | solution.py:121
  47.7 2.5 collective-permute-start.5
  53.3 3.2 collective-permute-done.5
  56.6 1.9 collective-permute-done.6
  60.3 1.6 collective-permute-start.10
  63.3 1.8 shard_map.240.router_ref
  65.1 17.7 %collective-permute-done.9 = bf16[256,384]{1,0:T(8,128)(2,1)S(1)} collective-permute-done((bf16[256,384]{1,0:T(8,128)(2,1)S(1)}, bf16[256,384]{1,0:T(8,128)(2,1)S(1)}, u32[]{:S(2)}, u32[]{:S(2)}) %collective-permute-start.9) | collective-permute-done | bytes 196640 | tf_op jit(solution)/shard_map/ppermute | solution.py:438
  88.1 1.8 collective-permute-start.15
  94.2 3.2 multiply_reduce_fusion.2
  100.1 9.8 %collective-permute-done.15 = bf16[256,1664]{1,0:T(8,128)(2,1)S(1)} collective-permute-done((bf16[256,1664]{1,0:T(8,128)(2,1)S(1)}, bf16[256,1664]{1,0:T(8,128)(2,1)S(1)}, u32[]{:S(2)}, u32[]{:S(2)}) %collective-permute-start.15) | collective-permute-done | bytes 852000 | tf_op jit(solution)/shard_map/ppermute | solution.py:433
  109.9 1.8 collective-permute-done.16
  111.7 7.5 %collective-permute-done.13 = bf16[128,1536]{1,0:T(8,128)(2,1)S(1)} collective-permute-done((bf16[128,1536]{1,0:T(8,128)(2,1)S(1)}, bf16[128,1536]{1,0:T(8,128)(2,1)S(1)}, u32[]{:S(2)}, u32[]{:S(2)}) %collective-permute-start.13) | collective-permute-done | bytes 393248 | tf_op jit(solution)/shard_map/ppermute | solution.py:433
  119.9 1.6 collective-permute-start.18
  125.5 12.7 %collective-permute-done.17 = bf16[256,1536]{1,0:T(8,128)(2,1)S(1)} collective-permute-done((bf16[256,1536]{1,0:T(8,128)(2,1)S(1)}, bf16[256,1536]{1,0:T(8,128)(2,1)S(1)}, u32[]{:S(2)}, u32[]{:S(2)}) %collective-permute-start.17) | collective-permute-done | bytes 786464 | tf_op jit(solution)/shard_map/ppermute | solution.py:433
  138.6 1.8 pad_maximum_fusion.near_ref
  140.3 5.3 %all-gather.2.cloned.1.call-done.parts_ref = bf16[1536,1536]{1,0:T(8,128)(2,1)} async-done(((bf16[384,1536]{1,0:T(8,128)(2,1)}), bf16[1536,1536]{1,0:T(8,128)(2,1)}) %all-gather.2.cloned.1.call-update) | async-done | bytes 4718608 | tf_op jit(solution)/shard_map/all_gather | solution.py:569
  146.3 44.9 %shard_map.241 = (bf16[1024,1536]{1,0:T(8,128)(2,1)}, bf16[1024,1536]{1,0:T(8,128)(2,1)}, bf16[1024,1664]{1,0:T(8,128)(2,1)}, bf16[512,1664]{1,0:T(8,128)(2,1)},...) custom-call(s32[2]{0:T(128)} %pad_add_fusion.order_ref, bf16[1024,1536]{1,0:T(8,128)(2,1)} %pad_maximum_fusion.near_ref, ...), custom_call_target="tpu_custom_call" | custom-call | flops 46000001024 | tf_op jit(solution)/shard_map/pallas_call | solution.py:360
  191.4 3.7 collective-permute-done.21
  195.1 3.0 add_convert_fusion.2
  201.6 1.6 shard_map.242
  203.2 17.1 %collective-permute-done.22 = bf16[256,1664]{1,0:T(8,128)(2,1)} collective-permute-done((bf16[256,1664]{1,0:T(8,128)(2,1)}, bf16[256,1664]{1,0:T(8,128)(2,1)}, u32[]{:S(2)}, u32[]{:S(2)}) %collective-permute-start.22) | collective-permute-done | bytes 852000 | tf_op jit(solution)/shard_map/ppermute | solution.py:433
  221.4 3.2 add_convert_fusion
  226.9 4.1 add_convert_fusion.8
  232.9 4.5 collective-permute-done.26
  237.4 1.6 collective-permute-done.27
  241.3 1.7 fusion.44
  249.0 2.5 copy.44
  253.9 1.7 add_convert_fusion.7
  258.6 1.6 fusion.7
  260.2 22.6 %collective-permute-done.29.refs_2_ = bf16[256,384]{1,0:T(8,128)(2,1)S(1)} collective-permute-done((bf16[256,384]{1,0:T(8,128)(2,1)}, bf16[256,384]{1,0:T(8,128)(2,1)S(1)}, u32[]{:S(2)}, u32[]{:S(2)}) %collective-permute-start.29) | collective-permute-done | bytes 196640 | tf_op jit(solution)/shard_map/ppermute | solution.py:438
  283.6 2.2 collective-permute-start.35
  285.8 1.7 collective-permute-start.36
  289.4 25.5 %shard_map.243 = (bf16[256,1536]{1,0:T(8,128)(2,1)S(1)}, bf16[256,1536]{1,0:T(8,128)(2,1)S(1)}, bf16[256,1536]{1,0:T(8,128)(2,1)S(1)}, bf16[256,1536]{1,0:T(8,12...) custom-call(s32[1]{0:T(128)} %bitcast.8.at_ref, bf16[6,1024,64]{2,1,0:T(8,128)(2,1)} %get-tuple-element.206.q_ref, ...), custom_call_target="tpu_custom_call" | custom-call | flops 23000000512 | tf_op jit(solution)/shard_map/pallas_call | solution.py:231
  316.7 5.8 %collective-permute-start.38 = (bf16[256,1536]{1,0:T(8,128)(2,1)}, bf16[256,1536]{1,0:T(8,128)(2,1)}, u32[]{:S(2)}, u32[]{:S(2)}) collective-permute-start(bf16[256,1536]{1,0:T(8,128)(2,1)} %get-tuple-element.316), channel_id=1, source_target_pairs={{0,1},{3,2},{4,5},{7,6},{8,9},{11,10},{12,13},{15,14},{16,17},{19,... | collective-permute-start | bytes 2359304 | tf_op jit(solution)/shard_map/ppermute | solution.py:453
  324.5 4.2 fusion.33
  333.7 1.7 convert_element_type.505
  335.4 4.3 convolution_convert_fusion.1
  339.6 7.3 %collective-permute-done.41 = bf16[208,1536]{1,0:T(8,128)(2,1)} collective-permute-done((bf16[208,1536]{1,0:T(8,128)(2,1)}, bf16[208,1536]{1,0:T(8,128)(2,1)}, u32[]{:S(2)}, u32[]{:S(2)}) %collective-permute-start.41) | collective-permute-done | bytes 639008 | tf_op jit(solution)/shard_map/ppermute | solution.py:433
  348.0 2.6 fusion.15
  350.7 5.3 %collective-permute-start.43 = (bf16[256,1536]{1,0:T(8,128)(2,1)}, bf16[256,1536]{1,0:T(8,128)(2,1)}, u32[]{:S(2)}, u32[]{:S(2)}) collective-permute-start(bf16[256,1536]{1,0:T(8,128)(2,1)} %get-tuple-element.447), channel_id=1, source_target_pairs={{0,1},{1,2},{4,5},{5,6},{8,9},{9,10},{12,13},{13,14},{16,17},{17,1... | collective-permute-start | bytes 2359304 | tf_op jit(solution)/shard_map/ppermute | solution.py:445
  356.0 1.6 collective-permute-start.44
  357.5 2.1 broadcast_select_fusion.1
  371.4 1.9 collective-permute-done.47
  373.3 6.1 %collective-permute-done.45 = bf16[256,1536]{1,0:T(8,128)(2,1)} collective-permute-done((bf16[256,1536]{1,0:T(8,128)(2,1)}, bf16[256,1536]{1,0:T(8,128)(2,1)}, u32[]{:S(2)}, u32[]{:S(2)}) %collective-permute-start.45) | collective-permute-done | bytes 786464 | tf_op jit(solution)/shard_map/ppermute | solution.py:453
  381.9 2.0 collective-permute-start.51
  387.7 6.7 %collective-permute-start.48 = (bf16[56,1536]{1,0:T(8,128)(2,1)S(1)}, bf16[56,1536]{1,0:T(8,128)(2,1)S(1)}, u32[]{:S(2)}, u32[]{:S(2)}) collective-permute-start(bf16[56,1536]{1,0:T(8,128)(2,1)S(1)} %get-tuple-element.464), channel_id=1, source_target_pairs={{0,3},{1,0},{2,1},{3,2},{4,7},{5,4},{6,5},{7,6},{8,11},{9,8},{10,9... | collective-permute-start | bytes 516104 | tf_op jit(solution)/shard_map/ppermute | solution.py:438
  395.1 6.6 %collective-permute-done.51 = bf16[256,1536]{1,0:T(8,128)(2,1)S(1)} collective-permute-done((bf16[256,1536]{1,0:T(8,128)(2,1)S(1)}, bf16[256,1536]{1,0:T(8,128)(2,1)S(1)}, u32[]{:S(2)}, u32[]{:S(2)}) %collective-permute-start.51) | collective-permute-done | bytes 786464 | tf_op jit(solution)/shard_map/ppermute | solution.py:445
  401.6 4.5 collective-permute-done.52
  406.9 2.2 fusion.20
  409.2 9.4 %collective-permute-start.56 = (bf16[256,1536]{1,0:T(8,128)(2,1)S(1)}, bf16[256,1536]{1,0:T(8,128)(2,1)S(1)}, u32[]{:S(2)}, u32[]{:S(2)}) collective-permute-start(bf16[256,1536]{1,0:T(8,128)(2,1)S(1)} %fusion.20), channel_id=1, source_target_pairs={{0,1},{1,2},{2,3},{4,5},{5,6},{6,7},{8,9},{9,10},{10,11},{12,13},{... | collective-permute-start | bytes 2359304 | tf_op jit(solution)/shard_map/ppermute | solution.py:445
  423.0 2.7 collective-permute-start.53
  426.7 2.0 collective-permute-start.55
  428.8 6.8 %collective-permute-done.53 = f32[1,1536]{1,0:T(1,128)S(1)} collective-permute-done((f32[1,1536]{1,0:T(1,128)S(1)}, f32[1,1536]{1,0:T(1,128)S(1)}, u32[]{:S(2)}, u32[]{:S(2)}) %collective-permute-start.53) | collective-permute-done | bytes 6176 | tf_op jit(solution)/shard_map/ppermute | solution.py:438
  435.6 2.6 collective-permute-done.54
  442.5 1.6 collective-permute-start.60
  444.1 1.9 broadcast.86.clone
  446.9 2.1 constant_dynamic-update-slice_fusion.13
  449.4 7.1 %collective-permute-done.62 = bf16[256,1536]{1,0:T(8,128)(2,1)S(1)} collective-permute-done((bf16[256,1536]{1,0:T(8,128)(2,1)}, bf16[256,1536]{1,0:T(8,128)(2,1)S(1)}, u32[]{:S(2)}, u32[]{:S(2)}) %collective-permute-start.62) | collective-permute-done | bytes 786464 | tf_op jit(solution)/shard_map/ppermute | solution.py:445
  458.5 2.6 constant_dynamic-update-slice_fusion.23
  464.7 2.1 shard_map.244
  466.9 3.0 slice.442
  471.7 11.4 %collective-permute-done.64 = bf16[256,1536]{1,0:T(8,128)(2,1)} collective-permute-done((bf16[256,1536]{1,0:T(8,128)(2,1)}, bf16[256,1536]{1,0:T(8,128)(2,1)}, u32[]{:S(2)}, u32[]{:S(2)}) %collective-permute-start.64) | collective-permute-done | bytes 786464 | tf_op jit(solution)/shard_map/ppermute | solution.py:453
  484.4 2.1 constant_dynamic-update-slice_fusion.22
  (385 shorter events, 115.4 us)
Async XLA Ops:
  7.2 138.4 %all-gather.2.cloned.1.call-start = ((), (), s32[]{:S(2)}) async-start(), calls=%async_computation.1 | async-start | bytes 5898240 | tf_op jit(solution)/shard_map/all_gather | solution.py:569
  8.5 35.7 %collective-permute-start = (bf16[48,1536]{1,0:T(8,128)(2,1)S(1)}, bf16[48,1536]{1,0:T(8,128)(2,1)}, u32[]{:S(2)}, u32[]{:S(2)}) collective-permute-start(bf16[48,1536]{1,0:T(8,128)(2,1)S(1)} %constant_dynamic-slice_fusion.2), channel_id=1, source_target_pairs={{0,3},{1,0},{2,1},{3,2},{4,7},{5,4},{6,5},{7,6},{8,11},{9,8},{10,9... | collective-permute-start | bytes 442376 | tf_op jit(solution)/shard_map/ppermute | solution.py:438
  13.6 30.6 %collective-permute-start.1 = (bf16[48,1536]{1,0:T(8,128)(2,1)S(1)}, bf16[48,1536]{1,0:T(8,128)(2,1)}, u32[]{:S(2)}, u32[]{:S(2)}) collective-permute-start(bf16[48,1536]{1,0:T(8,128)(2,1)S(1)} %constant_dynamic-slice_fusion.2), channel_id=1, source_target_pairs={{0,2},{1,3},{2,0},{3,1},{4,6},{5,7},{6,4},{7,5},{8,10},{9,11},{10,... | collective-permute-start | bytes 442376 | tf_op jit(solution)/shard_map/ppermute | solution.py:438
  13.6 30.6 %collective-permute-start.2 = (bf16[48,1536]{1,0:T(8,128)(2,1)S(1)}, bf16[48,1536]{1,0:T(8,128)(2,1)}, u32[]{:S(2)}, u32[]{:S(2)}) collective-permute-start(bf16[48,1536]{1,0:T(8,128)(2,1)S(1)} %constant_dynamic-slice_fusion.2), channel_id=1, source_target_pairs={{0,1},{1,2},{2,3},{3,0},{4,5},{5,6},{6,7},{7,4},{8,9},{9,10},{10,1... | collective-permute-start | bytes 442376 | tf_op jit(solution)/shard_map/ppermute | solution.py:438
  17.9 26.3 %collective-permute-start.3 = (bf16[128,1664]{1,0:T(8,128)(2,1)}, bf16[128,1664]{1,0:T(8,128)(2,1)}, u32[]{:S(2)}, u32[]{:S(2)}) collective-permute-start(bf16[128,1664]{1,0:T(8,128)(2,1)} %get-tuple-element.451), channel_id=1, source_target_pairs={{0,8},{4,12},{8,0},{12,4},{16,24},{20,28},{24,16},{28,20},{1,9},{5... | collective-permute-start | bytes 1277960 | tf_op jit(solution)/shard_map/ppermute | solution.py:433
  19.4 24.8 %collective-permute-start.4 = (bf16[128,1664]{1,0:T(8,128)(2,1)}, bf16[128,1664]{1,0:T(8,128)(2,1)}, u32[]{:S(2)}, u32[]{:S(2)}) collective-permute-start(bf16[128,1664]{1,0:T(8,128)(2,1)} %get-tuple-element.450), channel_id=1, source_target_pairs={{0,16},{4,20},{8,24},{12,28},{16,0},{20,4},{24,8},{28,12},{1,17},{... | collective-permute-start | bytes 1277960 | tf_op jit(solution)/shard_map/ppermute | solution.py:433
  45.1 13.4 %collective-permute-start.7 = (bf16[96,1536]{1,0:T(8,128)(2,1)S(1)}, bf16[96,1536]{1,0:T(8,128)(2,1)S(1)}, u32[]{:S(2)}, u32[]{:S(2)}) collective-permute-start(bf16[96,1536]{1,0:T(8,128)(2,1)S(1)} %pad_maximum_fusion.10), channel_id=1, source_target_pairs={{0,8},{4,12},{8,0},{12,4},{16,24},{20,28},{24,16},{28,20},{1,9},{5... | collective-permute-start | bytes 884744 | tf_op jit(solution)/shard_map/ppermute | solution.py:433
  46.7 11.8 %collective-permute-start.8 = (bf16[96,1536]{1,0:T(8,128)(2,1)S(1)}, bf16[96,1536]{1,0:T(8,128)(2,1)S(1)}, u32[]{:S(2)}, u32[]{:S(2)}) collective-permute-start(bf16[96,1536]{1,0:T(8,128)(2,1)S(1)} %pad_maximum_fusion.11), channel_id=1, source_target_pairs={{0,16},{4,20},{8,24},{12,28},{16,0},{20,4},{24,8},{28,12},{1,17},{... | collective-permute-start | bytes 884744 | tf_op jit(solution)/shard_map/ppermute | solution.py:433
  47.3 269.4 %reduce-scatter.2.cloned.1.call-start = ((), (), s32[]{:S(2)}) async-start(), calls=%async_computation.2 | async-start | bytes 5898240 | tf_op jit(solution)/shard_map/reduce_scatter | solution.py:660
  47.7 8.9 %collective-permute-start.5 = (bf16[256,384]{1,0:T(8,128)(2,1)S(1)}, bf16[256,384]{1,0:T(8,128)(2,1)}, u32[]{:S(2)}, u32[]{:S(2)}) collective-permute-start(bf16[256,384]{1,0:T(8,128)(2,1)S(1)} %get-tuple-element.214), channel_id=1, source_target_pairs={{0,1},{1,2},{2,3},{3,0},{4,5},{5,6},{6,7},{7,4},{8,9},{9,10},{10,1... | collective-permute-start | bytes 589832 | tf_op jit(solution)/shard_map/ppermute | solution.py:438
  50.2 8.3 %collective-permute-start.6 = (bf16[256,384]{1,0:T(8,128)(2,1)S(1)}, bf16[256,384]{1,0:T(8,128)(2,1)}, u32[]{:S(2)}, u32[]{:S(2)}) collective-permute-start(bf16[256,384]{1,0:T(8,128)(2,1)S(1)} %get-tuple-element.215), channel_id=1, source_target_pairs={{0,3},{1,0},{2,1},{3,2},{4,7},{5,4},{6,5},{7,6},{8,11},{9,8},{10,9... | collective-permute-start | bytes 589832 | tf_op jit(solution)/shard_map/ppermute | solution.py:438
  58.5 24.3 %collective-permute-start.9 = (bf16[256,384]{1,0:T(8,128)(2,1)S(1)}, bf16[256,384]{1,0:T(8,128)(2,1)S(1)}, u32[]{:S(2)}, u32[]{:S(2)}) collective-permute-start(bf16[256,384]{1,0:T(8,128)(2,1)S(1)} %get-tuple-element.224), channel_id=1, source_target_pairs={{0,2},{1,3},{2,0},{3,1},{4,6},{5,7},{6,4},{7,5},{8,10},{9,11},{10,... | collective-permute-start | bytes 589832 | tf_op jit(solution)/shard_map/ppermute | solution.py:438
  60.3 22.6 %collective-permute-start.10 = (bf16[192,1536]{1,0:T(8,128)(2,1)S(1)}, bf16[192,1536]{1,0:T(8,128)(2,1)}, u32[]{:S(2)}, u32[]{:S(2)}) collective-permute-start(bf16[192,1536]{1,0:T(8,128)(2,1)S(1)} %get-tuple-element.237), channel_id=1, source_target_pairs={{0,16},{4,20},{8,24},{12,28},{16,0},{20,4},{24,8},{28,12},{1,17},{... | collective-permute-start | bytes 1769480 | tf_op jit(solution)/shard_map/ppermute | solution.py:433
  61.9 21.0 %collective-permute-start.11 = (bf16[192,1536]{1,0:T(8,128)(2,1)S(1)}, bf16[192,1536]{1,0:T(8,128)(2,1)S(1)}, u32[]{:S(2)}, u32[]{:S(2)}) collective-permute-start(bf16[192,1536]{1,0:T(8,128)(2,1)S(1)} %get-tuple-element.239), channel_id=1, source_target_pairs={{0,8},{4,12},{8,0},{12,4},{16,24},{20,28},{24,16},{28,20},{1,9},{5... | collective-permute-start | bytes 1769480 | tf_op jit(solution)/shard_map/ppermute | solution.py:433
  84.1 9.4 %collective-permute-start.12 = (bf16[768,1536]{1,0:T(8,128)(2,1)S(1)}, bf16[768,1536]{1,0:T(8,128)(2,1)S(1)}, u32[]{:S(2)}, u32[]{:S(2)}) collective-permute-start(bf16[768,1536]{1,0:T(8,128)(2,1)S(1)} %constant_dynamic-update-slice_fusion.4), channel_id=1, source_target_pairs={{0,4},{4,0},{8,12},{12,8},{16,20},{20,16},{24,28},{28,24},{1,5},{5... | collective-permute-start | bytes 7077896 | tf_op jit(solution)/shard_map/ppermute | solution.py:433
  88.1 21.8 %collective-permute-start.15 = (bf16[256,1664]{1,0:T(8,128)(2,1)S(1)}, bf16[256,1664]{1,0:T(8,128)(2,1)S(1)}, u32[]{:S(2)}, u32[]{:S(2)}) collective-permute-start(bf16[256,1664]{1,0:T(8,128)(2,1)S(1)} %pad_maximum_fusion.1), channel_id=1, source_target_pairs={{0,16},{4,20},{8,24},{12,28},{16,0},{20,4},{24,8},{28,12},{1,17},{... | collective-permute-start | bytes 2555912 | tf_op jit(solution)/shard_map/ppermute | solution.py:433
  89.9 21.8 %collective-permute-start.16 = (bf16[256,1664]{1,0:T(8,128)(2,1)S(1)}, bf16[256,1664]{1,0:T(8,128)(2,1)S(1)}, u32[]{:S(2)}, u32[]{:S(2)}) collective-permute-start(bf16[256,1664]{1,0:T(8,128)(2,1)S(1)} %pad_maximum_fusion.2), channel_id=1, source_target_pairs={{0,8},{4,12},{8,0},{12,4},{16,24},{20,28},{24,16},{28,20},{1,9},{5... | collective-permute-start | bytes 2555912 | tf_op jit(solution)/shard_map/ppermute | solution.py:433
  97.8 21.5 %collective-permute-start.13 = (bf16[128,1536]{1,0:T(8,128)(2,1)S(1)}, bf16[128,1536]{1,0:T(8,128)(2,1)S(1)}, u32[]{:S(2)}, u32[]{:S(2)}) collective-permute-start(bf16[128,1536]{1,0:T(8,128)(2,1)S(1)} %get-tuple-element.459), channel_id=1, source_target_pairs={{0,8},{4,12},{8,0},{12,4},{16,24},{20,28},{24,16},{28,20},{1,9},{5... | collective-permute-start | bytes 1179656 | tf_op jit(solution)/shard_map/ppermute | solution.py:433
  98.4 20.8 %collective-permute-start.14 = (bf16[128,1536]{1,0:T(8,128)(2,1)S(1)}, bf16[128,1536]{1,0:T(8,128)(2,1)S(1)}, u32[]{:S(2)}, u32[]{:S(2)}) collective-permute-start(bf16[128,1536]{1,0:T(8,128)(2,1)S(1)} %get-tuple-element.458), channel_id=1, source_target_pairs={{0,16},{4,20},{8,24},{12,28},{16,0},{20,4},{24,8},{28,12},{1,17},{... | collective-permute-start | bytes 1179656 | tf_op jit(solution)/shard_map/ppermute | solution.py:433
  119.4 18.8 %collective-permute-start.17 = (bf16[256,1536]{1,0:T(8,128)(2,1)S(1)}, bf16[256,1536]{1,0:T(8,128)(2,1)S(1)}, u32[]{:S(2)}, u32[]{:S(2)}) collective-permute-start(bf16[256,1536]{1,0:T(8,128)(2,1)S(1)} %pad_maximum_fusion.3), channel_id=1, source_target_pairs={{0,16},{4,20},{8,24},{12,28},{16,0},{20,4},{24,8},{28,12},{1,17},{... | collective-permute-start | bytes 2359304 | tf_op jit(solution)/shard_map/ppermute | solution.py:433
  119.9 18.7 %collective-permute-start.18 = (bf16[256,1536]{1,0:T(8,128)(2,1)S(1)}, bf16[256,1536]{1,0:T(8,128)(2,1)S(1)}, u32[]{:S(2)}, u32[]{:S(2)}) collective-permute-start(bf16[256,1536]{1,0:T(8,128)(2,1)S(1)} %pad_maximum_fusion.4), channel_id=1, source_target_pairs={{0,8},{4,12},{8,0},{12,4},{16,24},{20,28},{24,16},{28,20},{1,9},{5... | collective-permute-start | bytes 2359304 | tf_op jit(solution)/shard_map/ppermute | solution.py:433
  125.5 20.1 %collective-permute-start.20 = (bf16[1024,1664]{1,0:T(8,128)(2,1)}, bf16[1024,1664]{1,0:T(8,128)(2,1)}, u32[]{:S(2)}, u32[]{:S(2)}) collective-permute-start(bf16[1024,1664]{1,0:T(8,128)(2,1)} %constant_dynamic-update-slice_fusion.8.extra_near_ref), channel_id=1, source_target_pairs={{0,4},{4,0},{8,12},{12,8},{16,20},{20,16},{24,28},{28,24},{1,5},{5... | collective-permute-start | bytes 10223624 | tf_op jit(solution)/shard_map/ppermute | solution.py:433
  198.1 23.3 %collective-permute-start.24 = (bf16[1024,1536]{1,0:T(8,128)(2,1)}, bf16[1024,1536]{1,0:T(8,128)(2,1)}, u32[]{:S(2)}, u32[]{:S(2)}) collective-permute-start(bf16[1024,1536]{1,0:T(8,128)(2,1)} %get-tuple-element.268), channel_id=1, source_target_pairs={{0,4},{4,0},{8,12},{12,8},{16,20},{20,16},{24,28},{28,24},{1,5},{5... | collective-permute-start | bytes 9437192 | tf_op jit(solution)/shard_map/ppermute | solution.py:433
  198.4 266.3 %all-reduce.7.cloned.1.call-start = ((), (), s32[]{:S(2)}) async-start(), calls=%async_computation.3 | async-start | bytes 3932160 | tf_op jit(solution)/shard_map/psum | solution.py:768
  198.6 21.6 %collective-permute-start.22 = (bf16[256,1664]{1,0:T(8,128)(2,1)}, bf16[256,1664]{1,0:T(8,128)(2,1)}, u32[]{:S(2)}, u32[]{:S(2)}) collective-permute-start(bf16[256,1664]{1,0:T(8,128)(2,1)} %get-tuple-element.263), channel_id=1, source_target_pairs={{0,16},{4,20},{8,24},{12,28},{16,0},{20,4},{24,8},{28,12},{1,17},{... | collective-permute-start | bytes 2555912 | tf_op jit(solution)/shard_map/ppermute | solution.py:433
  200.1 21.2 %collective-permute-start.23 = (bf16[256,1664]{1,0:T(8,128)(2,1)}, bf16[256,1664]{1,0:T(8,128)(2,1)}, u32[]{:S(2)}, u32[]{:S(2)}) collective-permute-start(bf16[256,1664]{1,0:T(8,128)(2,1)} %get-tuple-element.264), channel_id=1, source_target_pairs={{0,8},{4,12},{8,0},{12,4},{16,24},{20,28},{24,16},{28,20},{1,9},{5... | collective-permute-start | bytes 2555912 | tf_op jit(solution)/shard_map/ppermute | solution.py:433
  201.6 19.8 %collective-permute-start.25 = (bf16[512,1664]{1,0:T(8,128)(2,1)}, bf16[512,1664]{1,0:T(8,128)(2,1)}, u32[]{:S(2)}, u32[]{:S(2)}) collective-permute-start(bf16[512,1664]{1,0:T(8,128)(2,1)} %get-tuple-element.269), channel_id=1, source_target_pairs={{0,4},{4,0},{8,12},{12,8},{16,20},{20,16},{24,28},{28,24},{1,5},{5... | collective-permute-start | bytes 5111816 | tf_op jit(solution)/shard_map/ppermute | solution.py:433
  224.6 12.8 %collective-permute-start.26 = (bf16[128,1664]{1,0:T(8,128)(2,1)S(1)}, bf16[128,1664]{1,0:T(8,128)(2,1)S(1)}, u32[]{:S(2)}, u32[]{:S(2)}) collective-permute-start(bf16[128,1664]{1,0:T(8,128)(2,1)S(1)} %slice.347), channel_id=1, source_target_pairs={{0,8},{4,12},{8,0},{12,4},{16,24},{20,28},{24,16},{28,20},{1,9},{5... | collective-permute-start | bytes 1277960 | tf_op jit(solution)/shard_map/ppermute | solution.py:433
  226.2 12.8 %collective-permute-start.27 = (bf16[128,1664]{1,0:T(8,128)(2,1)S(1)}, bf16[128,1664]{1,0:T(8,128)(2,1)S(1)}, u32[]{:S(2)}, u32[]{:S(2)}) collective-permute-start(bf16[128,1664]{1,0:T(8,128)(2,1)S(1)} %slice.348), channel_id=1, source_target_pairs={{0,16},{4,20},{8,24},{12,28},{16,0},{20,4},{24,8},{28,12},{1,17},{... | collective-permute-start | bytes 1277960 | tf_op jit(solution)/shard_map/ppermute | solution.py:433
  230.9 22.9 %collective-permute-start.31 = (bf16[256,1536]{1,0:T(8,128)(2,1)}, bf16[256,1536]{1,0:T(8,128)(2,1)}, u32[]{:S(2)}, u32[]{:S(2)}) collective-permute-start(bf16[256,1536]{1,0:T(8,128)(2,1)} %get-tuple-element.288), channel_id=1, source_target_pairs={{0,16},{4,20},{8,24},{12,28},{16,0},{20,4},{24,8},{28,12},{1,17},{... | collective-permute-start | bytes 2359304 | tf_op jit(solution)/shard_map/ppermute | solution.py:433
  232.3 23.3 %collective-permute-start.32 = (bf16[256,1536]{1,0:T(8,128)(2,1)}, bf16[256,1536]{1,0:T(8,128)(2,1)}, u32[]{:S(2)}, u32[]{:S(2)}) collective-permute-start(bf16[256,1536]{1,0:T(8,128)(2,1)} %get-tuple-element.290), channel_id=1, source_target_pairs={{0,8},{4,12},{8,0},{12,4},{16,24},{20,28},{24,16},{28,20},{1,9},{5... | collective-permute-start | bytes 2359304 | tf_op jit(solution)/shard_map/ppermute | solution.py:433
  245.3 15.0 %collective-permute-start.28 = (bf16[256,384]{1,0:T(8,128)(2,1)}, bf16[256,384]{1,0:T(8,128)(2,1)S(1)}, u32[]{:S(2)}, u32[]{:S(2)}) collective-permute-start(bf16[256,384]{1,0:T(8,128)(2,1)} %get-tuple-element.282), channel_id=1, source_target_pairs={{0,3},{1,0},{2,1},{3,2},{4,7},{5,4},{6,5},{7,6},{8,11},{9,8},{10,9... | collective-permute-start | bytes 589832 | tf_op jit(solution)/shard_map/ppermute | solution.py:438
  245.9 36.9 %collective-permute-start.29 = (bf16[256,384]{1,0:T(8,128)(2,1)}, bf16[256,384]{1,0:T(8,128)(2,1)S(1)}, u32[]{:S(2)}, u32[]{:S(2)}) collective-permute-start(bf16[256,384]{1,0:T(8,128)(2,1)} %get-tuple-element.283), channel_id=1, source_target_pairs={{0,2},{1,3},{2,0},{3,1},{4,6},{5,7},{6,4},{7,5},{8,10},{9,11},{10,... | collective-permute-start | bytes 589832 | tf_op jit(solution)/shard_map/ppermute | solution.py:438
  246.0 36.9 %collective-permute-start.30 = (bf16[256,384]{1,0:T(8,128)(2,1)}, bf16[256,384]{1,0:T(8,128)(2,1)S(1)}, u32[]{:S(2)}, u32[]{:S(2)}) collective-permute-start(bf16[256,384]{1,0:T(8,128)(2,1)} %get-tuple-element.284), channel_id=1, source_target_pairs={{0,1},{1,2},{2,3},{3,0},{4,5},{5,6},{6,7},{7,4},{8,9},{9,10},{10,1... | collective-permute-start | bytes 589832 | tf_op jit(solution)/shard_map/ppermute | solution.py:438
  257.1 25.7 %collective-permute-start.33 = (bf16[128,1536]{1,0:T(8,128)(2,1)S(1)}, bf16[128,1536]{1,0:T(8,128)(2,1)S(1)}, u32[]{:S(2)}, u32[]{:S(2)}) collective-permute-start(bf16[128,1536]{1,0:T(8,128)(2,1)S(1)} %slice.366), channel_id=1, source_target_pairs={{0,8},{4,12},{8,0},{12,4},{16,24},{20,28},{24,16},{28,20},{1,9},{5... | collective-permute-start | bytes 1179656 | tf_op jit(solution)/shard_map/ppermute | solution.py:433
  257.8 25.1 %collective-permute-start.34 = (bf16[128,1536]{1,0:T(8,128)(2,1)S(1)}, bf16[128,1536]{1,0:T(8,128)(2,1)S(1)}, u32[]{:S(2)}, u32[]{:S(2)}) collective-permute-start(bf16[128,1536]{1,0:T(8,128)(2,1)S(1)} %slice.367), channel_id=1, source_target_pairs={{0,16},{4,20},{8,24},{12,28},{16,0},{20,4},{24,8},{28,12},{1,17},{... | collective-permute-start | bytes 1179656 | tf_op jit(solution)/shard_map/ppermute | solution.py:433
  282.9 33.8 %collective-permute-start.37 = (bf16[4,208,1536]{2,1,0:T(8,128)(2,1)S(1)}, bf16[4,208,1536]{2,1,0:T(8,128)(2,1)}, u32[]{:S(2)}, u32[]{:S(2)}) collective-permute-start(bf16[4,208,1536]{2,1,0:T(8,128)(2,1)S(1)} %get-tuple-element.313), channel_id=1, source_target_pairs={{0,4},{4,0},{8,12},{12,8},{16,20},{20,16},{24,28},{28,24},{1,5},{5... | collective-permute-start | bytes 7667720 | tf_op jit(solution)/shard_map/ppermute | solution.py:433
  283.6 31.3 %collective-permute-start.35 = (bf16[256,1536]{1,0:T(8,128)(2,1)S(1)}, bf16[256,1536]{1,0:T(8,128)(2,1)S(1)}, u32[]{:S(2)}, u32[]{:S(2)}) collective-permute-start(bf16[256,1536]{1,0:T(8,128)(2,1)S(1)} %fusion.24), channel_id=1, source_target_pairs={{0,1},{1,2},{2,3},{4,5},{5,6},{6,7},{8,9},{9,10},{10,11},{12,13},{... | collective-permute-start | bytes 2359304 | tf_op jit(solution)/shard_map/ppermute | solution.py:445
  285.8 29.1 %collective-permute-start.36 = (bf16[256,1536]{1,0:T(8,128)(2,1)S(1)}, bf16[256,1536]{1,0:T(8,128)(2,1)S(1)}, u32[]{:S(2)}, u32[]{:S(2)}) collective-permute-start(bf16[256,1536]{1,0:T(8,128)(2,1)S(1)} %fusion.24), channel_id=1, source_target_pairs={{3,2},{2,1},{1,0},{7,6},{6,5},{5,4},{11,10},{10,9},{9,8},{15,14},{... | collective-permute-start | bytes 2359304 | tf_op jit(solution)/shard_map/ppermute | solution.py:445
  316.7 31.3 %collective-permute-start.38 = (bf16[256,1536]{1,0:T(8,128)(2,1)}, bf16[256,1536]{1,0:T(8,128)(2,1)}, u32[]{:S(2)}, u32[]{:S(2)}) collective-permute-start(bf16[256,1536]{1,0:T(8,128)(2,1)} %get-tuple-element.316), channel_id=1, source_target_pairs={{0,1},{3,2},{4,5},{7,6},{8,9},{11,10},{12,13},{15,14},{16,17},{19,... | collective-permute-start | bytes 2359304 | tf_op jit(solution)/shard_map/ppermute | solution.py:453
  322.5 25.6 %collective-permute-start.39 = (bf16[256,1536]{1,0:T(8,128)(2,1)}, bf16[256,1536]{1,0:T(8,128)(2,1)S(1)}, u32[]{:S(2)}, u32[]{:S(2)}) collective-permute-start(bf16[256,1536]{1,0:T(8,128)(2,1)} %copy-done.55), channel_id=1, source_target_pairs={{1,2},{2,3},{5,6},{6,7},{9,10},{10,11},{13,14},{14,15},{17,18},{18... | collective-permute-start | bytes 2359304 | tf_op jit(solution)/shard_map/ppermute | solution.py:445
  323.2 24.8 %collective-permute-start.40 = (bf16[256,1536]{1,0:T(8,128)(2,1)}, bf16[256,1536]{1,0:T(8,128)(2,1)}, u32[]{:S(2)}, u32[]{:S(2)}) collective-permute-start(bf16[256,1536]{1,0:T(8,128)(2,1)} %copy-done.57), channel_id=1, source_target_pairs={{2,1},{1,0},{6,5},{5,4},{10,9},{9,8},{14,13},{13,12},{18,17},{17,1... | collective-permute-start | bytes 2359304 | tf_op jit(solution)/shard_map/ppermute | solution.py:445
  330.5 16.5 %collective-permute-start.41 = (bf16[208,1536]{1,0:T(8,128)(2,1)}, bf16[208,1536]{1,0:T(8,128)(2,1)}, u32[]{:S(2)}, u32[]{:S(2)}) collective-permute-start(bf16[208,1536]{1,0:T(8,128)(2,1)} %pad_maximum_fusion.6), channel_id=1, source_target_pairs={{0,16},{4,20},{8,24},{12,28},{16,0},{20,4},{24,8},{28,12},{1,17},{... | collective-permute-start | bytes 1916936 | tf_op jit(solution)/shard_map/ppermute | solution.py:433
  331.8 16.2 %collective-permute-start.42 = (bf16[208,1536]{1,0:T(8,128)(2,1)}, bf16[208,1536]{1,0:T(8,128)(2,1)}, u32[]{:S(2)}, u32[]{:S(2)}) collective-permute-start(bf16[208,1536]{1,0:T(8,128)(2,1)} %pad_maximum_fusion.7), channel_id=1, source_target_pairs={{0,8},{4,12},{8,0},{12,4},{16,24},{20,28},{24,16},{28,20},{1,9},{5... | collective-permute-start | bytes 1916936 | tf_op jit(solution)/shard_map/ppermute | solution.py:433
  350.7 22.6 %collective-permute-start.43 = (bf16[256,1536]{1,0:T(8,128)(2,1)}, bf16[256,1536]{1,0:T(8,128)(2,1)}, u32[]{:S(2)}, u32[]{:S(2)}) collective-permute-start(bf16[256,1536]{1,0:T(8,128)(2,1)} %get-tuple-element.447), channel_id=1, source_target_pairs={{0,1},{1,2},{4,5},{5,6},{8,9},{9,10},{12,13},{13,14},{16,17},{17,1... | collective-permute-start | bytes 2359304 | tf_op jit(solution)/shard_map/ppermute | solution.py:445
  356.0 17.3 %collective-permute-start.44 = (bf16[256,1536]{1,0:T(8,128)(2,1)}, bf16[256,1536]{1,0:T(8,128)(2,1)}, u32[]{:S(2)}, u32[]{:S(2)}) collective-permute-start(bf16[256,1536]{1,0:T(8,128)(2,1)} %get-tuple-element.446), channel_id=1, source_target_pairs={{3,2},{2,1},{7,6},{6,5},{11,10},{10,9},{15,14},{14,13},{19,18},{18... | collective-permute-start | bytes 2359304 | tf_op jit(solution)/shard_map/ppermute | solution.py:445
  359.6 19.8 %collective-permute-start.45 = (bf16[256,1536]{1,0:T(8,128)(2,1)}, bf16[256,1536]{1,0:T(8,128)(2,1)}, u32[]{:S(2)}, u32[]{:S(2)}) collective-permute-start(bf16[256,1536]{1,0:T(8,128)(2,1)} %broadcast_select_fusion.1), channel_id=1, source_target_pairs={{2,3},{1,0},{6,7},{5,4},{10,11},{9,8},{14,15},{13,12},{18,19},{17,... | collective-permute-start | bytes 2359304 | tf_op jit(solution)/shard_map/ppermute | solution.py:453
  363.6 7.8 %collective-permute-start.46 = (bf16[104,1536]{1,0:T(8,128)(2,1)S(1)}, bf16[104,1536]{1,0:T(8,128)(2,1)}, u32[]{:S(2)}, u32[]{:S(2)}) collective-permute-start(bf16[104,1536]{1,0:T(8,128)(2,1)S(1)} %slice.370), channel_id=1, source_target_pairs={{0,8},{4,12},{8,0},{12,4},{16,24},{20,28},{24,16},{28,20},{1,9},{5... | collective-permute-start | bytes 958472 | tf_op jit(solution)/shard_map/ppermute | solution.py:433
  365.6 7.6 %collective-permute-start.47 = (bf16[104,1536]{1,0:T(8,128)(2,1)}, bf16[104,1536]{1,0:T(8,128)(2,1)}, u32[]{:S(2)}, u32[]{:S(2)}) collective-permute-start(bf16[104,1536]{1,0:T(8,128)(2,1)} %slice.371), channel_id=1, source_target_pairs={{0,16},{4,20},{8,24},{12,28},{16,0},{20,4},{24,8},{28,12},{1,17},{... | collective-permute-start | bytes 958472 | tf_op jit(solution)/shard_map/ppermute | solution.py:433
  381.9 19.7 %collective-permute-start.51 = (bf16[256,1536]{1,0:T(8,128)(2,1)S(1)}, bf16[256,1536]{1,0:T(8,128)(2,1)S(1)}, u32[]{:S(2)}, u32[]{:S(2)}) collective-permute-start(bf16[256,1536]{1,0:T(8,128)(2,1)S(1)} %add_convert_fusion.5), channel_id=1, source_target_pairs={{0,1},{1,2},{2,3},{4,5},{5,6},{6,7},{8,9},{9,10},{10,11},{12,13},{... | collective-permute-start | bytes 2359304 | tf_op jit(solution)/shard_map/ppermute | solution.py:445
  385.2 20.9 %collective-permute-start.52 = (bf16[256,1536]{1,0:T(8,128)(2,1)S(1)}, bf16[256,1536]{1,0:T(8,128)(2,1)S(1)}, u32[]{:S(2)}, u32[]{:S(2)}) collective-permute-start(bf16[256,1536]{1,0:T(8,128)(2,1)S(1)} %add_convert_fusion.4), channel_id=1, source_target_pairs={{3,2},{2,1},{1,0},{7,6},{6,5},{5,4},{11,10},{10,9},{9,8},{15,14},{... | collective-permute-start | bytes 2359304 | tf_op jit(solution)/shard_map/ppermute | solution.py:445
  387.7 35.3 %collective-permute-start.48 = (bf16[56,1536]{1,0:T(8,128)(2,1)S(1)}, bf16[56,1536]{1,0:T(8,128)(2,1)S(1)}, u32[]{:S(2)}, u32[]{:S(2)}) collective-permute-start(bf16[56,1536]{1,0:T(8,128)(2,1)S(1)} %get-tuple-element.464), channel_id=1, source_target_pairs={{0,3},{1,0},{2,1},{3,2},{4,7},{5,4},{6,5},{7,6},{8,11},{9,8},{10,9... | collective-permute-start | bytes 516104 | tf_op jit(solution)/shard_map/ppermute | solution.py:438
  394.4 31.3 %collective-permute-start.49 = (bf16[56,1536]{1,0:T(8,128)(2,1)S(1)}, bf16[56,1536]{1,0:T(8,128)(2,1)S(1)}, u32[]{:S(2)}, u32[]{:S(2)}) collective-permute-start(bf16[56,1536]{1,0:T(8,128)(2,1)S(1)} %get-tuple-element.463), channel_id=1, source_target_pairs={{0,2},{1,3},{2,0},{3,1},{4,6},{5,7},{6,4},{7,5},{8,10},{9,11},{10,... | collective-permute-start | bytes 516104 | tf_op jit(solution)/shard_map/ppermute | solution.py:438
  394.4 32.3 %collective-permute-start.50 = (bf16[56,1536]{1,0:T(8,128)(2,1)S(1)}, bf16[56,1536]{1,0:T(8,128)(2,1)S(1)}, u32[]{:S(2)}, u32[]{:S(2)}) collective-permute-start(bf16[56,1536]{1,0:T(8,128)(2,1)S(1)} %get-tuple-element.462), channel_id=1, source_target_pairs={{0,1},{1,2},{2,3},{3,0},{4,5},{5,6},{6,7},{7,4},{8,9},{9,10},{10,1... | collective-permute-start | bytes 516104 | tf_op jit(solution)/shard_map/ppermute | solution.py:438
  409.2 29.0 %collective-permute-start.56 = (bf16[256,1536]{1,0:T(8,128)(2,1)S(1)}, bf16[256,1536]{1,0:T(8,128)(2,1)S(1)}, u32[]{:S(2)}, u32[]{:S(2)}) collective-permute-start(bf16[256,1536]{1,0:T(8,128)(2,1)S(1)} %fusion.20), channel_id=1, source_target_pairs={{0,1},{1,2},{2,3},{4,5},{5,6},{6,7},{8,9},{9,10},{10,11},{12,13},{... | collective-permute-start | bytes 2359304 | tf_op jit(solution)/shard_map/ppermute | solution.py:445
  418.6 19.6 %collective-permute-start.57 = (bf16[256,1536]{1,0:T(8,128)(2,1)S(1)}, bf16[256,1536]{1,0:T(8,128)(2,1)}, u32[]{:S(2)}, u32[]{:S(2)}) collective-permute-start(bf16[256,1536]{1,0:T(8,128)(2,1)S(1)} %fusion.20), channel_id=1, source_target_pairs={{3,2},{2,1},{1,0},{7,6},{6,5},{5,4},{11,10},{10,9},{9,8},{15,14},{... | collective-permute-start | bytes 2359304 | tf_op jit(solution)/shard_map/ppermute | solution.py:445
  423.0 12.6 %collective-permute-start.53 = (f32[1,1536]{1,0:T(1,128)S(1)}, f32[1,1536]{1,0:T(1,128)S(1)}, u32[]{:S(2)}, u32[]{:S(2)}) collective-permute-start(f32[1,1536]{1,0:T(1,128)S(1)} %broadcast_in_dim.61), channel_id=1, source_target_pairs={{0,1},{1,2},{2,3},{3,0},{4,5},{5,6},{6,7},{7,4},{8,9},{9,10},{10,1... | collective-permute-start | bytes 18440 | tf_op jit(solution)/shard_map/ppermute | solution.py:438
  425.7 12.5 %collective-permute-start.54 = (f32[1,1536]{1,0:T(1,128)S(1)}, f32[1,1536]{1,0:T(1,128)S(1)}, u32[]{:S(2)}, u32[]{:S(2)}) collective-permute-start(f32[1,1536]{1,0:T(1,128)S(1)} %broadcast_in_dim.61), channel_id=1, source_target_pairs={{0,2},{1,3},{2,0},{3,1},{4,6},{5,7},{6,4},{7,5},{8,10},{9,11},{10,... | collective-permute-start | bytes 18440 | tf_op jit(solution)/shard_map/ppermute | solution.py:438
  426.7 11.5 %collective-permute-start.55 = (f32[1,1536]{1,0:T(1,128)S(1)}, f32[1,1536]{1,0:T(1,128)S(1)}, u32[]{:S(2)}, u32[]{:S(2)}) collective-permute-start(f32[1,1536]{1,0:T(1,128)S(1)} %broadcast_in_dim.61), channel_id=1, source_target_pairs={{0,3},{1,0},{2,1},{3,2},{4,7},{5,4},{6,5},{7,6},{8,11},{9,8},{10,9... | collective-permute-start | bytes 18440 | tf_op jit(solution)/shard_map/ppermute | solution.py:438
  438.2 11.2 %collective-permute-start.61 = (bf16[256,1536]{1,0:T(8,128)(2,1)S(1)}, bf16[256,1536]{1,0:T(8,128)(2,1)S(1)}, u32[]{:S(2)}, u32[]{:S(2)}) collective-permute-start(bf16[256,1536]{1,0:T(8,128)(2,1)S(1)} %collective-permute-done.56), channel_id=1, source_target_pairs={{1,2},{2,3},{5,6},{6,7},{9,10},{10,11},{13,14},{14,15},{17,18},{18... | collective-permute-start | bytes 2359304 | tf_op jit(solution)/shard_map/ppermute | solution.py:445
  438.9 17.6 %collective-permute-start.62 = (bf16[256,1536]{1,0:T(8,128)(2,1)}, bf16[256,1536]{1,0:T(8,128)(2,1)S(1)}, u32[]{:S(2)}, u32[]{:S(2)}) collective-permute-start(bf16[256,1536]{1,0:T(8,128)(2,1)} %collective-permute-done.57), channel_id=1, source_target_pairs={{2,1},{1,0},{6,5},{5,4},{10,9},{9,8},{14,13},{13,12},{18,17},{17,1... | collective-permute-start | bytes 2359304 | tf_op jit(solution)/shard_map/ppermute | solution.py:445
  440.5 8.4 %collective-permute-start.58 = (bf16[64,1536]{1,0:T(8,128)(2,1)S(1)}, bf16[64,1536]{1,0:T(8,128)(2,1)S(1)}, u32[]{:S(2)}, u32[]{:S(2)}) collective-permute-start(bf16[64,1536]{1,0:T(8,128)(2,1)S(1)} %scatter.4), channel_id=1, source_target_pairs={{0,8},{4,12},{8,0},{12,4},{16,24},{20,28},{24,16},{28,20},{1,9},{5... | collective-permute-start | bytes 589832 | tf_op jit(solution)/shard_map/ppermute | solution.py:433
  441.6 7.8 %collective-permute-start.59 = (bf16[64,1536]{1,0:T(8,128)(2,1)S(1)}, bf16[64,1536]{1,0:T(8,128)(2,1)S(1)}, u32[]{:S(2)}, u32[]{:S(2)}) collective-permute-start(bf16[64,1536]{1,0:T(8,128)(2,1)S(1)} %scatter.4), channel_id=1, source_target_pairs={{0,16},{4,20},{8,24},{12,28},{16,0},{20,4},{24,8},{28,12},{1,17},{... | collective-permute-start | bytes 589832 | tf_op jit(solution)/shard_map/ppermute | solution.py:433
  461.1 22.1 %collective-permute-start.64 = (bf16[256,1536]{1,0:T(8,128)(2,1)}, bf16[256,1536]{1,0:T(8,128)(2,1)}, u32[]{:S(2)}, u32[]{:S(2)}) collective-permute-start(bf16[256,1536]{1,0:T(8,128)(2,1)} %get-tuple-element.453), channel_id=1, source_target_pairs={{2,3},{1,0},{6,7},{5,4},{10,11},{9,8},{14,15},{13,12},{18,19},{17,... | collective-permute-start | bytes 2359304 | tf_op jit(solution)/shard_map/ppermute | solution.py:453
  (75 other events, 693.7 us)
Sparse Core Ops, SparseCore 0:
  47.5 98.0 all-gather.1
  198.5 99.2 reduce-scatter.1
  370.3 63.3 all-reduce.6

commit v9 on v8

--- a/solution.py
+++ b/solution.py
@@ -607,7 +607,7 @@
         mixed, output_held, output_got, router, extra, extra_got = join(
             mixed, output_held, output_got, router, extra, extra_got
         )
-        near = gather_near(output_held, output_got)
+        (near,) = join(gather_near(output_held, output_got))
         far = swap(near, 1)
         extra_held, extra_got = gather_second(extra, extra_got)
     else:
@@ -645,7 +645,7 @@
         got, gates, router, order, extra_held, extra_got = join(
             got, gates, router, order, extra_held, extra_got
         )
-        extra_near = gather_near(extra_held, extra_got)
+        (extra_near,) = join(gather_near(extra_held, extra_got))
         extra_far = swap(extra_near, 1)
         held, got = gather_second(routed_in, got)
         held, got = join(held, got)

time: 500 us -> 502 us (level)
  other arithmetic: 55 us -> 63.1 us
  local copies, waits for them, and re-layouts: 52.5 us -> 47.3 us
    concatenate x1 -> x3, other arithmetic: 1.76 us -> 9.83 us  [gather_near(): return jnp.concatenate([held[0], got[0], held[1], got[1]], axis=0)]
    unnamed x155 -> x149, local copies, waits for them, and re-layouts: 19.6 us -> 15.4 us
where the time goes in v9:
time: 502 us; the launch traced here: 494 us
  waiting for transfers between devices  167 us (33%)
  Pallas kernels  95.7 us (19%)
  starting transfers between devices  94 us (19%)
  other arithmetic  63.1 us (13%)
  local copies, waits for them, and re-layouts  47.3 us (9%)
  between operations  15.6 us (3%)
  matrix products  11.6 us (2%)
    ppermute x35, waiting for transfers between devices, swap(): lax.ppermute(x, 'ep', [(i, i ^ bit) for i in range(lax.axis_size('ep'))])  70.5 us
    ppermute x15, waiting for transfers between devices, turn(): return lax.ppermute(x, 'tp', [(i, (i + by) % n) for i in range(n)])  55.1 us
    pallas_call x1, Pallas kernels, run_experts(): pl.pallas_call(functools.partial(expert_kernel, top=top, count=count), gr...  44.9 us
    ppermute x35, starting transfers between devices, swap(): lax.ppermute(x, 'ep', [(i, i ^ bit) for i in range(lax.axis_size('ep'))])  31 us
    ppermute x12, starting transfers between devices, step_both(): return (lax.ppermute(right, 'tp', pairs), lax.ppermute(left, 'tp', mirror))  28.4 us
    ppermute x15, starting transfers between devices, turn(): return lax.ppermute(x, 'tp', [(i, (i + by) % n) for i in range(n)])  25.6 us
    convert_element_type x11, other arithmetic, add(): return (a.astype(F32) + b.astype(F32)).astype(BF)  25.6 us
    pallas_call x1, Pallas kernels, attend_back(): pl.pallas_call(attend_back_kernel, in_specs=[SMEM] + [VMEM] * (9 + count)...  25.5 us
  transfers between devices with their start and end apart: 68, of which 29 were waited for; matrix products, arithmetic and copies ran while one was open for 20% of the time, Pallas kernels for 10%

profile of v9, /device:TPU:0, one launch (start us, length us, event | category | flops | bytes accessed | tf_op | source)
XLA Modules:
  0.0 494.1 jit_solution(17743043883745759507)
XLA Ops:
  8.5 5.1 %collective-permute-start = (bf16[48,1536]{1,0:T(8,128)(2,1)S(1)}, bf16[48,1536]{1,0:T(8,128)(2,1)}, u32[]{:S(2)}, u32[]{:S(2)}) collective-permute-start(bf16[48,1536]{1,0:T(8,128)(2,1)S(1)} %constant_dynamic-slice_fusion.2), channel_id=1, source_target_pairs={{0,3},{1,0},{2,1},{3,2},{4,7},{5,4},{6,5},{7,6},{8,11},{9,8},{10,9... | collective-permute-start | bytes 442376 | tf_op jit(solution)/shard_map/ppermute | solution.py:438
  24.1 18.5 %shard_map.239 = (bf16[256,384]{1,0:T(8,128)(2,1)S(1)}, bf16[256,384]{1,0:T(8,128)(2,1)S(1)}, bf16[256,384]{1,0:T(8,128)(2,1)S(1)}, bf16[256,384]{1,0:T(8,128)(2...) custom-call(s32[1]{0:T(128)} %bitcast.8.at_ref, ...), custom_call_target="tpu_custom_call" | custom-call | flops 23000000512 | tf_op jit(solution)/shard_map/pallas_call | solution.py:121
  47.7 2.5 collective-permute-start.5
  53.2 3.4 collective-permute-done.5
  56.6 1.9 collective-permute-done.6
  60.3 1.6 collective-permute-start.10
  61.9 1.5 collective-permute-start.11
  63.5 1.8 shard_map.240.router_ref
  65.2 17.8 %collective-permute-done.9 = bf16[256,384]{1,0:T(8,128)(2,1)S(1)} collective-permute-done((bf16[256,384]{1,0:T(8,128)(2,1)S(1)}, bf16[256,384]{1,0:T(8,128)(2,1)S(1)}, u32[]{:S(2)}, u32[]{:S(2)}) %collective-permute-start.9) | collective-permute-done | bytes 196640 | tf_op jit(solution)/shard_map/ppermute | solution.py:438
  88.4 1.6 collective-permute-start.15
  94.2 3.3 multiply_reduce_fusion.2
  100.4 9.8 %collective-permute-done.15 = bf16[256,1664]{1,0:T(8,128)(2,1)S(1)} collective-permute-done((bf16[256,1664]{1,0:T(8,128)(2,1)S(1)}, bf16[256,1664]{1,0:T(8,128)(2,1)S(1)}, u32[]{:S(2)}, u32[]{:S(2)}) %collective-permute-start.15) | collective-permute-done | bytes 852000 | tf_op jit(solution)/shard_map/ppermute | solution.py:433
  111.7 7.5 %collective-permute-done.13 = bf16[128,1536]{1,0:T(8,128)(2,1)S(1)} collective-permute-done((bf16[128,1536]{1,0:T(8,128)(2,1)S(1)}, bf16[128,1536]{1,0:T(8,128)(2,1)S(1)}, u32[]{:S(2)}, u32[]{:S(2)}) %collective-permute-start.13) | collective-permute-done | bytes 393248 | tf_op jit(solution)/shard_map/ppermute | solution.py:433
  121.5 6.8 %pad_maximum_fusion.extra_near_ref = bf16[1024,1664]{1,0:T(8,128)(2,1)} fusion(bf16[256,1664]{1,0:T(8,128)(2,1)S(1)} %collective-permute-done.16, bf16[256,1664]{1,0:T(8,128)(2,1)S(1)} %pad_maximum_fusion.4, bf16[256,1664]{1,0:T(8,128)(2,1)S(1)} %collective-permute-done.15, bf16[256,1664]{1,0:T(8,128)(2,1)S(1)} %pad_maximum_fusion.3), kind=kLoop, calls=%fused_computation.10 | loop fusion | flops 13631488 | bytes 6815744 | tf_op jit(solution)/shard_map/concatenate | solution.py:476
  128.3 9.9 %collective-permute-done.17 = bf16[256,1536]{1,0:T(8,128)(2,1)S(1)} collective-permute-done((bf16[256,1536]{1,0:T(8,128)(2,1)S(1)}, bf16[256,1536]{1,0:T(8,128)(2,1)S(1)}, u32[]{:S(2)}, u32[]{:S(2)}) %collective-permute-start.17) | collective-permute-done | bytes 786464 | tf_op jit(solution)/shard_map/ppermute | solution.py:433
  138.6 1.8 pad_maximum_fusion.1.near_ref
  140.3 5.4 %all-gather.2.cloned.1.call-done.parts_ref = bf16[1536,1536]{1,0:T(8,128)(2,1)} async-done(((bf16[384,1536]{1,0:T(8,128)(2,1)}), bf16[1536,1536]{1,0:T(8,128)(2,1)}) %all-gather.2.cloned.1.call-update) | async-done | bytes 4718608 | tf_op jit(solution)/shard_map/all_gather | solution.py:569
  146.3 44.9 %shard_map.241 = (bf16[1024,1536]{1,0:T(8,128)(2,1)}, bf16[1024,1536]{1,0:T(8,128)(2,1)}, bf16[1024,1664]{1,0:T(8,128)(2,1)}, bf16[512,1664]{1,0:T(8,128)(2,1)},...) custom-call(s32[2]{0:T(128)} %pad_add_fusion.order_ref, bf16[1024,1536]{1,0:T(8,128)(2,1)} %pad_maximum_fusion.1.near_ref, ...), custom_call_target="tpu_custom_call" | custom-call | flops 46000001024 | tf_op jit(solution)/shard_map/pallas_call | solution.py:360
  191.4 3.7 collective-permute-done.21
  195.1 3.0 add_convert_fusion.2
  201.9 1.6 shard_map.242
  203.5 17.0 %collective-permute-done.22 = bf16[256,1664]{1,0:T(8,128)(2,1)} collective-permute-done((bf16[256,1664]{1,0:T(8,128)(2,1)}, bf16[256,1664]{1,0:T(8,128)(2,1)}, u32[]{:S(2)}, u32[]{:S(2)}) %collective-permute-start.22) | collective-permute-done | bytes 852000 | tf_op jit(solution)/shard_map/ppermute | solution.py:433
  221.7 3.2 add_convert_fusion
  224.9 1.5 collective-permute-start.26
  227.2 4.1 add_convert_fusion.8
  233.2 4.5 collective-permute-done.26
  237.8 1.6 collective-permute-done.27
  241.6 1.7 fusion.44
  249.3 2.5 copy.44
  254.2 1.7 add_convert_fusion.7
  258.9 1.6 fusion.7
  260.6 22.6 %collective-permute-done.29.refs_2_ = bf16[256,384]{1,0:T(8,128)(2,1)S(1)} collective-permute-done((bf16[256,384]{1,0:T(8,128)(2,1)}, bf16[256,384]{1,0:T(8,128)(2,1)S(1)}, u32[]{:S(2)}, u32[]{:S(2)}) %collective-permute-start.29) | collective-permute-done | bytes 196640 | tf_op jit(solution)/shard_map/ppermute | solution.py:438
  283.9 2.1 collective-permute-start.35
  289.4 25.5 %shard_map.243 = (bf16[256,1536]{1,0:T(8,128)(2,1)S(1)}, bf16[256,1536]{1,0:T(8,128)(2,1)S(1)}, bf16[256,1536]{1,0:T(8,128)(2,1)S(1)}, bf16[256,1536]{1,0:T(8,12...) custom-call(s32[1]{0:T(128)} %bitcast.8.at_ref, bf16[6,1024,64]{2,1,0:T(8,128)(2,1)} %get-tuple-element.206.q_ref, ...), custom_call_target="tpu_custom_call" | custom-call | flops 23000000512 | tf_op jit(solution)/shard_map/pallas_call | solution.py:231
  316.7 5.8 %collective-permute-start.38 = (bf16[256,1536]{1,0:T(8,128)(2,1)}, bf16[256,1536]{1,0:T(8,128)(2,1)}, u32[]{:S(2)}, u32[]{:S(2)}) collective-permute-start(bf16[256,1536]{1,0:T(8,128)(2,1)} %get-tuple-element.316), channel_id=1, source_target_pairs={{0,1},{3,2},{4,5},{7,6},{8,9},{11,10},{12,13},{15,14},{16,17},{19,... | collective-permute-start | bytes 2359304 | tf_op jit(solution)/shard_map/ppermute | solution.py:453
  324.5 4.2 fusion.33
  333.6 1.7 convert_element_type.505
  335.3 4.3 convolution_convert_fusion.1
  339.6 7.3 %collective-permute-done.41 = bf16[208,1536]{1,0:T(8,128)(2,1)} collective-permute-done((bf16[208,1536]{1,0:T(8,128)(2,1)}, bf16[208,1536]{1,0:T(8,128)(2,1)}, u32[]{:S(2)}, u32[]{:S(2)}) %collective-permute-start.41) | collective-permute-done | bytes 639008 | tf_op jit(solution)/shard_map/ppermute | solution.py:433
  348.0 2.6 fusion.15
  350.6 5.3 %collective-permute-start.43 = (bf16[256,1536]{1,0:T(8,128)(2,1)}, bf16[256,1536]{1,0:T(8,128)(2,1)}, u32[]{:S(2)}, u32[]{:S(2)}) collective-permute-start(bf16[256,1536]{1,0:T(8,128)(2,1)} %get-tuple-element.447), channel_id=1, source_target_pairs={{0,1},{1,2},{4,5},{5,6},{8,9},{9,10},{12,13},{13,14},{16,17},{17,1... | collective-permute-start | bytes 2359304 | tf_op jit(solution)/shard_map/ppermute | solution.py:445
  355.9 1.6 collective-permute-start.44
  357.5 2.1 broadcast_select_fusion.1
  371.4 1.9 collective-permute-done.47
  373.3 6.1 %collective-permute-done.45 = bf16[256,1536]{1,0:T(8,128)(2,1)} collective-permute-done((bf16[256,1536]{1,0:T(8,128)(2,1)}, bf16[256,1536]{1,0:T(8,128)(2,1)}, u32[]{:S(2)}, u32[]{:S(2)}) %collective-permute-start.45) | collective-permute-done | bytes 786464 | tf_op jit(solution)/shard_map/ppermute | solution.py:453
  381.9 2.0 collective-permute-start.51
  387.7 6.7 %collective-permute-start.48 = (bf16[56,1536]{1,0:T(8,128)(2,1)S(1)}, bf16[56,1536]{1,0:T(8,128)(2,1)S(1)}, u32[]{:S(2)}, u32[]{:S(2)}) collective-permute-start(bf16[56,1536]{1,0:T(8,128)(2,1)S(1)} %get-tuple-element.464), channel_id=1, source_target_pairs={{0,3},{1,0},{2,1},{3,2},{4,7},{5,4},{6,5},{7,6},{8,11},{9,8},{10,9... | collective-permute-start | bytes 516104 | tf_op jit(solution)/shard_map/ppermute | solution.py:438
  395.0 6.6 %collective-permute-done.51 = bf16[256,1536]{1,0:T(8,128)(2,1)S(1)} collective-permute-done((bf16[256,1536]{1,0:T(8,128)(2,1)S(1)}, bf16[256,1536]{1,0:T(8,128)(2,1)S(1)}, u32[]{:S(2)}, u32[]{:S(2)}) %collective-permute-start.51) | collective-permute-done | bytes 786464 | tf_op jit(solution)/shard_map/ppermute | solution.py:445
  401.6 4.5 collective-permute-done.52
  406.9 2.2 fusion.20
  409.2 9.4 %collective-permute-start.56 = (bf16[256,1536]{1,0:T(8,128)(2,1)S(1)}, bf16[256,1536]{1,0:T(8,128)(2,1)S(1)}, u32[]{:S(2)}, u32[]{:S(2)}) collective-permute-start(bf16[256,1536]{1,0:T(8,128)(2,1)S(1)} %fusion.20), channel_id=1, source_target_pairs={{0,1},{1,2},{2,3},{4,5},{5,6},{6,7},{8,9},{9,10},{10,11},{12,13},{... | collective-permute-start | bytes 2359304 | tf_op jit(solution)/shard_map/ppermute | solution.py:445
  422.9 2.7 collective-permute-start.53
  426.6 2.0 collective-permute-start.55
  428.7 6.8 %collective-permute-done.53 = f32[1,1536]{1,0:T(1,128)S(1)} collective-permute-done((f32[1,1536]{1,0:T(1,128)S(1)}, f32[1,1536]{1,0:T(1,128)S(1)}, u32[]{:S(2)}, u32[]{:S(2)}) %collective-permute-start.53) | collective-permute-done | bytes 6176 | tf_op jit(solution)/shard_map/ppermute | solution.py:438
  435.5 2.6 collective-permute-done.54
  442.5 1.5 collective-permute-start.60
  444.0 1.9 broadcast.86.clone
  446.8 2.1 constant_dynamic-update-slice_fusion.1
  449.4 7.0 %collective-permute-done.62 = bf16[256,1536]{1,0:T(8,128)(2,1)S(1)} collective-permute-done((bf16[256,1536]{1,0:T(8,128)(2,1)}, bf16[256,1536]{1,0:T(8,128)(2,1)S(1)}, u32[]{:S(2)}, u32[]{:S(2)}) %collective-permute-start.62) | collective-permute-done | bytes 786464 | tf_op jit(solution)/shard_map/ppermute | solution.py:445
  458.4 2.6 constant_dynamic-update-slice_fusion.11
  464.6 2.1 shard_map.244
  466.8 3.0 slice.442
  471.7 11.4 %collective-permute-done.64 = bf16[256,1536]{1,0:T(8,128)(2,1)} collective-permute-done((bf16[256,1536]{1,0:T(8,128)(2,1)}, bf16[256,1536]{1,0:T(8,128)(2,1)}, u32[]{:S(2)}, u32[]{:S(2)}) %collective-permute-start.64) | collective-permute-done | bytes 786464 | tf_op jit(solution)/shard_map/ppermute | solution.py:453
  484.4 2.1 constant_dynamic-update-slice_fusion.10
  (379 shorter events, 113.4 us)
Async XLA Ops:
  7.2 138.5 %all-gather.2.cloned.1.call-start = ((), (), s32[]{:S(2)}) async-start(), calls=%async_computation.1 | async-start | bytes 5898240 | tf_op jit(solution)/shard_map/all_gather | solution.py:569
  8.5 35.7 %collective-permute-start = (bf16[48,1536]{1,0:T(8,128)(2,1)S(1)}, bf16[48,1536]{1,0:T(8,128)(2,1)}, u32[]{:S(2)}, u32[]{:S(2)}) collective-permute-start(bf16[48,1536]{1,0:T(8,128)(2,1)S(1)} %constant_dynamic-slice_fusion.2), channel_id=1, source_target_pairs={{0,3},{1,0},{2,1},{3,2},{4,7},{5,4},{6,5},{7,6},{8,11},{9,8},{10,9... | collective-permute-start | bytes 442376 | tf_op jit(solution)/shard_map/ppermute | solution.py:438
  13.6 30.6 %collective-permute-start.1 = (bf16[48,1536]{1,0:T(8,128)(2,1)S(1)}, bf16[48,1536]{1,0:T(8,128)(2,1)}, u32[]{:S(2)}, u32[]{:S(2)}) collective-permute-start(bf16[48,1536]{1,0:T(8,128)(2,1)S(1)} %constant_dynamic-slice_fusion.2), channel_id=1, source_target_pairs={{0,2},{1,3},{2,0},{3,1},{4,6},{5,7},{6,4},{7,5},{8,10},{9,11},{10,... | collective-permute-start | bytes 442376 | tf_op jit(solution)/shard_map/ppermute | solution.py:438
  13.6 30.6 %collective-permute-start.2 = (bf16[48,1536]{1,0:T(8,128)(2,1)S(1)}, bf16[48,1536]{1,0:T(8,128)(2,1)}, u32[]{:S(2)}, u32[]{:S(2)}) collective-permute-start(bf16[48,1536]{1,0:T(8,128)(2,1)S(1)} %constant_dynamic-slice_fusion.2), channel_id=1, source_target_pairs={{0,1},{1,2},{2,3},{3,0},{4,5},{5,6},{6,7},{7,4},{8,9},{9,10},{10,1... | collective-permute-start | bytes 442376 | tf_op jit(solution)/shard_map/ppermute | solution.py:438
  17.9 26.3 %collective-permute-start.3 = (bf16[128,1664]{1,0:T(8,128)(2,1)}, bf16[128,1664]{1,0:T(8,128)(2,1)}, u32[]{:S(2)}, u32[]{:S(2)}) collective-permute-start(bf16[128,1664]{1,0:T(8,128)(2,1)} %get-tuple-element.451), channel_id=1, source_target_pairs={{0,8},{4,12},{8,0},{12,4},{16,24},{20,28},{24,16},{28,20},{1,9},{5... | collective-permute-start | bytes 1277960 | tf_op jit(solution)/shard_map/ppermute | solution.py:433
  19.4 24.8 %collective-permute-start.4 = (bf16[128,1664]{1,0:T(8,128)(2,1)}, bf16[128,1664]{1,0:T(8,128)(2,1)}, u32[]{:S(2)}, u32[]{:S(2)}) collective-permute-start(bf16[128,1664]{1,0:T(8,128)(2,1)} %get-tuple-element.450), channel_id=1, source_target_pairs={{0,16},{4,20},{8,24},{12,28},{16,0},{20,4},{24,8},{28,12},{1,17},{... | collective-permute-start | bytes 1277960 | tf_op jit(solution)/shard_map/ppermute | solution.py:433
  45.2 13.4 %collective-permute-start.7 = (bf16[96,1536]{1,0:T(8,128)(2,1)S(1)}, bf16[96,1536]{1,0:T(8,128)(2,1)S(1)}, u32[]{:S(2)}, u32[]{:S(2)}) collective-permute-start(bf16[96,1536]{1,0:T(8,128)(2,1)S(1)} %pad_maximum_fusion.12), channel_id=1, source_target_pairs={{0,8},{4,12},{8,0},{12,4},{16,24},{20,28},{24,16},{28,20},{1,9},{5... | collective-permute-start | bytes 884744 | tf_op jit(solution)/shard_map/ppermute | solution.py:433
  46.8 11.7 %collective-permute-start.8 = (bf16[96,1536]{1,0:T(8,128)(2,1)S(1)}, bf16[96,1536]{1,0:T(8,128)(2,1)S(1)}, u32[]{:S(2)}, u32[]{:S(2)}) collective-permute-start(bf16[96,1536]{1,0:T(8,128)(2,1)S(1)} %pad_maximum_fusion.13), channel_id=1, source_target_pairs={{0,16},{4,20},{8,24},{12,28},{16,0},{20,4},{24,8},{28,12},{1,17},{... | collective-permute-start | bytes 884744 | tf_op jit(solution)/shard_map/ppermute | solution.py:433
  47.4 269.3 %reduce-scatter.2.cloned.1.call-start = ((), (), s32[]{:S(2)}) async-start(), calls=%async_computation.2 | async-start | bytes 5898240 | tf_op jit(solution)/shard_map/reduce_scatter | solution.py:660
  47.7 8.9 %collective-permute-start.5 = (bf16[256,384]{1,0:T(8,128)(2,1)S(1)}, bf16[256,384]{1,0:T(8,128)(2,1)}, u32[]{:S(2)}, u32[]{:S(2)}) collective-permute-start(bf16[256,384]{1,0:T(8,128)(2,1)S(1)} %get-tuple-element.214), channel_id=1, source_target_pairs={{0,1},{1,2},{2,3},{3,0},{4,5},{5,6},{6,7},{7,4},{8,9},{9,10},{10,1... | collective-permute-start | bytes 589832 | tf_op jit(solution)/shard_map/ppermute | solution.py:438
  50.2 8.3 %collective-permute-start.6 = (bf16[256,384]{1,0:T(8,128)(2,1)S(1)}, bf16[256,384]{1,0:T(8,128)(2,1)}, u32[]{:S(2)}, u32[]{:S(2)}) collective-permute-start(bf16[256,384]{1,0:T(8,128)(2,1)S(1)} %get-tuple-element.215), channel_id=1, source_target_pairs={{0,3},{1,0},{2,1},{3,2},{4,7},{5,4},{6,5},{7,6},{8,11},{9,8},{10,9... | collective-permute-start | bytes 589832 | tf_op jit(solution)/shard_map/ppermute | solution.py:438
  58.5 24.5 %collective-permute-start.9 = (bf16[256,384]{1,0:T(8,128)(2,1)S(1)}, bf16[256,384]{1,0:T(8,128)(2,1)S(1)}, u32[]{:S(2)}, u32[]{:S(2)}) collective-permute-start(bf16[256,384]{1,0:T(8,128)(2,1)S(1)} %get-tuple-element.224), channel_id=1, source_target_pairs={{0,2},{1,3},{2,0},{3,1},{4,6},{5,7},{6,4},{7,5},{8,10},{9,11},{10,... | collective-permute-start | bytes 589832 | tf_op jit(solution)/shard_map/ppermute | solution.py:438
  60.3 22.7 %collective-permute-start.10 = (bf16[192,1536]{1,0:T(8,128)(2,1)S(1)}, bf16[192,1536]{1,0:T(8,128)(2,1)S(1)}, u32[]{:S(2)}, u32[]{:S(2)}) collective-permute-start(bf16[192,1536]{1,0:T(8,128)(2,1)S(1)} %get-tuple-element.237), channel_id=1, source_target_pairs={{0,16},{4,20},{8,24},{12,28},{16,0},{20,4},{24,8},{28,12},{1,17},{... | collective-permute-start | bytes 1769480 | tf_op jit(solution)/shard_map/ppermute | solution.py:433
  61.9 21.1 %collective-permute-start.11 = (bf16[192,1536]{1,0:T(8,128)(2,1)S(1)}, bf16[192,1536]{1,0:T(8,128)(2,1)}, u32[]{:S(2)}, u32[]{:S(2)}) collective-permute-start(bf16[192,1536]{1,0:T(8,128)(2,1)S(1)} %get-tuple-element.239), channel_id=1, source_target_pairs={{0,8},{4,12},{8,0},{12,4},{16,24},{20,28},{24,16},{28,20},{1,9},{5... | collective-permute-start | bytes 1769480 | tf_op jit(solution)/shard_map/ppermute | solution.py:433
  84.2 9.3 %collective-permute-start.12 = (bf16[768,1536]{1,0:T(8,128)(2,1)S(1)}, bf16[768,1536]{1,0:T(8,128)(2,1)S(1)}, u32[]{:S(2)}, u32[]{:S(2)}) collective-permute-start(bf16[768,1536]{1,0:T(8,128)(2,1)S(1)} %pad_maximum_fusion.2), channel_id=1, source_target_pairs={{0,4},{4,0},{8,12},{12,8},{16,20},{20,16},{24,28},{28,24},{1,5},{5... | collective-permute-start | bytes 7077896 | tf_op jit(solution)/shard_map/ppermute | solution.py:433
  88.4 21.8 %collective-permute-start.15 = (bf16[256,1664]{1,0:T(8,128)(2,1)S(1)}, bf16[256,1664]{1,0:T(8,128)(2,1)S(1)}, u32[]{:S(2)}, u32[]{:S(2)}) collective-permute-start(bf16[256,1664]{1,0:T(8,128)(2,1)S(1)} %pad_maximum_fusion.3), channel_id=1, source_target_pairs={{0,16},{4,20},{8,24},{12,28},{16,0},{20,4},{24,8},{28,12},{1,17},{... | collective-permute-start | bytes 2555912 | tf_op jit(solution)/shard_map/ppermute | solution.py:433
  89.9 21.8 %collective-permute-start.16 = (bf16[256,1664]{1,0:T(8,128)(2,1)S(1)}, bf16[256,1664]{1,0:T(8,128)(2,1)S(1)}, u32[]{:S(2)}, u32[]{:S(2)}) collective-permute-start(bf16[256,1664]{1,0:T(8,128)(2,1)S(1)} %pad_maximum_fusion.4), channel_id=1, source_target_pairs={{0,8},{4,12},{8,0},{12,4},{16,24},{20,28},{24,16},{28,20},{1,9},{5... | collective-permute-start | bytes 2555912 | tf_op jit(solution)/shard_map/ppermute | solution.py:433
  97.8 21.5 %collective-permute-start.13 = (bf16[128,1536]{1,0:T(8,128)(2,1)S(1)}, bf16[128,1536]{1,0:T(8,128)(2,1)S(1)}, u32[]{:S(2)}, u32[]{:S(2)}) collective-permute-start(bf16[128,1536]{1,0:T(8,128)(2,1)S(1)} %get-tuple-element.459), channel_id=1, source_target_pairs={{0,8},{4,12},{8,0},{12,4},{16,24},{20,28},{24,16},{28,20},{1,9},{5... | collective-permute-start | bytes 1179656 | tf_op jit(solution)/shard_map/ppermute | solution.py:433
  98.4 20.8 %collective-permute-start.14 = (bf16[128,1536]{1,0:T(8,128)(2,1)S(1)}, bf16[128,1536]{1,0:T(8,128)(2,1)S(1)}, u32[]{:S(2)}, u32[]{:S(2)}) collective-permute-start(bf16[128,1536]{1,0:T(8,128)(2,1)S(1)} %get-tuple-element.458), channel_id=1, source_target_pairs={{0,16},{4,20},{8,24},{12,28},{16,0},{20,4},{24,8},{28,12},{1,17},{... | collective-permute-start | bytes 1179656 | tf_op jit(solution)/shard_map/ppermute | solution.py:433
  119.4 18.8 %collective-permute-start.17 = (bf16[256,1536]{1,0:T(8,128)(2,1)S(1)}, bf16[256,1536]{1,0:T(8,128)(2,1)S(1)}, u32[]{:S(2)}, u32[]{:S(2)}) collective-permute-start(bf16[256,1536]{1,0:T(8,128)(2,1)S(1)} %pad_maximum_fusion.5), channel_id=1, source_target_pairs={{0,16},{4,20},{8,24},{12,28},{16,0},{20,4},{24,8},{28,12},{1,17},{... | collective-permute-start | bytes 2359304 | tf_op jit(solution)/shard_map/ppermute | solution.py:433
  120.0 18.6 %collective-permute-start.18 = (bf16[256,1536]{1,0:T(8,128)(2,1)S(1)}, bf16[256,1536]{1,0:T(8,128)(2,1)S(1)}, u32[]{:S(2)}, u32[]{:S(2)}) collective-permute-start(bf16[256,1536]{1,0:T(8,128)(2,1)S(1)} %pad_maximum_fusion.6), channel_id=1, source_target_pairs={{0,8},{4,12},{8,0},{12,4},{16,24},{20,28},{24,16},{28,20},{1,9},{5... | collective-permute-start | bytes 2359304 | tf_op jit(solution)/shard_map/ppermute | solution.py:433
  128.3 17.4 %collective-permute-start.20 = (bf16[1024,1664]{1,0:T(8,128)(2,1)}, bf16[1024,1664]{1,0:T(8,128)(2,1)}, u32[]{:S(2)}, u32[]{:S(2)}) collective-permute-start(bf16[1024,1664]{1,0:T(8,128)(2,1)} %pad_maximum_fusion.extra_near_ref), channel_id=1, source_target_pairs={{0,4},{4,0},{8,12},{12,8},{16,20},{20,16},{24,28},{28,24},{1,5},{5... | collective-permute-start | bytes 10223624 | tf_op jit(solution)/shard_map/ppermute | solution.py:433
  198.1 23.6 %collective-permute-start.24 = (bf16[1024,1536]{1,0:T(8,128)(2,1)}, bf16[1024,1536]{1,0:T(8,128)(2,1)}, u32[]{:S(2)}, u32[]{:S(2)}) collective-permute-start(bf16[1024,1536]{1,0:T(8,128)(2,1)} %get-tuple-element.268), channel_id=1, source_target_pairs={{0,4},{4,0},{8,12},{12,8},{16,20},{20,16},{24,28},{28,24},{1,5},{5... | collective-permute-start | bytes 9437192 | tf_op jit(solution)/shard_map/ppermute | solution.py:433
  198.4 266.2 %all-reduce.7.cloned.1.call-start = ((), (), s32[]{:S(2)}) async-start(), calls=%async_computation.3 | async-start | bytes 3932160 | tf_op jit(solution)/shard_map/psum | solution.py:768
  198.9 21.6 %collective-permute-start.22 = (bf16[256,1664]{1,0:T(8,128)(2,1)}, bf16[256,1664]{1,0:T(8,128)(2,1)}, u32[]{:S(2)}, u32[]{:S(2)}) collective-permute-start(bf16[256,1664]{1,0:T(8,128)(2,1)} %get-tuple-element.263), channel_id=1, source_target_pairs={{0,16},{4,20},{8,24},{12,28},{16,0},{20,4},{24,8},{28,12},{1,17},{... | collective-permute-start | bytes 2555912 | tf_op jit(solution)/shard_map/ppermute | solution.py:433
  200.4 21.2 %collective-permute-start.23 = (bf16[256,1664]{1,0:T(8,128)(2,1)}, bf16[256,1664]{1,0:T(8,128)(2,1)}, u32[]{:S(2)}, u32[]{:S(2)}) collective-permute-start(bf16[256,1664]{1,0:T(8,128)(2,1)} %get-tuple-element.264), channel_id=1, source_target_pairs={{0,8},{4,12},{8,0},{12,4},{16,24},{20,28},{24,16},{28,20},{1,9},{5... | collective-permute-start | bytes 2555912 | tf_op jit(solution)/shard_map/ppermute | solution.py:433
  201.9 19.8 %collective-permute-start.25 = (bf16[512,1664]{1,0:T(8,128)(2,1)}, bf16[512,1664]{1,0:T(8,128)(2,1)}, u32[]{:S(2)}, u32[]{:S(2)}) collective-permute-start(bf16[512,1664]{1,0:T(8,128)(2,1)} %get-tuple-element.269), channel_id=1, source_target_pairs={{0,4},{4,0},{8,12},{12,8},{16,20},{20,16},{24,28},{28,24},{1,5},{5... | collective-permute-start | bytes 5111816 | tf_op jit(solution)/shard_map/ppermute | solution.py:433
  224.9 12.8 %collective-permute-start.26 = (bf16[128,1664]{1,0:T(8,128)(2,1)S(1)}, bf16[128,1664]{1,0:T(8,128)(2,1)S(1)}, u32[]{:S(2)}, u32[]{:S(2)}) collective-permute-start(bf16[128,1664]{1,0:T(8,128)(2,1)S(1)} %slice.347), channel_id=1, source_target_pairs={{0,8},{4,12},{8,0},{12,4},{16,24},{20,28},{24,16},{28,20},{1,9},{5... | collective-permute-start | bytes 1277960 | tf_op jit(solution)/shard_map/ppermute | solution.py:433
  226.5 12.8 %collective-permute-start.27 = (bf16[128,1664]{1,0:T(8,128)(2,1)S(1)}, bf16[128,1664]{1,0:T(8,128)(2,1)S(1)}, u32[]{:S(2)}, u32[]{:S(2)}) collective-permute-start(bf16[128,1664]{1,0:T(8,128)(2,1)S(1)} %slice.348), channel_id=1, source_target_pairs={{0,16},{4,20},{8,24},{12,28},{16,0},{20,4},{24,8},{28,12},{1,17},{... | collective-permute-start | bytes 1277960 | tf_op jit(solution)/shard_map/ppermute | solution.py:433
  231.2 23.0 %collective-permute-start.31 = (bf16[256,1536]{1,0:T(8,128)(2,1)}, bf16[256,1536]{1,0:T(8,128)(2,1)}, u32[]{:S(2)}, u32[]{:S(2)}) collective-permute-start(bf16[256,1536]{1,0:T(8,128)(2,1)} %get-tuple-element.288), channel_id=1, source_target_pairs={{0,16},{4,20},{8,24},{12,28},{16,0},{20,4},{24,8},{28,12},{1,17},{... | collective-permute-start | bytes 2359304 | tf_op jit(solution)/shard_map/ppermute | solution.py:433
  232.7 23.3 %collective-permute-start.32 = (bf16[256,1536]{1,0:T(8,128)(2,1)}, bf16[256,1536]{1,0:T(8,128)(2,1)}, u32[]{:S(2)}, u32[]{:S(2)}) collective-permute-start(bf16[256,1536]{1,0:T(8,128)(2,1)} %get-tuple-element.290), channel_id=1, source_target_pairs={{0,8},{4,12},{8,0},{12,4},{16,24},{20,28},{24,16},{28,20},{1,9},{5... | collective-permute-start | bytes 2359304 | tf_op jit(solution)/shard_map/ppermute | solution.py:433
  245.6 15.0 %collective-permute-start.28 = (bf16[256,384]{1,0:T(8,128)(2,1)}, bf16[256,384]{1,0:T(8,128)(2,1)S(1)}, u32[]{:S(2)}, u32[]{:S(2)}) collective-permute-start(bf16[256,384]{1,0:T(8,128)(2,1)} %get-tuple-element.282), channel_id=1, source_target_pairs={{0,3},{1,0},{2,1},{3,2},{4,7},{5,4},{6,5},{7,6},{8,11},{9,8},{10,9... | collective-permute-start | bytes 589832 | tf_op jit(solution)/shard_map/ppermute | solution.py:438
  246.4 36.7 %collective-permute-start.29 = (bf16[256,384]{1,0:T(8,128)(2,1)}, bf16[256,384]{1,0:T(8,128)(2,1)S(1)}, u32[]{:S(2)}, u32[]{:S(2)}) collective-permute-start(bf16[256,384]{1,0:T(8,128)(2,1)} %get-tuple-element.283), channel_id=1, source_target_pairs={{0,2},{1,3},{2,0},{3,1},{4,6},{5,7},{6,4},{7,5},{8,10},{9,11},{10,... | collective-permute-start | bytes 589832 | tf_op jit(solution)/shard_map/ppermute | solution.py:438
  246.4 36.7 %collective-permute-start.30 = (bf16[256,384]{1,0:T(8,128)(2,1)}, bf16[256,384]{1,0:T(8,128)(2,1)S(1)}, u32[]{:S(2)}, u32[]{:S(2)}) collective-permute-start(bf16[256,384]{1,0:T(8,128)(2,1)} %get-tuple-element.284), channel_id=1, source_target_pairs={{0,1},{1,2},{2,3},{3,0},{4,5},{5,6},{6,7},{7,4},{8,9},{9,10},{10,1... | collective-permute-start | bytes 589832 | tf_op jit(solution)/shard_map/ppermute | solution.py:438
  257.5 25.7 %collective-permute-start.33 = (bf16[128,1536]{1,0:T(8,128)(2,1)S(1)}, bf16[128,1536]{1,0:T(8,128)(2,1)S(1)}, u32[]{:S(2)}, u32[]{:S(2)}) collective-permute-start(bf16[128,1536]{1,0:T(8,128)(2,1)S(1)} %slice.366), channel_id=1, source_target_pairs={{0,8},{4,12},{8,0},{12,4},{16,24},{20,28},{24,16},{28,20},{1,9},{5... | collective-permute-start | bytes 1179656 | tf_op jit(solution)/shard_map/ppermute | solution.py:433
  258.1 25.0 %collective-permute-start.34 = (bf16[128,1536]{1,0:T(8,128)(2,1)S(1)}, bf16[128,1536]{1,0:T(8,128)(2,1)S(1)}, u32[]{:S(2)}, u32[]{:S(2)}) collective-permute-start(bf16[128,1536]{1,0:T(8,128)(2,1)S(1)} %slice.367), channel_id=1, source_target_pairs={{0,16},{4,20},{8,24},{12,28},{16,0},{20,4},{24,8},{28,12},{1,17},{... | collective-permute-start | bytes 1179656 | tf_op jit(solution)/shard_map/ppermute | solution.py:433
  283.1 33.5 %collective-permute-start.37 = (bf16[4,208,1536]{2,1,0:T(8,128)(2,1)S(1)}, bf16[4,208,1536]{2,1,0:T(8,128)(2,1)}, u32[]{:S(2)}, u32[]{:S(2)}) collective-permute-start(bf16[4,208,1536]{2,1,0:T(8,128)(2,1)S(1)} %get-tuple-element.313), channel_id=1, source_target_pairs={{0,4},{4,0},{8,12},{12,8},{16,20},{20,16},{24,28},{28,24},{1,5},{5... | collective-permute-start | bytes 7667720 | tf_op jit(solution)/shard_map/ppermute | solution.py:433
  283.9 31.0 %collective-permute-start.35 = (bf16[256,1536]{1,0:T(8,128)(2,1)S(1)}, bf16[256,1536]{1,0:T(8,128)(2,1)S(1)}, u32[]{:S(2)}, u32[]{:S(2)}) collective-permute-start(bf16[256,1536]{1,0:T(8,128)(2,1)S(1)} %fusion.24), channel_id=1, source_target_pairs={{0,1},{1,2},{2,3},{4,5},{5,6},{6,7},{8,9},{9,10},{10,11},{12,13},{... | collective-permute-start | bytes 2359304 | tf_op jit(solution)/shard_map/ppermute | solution.py:445
  286.0 28.9 %collective-permute-start.36 = (bf16[256,1536]{1,0:T(8,128)(2,1)S(1)}, bf16[256,1536]{1,0:T(8,128)(2,1)S(1)}, u32[]{:S(2)}, u32[]{:S(2)}) collective-permute-start(bf16[256,1536]{1,0:T(8,128)(2,1)S(1)} %fusion.24), channel_id=1, source_target_pairs={{3,2},{2,1},{1,0},{7,6},{6,5},{5,4},{11,10},{10,9},{9,8},{15,14},{... | collective-permute-start | bytes 2359304 | tf_op jit(solution)/shard_map/ppermute | solution.py:445
  316.7 31.3 %collective-permute-start.38 = (bf16[256,1536]{1,0:T(8,128)(2,1)}, bf16[256,1536]{1,0:T(8,128)(2,1)}, u32[]{:S(2)}, u32[]{:S(2)}) collective-permute-start(bf16[256,1536]{1,0:T(8,128)(2,1)} %get-tuple-element.316), channel_id=1, source_target_pairs={{0,1},{3,2},{4,5},{7,6},{8,9},{11,10},{12,13},{15,14},{16,17},{19,... | collective-permute-start | bytes 2359304 | tf_op jit(solution)/shard_map/ppermute | solution.py:453
  322.4 25.6 %collective-permute-start.39 = (bf16[256,1536]{1,0:T(8,128)(2,1)}, bf16[256,1536]{1,0:T(8,128)(2,1)S(1)}, u32[]{:S(2)}, u32[]{:S(2)}) collective-permute-start(bf16[256,1536]{1,0:T(8,128)(2,1)} %copy-done.55), channel_id=1, source_target_pairs={{1,2},{2,3},{5,6},{6,7},{9,10},{10,11},{13,14},{14,15},{17,18},{18... | collective-permute-start | bytes 2359304 | tf_op jit(solution)/shard_map/ppermute | solution.py:445
  323.2 24.8 %collective-permute-start.40 = (bf16[256,1536]{1,0:T(8,128)(2,1)}, bf16[256,1536]{1,0:T(8,128)(2,1)}, u32[]{:S(2)}, u32[]{:S(2)}) collective-permute-start(bf16[256,1536]{1,0:T(8,128)(2,1)} %copy-done.57), channel_id=1, source_target_pairs={{2,1},{1,0},{6,5},{5,4},{10,9},{9,8},{14,13},{13,12},{18,17},{17,1... | collective-permute-start | bytes 2359304 | tf_op jit(solution)/shard_map/ppermute | solution.py:445
  330.4 16.5 %collective-permute-start.41 = (bf16[208,1536]{1,0:T(8,128)(2,1)}, bf16[208,1536]{1,0:T(8,128)(2,1)}, u32[]{:S(2)}, u32[]{:S(2)}) collective-permute-start(bf16[208,1536]{1,0:T(8,128)(2,1)} %pad_maximum_fusion.8), channel_id=1, source_target_pairs={{0,16},{4,20},{8,24},{12,28},{16,0},{20,4},{24,8},{28,12},{1,17},{... | collective-permute-start | bytes 1916936 | tf_op jit(solution)/shard_map/ppermute | solution.py:433
  331.7 16.3 %collective-permute-start.42 = (bf16[208,1536]{1,0:T(8,128)(2,1)}, bf16[208,1536]{1,0:T(8,128)(2,1)}, u32[]{:S(2)}, u32[]{:S(2)}) collective-permute-start(bf16[208,1536]{1,0:T(8,128)(2,1)} %pad_maximum_fusion.9), channel_id=1, source_target_pairs={{0,8},{4,12},{8,0},{12,4},{16,24},{20,28},{24,16},{28,20},{1,9},{5... | collective-permute-start | bytes 1916936 | tf_op jit(solution)/shard_map/ppermute | solution.py:433
  350.6 22.6 %collective-permute-start.43 = (bf16[256,1536]{1,0:T(8,128)(2,1)}, bf16[256,1536]{1,0:T(8,128)(2,1)}, u32[]{:S(2)}, u32[]{:S(2)}) collective-permute-start(bf16[256,1536]{1,0:T(8,128)(2,1)} %get-tuple-element.447), channel_id=1, source_target_pairs={{0,1},{1,2},{4,5},{5,6},{8,9},{9,10},{12,13},{13,14},{16,17},{17,1... | collective-permute-start | bytes 2359304 | tf_op jit(solution)/shard_map/ppermute | solution.py:445
  355.9 17.3 %collective-permute-start.44 = (bf16[256,1536]{1,0:T(8,128)(2,1)}, bf16[256,1536]{1,0:T(8,128)(2,1)}, u32[]{:S(2)}, u32[]{:S(2)}) collective-permute-start(bf16[256,1536]{1,0:T(8,128)(2,1)} %get-tuple-element.446), channel_id=1, source_target_pairs={{3,2},{2,1},{7,6},{6,5},{11,10},{10,9},{15,14},{14,13},{19,18},{18... | collective-permute-start | bytes 2359304 | tf_op jit(solution)/shard_map/ppermute | solution.py:445
  359.6 19.8 %collective-permute-start.45 = (bf16[256,1536]{1,0:T(8,128)(2,1)}, bf16[256,1536]{1,0:T(8,128)(2,1)}, u32[]{:S(2)}, u32[]{:S(2)}) collective-permute-start(bf16[256,1536]{1,0:T(8,128)(2,1)} %broadcast_select_fusion.1), channel_id=1, source_target_pairs={{2,3},{1,0},{6,7},{5,4},{10,11},{9,8},{14,15},{13,12},{18,19},{17,... | collective-permute-start | bytes 2359304 | tf_op jit(solution)/shard_map/ppermute | solution.py:453
  363.6 7.8 %collective-permute-start.46 = (bf16[104,1536]{1,0:T(8,128)(2,1)S(1)}, bf16[104,1536]{1,0:T(8,128)(2,1)}, u32[]{:S(2)}, u32[]{:S(2)}) collective-permute-start(bf16[104,1536]{1,0:T(8,128)(2,1)S(1)} %slice.370), channel_id=1, source_target_pairs={{0,8},{4,12},{8,0},{12,4},{16,24},{20,28},{24,16},{28,20},{1,9},{5... | collective-permute-start | bytes 958472 | tf_op jit(solution)/shard_map/ppermute | solution.py:433
  365.6 7.6 %collective-permute-start.47 = (bf16[104,1536]{1,0:T(8,128)(2,1)}, bf16[104,1536]{1,0:T(8,128)(2,1)}, u32[]{:S(2)}, u32[]{:S(2)}) collective-permute-start(bf16[104,1536]{1,0:T(8,128)(2,1)} %slice.371), channel_id=1, source_target_pairs={{0,16},{4,20},{8,24},{12,28},{16,0},{20,4},{24,8},{28,12},{1,17},{... | collective-permute-start | bytes 958472 | tf_op jit(solution)/shard_map/ppermute | solution.py:433
  381.9 19.7 %collective-permute-start.51 = (bf16[256,1536]{1,0:T(8,128)(2,1)S(1)}, bf16[256,1536]{1,0:T(8,128)(2,1)S(1)}, u32[]{:S(2)}, u32[]{:S(2)}) collective-permute-start(bf16[256,1536]{1,0:T(8,128)(2,1)S(1)} %add_convert_fusion.5), channel_id=1, source_target_pairs={{0,1},{1,2},{2,3},{4,5},{5,6},{6,7},{8,9},{9,10},{10,11},{12,13},{... | collective-permute-start | bytes 2359304 | tf_op jit(solution)/shard_map/ppermute | solution.py:445
  385.3 20.9 %collective-permute-start.52 = (bf16[256,1536]{1,0:T(8,128)(2,1)S(1)}, bf16[256,1536]{1,0:T(8,128)(2,1)S(1)}, u32[]{:S(2)}, u32[]{:S(2)}) collective-permute-start(bf16[256,1536]{1,0:T(8,128)(2,1)S(1)} %add_convert_fusion.4), channel_id=1, source_target_pairs={{3,2},{2,1},{1,0},{7,6},{6,5},{5,4},{11,10},{10,9},{9,8},{15,14},{... | collective-permute-start | bytes 2359304 | tf_op jit(solution)/shard_map/ppermute | solution.py:445
  387.7 35.2 %collective-permute-start.48 = (bf16[56,1536]{1,0:T(8,128)(2,1)S(1)}, bf16[56,1536]{1,0:T(8,128)(2,1)S(1)}, u32[]{:S(2)}, u32[]{:S(2)}) collective-permute-start(bf16[56,1536]{1,0:T(8,128)(2,1)S(1)} %get-tuple-element.464), channel_id=1, source_target_pairs={{0,3},{1,0},{2,1},{3,2},{4,7},{5,4},{6,5},{7,6},{8,11},{9,8},{10,9... | collective-permute-start | bytes 516104 | tf_op jit(solution)/shard_map/ppermute | solution.py:438
  394.4 31.3 %collective-permute-start.49 = (bf16[56,1536]{1,0:T(8,128)(2,1)S(1)}, bf16[56,1536]{1,0:T(8,128)(2,1)S(1)}, u32[]{:S(2)}, u32[]{:S(2)}) collective-permute-start(bf16[56,1536]{1,0:T(8,128)(2,1)S(1)} %get-tuple-element.463), channel_id=1, source_target_pairs={{0,2},{1,3},{2,0},{3,1},{4,6},{5,7},{6,4},{7,5},{8,10},{9,11},{10,... | collective-permute-start | bytes 516104 | tf_op jit(solution)/shard_map/ppermute | solution.py:438
  394.4 32.2 %collective-permute-start.50 = (bf16[56,1536]{1,0:T(8,128)(2,1)S(1)}, bf16[56,1536]{1,0:T(8,128)(2,1)S(1)}, u32[]{:S(2)}, u32[]{:S(2)}) collective-permute-start(bf16[56,1536]{1,0:T(8,128)(2,1)S(1)} %get-tuple-element.462), channel_id=1, source_target_pairs={{0,1},{1,2},{2,3},{3,0},{4,5},{5,6},{6,7},{7,4},{8,9},{9,10},{10,1... | collective-permute-start | bytes 516104 | tf_op jit(solution)/shard_map/ppermute | solution.py:438
  409.2 29.0 %collective-permute-start.56 = (bf16[256,1536]{1,0:T(8,128)(2,1)S(1)}, bf16[256,1536]{1,0:T(8,128)(2,1)S(1)}, u32[]{:S(2)}, u32[]{:S(2)}) collective-permute-start(bf16[256,1536]{1,0:T(8,128)(2,1)S(1)} %fusion.20), channel_id=1, source_target_pairs={{0,1},{1,2},{2,3},{4,5},{5,6},{6,7},{8,9},{9,10},{10,11},{12,13},{... | collective-permute-start | bytes 2359304 | tf_op jit(solution)/shard_map/ppermute | solution.py:445
  418.6 19.5 %collective-permute-start.57 = (bf16[256,1536]{1,0:T(8,128)(2,1)S(1)}, bf16[256,1536]{1,0:T(8,128)(2,1)}, u32[]{:S(2)}, u32[]{:S(2)}) collective-permute-start(bf16[256,1536]{1,0:T(8,128)(2,1)S(1)} %fusion.20), channel_id=1, source_target_pairs={{3,2},{2,1},{1,0},{7,6},{6,5},{5,4},{11,10},{10,9},{9,8},{15,14},{... | collective-permute-start | bytes 2359304 | tf_op jit(solution)/shard_map/ppermute | solution.py:445
  422.9 12.6 %collective-permute-start.53 = (f32[1,1536]{1,0:T(1,128)S(1)}, f32[1,1536]{1,0:T(1,128)S(1)}, u32[]{:S(2)}, u32[]{:S(2)}) collective-permute-start(f32[1,1536]{1,0:T(1,128)S(1)} %broadcast_in_dim.61), channel_id=1, source_target_pairs={{0,1},{1,2},{2,3},{3,0},{4,5},{5,6},{6,7},{7,4},{8,9},{9,10},{10,1... | collective-permute-start | bytes 18440 | tf_op jit(solution)/shard_map/ppermute | solution.py:438
  425.6 12.5 %collective-permute-start.54 = (f32[1,1536]{1,0:T(1,128)S(1)}, f32[1,1536]{1,0:T(1,128)S(1)}, u32[]{:S(2)}, u32[]{:S(2)}) collective-permute-start(f32[1,1536]{1,0:T(1,128)S(1)} %broadcast_in_dim.61), channel_id=1, source_target_pairs={{0,2},{1,3},{2,0},{3,1},{4,6},{5,7},{6,4},{7,5},{8,10},{9,11},{10,... | collective-permute-start | bytes 18440 | tf_op jit(solution)/shard_map/ppermute | solution.py:438
  426.6 11.5 %collective-permute-start.55 = (f32[1,1536]{1,0:T(1,128)S(1)}, f32[1,1536]{1,0:T(1,128)S(1)}, u32[]{:S(2)}, u32[]{:S(2)}) collective-permute-start(f32[1,1536]{1,0:T(1,128)S(1)} %broadcast_in_dim.61), channel_id=1, source_target_pairs={{0,3},{1,0},{2,1},{3,2},{4,7},{5,4},{6,5},{7,6},{8,11},{9,8},{10,9... | collective-permute-start | bytes 18440 | tf_op jit(solution)/shard_map/ppermute | solution.py:438
  438.2 11.3 %collective-permute-start.61 = (bf16[256,1536]{1,0:T(8,128)(2,1)S(1)}, bf16[256,1536]{1,0:T(8,128)(2,1)S(1)}, u32[]{:S(2)}, u32[]{:S(2)}) collective-permute-start(bf16[256,1536]{1,0:T(8,128)(2,1)S(1)} %collective-permute-done.56), channel_id=1, source_target_pairs={{1,2},{2,3},{5,6},{6,7},{9,10},{10,11},{13,14},{14,15},{17,18},{18... | collective-permute-start | bytes 2359304 | tf_op jit(solution)/shard_map/ppermute | solution.py:445
  438.9 17.6 %collective-permute-start.62 = (bf16[256,1536]{1,0:T(8,128)(2,1)}, bf16[256,1536]{1,0:T(8,128)(2,1)S(1)}, u32[]{:S(2)}, u32[]{:S(2)}) collective-permute-start(bf16[256,1536]{1,0:T(8,128)(2,1)} %collective-permute-done.57), channel_id=1, source_target_pairs={{2,1},{1,0},{6,5},{5,4},{10,9},{9,8},{14,13},{13,12},{18,17},{17,1... | collective-permute-start | bytes 2359304 | tf_op jit(solution)/shard_map/ppermute | solution.py:445
  440.4 8.4 %collective-permute-start.58 = (bf16[64,1536]{1,0:T(8,128)(2,1)S(1)}, bf16[64,1536]{1,0:T(8,128)(2,1)S(1)}, u32[]{:S(2)}, u32[]{:S(2)}) collective-permute-start(bf16[64,1536]{1,0:T(8,128)(2,1)S(1)} %scatter.4), channel_id=1, source_target_pairs={{0,8},{4,12},{8,0},{12,4},{16,24},{20,28},{24,16},{28,20},{1,9},{5... | collective-permute-start | bytes 589832 | tf_op jit(solution)/shard_map/ppermute | solution.py:433
  441.7 7.8 %collective-permute-start.59 = (bf16[64,1536]{1,0:T(8,128)(2,1)S(1)}, bf16[64,1536]{1,0:T(8,128)(2,1)S(1)}, u32[]{:S(2)}, u32[]{:S(2)}) collective-permute-start(bf16[64,1536]{1,0:T(8,128)(2,1)S(1)} %scatter.4), channel_id=1, source_target_pairs={{0,16},{4,20},{8,24},{12,28},{16,0},{20,4},{24,8},{28,12},{1,17},{... | collective-permute-start | bytes 589832 | tf_op jit(solution)/shard_map/ppermute | solution.py:433
  461.0 22.1 %collective-permute-start.64 = (bf16[256,1536]{1,0:T(8,128)(2,1)}, bf16[256,1536]{1,0:T(8,128)(2,1)}, u32[]{:S(2)}, u32[]{:S(2)}) collective-permute-start(bf16[256,1536]{1,0:T(8,128)(2,1)} %get-tuple-element.453), channel_id=1, source_target_pairs={{2,3},{1,0},{6,7},{5,4},{10,11},{9,8},{14,15},{13,12},{18,19},{17,... | collective-permute-start | bytes 2359304 | tf_op jit(solution)/shard_map/ppermute | solution.py:453
  (75 other events, 692.3 us)
Sparse Core Ops, SparseCore 0:
  47.5 98.2 all-gather.1
  198.5 99.2 reduce-scatter.1
  370.3 63.3 all-reduce.6
